TPU v7x, 32 devices: a whole 2x2x4 slice. The times are simulated.
32 devices in a mesh: dp: 8 (over z, y), blk: 4 (over x, core).
Axes of the slice: x: 2, y: 2, z: 4, core: 2. Of those that a mesh axis runs over, the one named last changes fastest.
Arguments:
- tokens: bfloat16 [8, 1024, 768], P('dp', 'blk'), may hold values from -6 to 6
- segment_ids: int32 [8, 1024], P('dp', 'blk'), may hold values from 0 to 510, as said below
- w_query: bfloat16 [768, 768], P(('dp', 'blk')), may hold values from -0.109375 to 0.109375
- w_key: bfloat16 [768, 768], P(('dp', 'blk')), may hold values from -0.109375 to 0.109375
- w_value: bfloat16 [768, 768], P(('dp', 'blk')), may hold values from -0.21875 to 0.21875
- w_attn_out: bfloat16 [768, 768], P(('dp', 'blk')), may hold values from -1.75 to 1.75
- attn_gain: bfloat16 [768], P(('dp', 'blk')), may hold values from 0.099609375 to 1.8984375
- rel_bias: bfloat16 [32, 12], replicated, may hold values from -4 to 4
- w_gate: bfloat16 [768, 2048], P(('dp', 'blk')), may hold values from -0.21875 to 0.21875
- w_up: bfloat16 [768, 2048], P(('dp', 'blk')), may hold values from -0.21875 to 0.21875
- w_down: bfloat16 [2048, 768], P(('dp', 'blk')), may hold values from -0.125 to 0.125
- ffn_gain: bfloat16 [768], P(('dp', 'blk')), may hold values from 0.099609375 to 1.8984375
- cotangent: bfloat16 [8, 1024, 768], P('dp', 'blk'), may hold values from -6 to 6
Outputs:
- layer_out: bfloat16 [8, 1024, 768], P('dp', 'blk')
- tokens_grad: float32 [8, 1024, 768], P('dp', 'blk')
- w_query_grad: float32 [768, 768], P(('dp', 'blk'))
- w_key_grad: float32 [768, 768], P(('dp', 'blk'))
- w_value_grad: float32 [768, 768], P(('dp', 'blk'))
- w_attn_out_grad: float32 [768, 768], P(('dp', 'blk'))
- attn_gain_grad: float32 [768], P(('dp', 'blk'))
- rel_bias_grad: float32 [32, 12], replicated
- w_gate_grad: float32 [768, 2048], P(('dp', 'blk'))
- w_up_grad: float32 [768, 2048], P(('dp', 'blk'))
- w_down_grad: float32 [2048, 768], P(('dp', 'blk'))
- ffn_gain_grad: float32 [768], P(('dp', 'blk'))
Inputs may be any that keep to these rules, and one draw needn't show every extreme that they name: `segment_ids`: segment ids start at 0 in each row, never fall along it, and end at 510 in each row; ids need not be consecutive. Each row holds one document that begins within its first 256 tokens and ends within its last 256 tokens; every other document is shorter than 256 tokens.
All inputs are finite; a program needn't handle non-finite values.
Results may differ from a plain program's by a relative error of at most 0.02.
Values may be sent and summed in bfloat16 or wider, within the bound.
No kernel may reach another device: no remote copies, remote signals or barrier semaphores. Data moves between devices by JAX's collectives and lax.ppermute only.
A program may use at most 128 MiB of HBM per device.

v0:
```python
import math

import jax
import jax.numpy as jnp
from jax import lax
from jax.sharding import PartitionSpec as P

H = 12
DH = 64
NB = 32


THRESHOLDS = (12, 16, 23, 32, 46, 64, 91)
MASKED = -1e30
EPSILON = 1e-06
KEY_BLOCK = 256
HIGHEST = lax.Precision.HIGHEST


def bucket_of(relative):
    distance = jnp.abs(relative)
    far_bucket = 8 + sum([(distance >= threshold).astype(jnp.int32) for threshold in THRESHOLDS])
    near_bucket = jnp.where(distance < 8, distance, far_bucket)
    return jnp.where(relative > 0, NB // 2, 0) + near_bucket


def rms_norm(values, gain):
    return values * lax.rsqrt(jnp.mean(values * values, axis=-1, keepdims=True) + EPSILON) * gain


def split_heads(flat_rows):
    return flat_rows.reshape(flat_rows.shape[0], flat_rows.shape[1], H, DH)


def join_heads(per_head):
    return per_head.reshape(per_head.shape[0], per_head.shape[1], H * DH)


def project(left, matrix):
    return jnp.einsum("rtd,de->rte", left, matrix, preferred_element_type=jnp.float32)


def project_back(left, matrix):
    return jnp.einsum("rte,de->rtd", left, matrix, preferred_element_type=jnp.float32)


def weight_grad(left, right):
    return jnp.einsum("rtd,rte->de", left, right, preferred_element_type=jnp.float32)


def block_scores(queries, key_block, query_pos, key_pos, query_seg, key_seg, bias_table):
    raw_scores = jnp.einsum(
        "rqhd,rkhd->rhqk", queries, key_block, preferred_element_type=jnp.float32
    )
    buckets = bucket_of(key_pos[None, :] - query_pos[:, None])
    one_hot = (buckets[:, :, None] == jnp.arange(NB, dtype=jnp.int32)[None, None, :]).astype(
        jnp.float32
    )
    rel_term = jnp.einsum("qkb,bh->hqk", one_hot, bias_table, precision=HIGHEST)
    allowed = (query_seg[:, :, None] == key_seg[:, None, :])[:, None]
    return (raw_scores + rel_term[None], allowed, one_hot)


def absorb(
    running, queries, key_block, value_block, query_pos, key_pos, query_seg, key_seg, bias_table
):
    row_peak, row_total, weighted = running
    scores, allowed, unused = block_scores(
        queries, key_block, query_pos, key_pos, query_seg, key_seg, bias_table
    )
    block_peak = jnp.max(jnp.where(allowed, scores, MASKED), axis=-1)
    new_peak = jnp.maximum(row_peak, block_peak)
    weights = jnp.where(allowed, jnp.exp(scores - new_peak[..., None]), 0.0)
    factor = jnp.exp(row_peak - new_peak)
    row_total = row_total * factor + jnp.sum(weights, axis=-1)
    weighted = weighted * factor[..., None] + jnp.einsum(
        "rhqk,rkhd->rhqd",
        weights.astype(jnp.bfloat16),
        value_block,
        preferred_element_type=jnp.float32,
    )
    return (new_peak, row_total, weighted)


def pair_grads(
    queries,
    out_grad,
    log_total,
    row_delta,
    key_block,
    value_block,
    query_pos,
    key_pos,
    query_seg,
    key_seg,
    bias_table,
):
    scores, allowed, one_hot = block_scores(
        queries, key_block, query_pos, key_pos, query_seg, key_seg, bias_table
    )
    prob_map = jnp.where(allowed, jnp.exp(scores - log_total[..., None]), 0.0)
    prob_grad = jnp.einsum(
        "rqhd,rkhd->rhqk", out_grad, value_block, preferred_element_type=jnp.float32
    )
    score_grad = prob_map * (prob_grad - row_delta[..., None])
    score_low = score_grad.astype(jnp.bfloat16)
    query_grad = jnp.einsum(
        "rhqk,rkhd->rqhd", score_low, key_block, preferred_element_type=jnp.float32
    )
    key_grad = jnp.einsum("rhqk,rqhd->rkhd", score_low, queries, preferred_element_type=jnp.float32)
    value_grad = jnp.einsum(
        "rhqk,rqhd->rkhd",
        prob_map.astype(jnp.bfloat16),
        out_grad,
        preferred_element_type=jnp.float32,
    )
    table_grad = jnp.einsum("rhqk,qkb->bh", score_grad, one_hot, precision=HIGHEST)
    return (query_grad, key_grad, value_grad, table_grad)


def in_blocks(step_fn, running, pieces):
    length = pieces[0].shape[1]
    block_size = math.gcd(length, KEY_BLOCK)
    block_count = length // block_size
    stacked = tuple(
        (
            jnp.moveaxis(
                member.reshape((member.shape[0], block_count, block_size) + member.shape[2:]), 1, 0
            )
            for member in pieces
        )
    )
    starts = block_size * jnp.arange(block_count, dtype=jnp.int32)

    def scan_step(inner_state, item_pair):
        return (step_fn(inner_state, item_pair[0], item_pair[1]), None)

    running, unused = lax.scan(scan_step, running, (stacked, starts))
    return running


def local(
    tokens,
    segment_ids,
    w_query,
    w_key,
    w_value,
    w_attn_out,
    attn_gain,
    rel_bias,
    w_gate,
    w_up,
    w_down,
    ffn_gain,
    cotangent,
):
    row_count, local_len, unused_dim = tokens.shape
    my_block = lax.axis_index("blk")
    full_query, full_key, full_value, full_out, gain_one = (
        lax.all_gather(w_query, ("dp", "blk"), axis=0, tiled=True),
        lax.all_gather(w_key, ("dp", "blk"), axis=0, tiled=True),
        lax.all_gather(w_value, ("dp", "blk"), axis=0, tiled=True),
        lax.all_gather(w_attn_out, ("dp", "blk"), axis=0, tiled=True),
        lax.all_gather(attn_gain, ("dp", "blk"), axis=0, tiled=True),
    )
    full_gate, full_up, full_down, gain_two = (
        lax.all_gather(w_gate, ("dp", "blk"), axis=0, tiled=True),
        lax.all_gather(w_up, ("dp", "blk"), axis=0, tiled=True),
        lax.all_gather(w_down, ("dp", "blk"), axis=0, tiled=True),
        lax.all_gather(ffn_gain, ("dp", "blk"), axis=0, tiled=True),
    )
    row_segs = lax.all_gather(segment_ids, "blk", axis=1, tiled=True)
    bias_table = rel_bias.astype(jnp.float32)
    gain_one_f = gain_one.astype(jnp.float32)
    gain_two_f = gain_two.astype(jnp.float32)
    inputs = tokens.astype(jnp.float32)
    query_pos = my_block * local_len + jnp.arange(local_len, dtype=jnp.int32)
    normed_one = rms_norm(inputs, gain_one_f).astype(jnp.bfloat16)
    query_flat = project(normed_one, full_query).astype(jnp.bfloat16)
    key_flat = project(normed_one, full_key).astype(jnp.bfloat16)
    value_flat = project(normed_one, full_value).astype(jnp.bfloat16)
    queries = split_heads(query_flat)
    key_heads = split_heads(key_flat)
    value_heads = split_heads(value_flat)

    def forward_piece(running, pieces):

        def step_fn(inner_state, blocks, block_start):
            block_len = blocks[0].shape[1]
            key_pos = block_start + jnp.arange(block_len, dtype=jnp.int32)
            key_seg = lax.dynamic_slice_in_dim(row_segs, block_start, block_len, 1)
            return absorb(
                inner_state,
                queries,
                split_heads(blocks[0]),
                split_heads(blocks[1]),
                query_pos,
                key_pos,
                segment_ids,
                key_seg,
                bias_table,
            )

        return in_blocks(step_fn, running, pieces)

    stat_shape = (row_count, H, local_len)
    start_state = (
        jnp.full(stat_shape, MASKED, jnp.float32),
        jnp.zeros(stat_shape, jnp.float32),
        jnp.zeros(stat_shape + (DH,), jnp.float32),
    )
    row_peak, row_total, weighted = forward_piece(
        start_state,
        (
            lax.all_gather(key_flat, "blk", axis=1, tiled=True),
            lax.all_gather(value_flat, "blk", axis=1, tiled=True),
        ),
    )
    log_total = row_peak + jnp.log(row_total)
    attended_f = jnp.transpose(weighted / row_total[..., None], (0, 2, 1, 3))
    attended = join_heads(attended_f).astype(jnp.bfloat16)
    mixed_in = inputs + project(attended, full_out)
    normed_two = rms_norm(mixed_in, gain_two_f).astype(jnp.bfloat16)
    gate_act = project(normed_two, full_gate)
    up_act = project(normed_two, full_up)

    def gated(gate_in, up_in):
        return jax.nn.gelu(gate_in, approximate=True) * up_in

    hidden_f, gated_back = jax.vjp(gated, gate_act, up_act)
    hidden = hidden_f.astype(jnp.bfloat16)
    layer_out = (mixed_in + project(hidden, full_down)).astype(jnp.bfloat16)
    down_grad = weight_grad(hidden, cotangent)
    hidden_grad = project_back(cotangent, full_down)
    gate_grad, up_grad = gated_back(hidden_grad)
    gate_low = gate_grad.astype(jnp.bfloat16)
    up_low = up_grad.astype(jnp.bfloat16)
    gate_w_grad = weight_grad(normed_two, gate_low)
    up_w_grad = weight_grad(normed_two, up_low)
    two_grad = project_back(gate_low, full_gate) + project_back(up_low, full_up)
    unused_two, norm_two_back = jax.vjp(rms_norm, mixed_in, gain_two_f)
    mixed_part, gain_two_grad = norm_two_back(two_grad)
    mixed_grad = cotangent.astype(jnp.float32) + mixed_part
    mixed_low = mixed_grad.astype(jnp.bfloat16)
    out_w_grad = weight_grad(attended, mixed_low)
    attended_grad = project_back(mixed_low, full_out).astype(jnp.bfloat16)
    grad_heads = split_heads(attended_grad)
    row_delta = jnp.sum(
        jnp.transpose(grad_heads.astype(jnp.float32), (0, 2, 1, 3))
        * (weighted / row_total[..., None]),
        axis=-1,
    )
    zero_heads = jnp.zeros(queries.shape, jnp.float32)
    zero_table = jnp.zeros((NB, H), jnp.float32)

    def query_piece(running, pieces):

        def step_fn(inner_state, blocks, block_start):
            block_len = blocks[0].shape[1]
            key_pos = block_start + jnp.arange(block_len, dtype=jnp.int32)
            key_seg = lax.dynamic_slice_in_dim(row_segs, block_start, block_len, 1)
            pair_parts = pair_grads(
                queries,
                grad_heads,
                log_total,
                row_delta,
                split_heads(blocks[0]),
                split_heads(blocks[1]),
                query_pos,
                key_pos,
                segment_ids,
                key_seg,
                bias_table,
            )
            return inner_state + pair_parts[0]

        return in_blocks(step_fn, running, pieces)

    query_grad = join_heads(
        query_piece(
            zero_heads,
            (
                lax.all_gather(key_flat, "blk", axis=1, tiled=True),
                lax.all_gather(value_flat, "blk", axis=1, tiled=True),
            ),
        )
    )
    log_rows, delta_rows = (
        lax.all_gather(log_total, "blk", axis=2, tiled=True),
        lax.all_gather(row_delta, "blk", axis=2, tiled=True),
    )

    def key_piece(running, pieces):

        def step_fn(inner_state, blocks, block_start):
            block_len = blocks[0].shape[1]
            piece_pos = block_start + jnp.arange(block_len, dtype=jnp.int32)
            piece_seg = lax.dynamic_slice_in_dim(row_segs, block_start, block_len, 1)
            piece_log = lax.dynamic_slice_in_dim(log_rows, block_start, block_len, 2)
            piece_delta = lax.dynamic_slice_in_dim(delta_rows, block_start, block_len, 2)
            pair_parts = pair_grads(
                split_heads(blocks[0]),
                split_heads(blocks[1]),
                piece_log,
                piece_delta,
                key_heads,
                value_heads,
                piece_pos,
                query_pos,
                piece_seg,
                segment_ids,
                bias_table,
            )
            return (
                inner_state[0] + pair_parts[1],
                inner_state[1] + pair_parts[2],
                inner_state[2] + pair_parts[3],
            )

        return in_blocks(step_fn, running, pieces)

    key_grad, value_grad, table_grad = key_piece(
        (zero_heads, zero_heads, zero_table),
        (
            lax.all_gather(query_flat, "blk", axis=1, tiled=True),
            lax.all_gather(attended_grad, "blk", axis=1, tiled=True),
        ),
    )
    query_low = query_grad.astype(jnp.bfloat16)
    key_low = join_heads(key_grad).astype(jnp.bfloat16)
    value_low = join_heads(value_grad).astype(jnp.bfloat16)
    query_w_grad = weight_grad(normed_one, query_low)
    key_w_grad = weight_grad(normed_one, key_low)
    value_w_grad = weight_grad(normed_one, value_low)
    one_grad = (
        project_back(query_low, full_query)
        + project_back(key_low, full_key)
        + project_back(value_low, full_value)
    )
    unused_one, norm_one_back = jax.vjp(rms_norm, inputs, gain_one_f)
    input_part, gain_one_grad = norm_one_back(one_grad)
    tokens_grad = mixed_grad + input_part
    table_sum = lax.psum(table_grad, ("dp", "blk"))
    all_sums = (
        lax.psum_scatter(query_w_grad, ("dp", "blk"), scatter_dimension=0, tiled=True),
        lax.psum_scatter(key_w_grad, ("dp", "blk"), scatter_dimension=0, tiled=True),
        lax.psum_scatter(value_w_grad, ("dp", "blk"), scatter_dimension=0, tiled=True),
        lax.psum_scatter(out_w_grad, ("dp", "blk"), scatter_dimension=0, tiled=True),
        lax.psum_scatter(gain_one_grad, ("dp", "blk"), scatter_dimension=0, tiled=True),
        lax.psum_scatter(gate_w_grad, ("dp", "blk"), scatter_dimension=0, tiled=True),
        lax.psum_scatter(up_w_grad, ("dp", "blk"), scatter_dimension=0, tiled=True),
        lax.psum_scatter(down_grad, ("dp", "blk"), scatter_dimension=0, tiled=True),
        lax.psum_scatter(gain_two_grad, ("dp", "blk"), scatter_dimension=0, tiled=True),
    )
    return (
        layer_out,
        tokens_grad,
        all_sums[0],
        all_sums[1],
        all_sums[2],
        all_sums[3],
        all_sums[4],
        table_sum,
        all_sums[5],
        all_sums[6],
        all_sums[7],
        all_sums[8],
    )


def solution(mesh):
    placed = (
        P("dp", "blk", None),
        P("dp", "blk"),
        P(("dp", "blk"), None),
        P(("dp", "blk"), None),
        P(("dp", "blk"), None),
        P(("dp", "blk"), None),
        P(("dp", "blk")),
        P(),
        P(("dp", "blk"), None),
        P(("dp", "blk"), None),
        P(("dp", "blk"), None),
        P(("dp", "blk")),
        P("dp", "blk", None),
    )
    return jax.shard_map(
        local,
        mesh=mesh,
        in_specs=placed,
        out_specs=(
            P("dp", "blk", None),
            P("dp", "blk", None),
            P(("dp", "blk"), None),
            P(("dp", "blk"), None),
            P(("dp", "blk"), None),
            P(("dp", "blk"), None),
            P(("dp", "blk")),
            P(),
            P(("dp", "blk"), None),
            P(("dp", "blk"), None),
            P(("dp", "blk"), None),
            P(("dp", "blk")),
        ),
        check_vma=False,
    )
```

profile of v0, /device:TPU:0, one launch (start us, length us, event | category | flops | bytes accessed | tf_op | source)
XLA Modules:
  0.0 1351.2 jit_solution(6200037508255293345)
XLA Ops:
  11.2 42.1 %all-reduce.5 = (bf16[768]{0:T(1024)(128)(2,1)S(1)}, bf16[768]{0:T(1024)(128)(2,1)S(1)}) all-reduce(bf16[768]{0:T(1024)(128)(2,1)S(1)} %dynamic-update-slice, bf16[768]{0:T(1024)(128)(2,1)S(1)} %dynamic-update-slice.1), channel_id=1, replica_groups=mesh['dp'=8,'blk'=4] {'dp','blk'}, use_global_device_ids=true, to_apply=%add | all-reduce | flops 1536 | bytes 6144
  54.4 13.4 all-gather.17.cloned.1.call-done
  70.6 53.2 %all-gather.21.cloned.1.call-done = bf16[768,768]{1,0:T(8,128)(2,1)} async-done(((bf16[24,768]{1,0:T(8,128)(2,1)}), bf16[768,768]{1,0:T(8,128)(2,1)}) %all-gather.21.cloned.1.call-update) | async-done | bytes 1179664 | tf_op jit(solution)/shard_map/all_gather | solution.py:162
  129.8 5.5 all_gather.50
  135.8 43.8 %all-gather.19.cloned.1.call-done = bf16[768,768]{1,0:T(8,128)(2,1)} async-done(((bf16[24,768]{1,0:T(8,128)(2,1)}), bf16[768,768]{1,0:T(8,128)(2,1)}) %all-gather.19.cloned.1.call-update) | async-done | bytes 1179664 | tf_op jit(solution)/shard_map/all_gather | solution.py:160
  182.6 17.6 %all-gather.31.cloned.1.call-done = bf16[1024,768]{1,0:T(8,128)(2,1)} async-done(((bf16[256,768]{1,0:T(8,128)(2,1)}), bf16[1024,768]{1,0:T(8,128)(2,1)}) %all-gather.31.cloned.1.call-update) | async-done | bytes 1572880 | tf_op jit(solution)/shard_map/all_gather | solution.py:215
  202.8 18.5 %all-gather.33.cloned.1.call-done = bf16[1024,768]{1,0:T(8,128)(2,1)} async-done(((bf16[256,768]{1,0:T(8,128)(2,1)}), bf16[1024,768]{1,0:T(8,128)(2,1)}) %all-gather.33.cloned.1.call-update) | async-done | bytes 1572880 | tf_op jit(solution)/shard_map/all_gather | solution.py:216
  223.9 95.8 %while.41 = (s32[]{:T(128)}, f32[1,12,256]{2,1,0:T(8,128)}, f32[1,12,256]{2,1,0:T(8,128)}, f32[1,12,256,64]{2,3,1,0:T(8,128)}, s32[1,256]{1,0:T(1,128)S(1)}, /*i...) while((s32[]{:T(128)}, f32[1,12,256]{2,1,0:T(8,128)}, ...), condition=%wide.region_4.5_spmd.clone, body=%wide.region_1.4_spmd.clone.sunk | while | flops 515000832 | bytes 34039684 | solution.py:138
  324.1 14.9 %all-gather.25.cloned.1.call-done = bf16[768,2048]{1,0:T(8,128)(2,1)} async-done(((bf16[24,2048]{1,0:T(8,128)(2,1)}), bf16[768,2048]{1,0:T(8,128)(2,1)}) %all-gather.25.cloned.1.call-update) | async-done | bytes 3145744 | tf_op jit(solution)/shard_map/all_gather | solution.py:167
  343.1 56.5 %all-gather.27.cloned.1.call-done = bf16[768,2048]{1,0:T(8,128)(2,1)} async-done(((bf16[24,2048]{1,0:T(8,128)(2,1)}), bf16[768,2048]{1,0:T(8,128)(2,1)}) %all-gather.27.cloned.1.call-update) | async-done | bytes 3145744 | tf_op jit(solution)/shard_map/all_gather | solution.py:168
  403.8 56.4 %all-gather.29.cloned.1.call-done = bf16[2048,768]{1,0:T(8,128)(2,1)} async-done(((bf16[64,768]{1,0:T(8,128)(2,1)}), bf16[2048,768]{1,0:T(8,128)(2,1)}) %all-gather.29.cloned.1.call-update) | async-done | bytes 3145744 | tf_op jit(solution)/shard_map/all_gather | solution.py:169
  460.3 6.5 multiply_convert_fusion
  476.1 91.7 %while.42 = (s32[]{:T(128)}, f32[1,256,12,64]{1,3,2,0:T(8,128)}, bf16[4,1,256,768]{2,3,1,0:T(8,128)(2,1)}, s32[1,256]{1,0:T(1,128)S(1)}, s32[4]{0:T(128)}, /*ind...) while((s32[]{:T(128)}, f32[1,256,12,64]{1,3,2,0:T(8,128)}, ...), condition=%wide.region_9.10_spmd.clone, body=%wide.region_8.9_spmd.clone.sunk | while | flops 613089792 | bytes 24676068 | solution.py:138
  575.0 5.4 all_gather.63
  580.4 5.2 all-gather.4
  587.7 173.6 %while.43 = (s32[]{:T(128)}, f32[1,256,12,64]{1,3,2,0:T(8,128)}, f32[1,256,12,64]{1,3,2,0:T(8,128)}, f32[32,12]{0,1:T(8,128)S(1)}, bf16[4,1,256,768]{3,2,0,1:T(8...) while((s32[]{:T(128)}, f32[1,256,12,64]{1,3,2,0:T(8,128)}, ...), condition=%wide.region_11.12_spmd.clone, body=%wide.region_10.11_spmd.clone.sunk | while | flops 1019020544 | bytes 51864544 | solution.py:138
  596.9 5.0 copy.87
  618.6 5.2 copy.89
  623.8 6.2 fusion.252
  639.3 5.1 copy.87
  662.3 5.2 copy.89
  667.5 6.2 fusion.252
  706.0 5.3 copy.89
  711.3 6.2 fusion.252
  749.8 5.2 copy.89
  755.0 6.2 fusion.252
  790.9 38.3 %all-reduce.4 = (f32[768]{0:T(1024)S(1)}, f32[32,12]{0,1:T(8,128)}, f32[768]{0:T(1024)S(1)}) all-reduce(f32[768]{0:T(1024)S(1)} %get-tuple-element.489, f32[32,12]{0,1:T(8,128)S(1)} %get-tuple-element.1086, f32[768]{0:T(1024)S(1)} %copy-done.56), channel_id=11, replica_groups=mesh['dp'=8,'blk'=4] {'dp','blk'}, use_global_device_ids=true, to_apply=%region_18.19.clone | all-reduce | flops 1920 | bytes 15360
  831.5 47.9 %reduce-scatter.10.cloned.1.call-done = f32[24,768]{1,0:T(8,128)} async-done(((f32[768,768]{1,0:T(8,128)}), f32[24,768]{1,0:T(8,128)}) %reduce-scatter.10.cloned.1.call-update) | async-done | bytes 73744 | tf_op jit(solution)/shard_map/reduce_scatter | solution.py:346
  879.4 104.5 %reduce-scatter.12.cloned.1.call-done = f32[24,768]{1,0:T(8,128)} async-done(((f32[768,768]{1,0:T(8,128)}), f32[24,768]{1,0:T(8,128)}) %reduce-scatter.12.cloned.1.call-update) | async-done | bytes 73744 | tf_op jit(solution)/shard_map/reduce_scatter | solution.py:347
  983.9 119.4 %reduce-scatter.16.cloned.1.call-done = f32[24,2048]{1,0:T(8,128)} async-done(((f32[768,2048]{1,0:T(8,128)}), f32[24,2048]{1,0:T(8,128)}) %reduce-scatter.16.cloned.1.call-update) | async-done | bytes 196624 | tf_op jit(solution)/shard_map/reduce_scatter | solution.py:350
  1103.3 120.8 %reduce-scatter.18.cloned.1.call-done = f32[24,2048]{1,0:T(8,128)} async-done(((f32[768,2048]{1,0:T(8,128)}), f32[24,2048]{1,0:T(8,128)}) %reduce-scatter.18.cloned.1.call-update) | async-done | bytes 196624 | tf_op jit(solution)/shard_map/reduce_scatter | solution.py:351
  1224.1 119.9 %reduce-scatter.20.cloned.1.call-done = f32[64,768]{1,0:T(8,128)} async-done(((f32[2048,768]{1,0:T(8,128)}), f32[64,768]{1,0:T(8,128)}) %reduce-scatter.20.cloned.1.call-update) | async-done | bytes 196624 | tf_op jit(solution)/shard_map/reduce_scatter | solution.py:352
  (456 shorter events, 366.1 us)
Async XLA Ops:
  7.2 116.6 %copy-start.7 = (bf16[1,256,768]{2,1,0:T(8,128)(2,1)S(1)}, bf16[1,256,768]{2,1,0:T(8,128)(2,1)}, u32[]{:S(2)}) copy-start(bf16[1,256,768]{2,1,0:T(8,128)(2,1)} %param.19) | copy-start | bytes 1179652
  7.2 122.0 %copy-start.59 = (bf16[32,12]{0,1:T(8,128)(2,1)S(1)}, bf16[32,12]{0,1:T(8,128)(2,1)}, u32[]{:S(2)}) copy-start(bf16[32,12]{0,1:T(8,128)(2,1)} %param.26) | copy-start | bytes 2308
  7.2 122.6 %copy-start.47 = (s32[1,256]{1,0:T(1,128)S(1)}, s32[1,256]{1,0:T(1,128)}, u32[]{:S(2)}) copy-start(s32[1,256]{1,0:T(1,128)} %param.20) | copy-start | bytes 3076
  7.2 60.6 %all-gather.17.cloned.1.call-start = ((), (), s32[]{:S(2)}) async-start(), calls=%async_computation.7 | async-start | bytes 1216512 | tf_op jit(solution)/shard_map/all_gather | solution.py:161
  7.9 115.8 %all-gather.21.cloned.1.call-start = ((), (), s32[]{:S(2)}) async-start(), calls=%async_computation.9 | async-start | bytes 1216512 | tf_op jit(solution)/shard_map/all_gather | solution.py:162
  8.7 170.9 %all-gather.19.cloned.1.call-start = ((), (), s32[]{:S(2)}) async-start(), calls=%async_computation.8 | async-start | bytes 1216512 | tf_op jit(solution)/shard_map/all_gather | solution.py:160
  9.4 190.8 %all-gather.31.cloned.1.call-start = ((), (), s32[]{:S(2)}) async-start(), calls=%async_computation.21 | async-start | bytes 1966080 | tf_op jit(solution)/shard_map/all_gather | solution.py:215
  53.2 515.8 %copy-start.51 = (f32[768]{0:T(1024)}, f32[768]{0:T(1024)S(1)}, u32[]{:S(2)}) copy-start(f32[768]{0:T(1024)S(1)} %convert_element_type.287) | copy-start | bytes 9220
  54.4 81.4 %copy-start.57 = (f32[256]{0:T(256)}, f32[256]{0:T(256)S(1)}, u32[]{:S(2)}) copy-start(f32[256]{0:T(256)S(1)} %fusion.107) | copy-start | bytes 3076
  54.4 127.0 %copy-start.54 = (f32[256]{0:T(256)}, f32[256]{0:T(256)S(1)}, u32[]{:S(2)}) copy-start(f32[256]{0:T(256)S(1)} %fusion.124) | copy-start | bytes 3076
  70.5 150.8 %all-gather.33.cloned.1.call-start = ((), (), s32[]{:S(2)}) async-start(), calls=%async_computation.22 | async-start | bytes 1966080 | tf_op jit(solution)/shard_map/all_gather | solution.py:216
  126.3 194.7 %all-gather.23.cloned.1.call-start = ((), (), s32[]{:S(2)}) async-start(), calls=%async_computation.10 | async-start | bytes 1216512 | tf_op jit(solution)/shard_map/all_gather | solution.py:163
  126.9 212.1 %all-gather.25.cloned.1.call-start = ((), (), s32[]{:S(2)}) async-start(), calls=%async_computation.11 | async-start | bytes 3244032 | tf_op jit(solution)/shard_map/all_gather | solution.py:167
  127.6 272.0 %all-gather.27.cloned.1.call-start = ((), (), s32[]{:S(2)}) async-start(), calls=%async_computation.12 | async-start | bytes 3244032 | tf_op jit(solution)/shard_map/all_gather | solution.py:168
  128.4 331.9 %all-gather.29.cloned.1.call-start = ((), (), s32[]{:S(2)}) async-start(), calls=%async_computation.13 | async-start | bytes 3244032 | tf_op jit(solution)/shard_map/all_gather | solution.py:169
  129.1 458.5 %all-gather.35.cloned.1.call-start = ((), (), s32[]{:S(2)}) async-start(), calls=%async_computation.23 | async-start | bytes 1966080 | tf_op jit(solution)/shard_map/all_gather | solution.py:325
  182.4 405.2 %all-gather.37.cloned.1.call-start = ((), (), s32[]{:S(2)}) async-start(), calls=%async_computation.24 | async-start | bytes 1966080 | tf_op jit(solution)/shard_map/all_gather | solution.py:326
  323.2 148.2 %copy-start.12 = (f32[1,256,768]{2,1,0:T(8,128)}, f32[1,256,768]{2,1,0:T(8,128)S(1)}, u32[]{:S(2)}) copy-start(f32[1,256,768]{2,1,0:T(8,128)S(1)} %get-tuple-element.598) | copy-start | bytes 2359300
  324.1 79.8 %copy-start.9 = (bf16[256,768]{1,0:T(8,128)(2,1)}, bf16[256,768]{1,0:T(8,128)(2,1)S(1)}, u32[]{:S(2)}) copy-start(bf16[256,768]{1,0:T(8,128)(2,1)S(1)} %fusion.112) | copy-start | bytes 1179652
  343.1 117.1 %copy-start.29 = (bf16[1,256,768]{2,1,0:T(8,128)(2,1)S(1)}, bf16[1,256,768]{2,1,0:T(8,128)(2,1)}, u32[]{:S(2)}) copy-start(bf16[1,256,768]{2,1,0:T(8,128)(2,1)} %param.31) | copy-start | bytes 1179652
  475.8 355.7 %reduce-scatter.8.cloned.1.call-start = ((), (), s32[]{:S(2)}) async-start(), calls=%async_computation.14 | async-start | bytes 2433024 | tf_op jit(solution)/shard_map/reduce_scatter | solution.py:345
  573.0 258.4 %reduce-scatter.14.cloned.1.call-start = ((), (), s32[]{:S(2)}) async-start(), calls=%async_computation.17 | async-start | bytes 2433024 | tf_op jit(solution)/shard_map/reduce_scatter | solution.py:348
  587.5 291.8 %reduce-scatter.10.cloned.1.call-start = ((), (), s32[]{:S(2)}) async-start(), calls=%async_computation.15 | async-start | bytes 2433024 | tf_op jit(solution)/shard_map/reduce_scatter | solution.py:346
  587.7 16.2 %copy-start.43 = (f32[1,12,1024]{2,1,0:T(8,128)}, f32[1,12,1024]{2,1,0:T(8,128)S(1)}, u32[]{:S(2)}) copy-start(f32[1,12,1024]{2,1,0:T(8,128)S(1)} %get-tuple-element.1019) | copy-start | bytes 147460 | tf_op jit(solution)/shard_map/while
  630.0 16.3 %copy-start.43 = (f32[1,12,1024]{2,1,0:T(8,128)}, f32[1,12,1024]{2,1,0:T(8,128)S(1)}, u32[]{:S(2)}) copy-start(f32[1,12,1024]{2,1,0:T(8,128)S(1)} %get-tuple-element.1019) | copy-start | bytes 147460 | tf_op jit(solution)/shard_map/while
  630.0 16.2 %copy-start.45 = (f32[1,12,1024]{2,1,0:T(8,128)}, f32[1,12,1024]{2,1,0:T(8,128)S(1)}, u32[]{:S(2)}) copy-start(f32[1,12,1024]{2,1,0:T(8,128)S(1)} %get-tuple-element.1022) | copy-start | bytes 147460 | tf_op jit(solution)/shard_map/while
  765.7 218.1 %reduce-scatter.12.cloned.1.call-start = ((), (), s32[]{:S(2)}) async-start(), calls=%async_computation.16 | async-start | bytes 2433024 | tf_op jit(solution)/shard_map/reduce_scatter | solution.py:347
  769.1 334.2 %reduce-scatter.16.cloned.1.call-start = ((), (), s32[]{:S(2)}) async-start(), calls=%async_computation.18 | async-start | bytes 6488064 | tf_op jit(solution)/shard_map/reduce_scatter | solution.py:350
  772.9 451.2 %reduce-scatter.18.cloned.1.call-start = ((), (), s32[]{:S(2)}) async-start(), calls=%async_computation.19 | async-start | bytes 6488064 | tf_op jit(solution)/shard_map/reduce_scatter | solution.py:351
  777.8 566.1 %reduce-scatter.20.cloned.1.call-start = ((), (), s32[]{:S(2)}) async-start(), calls=%async_computation.20 | async-start | bytes 6488064 | tf_op jit(solution)/shard_map/reduce_scatter | solution.py:352
  789.7 40.7 %copy-start.58 = (f32[256]{0:T(256)S(1)}, f32[256]{0:T(256)}, u32[]{:S(2)}) copy-start(f32[256]{0:T(256)} %copy-done.57) | copy-start | bytes 3076
  789.7 40.7 %copy-start.16 = (f32[1,256,768]{2,1,0:T(8,128)S(1)}, f32[1,256,768]{2,1,0:T(8,128)}, u32[]{:S(2)}) copy-start(f32[1,256,768]{2,1,0:T(8,128)} %copy-done.14) | copy-start | bytes 2359300
  (88 other events, 400.7 us)
Sparse Core Ops, SparseCore 0:
  10.9 56.8 all-gather.16
  70.7 52.9 all-gather.20
  126.6 52.9 all-gather.18
  181.6 18.5 all-gather.30
  201.6 19.6 all-gather.32
  224.1 54.0 all-gather.22
  281.0 57.8 all-gather.24
  341.8 57.7 all-gather.26
  402.5 57.7 all-gather.28
  461.7 18.4 all-gather.34
  481.7 19.6 all-gather.36
  573.2 97.7 reduce-scatter.7
  677.7 97.8 reduce-scatter.13
  781.3 98.0 reduce-scatter.9
  885.9 97.8 reduce-scatter.11
  989.9 113.3 reduce-scatter.15
  1110.3 113.7 reduce-scatter.17
  1230.2 113.7 reduce-scatter.19
where the time goes:
time: 1360 us; the launch traced here: 1350 us
  waiting for transfers between devices  792 us (58%)
  matrix products  227 us (17%)
  local copies, waits for them, and re-layouts  157 us (12%)
  blocking collectives  96.4 us (7%)
  other arithmetic  38.2 us (3%)
  loops' own time  24.3 us (2%)
  between operations  15.3 us (1%)
    reduce_scatter x1, waiting for transfers between devices, local(): lax.psum_scatter(up_w_grad, ('dp', 'blk'), scatter_dimension=0, tiled=True)  121 us
    reduce_scatter x1, waiting for transfers between devices, local(): lax.psum_scatter(down_grad, ('dp', 'blk'), scatter_dimension=0, tiled=True)  120 us
    reduce_scatter x1, waiting for transfers between devices, local(): lax.psum_scatter(gate_w_grad, ('dp', 'blk'), scatter_dimension=0, tiled=T...  119 us
    reduce_scatter x1, waiting for transfers between devices, local(): lax.psum_scatter(value_w_grad, ('dp', 'blk'), scatter_dimension=0, tiled=...  104 us
    unnamed x2, blocking collectives  80.3 us
    all_gather x1, waiting for transfers between devices, local(): lax.all_gather(w_up, ('dp', 'blk'), axis=0, tiled=True)  56.5 us
    all_gather x1, waiting for transfers between devices, local(): lax.all_gather(w_down, ('dp', 'blk'), axis=0, tiled=True)  56.4 us
    dot_general x12, local copies, waits for them, and re-layouts, block_scores(): rel_term = jnp.einsum('qkb,bh->hqk', one_hot, bias_table, precision=HIGHEST)  53.9 us
  transfers between devices with their start and end apart: 18, of which 13 were waited for; matrix products, arithmetic and copies ran while one was open for 30% of the time, Pallas kernels for 0%

commit v1 on v0

--- a/solution.py
+++ b/solution.py
@@ -1,27 +1,827 @@
+import functools
 import math
 
 import jax
 import jax.numpy as jnp
 from jax import lax
+from jax.experimental import pallas as pl
+from jax.experimental.pallas import tpu as pltpu
 from jax.sharding import PartitionSpec as P
 
+D = 768
 H = 12
 DH = 64
 NB = 32
-
-
 THRESHOLDS = (12, 16, 23, 32, 46, 64, 91)
 MASKED = -1e30
 EPSILON = 1e-06
+TP = 4
+T = 256
+HT = 3
+F32 = jnp.float32
+BF16 = jnp.bfloat16
+MIB = 1 << 20
+
+
+def dot(a, b):
+    return lax.dot_general(a, b, (((1,), (0,)), ((), ())), preferred_element_type=F32)
+
+
+def dot_nt(a, b):
+    return lax.dot_general(a, b, (((1,), (1,)), ((), ())), preferred_element_type=F32)
+
+
+def dot_tn(a, b):
+    return lax.dot_general(a, b, (((0,), (0,)), ((), ())), preferred_element_type=F32)
+
+
+def bucket_of(relative):
+    distance = jnp.abs(relative)
+    far = jnp.full(relative.shape, 8, jnp.int32)
+    for threshold in THRESHOLDS:
+        far = far + (distance >= threshold).astype(jnp.int32)
+    return jnp.where(relative > 0, NB // 2, 0) + jnp.where(distance < 8, distance, far)
+
+
+def call(kernel, out_shape, *args, scratch=(), smem=(), vmem=48, flops=0, nbytes=0, name=None):
+    vspec = pl.BlockSpec(memory_space=pltpu.VMEM)
+    sspec = pl.BlockSpec(memory_space=pltpu.SMEM)
+    return pl.pallas_call(
+        kernel,
+        out_shape=out_shape,
+        in_specs=[sspec if n in smem else vspec for n in range(len(args))],
+        out_specs=jax.tree.map(lambda _: vspec, out_shape),
+        scratch_shapes=list(scratch),
+        compiler_params=pltpu.CompilerParams(vmem_limit_bytes=vmem * MIB),
+        cost_estimate=pl.CostEstimate(flops=flops, bytes_accessed=nbytes, transcendentals=0),
+        name=name,
+    )(*args)
+
+
+def sds(shape, dtype):
+    return jax.ShapeDtypeStruct(shape, dtype)
+
+
+def low_half(rows):
+    return lax.broadcasted_iota(jnp.int32, (rows, 128), 1) < 64
+
+
+def prep_kernel(wq, wk, wv, wg, wu, g1, g2, s0, s1, s2, s3, slabs):
+    j_me = lax.axis_index("blk")
+    rows = wq.shape[0]
+    low = low_half(rows)
+    lane = lax.broadcasted_iota(jnp.int32, (rows, 128), 1)
+    gains = jnp.where(lane == 64, g1[...], jnp.where(lane == 65, g2[...], 0.0))
+
+    def tile(ref, index):
+        return ref[:, 128 * index : 128 * index + 128].astype(F32)
+
+    for j in range(TP):
+        first, second = [], []
+        for ref in (wq, wk, wv):
+            at = 192 * j // 128
+            a, b = tile(ref, at), tile(ref, at + 1)
+            if j % 2:
+                a, b = pltpu.roll(a, 64, 1), pltpu.roll(b, 64, 1)
+                a = jnp.where(low, a, b)
+            first.append(a)
+            second.append(b)
+        tiles = first + [
+            jnp.where(low, second[0], pltpu.roll(second[1], 64, 1)),
+            jnp.where(low, second[2], gains),
+        ]
+        for ref in (wg, wu):
+            for t in range(4):
+                a = tile(ref, 4 * t + j // 2)
+                b = tile(ref, 4 * t + 2 + j // 2)
+                if j % 2:
+                    tiles.append(jnp.where(low, pltpu.roll(a, 64, 1), b))
+                else:
+                    tiles.append(jnp.where(low, a, pltpu.roll(b, 64, 1)))
+        for n, v in enumerate(tiles):
+            slabs[j ^ j_me, :, 128 * n : 128 * n + 128] = v.astype(BF16)
+    for k, ref in enumerate((s0, s1, s2, s3)):
+        ref[...] = slabs[k]
+
+
+def pack_kernel(s0, s1, s2, s3, wd, first, second, whole):
+    j = lax.axis_index("blk")
+    rows = s0.shape[0]
+    for k, ref in enumerate((s0, s1, s2, s3)):
+        whole[pl.ds(pl.multiple_of(rows * (j ^ k), 8), rows)] = ref[...].astype(F32)
+    first[...] = whole[:, 0:640].astype(BF16)
+    for n in range(4):
+        second[96 * n : 96 * n + 96] = whole[:, 640 + 256 * n : 896 + 256 * n].astype(BF16)
+    for n in range(3):
+        second[384 + 64 * n : 448 + 64 * n] = wd[:, 256 * n : 256 * n + 256]
+
+
+def bias_kernel(table, out):
+    j = lax.axis_index("blk")
+    lane = lax.broadcasted_iota(jnp.int32, (8, 512), 1)
+    for n in range(3):
+        off = (n - 1) * T
+        rel = jnp.where(lane < 256, off - lane, off + 512 - lane)
+        bucket = bucket_of(rel)
+        for h in range(HT):
+            row = jnp.zeros((8, 512), F32)
+            for b in range(NB):
+                row = jnp.where(bucket == b, table[b, HT * j + h], row)
+            wide = jnp.broadcast_to(row[0:1], (T, 512))
+            out[h, n] = pltpu.roll(wide, 0, 1, stride=1, stride_axis=0)[:, :T]
+
+
+def piece_at(n):
+    return 2 * (n % 4) + n // 4
+
+
+def qkv_kernel(t0, t1, t2, t3, p0, p1, p2, p3, p4, p5, p6, p7, tok, n1, qkv, w, gains):
+    j = lax.axis_index("blk")
+    dp = lax.axis_index("dp")
+    for k, ref in enumerate((t0, t1, t2, t3)):
+        tok[j ^ k] = ref[...]
+    for n, ref in enumerate((p0, p1, p2, p3, p4, p5, p6, p7)):
+        w[pl.ds(pl.multiple_of(96 * (dp ^ piece_at(n)), 32), 96)] = ref[...]
+    turned = jnp.transpose(w[:, 512:640].astype(F32))
+    gains[...] = turned[64:72]
+
+    def body(b, carry):
+        x = tok[b].astype(F32)
+        rstd = lax.rsqrt(jnp.mean(x * x, axis=-1, keepdims=True) + EPSILON)
+        n = (x * rstd * gains[0:1]).astype(BF16)
+        n1[b] = n
+        y = dot(n, w[...])
+        for t in range(5):
+            qkv[t, b] = y[:, 128 * t : 128 * t + 128].astype(BF16)
+        return carry
+
+    lax.fori_loop(0, TP, body, 0)
+
+
+def attn_fwd_kernel(
+    table, bias, qkv, s0, s1, s2, s3, prob, inv_tot, out_t, att, segq, segk, qtm, vt, sc
+):
+    j_me = lax.axis_index("blk")
+    for k, ref in enumerate((s0, s1, s2, s3)):
+        row = ref[...].astype(F32)
+        segq[j_me ^ k] = jnp.broadcast_to(row, (8, T))
+        col = jnp.transpose(jnp.broadcast_to(row, (128, T)))
+        segk[j_me ^ k, :, 0:128] = col
+        segk[j_me ^ k, :, 128:256] = col
+    rows_low = lax.broadcasted_iota(jnp.int32, (128, T), 0) < 64
+    for i in range(TP):
+        q0 = jnp.transpose(qkv[0, i].astype(F32))
+        q1 = jnp.transpose(pltpu.roll(qkv[3, i].astype(F32), 64, 1))
+        qtm[0, i] = jnp.where(rows_low, q0, 0.0).astype(BF16)
+        qtm[1, i] = jnp.where(rows_low, 0.0, q0).astype(BF16)
+        qtm[2, i] = jnp.where(rows_low, 0.0, q1).astype(BF16)
+        v0 = jnp.transpose(qkv[2, i].astype(F32)).astype(BF16)
+        v1 = jnp.transpose(qkv[4, i].astype(F32)).astype(BF16)
+        vt[0, :, T * i : T * i + T] = v0[0:64]
+        vt[1, :, T * i : T * i + T] = v0[64:128]
+        vt[2, :, T * i : T * i + T] = v1[0:64]
+
+    def head(h, carry):
+        tile = 1 + 2 * (h // 2)
+        far = (table[15, HT * j_me + h], table[31, HT * j_me + h])
+        for i in range(TP):
+            peak = jnp.full((1, T), MASKED, F32)
+            for j in range(TP):
+                s = dot(qkv[tile, j], qtm[h, i])
+                if abs(j - i) <= 1:
+                    s = s + bias[h, j - i + 1]
+                else:
+                    s = s + far[j > i]
+                if i in (0, TP - 1) or j in (0, TP - 1):
+                    s = jnp.where(segk[j] == segq[i, 0:1], s, MASKED)
+                sc[j] = s
+                peak = jnp.maximum(peak, jnp.max(s, axis=0, keepdims=True))
+            total = jnp.zeros((1, T), F32)
+            for j in range(TP):
+                p = jnp.exp(sc[j] - peak)
+                total = total + jnp.sum(p, axis=0, keepdims=True)
+                prob[h, i, j] = p.astype(BF16)
+            inv = 1.0 / total
+            inv_tot[h, i] = inv
+            o = dot(vt[h], prob[h, i].reshape(TP * T, T))
+            out_t[h, :, T * i : T * i + T] = o * inv
+        return carry
+
+    lax.fori_loop(0, HT, head, 0)
+    for b in range(TP):
+        both = jnp.concatenate(
+            [out_t[0, :, T * b : T * b + T], out_t[1, :, T * b : T * b + T]], axis=0
+        )
+        att[T * b : T * b + T, :] = jnp.transpose(both).astype(BF16)
+    for b in range(2):
+        both = jnp.concatenate(
+            [out_t[2, :, T * b : T * b + T], out_t[2, :, T * (b + 2) : T * (b + 2) + T]], axis=0
+        )
+        att[1024 + T * b : 1024 + T * b + T, :] = jnp.transpose(both).astype(BF16)
+
+
+def put_pair(keep, give, k, value):
+    @pl.when(k % 2 == 0)
+    def _():
+        keep[k // 2] = value
+
+    @pl.when(k % 2 == 1)
+    def _():
+        give[k // 2] = value
+
+
+def ffn_kernel(
+    a0, a1, a2, a3, wo, gains, p0, p1, p2, p3, p4, p5, p6, p7, tok, c0, c1, c2, c3,
+    attc, wop, cot, n2, hid, ggug, two_keep, two_give, lo_keep, lo_give, mixed_own, wgu, wd,
+):
+    j = lax.axis_index("blk")
+    dp = lax.axis_index("dp")
+    for n, ref in enumerate((p0, p1, p2, p3, p4, p5, p6, p7)):
+        at = dp ^ piece_at(n)
+        for m in range(4):
+            wgu[pl.ds(pl.multiple_of(96 * at, 32), 96), 256 * m : 256 * m + 256] = ref[96 * m : 96 * m + 96]
+        for m in range(3):
+            wd[pl.ds(pl.multiple_of(64 * at, 64), 64), 256 * m : 256 * m + 256] = ref[384 + 64 * m : 448 + 64 * m]
+    for k, ref in enumerate((c0, c1, c2, c3)):
+        cot[j ^ k] = ref[...]
+        at = pl.multiple_of(192 * (j ^ k), 64)
+        wop[128 * k : 128 * k + 128] = wo[pl.ds(at, 128)]
+        wop[512 + 64 * k : 512 + 64 * k + 64] = wo[pl.ds(at + 128, 64)]
+    low = low_half(T)
+
+    def body(k, carry):
+        b = j ^ k
+        half = b // 2
+        refs = (a0, a1, a2, a3)
+        for n, ref in enumerate(refs):
+            attc[b, :, 128 * n : 128 * n + 128] = ref[pl.ds(pl.multiple_of(b * T, T), T)]
+        rest = [
+            ref[pl.ds(pl.multiple_of(1024 + (b % 2) * T, T), T)].astype(F32) for ref in refs
+        ]
+        for n in range(2):
+            lo = pltpu.roll(rest[2 * n], 64 * half, 1)
+            hi = pltpu.roll(rest[2 * n + 1], 64 * (1 - half), 1)
+            attc[b, :, 512 + 128 * n : 640 + 128 * n] = jnp.where(low, lo, hi).astype(BF16)
+        mixed = tok[b].astype(F32) + dot(attc[b], wop[...])
+
+        @pl.when(k == 0)
+        def _():
+            mixed_own[...] = mixed
+
+        rstd = lax.rsqrt(jnp.mean(mixed * mixed, axis=-1, keepdims=True) + EPSILON)
+        n = (mixed * rstd * gains[1:2]).astype(BF16)
+        n2[b] = n
+        gate = dot(n, wgu[:, 0:512])
+        up = dot(n, wgu[:, 512:1024])
+        c = 0.7978845608028654
+        sq = gate * gate
+        th = jnp.tanh(c * gate * (1.0 + 0.044715 * sq))
+        act = 0.5 * gate * (1.0 + th)
+        slope = 0.5 * (1.0 + th) + 0.5 * gate * (1.0 - th * th) * (c * (1.0 + 3 * 0.044715 * sq))
+        hidden = (act * up).astype(BF16)
+        hid[b] = hidden
+        hg = dot_nt(cot[b], wd[...])
+        ggug[b, :, 0:512] = (hg * up * slope).astype(BF16)
+        ggug[b, :, 512:1024] = (hg * act).astype(BF16)
+        two = dot_nt(ggug[b], wgu[...]).astype(BF16)
+        put_pair(two_keep, two_give, k, two)
+        put_pair(lo_keep, lo_give, k, dot(hidden, wd[...]).astype(BF16))
+        return carry
+
+    lax.fori_loop(0, TP, body, 0)
+
+
+def mid_kernel(keep, rc, rx, mixed_own, cot_own, attc, wop, gains, mixed_grad, g0, g1, g2, g3, wo_keep, wo_give, dw):
+    j = lax.axis_index("blk")
+    u = (keep[0].astype(F32) + rc[0].astype(F32) + rx[...].astype(F32)) * gains[1:2]
+    mixed = mixed_own[...]
+    rstd = lax.rsqrt(jnp.mean(mixed * mixed, axis=-1, keepdims=True) + EPSILON)
+    n = mixed * rstd
+    mg = cot_own[...].astype(F32) + rstd * (u - n * jnp.mean(u * n, axis=-1, keepdims=True))
+    mixed_grad[...] = mg
+    ml = mg.astype(BF16)
+    ag = dot_nt(ml, wop[...])
+    low = low_half(128)
+    for k, ref in enumerate((g0, g1, g2, g3)):
+        ref[0:256] = ag[:, 128 * k : 128 * k + 128].astype(BF16)
+        rest = ag[:, 512 + 128 * (k // 2) : 640 + 128 * (k // 2)]
+        top, bottom = rest[0:128], rest[128:256]
+        if k % 2 == 0:
+            v = jnp.where(low, top, pltpu.roll(bottom, 64, 1))
+        else:
+            v = jnp.where(low, pltpu.roll(top, 64, 1), bottom)
+        ref[256:384] = v.astype(BF16)
+    perm = dot_tn(attc[j], ml)
+    for k in range(TP):
+        at = pl.multiple_of(192 * (j ^ k), 64)
+        dw[pl.ds(at, 128)] = perm[128 * k : 128 * k + 128]
+        dw[pl.ds(at + 128, 64)] = perm[512 + 64 * k : 512 + 64 * k + 64]
+    for k in range(TP):
+        ref = wo_give if k % 2 else wo_keep
+        for d in range(8):
+            at = pl.multiple_of(24 * (TP * d + (j ^ k)), 8)
+            ref[k // 2, d] = dw[pl.ds(at, 24)].astype(BF16)
+
+
+SLOTS = (0, 2, 1, 3)
+WO_ROWS = 32
+CHUNK = 5 * 96 + 6 * WO_ROWS
+TAIL = 64
+
+
+def slots(body):
+    dp = lax.axis_index("dp")
+    for give in range(2):
+        for slot, z in enumerate(SLOTS):
+            body(give, slot, dp ^ (2 * z + give))
+
+
+def ffn_dw_kernel(n2, ggug, hid, cot, keep, give, dwgu, dwd):
+    for m in range(2):
+        at = slice(512 * m, 512 * m + 512)
+        dwgu[:, at] = dot_tn(n2[...], ggug[:, at])
+    for m in range(3):
+        at = slice(256 * m, 256 * m + 256)
+        dwd[:, at] = dot_tn(hid[...], cot[:, at])
+
+    def put(g, slot, owner):
+        ref = give if g else keep
+        a = pl.ds(pl.multiple_of(96 * owner, 32), 96)
+        for m in range(4):
+            ref[slot, 96 * m : 96 * m + 96] = dwgu[a, 256 * m : 256 * m + 256].astype(BF16)
+        a = pl.ds(pl.multiple_of(64 * owner, 64), 64)
+        for m in range(3):
+            ref[slot, 384 + 64 * m : 448 + 64 * m] = dwd[a, 256 * m : 256 * m + 256].astype(BF16)
+
+    slots(put)
+
+
+def split(x):
+    high = x.astype(BF16)
+    return high, (x - high.astype(F32)).astype(BF16)
+
+
+def attn_dw_kernel(n1, dqkv, wo_keep, wo_got, wo_along, table_grad, keep, give, dw, wo):
+    for t in range(5):
+        at = slice(128 * t, 128 * t + 128)
+        dw[:, at] = dot_tn(n1[...], dqkv[:, at])
+    for d in range(8):
+        wo[d] = wo_keep[0, d].astype(F32) + wo_got[0, d].astype(F32) + wo_along[d].astype(F32)
+
+    def put(g, slot, owner):
+        ref = give if g else keep
+        base = CHUNK * slot
+        a = pl.ds(pl.multiple_of(96 * owner, 32), 96)
+        for t in range(5):
+            ref[base + 96 * t : base + 96 * t + 96] = dw[a, 128 * t : 128 * t + 128].astype(BF16)
+        base = base + 480
+        pad = jnp.zeros((WO_ROWS - 24, 128), F32)
+        for t in range(6):
+            part = wo[owner, :, 128 * t : 128 * t + 128]
+            full = jnp.concatenate([part, pad], axis=0)
+            ref[base + WO_ROWS * t : base + WO_ROWS * t + WO_ROWS] = full.astype(BF16)
+
+    slots(put)
+    for ref in (keep, give):
+        for n, part in enumerate(split(table_grad[...])):
+            ref[4 * CHUNK + 32 * n : 4 * CHUNK + 32 * n + 32] = part
+
+
+def tail_of(ref, base):
+    return ref[base : base + 32].astype(F32) + ref[base + 32 : base + 64].astype(F32)
+
+
+def stage_kernel(n, keep, got, next_keep, next_give):
+    half = n // 2 * CHUNK
+    for at, ref in ((0, next_keep), (half, next_give)):
+        here = slice(at, at + half)
+        ref[0:half] = (keep[here].astype(F32) + got[here].astype(F32)).astype(BF16)
+        parts = split(tail_of(keep, n * CHUNK) + tail_of(got, n * CHUNK))
+        for m, part in enumerate(parts):
+            ref[half + 32 * m : half + 32 * m + 32] = part
+
+
+def back_kernel(keep, got, dwo, b0, b1, b2, b3, total):
+    j = lax.axis_index("blk")
+    total[...] = keep[0:CHUNK].astype(F32) + got[0:CHUNK].astype(F32)
+    parts = split(tail_of(keep, CHUNK) + tail_of(got, CHUNK))
+    for t in range(6):
+        at = 480 + WO_ROWS * t
+        dwo[:, 128 * t : 128 * t + 128] = total[at : at + 24]
+    pad = jnp.zeros((8, 128), F32)
+    for k, ref in enumerate((b0, b1, b2, b3)):
+        for t in range(5):
+            part = total[pl.ds(pl.multiple_of(96 * t + 24 * (j ^ k), 8), 24)]
+            ref[0:32, 128 * t : 128 * t + 128] = jnp.concatenate([part, pad], axis=0).astype(BF16)
+        for m, part in enumerate(parts):
+            ref[32:64, 128 * m : 128 * m + 128] = part
+        ref[32:64, 256:640] = jnp.zeros((32, 384), BF16)
+
+
+def ffn_back_kernel(keep, got, along, dwd, b0, b1, b2, b3, total):
+    j = lax.axis_index("blk")
+    total[...] = keep[0].astype(F32) + got[0].astype(F32) + along[...].astype(F32)
+    for m in range(3):
+        dwd[:, 256 * m : 256 * m + 256] = total[384 + 64 * m : 448 + 64 * m]
+    for k, ref in enumerate((b0, b1, b2, b3)):
+        for m in range(4):
+            part = total[pl.ds(pl.multiple_of(96 * m + 24 * (j ^ k), 8), 24)]
+            ref[:, 256 * m : 256 * m + 256] = part.astype(BF16)
+
+
+def attn_bwd_kernel(
+    qkv, prob, inv_tot, out_t, g0, g1, g2, g3, w,
+    dqkv, one_keep, one_give, table_grad,
+    dotm, dom, qm, ktm, delta, dst, dq_acc, dk_acc, dv_acc, near, far,
+):
+    j_me = lax.axis_index("blk")
+    low = low_half(T)
+    low_short = low_half(128)
+    rows_low = lax.broadcasted_iota(jnp.int32, (128, T), 0) < 64
+
+    for k, ref in enumerate((g0, g1, g2, g3)):
+        b = j_me ^ k
+        first = ref[0:256].astype(F32)
+        rest = ref[256:384].astype(F32)
+        second = jnp.concatenate([rest, pltpu.roll(rest, 64, 1)], axis=0)
+        t0 = jnp.transpose(first)
+        t1 = jnp.transpose(second)
+        t0 = t0 * jnp.where(rows_low, inv_tot[0, b], inv_tot[1, b])
+        t1 = jnp.where(rows_low, t1 * inv_tot[2, b], 0.0)
+        t0, t1 = t0.astype(BF16), t1.astype(BF16)
+        f0, f1 = t0.astype(F32), t1.astype(F32)
+        dotm[0, b] = jnp.where(rows_low, f0, 0.0).astype(BF16)
+        dotm[1, b] = jnp.where(rows_low, 0.0, f0).astype(BF16)
+        dotm[2, b] = t1
+        back = jnp.transpose(f0)
+        dom[0, b] = jnp.where(low, back, 0.0).astype(BF16)
+        dom[1, b] = jnp.where(low, 0.0, back).astype(BF16)
+        dom[2, b] = jnp.transpose(f1).astype(BF16)
+
+    for i in range(TP):
+        at = slice(T * i, T * i + T)
+        for h in range(HT):
+            g = dotm[h, i].astype(F32)
+            g = g[64:128] if h == 1 else g[0:64]
+            delta[h, i] = jnp.sum(out_t[h, :, at] * g, axis=0, keepdims=True)
+        q0 = qkv[0, i].astype(F32)
+        turned = pltpu.roll(qkv[3, i].astype(F32), 64, 1)
+        qm[0, i] = jnp.where(low, q0, 0.0).astype(BF16)
+        qm[1, i] = jnp.where(low, 0.0, q0).astype(BF16)
+        qm[2, i] = jnp.where(low, 0.0, turned).astype(BF16)
+        k0 = jnp.transpose(qkv[1, i].astype(F32))
+        k1 = jnp.transpose(turned)
+        ktm[0, :, at] = jnp.where(rows_low, k0, 0.0).astype(BF16)
+        ktm[1, :, at] = jnp.where(rows_low, 0.0, k0).astype(BF16)
+        ktm[2, :, at] = jnp.where(rows_low, k1, 0.0).astype(BF16)
+
+    dq_acc[...] = jnp.zeros(dq_acc.shape, F32)
+    dk_acc[...] = jnp.zeros(dk_acc.shape, F32)
+    dv_acc[...] = jnp.zeros(dv_acc.shape, F32)
+    table_grad[...] = jnp.zeros(table_grad.shape, F32)
+    key_at = lax.broadcasted_iota(jnp.int32, (128, 128), 0)
+    query_at = lax.broadcasted_iota(jnp.int32, (128, 128), 1)
+    upper = query_at >= key_at
+    turn = (key_at + query_at == 127).astype(F32)
+
+    def diagonals(m):
+        m = lax.dot_general(
+            turn, m, (((1,), (0,)), ((), ())), precision=HIGHEST, preferred_element_type=F32
+        )
+        return jnp.sum(pltpu.roll(m, 1, 1, stride=1, stride_axis=0), axis=0, keepdims=True)
+
+    row_id = lax.broadcasted_iota(jnp.int32, (NB, 128), 0)
+    lane_id = lax.broadcasted_iota(jnp.int32, (NB, 128), 1)
+    hot_neg = bucket_of(-lane_id) == row_id
+    hot_pos = bucket_of(128 - lane_id) == row_id
+
+    def head(h, carry):
+        second = h // 2
+        near[...] = jnp.zeros(near.shape, F32)
+        far[...] = jnp.zeros(far.shape, F32)
+        for i in range(TP):
+            at = slice(T * i, T * i + T)
+            row_delta = delta[h, i]
+            for j in range(TP):
+                dp = dot(qkv[2 + 2 * second, j], dotm[h, i])
+                ds = prob[h, i, j].astype(F32) * (dp - row_delta)
+                dst[j] = ds.astype(BF16)
+                for a in range(2):
+                    for c in range(2):
+                        gap = 2 * (j - i) + a - c
+                        part = ds[128 * a : 128 * a + 128, 128 * c : 128 * c + 128]
+                        if abs(gap) <= 1:
+                            near[gap + 1] += part
+                        else:
+                            far[int(gap > 0)] += jnp.sum(part.reshape(16, 8, 128), axis=0)
+            d_all = dst[...].reshape(TP * T, T)
+            dq_acc[second, :, at] += dot(ktm[h], d_all)
+            dk_acc[second] += dot(d_all, qm[h, i])
+            dv_acc[second] += dot(prob[h, i].reshape(TP * T, T), dom[h, i])
+        before, diagonal, after = near[0], near[1], near[2]
+        neg = jnp.where(upper, diagonal, before)
+        pos = jnp.where(upper, after, diagonal)
+        neg, pos = diagonals(neg), diagonals(pos)
+        far_neg = jnp.sum(far[0], axis=0, keepdims=True) + jnp.sum(
+            jnp.where(upper, before, 0.0), axis=0, keepdims=True
+        )
+        far_pos = jnp.sum(far[1], axis=0, keepdims=True) + jnp.sum(
+            jnp.where(upper, 0.0, after), axis=0, keepdims=True
+        )
+        spread = (
+            jnp.where(hot_neg, neg, 0.0)
+            + jnp.where(hot_pos, pos, 0.0)
+            + jnp.where(row_id == 15, far_neg, 0.0)
+            + jnp.where(row_id == 31, far_pos, 0.0)
+        )
+        sums = jnp.sum(spread, axis=1, keepdims=True)
+        table_grad[...] += jnp.where(lane_id == HT * j_me + h, sums, 0.0)
+        return carry
+
+    lax.fori_loop(0, HT, head, 0)
+    for i in range(TP):
+        at = slice(T * i, T * i + T)
+        dq0 = jnp.transpose(dq_acc[0, :, at])
+        dq1 = jnp.transpose(dq_acc[1, :, at])
+        dqkv[i, :, 0:128] = dq0.astype(BF16)
+        dqkv[i, :, 128:256] = dk_acc[0, at].astype(BF16)
+        dqkv[i, :, 256:384] = dv_acc[0, at].astype(BF16)
+        dqkv[i, :, 384:512] = (dq1 + dk_acc[1, at]).astype(BF16)
+        dqkv[i, :, 512:640] = dv_acc[1, at].astype(BF16)
+
+    def body(k, carry):
+        b = j_me ^ k
+        put_pair(one_keep, one_give, k, dot_nt(dqkv[b], w[...]).astype(BF16))
+        return carry
+
+    lax.fori_loop(0, TP, body, 0)
+
+
+def finish(parts, w, out, gain):
+    total = jnp.zeros((w.shape[0], 128), F32)
+    for n, part in enumerate(parts):
+        at = slice(128 * n, 128 * n + 128)
+        total = total + part * w[:, at].astype(F32)
+        out[:, at] = part
+    return jnp.sum(total, axis=1, keepdims=True) / gain
+
+
+def attn_final_kernel(b0, b1, b2, b3, g1, wq, wk, wv, dq, dk, dv, gg1, table, src):
+    j_me = lax.axis_index("blk")
+    rows = wq.shape[0]
+    low = low_half(rows)
+    sums = jnp.zeros((NB, 128), F32)
+    for k, ref in enumerate((b0, b1, b2, b3)):
+        src[j_me ^ k] = ref[0:32].astype(F32)
+        sums = sums + ref[32:64, 0:128].astype(F32) + ref[32:64, 128:256].astype(F32)
+    table[...] = sums
+
+    def one(j, n):
+        return src[j, 0:rows, 128 * n : 128 * n + 128]
+
+    gain_grad = jnp.zeros((rows, 128), F32)
+    for n, (w, out) in enumerate(((wq, dq), (wk, dk), (wv, dv))):
+        parts = []
+        for j in range(0, TP, 2):
+            rest = []
+            for m in (j, j + 1):
+                last = one(m, 4 if n == 2 else 3)
+                rest.append(pltpu.roll(last, 64, 1) if n == 1 else last)
+            mid = pltpu.roll(one(j + 1, n), 64, 1)
+            parts += [
+                one(j, n),
+                jnp.where(low, rest[0], mid),
+                jnp.where(low, mid, pltpu.roll(rest[1], 64, 1)),
+            ]
+        gain_grad = gain_grad + finish(parts, w, out, g1[...])
+    gg1[...] = gain_grad
+
+
+def ffn_final_kernel(b0, b1, b2, b3, g2, wg, wu, dg, du, gg2, src):
+    j_me = lax.axis_index("blk")
+    rows = wg.shape[0]
+    low = low_half(rows)
+    for k, ref in enumerate((b0, b1, b2, b3)):
+        src[j_me ^ k] = ref[...].astype(F32)
+    gain_grad = jnp.zeros((rows, 128), F32)
+    for n, (w, out) in enumerate(((wg, dg), (wu, du))):
+        parts = [None] * 16
+        for t in range(4):
+            at = slice(512 * n + 128 * t, 512 * n + 128 * t + 128)
+            for half in range(2):
+                a, b = src[2 * half, :, at], src[2 * half + 1, :, at]
+                parts[4 * t + half] = jnp.where(low, a, pltpu.roll(b, 64, 1))
+                parts[4 * t + 2 + half] = jnp.where(low, pltpu.roll(a, 64, 1), b)
+        gain_grad = gain_grad + finish(parts, w, out, g2[...])
+    gg2[...] = gain_grad
+
+
+AXES = ("dp", "blk")
+
+
+def group_local(
+    n_dp, n_blk,
+    tokens, segment_ids, w_query, w_key, w_value, w_attn_out, attn_gain, rel_bias,
+    w_gate, w_up, w_down, ffn_gain, cotangent,
+):
+    n_dev = n_dp * n_blk
+
+    def swap(x, mask):
+        return lax.ppermute(x, AXES, [(d, d ^ mask) for d in range(n_dev)])
+
+    def share(x):
+        along = swap(x, 2)
+        return (x, swap(x, 1), along, swap(along, 1))
+
+    def reduce_pair(keep, give):
+        got = swap(give, 1)
+        return got, swap(keep[1] + got[1], 2)
+
+    tok_own, cot_own = tokens[0], cotangent[0]
+    rows = w_query.shape[0]
+    table = rel_bias.astype(F32)
+    gain1 = jnp.broadcast_to(attn_gain.astype(F32)[:, None], (rows, 128))
+    gain2 = jnp.broadcast_to(ffn_gain.astype(F32)[:, None], (rows, 128))
+
+    def spread(x):
+        near, far = swap(x, 8), swap(x, 16)
+        last = swap(far, 8)
+        return (x, near, far, last) + tuple(swap(v, 4) for v in (x, near, far, last))
+
+    slabs = call(
+        prep_kernel, (sds((rows, 1664), BF16),) * TP,
+        w_query, w_key, w_value, w_gate, w_up, gain1, gain2, name="prep",
+        scratch=(pltpu.VMEM((TP, rows, 1664), BF16),),
+    )
+    slabs = (slabs[0], swap(slabs[1], 1), swap(slabs[2], 2), swap(slabs[3], 3))
+    first, second = call(
+        pack_kernel, (sds((96, 640), BF16), sds((576, 256), BF16)),
+        *slabs, w_down, name="pack", scratch=(pltpu.VMEM((96, 1664), F32),),
+    )
+    toks = share(tok_own)
+    firsts = spread(first)
+    segs = share(segment_ids)
+    seconds = spread(second)
+    wo = lax.all_gather(w_attn_out, AXES, axis=0, tiled=True)
+    cots = share(cot_own)
+
+    bias = call(bias_kernel, sds((HT, 3, T, T), F32), table, smem=(0,), name="bias")
+    tok, n1, qkv, w_qkv, gains = call(
+        qkv_kernel,
+        (
+            sds((TP, T, D), BF16), sds((TP, T, D), BF16), sds((5, TP, T, 128), BF16),
+            sds((D, 640), BF16), sds((8, D), F32),
+        ),
+        *toks, *firsts, name="qkv",
+        flops=2 * 1024 * 768 * 640, nbytes=8 * MIB,
+    )
+    prob, inv_tot, out_t, att = call(
+        attn_fwd_kernel,
+        (
+            sds((HT, TP, TP, T, T), BF16),
+            sds((HT, TP, 1, T), F32),
+            sds((HT, DH, TP * T), F32),
+            sds((1536, 128), BF16),
+        ),
+        table, bias, qkv, *segs, smem=(0,), name="attn_fwd",
+        scratch=(
+            pltpu.VMEM((TP, 8, T), F32),
+            pltpu.VMEM((TP, T, T), F32),
+            pltpu.VMEM((HT, TP, 128, T), BF16),
+            pltpu.VMEM((HT, DH, TP * T), BF16),
+            pltpu.VMEM((TP, T, T), F32),
+        ),
+        flops=8 * 1024 * 1024 * 768, nbytes=8 * MIB,
+    )
+    atts = share(att)
+    (
+        attc, wop, cot, n2, hid, ggug, two_keep, two_give, lo_keep, lo_give, mixed_own,
+    ) = call(
+        ffn_kernel,
+        (
+            sds((TP, T, D), BF16), sds((D, D), BF16), sds((TP, T, D), BF16), sds((TP, T, D), BF16),
+            sds((TP, T, 512), BF16), sds((TP, T, 1024), BF16),
+            sds((2, T, D), BF16), sds((2, T, D), BF16), sds((2, T, D), BF16), sds((2, T, D), BF16),
+            sds((T, D), F32),
+        ),
+        *atts, wo, gains, *seconds, tok, *cots, name="ffn",
+        scratch=(pltpu.VMEM((D, 1024), BF16), pltpu.VMEM((512, D), BF16)),
+        flops=2 * 1024 * 768 * (768 + 512 * 6), nbytes=16 * MIB,
+    )
+    two_c, two_x = reduce_pair(two_keep, two_give)
+    mixed_grad, g0, g1, g2, g3, wo_keep, wo_give = call(
+        mid_kernel,
+        (sds((T, D), F32),) + (sds((384, 128), BF16),) * 4 + (sds((2, 8, 24, D), BF16),) * 2,
+        two_keep, two_c, two_x, mixed_own, cot_own, attc, wop, gains, name="mid",
+        scratch=(pltpu.VMEM((D, D), F32),),
+        flops=4 * 256 * 768 * 768, nbytes=8 * MIB,
+    )
+    g1, g2, g3 = swap(g1, 1), swap(g2, 2), swap(g3, 3)
+    wo_got, wo_along = reduce_pair(wo_keep, wo_give)
+    flat = TP * T
+    keep, give = call(
+        ffn_dw_kernel, (sds((4, 576, 256), BF16),) * 2,
+        n2.reshape(flat, D), ggug.reshape(flat, 1024), hid.reshape(flat, 512), cot.reshape(flat, D),
+        name="ffn_dw", scratch=(pltpu.VMEM((D, 1024), F32), pltpu.VMEM((512, D), F32)),
+        flops=2 * 1024 * 768 * 512 * 3, nbytes=12 * MIB,
+    )
+    got = swap(give, 4)
+    f_give = keep[2:] + got[2:]
+    f_keep = keep[:2] + got[:2]
+    got = swap(f_give, 8)
+    along = swap(f_keep[1] + got[1], 16)
+    dwd, *backs = call(
+        ffn_back_kernel, (sds((64, D), F32),) + (sds((rows, 1024), BF16),) * 4,
+        f_keep, got, along, name="ffn_back", scratch=(pltpu.VMEM((576, 256), F32),),
+    )
+    backs = (backs[0], swap(backs[1], 1), swap(backs[2], 2), swap(backs[3], 3))
+    ff = w_gate.shape[1]
+    dg, du, gg2 = call(
+        ffn_final_kernel, (sds((rows, ff), F32),) * 2 + (sds((rows, 128), F32),),
+        *backs, gain2, w_gate, w_up, name="ffn_final",
+        scratch=(pltpu.VMEM((TP, rows, 1024), F32),),
+    )
+    dqkv, one_keep, one_give, table_grad = call(
+        attn_bwd_kernel,
+        (
+            sds((TP, T, 640), BF16),
+            sds((2, T, D), BF16),
+            sds((2, T, D), BF16),
+            sds((NB, 128), F32),
+        ),
+        qkv, prob, inv_tot, out_t, g0, g1, g2, g3, w_qkv, name="attn_bwd",
+        scratch=(
+            pltpu.VMEM((HT, TP, 128, T), BF16),
+            pltpu.VMEM((HT, TP, T, 128), BF16),
+            pltpu.VMEM((HT, TP, T, 128), BF16),
+            pltpu.VMEM((HT, 128, TP * T), BF16),
+            pltpu.VMEM((HT, TP, 1, T), F32),
+            pltpu.VMEM((TP, T, T), BF16),
+            pltpu.VMEM((2, 128, TP * T), F32),
+            pltpu.VMEM((2, TP * T, 128), F32),
+            pltpu.VMEM((2, TP * T, 128), F32),
+            pltpu.VMEM((3, 128, 128), F32),
+            pltpu.VMEM((2, 8, 128), F32),
+        ),
+        flops=16 * 1024 * 1024 * 768, nbytes=12 * MIB,
+    )
+    one_c, one_x = reduce_pair(one_keep, one_give)
+    lo_c, lo_x = reduce_pair(lo_keep, lo_give)
+    layer_out = mixed_own + lo_keep[0].astype(F32) + lo_c[0].astype(F32) + lo_x.astype(F32)
+
+    def chunks(n):
+        return sds((n * CHUNK + TAIL, 128), BF16)
+
+    keep, give = call(
+        attn_dw_kernel, (chunks(4),) * 2,
+        n1.reshape(flat, D), dqkv.reshape(flat, 640), wo_keep, wo_got, wo_along, table_grad,
+        name="attn_dw", scratch=(pltpu.VMEM((D, 640), F32), pltpu.VMEM((8, 24, D), F32)),
+        flops=2 * 1024 * 768 * 640, nbytes=6 * MIB,
+    )
+    got = swap(give, 4)
+    keep, give = call(
+        functools.partial(stage_kernel, 4), (chunks(2),) * 2, keep, got, name="stage_y"
+    )
+    got = swap(give, 8)
+    keep, give = call(
+        functools.partial(stage_kernel, 2), (chunks(1),) * 2, keep, got, name="stage_z"
+    )
+    got = swap(give, 16)
+    dwo, *backs = call(
+        back_kernel, (sds((rows, D), F32),) + (sds((64, 640), BF16),) * 4,
+        keep, got, name="back", scratch=(pltpu.VMEM((CHUNK, 128), F32),),
+    )
+    backs = (backs[0], swap(backs[1], 1), swap(backs[2], 2), swap(backs[3], 3))
+    dq, dk, dv, gg1, table_sum = call(
+        attn_final_kernel,
+        (sds((rows, D), F32),) * 3 + (sds((rows, 128), F32), sds((NB, 128), F32)),
+        *backs, gain1, w_query, w_key, w_value, name="attn_final",
+        scratch=(pltpu.VMEM((TP, 32, 640), F32),),
+    )
+
+    x = tok_own.astype(F32)
+    rstd = lax.rsqrt(jnp.mean(x * x, axis=-1, keepdims=True) + EPSILON)
+    n = x * rstd
+    u = (one_keep[0].astype(F32) + one_c[0].astype(F32) + one_x.astype(F32)) * gains[0:1]
+    tokens_grad = mixed_grad + rstd * (u - n * jnp.mean(u * n, axis=-1, keepdims=True))
+    return (
+        layer_out.astype(BF16)[None],
+        tokens_grad[None],
+        dq,
+        dk,
+        dv,
+        dwo,
+        gg1[:, 0],
+        table_sum[:, :H],
+        dg,
+        du,
+        dwd,
+        gg2[:, 0],
+    )
+
+
 KEY_BLOCK = 256
 HIGHEST = lax.Precision.HIGHEST
-
-
-def bucket_of(relative):
-    distance = jnp.abs(relative)
-    far_bucket = 8 + sum([(distance >= threshold).astype(jnp.int32) for threshold in THRESHOLDS])
-    near_bucket = jnp.where(distance < 8, distance, far_bucket)
-    return jnp.where(relative > 0, NB // 2, 0) + near_bucket
 
 
 def rms_norm(values, gain):
@@ -369,38 +1169,20 @@
 
 
 def solution(mesh):
-    placed = (
-        P("dp", "blk", None),
-        P("dp", "blk"),
-        P(("dp", "blk"), None),
-        P(("dp", "blk"), None),
-        P(("dp", "blk"), None),
-        P(("dp", "blk"), None),
-        P(("dp", "blk")),
-        P(),
-        P(("dp", "blk"), None),
-        P(("dp", "blk"), None),
-        P(("dp", "blk"), None),
-        P(("dp", "blk")),
-        P("dp", "blk", None),
-    )
+    whole = P(AXES, None)
+    rows = P("dp", "blk", None)
+    n_dp, n_blk = mesh.shape["dp"], mesh.shape["blk"]
+    grouped = functools.partial(group_local, n_dp, n_blk)
+    body = grouped if (n_dp, n_blk) == (8, TP) else local
     return jax.shard_map(
-        local,
+        body,
         mesh=mesh,
-        in_specs=placed,
+        in_specs=(
+            rows, P("dp", "blk"), whole, whole, whole, whole, P(AXES), P(),
+            whole, whole, whole, P(AXES), rows,
+        ),
         out_specs=(
-            P("dp", "blk", None),
-            P("dp", "blk", None),
-            P(("dp", "blk"), None),
-            P(("dp", "blk"), None),
-            P(("dp", "blk"), None),
-            P(("dp", "blk"), None),
-            P(("dp", "blk")),
-            P(),
-            P(("dp", "blk"), None),
-            P(("dp", "blk"), None),
-            P(("dp", "blk"), None),
-            P(("dp", "blk")),
+            rows, rows, whole, whole, whole, whole, P(AXES), P(), whole, whole, whole, P(AXES),
         ),
         check_vma=False,
     )

time: 1360 us -> 248 us (0.18)
  waiting for transfers between devices: 792 us -> 92.4 us
  matrix products: 227 us -> 0 us
  local copies, waits for them, and re-layouts: 157 us -> 30.3 us
  blocking collectives: 96.4 us -> 0 us
  Pallas kernels: 0 us -> 65.1 us
  starting transfers between devices: 1.36 us -> 42.1 us
  other arithmetic: 38.2 us -> 2.98 us
  loops' own time: 24.3 us -> 0 us
    reduce_scatter x7 -> x0, waiting for transfers between devices: 512 us -> none  [the longest x1 121 us: local(): lax.psum_scatter(up_w_grad, ('dp', 'blk'), scatter_dimension=0, tiled=True)]
    all_gather x11 -> x1, waiting for transfers between devices: 274 us -> 0.01 us  [group_local(): wo = lax.all_gather(w_attn_out, AXES, axis=0, tiled=True)]
    dot_general x69 -> x0, matrix products: 227 us -> none  [the longest x12 49.4 us: block_scores(): rel_term = jnp.einsum('qkb,bh->hqk', one_hot, bias_table, precision=HIGHEST)]
    ppermute x0 -> x52, waiting for transfers between devices: none -> 91.7 us  [swap(): return lax.ppermute(x, AXES, [(d, d ^ mask) for d in range(n_dev)])]
    unnamed x2 -> x0, blocking collectives: 80.3 us -> none
    pallas_call x0 -> x16, Pallas kernels: none -> 65.1 us  [call(): pl.pallas_call(kernel, out_shape=out_shape, in_specs=[sspec if n in smem...]
    dot_general x12 -> x0, local copies, waits for them, and re-layouts: 53.9 us -> none  [block_scores(): rel_term = jnp.einsum('qkb,bh->hqk', one_hot, bias_table, precision=HIGHEST)]
    dynamic_slice x44 -> x0, local copies, waits for them, and re-layouts: 52.4 us -> none  [the longest x32 43.5 us: in_blocks(): running, unused = lax.scan(scan_step, running, (stacked, starts))]
  transfers between devices with their start and end apart: 18 -> 53, of which waited for: 13 -> 23; matrix products, arithmetic and copies ran while one was open for 30% -> 2% of each run, Pallas kernels for 0% -> 18%
where the time goes in v1:
time: 248 us; the launch traced here: 247 us
  waiting for transfers between devices  92.4 us (37%)
  Pallas kernels  65.1 us (26%)
  starting transfers between devices  42.1 us (17%)
  local copies, waits for them, and re-layouts  30.3 us (12%)
  between operations  14.4 us (6%)
  other arithmetic  2.98 us (1%)
    ppermute x52, waiting for transfers between devices, swap(): return lax.ppermute(x, AXES, [(d, d ^ mask) for d in range(n_dev)])  91.7 us
    pallas_call x16, Pallas kernels, call(): pl.pallas_call(kernel, out_shape=out_shape, in_specs=[sspec if n in smem...  65.1 us
    ppermute x52, starting transfers between devices, swap(): return lax.ppermute(x, AXES, [(d, d ^ mask) for d in range(n_dev)])  42 us
    unnamed x96, local copies, waits for them, and re-layouts  27.6 us
  transfers between devices with their start and end apart: 53, of which 23 were waited for; matrix products, arithmetic and copies ran while one was open for 2% of the time, Pallas kernels for 18%

profile of v1, /device:TPU:0, one launch (start us, length us, event | category | flops | bytes accessed | tf_op | source)
XLA Modules:
  0.0 247.2 jit_solution(8031468575700132144)
XLA Ops:
  7.9 3.0 %collective-permute-start.1 = (bf16[256,768]{1,0:T(8,128)(2,1)}, bf16[256,768]{1,0:T(8,128)(2,1)S(1)}, u32[]{:S(2)}, u32[]{:S(2)}) collective-permute-start(bf16[256,768]{1,0:T(8,128)(2,1)} %bitcast.42), channel_id=1, source_target_pairs={{0,2},{1,3},{2,0},{3,1},{4,6},{5,7},{6,4},{7,5},{8,10},{9,11},{10,... | collective-permute-start | bytes 1179656 | tf_op jit(solution)/shard_map/ppermute | solution.py:630
  16.8 1.8 collective-permute-start.5
  19.0 1.8 collective-permute-done.1.t2
  20.8 1.5 collective-permute-done.4.s2
  24.4 2.7 %collective-permute-start.7 = (bf16[96,640]{1,0:T(8,128)(2,1)S(1)}, bf16[96,640]{1,0:T(8,128)(2,1)S(1)}, u32[]{:S(2)}, u32[]{:S(2)}) collective-permute-start(bf16[96,640]{1,0:T(8,128)(2,1)S(1)} %get-tuple-element.79.p0), channel_id=1, source_target_pairs={{0,16},{1,17},{2,18},{3,19},{4,20},{5,21},{6,22},{7,23},{8,24},{9,... | collective-permute-start | bytes 368648 | tf_op jit(solution)/shard_map/ppermute | solution.py:630
  28.2 1.6 collective-permute-start.6
  30.8 1.5 collective-permute-start.9
  32.3 2.2 collective-permute-done.7.p2
  35.9 1.6 collective-permute-start.11
  38.0 1.7 collective-permute-done.8.p3
  39.7 1.6 collective-permute-start.12
  42.1 1.5 bias.1
  46.8 3.4 %collective-permute-start.20 = (bf16[576,256]{1,0:T(8,128)(2,1)S(1)}, bf16[576,256]{1,0:T(8,128)(2,1)S(1)}, u32[]{:S(2)}, u32[]{:S(2)}) collective-permute-start(bf16[576,256]{1,0:T(8,128)(2,1)S(1)} %get-tuple-element.83.p0), channel_id=1, source_target_pairs={{0,16},{1,17},{2,18},{3,19},{4,20},{5,21},{6,22},{7,23},{8,24},{9,... | collective-permute-start | bytes 884744 | tf_op jit(solution)/shard_map/ppermute | solution.py:630
  52.9 4.7 %qkv.1 = (bf16[4,256,768]{2,1,0:T(8,128)(2,1)}, bf16[4,256,768]{2,1,0:T(8,128)(2,1)}, bf16[5,4,256,128]{3,2,1,0:T(8,128)(2,1)S(1)}, bf16[768,640]{1,0:T(8,128)(2,1)S(1)}, f32[8,768]{1,0:T(8,128)S(1)}) custom-call(bf16[256,768]{1,0:T(8,128)(2,1)S(1)} %bitcast.44, bf16[256,768]{1,0:T(8,128)(2,1)S(1)} %collective-permute-done.t1, ...), custom_call_target="tpu_custom_call" | custom-call | flops 1006632960 | bytes 8388608 | tf_op jit(solution)/shard_map/qkv/pallas_call | solution.py:49
  59.4 11.5 %attn_fwd.1 = (bf16[3,4,4,256,256]{4,3,2,1,0:T(8,128)(2,1)}, f32[3,4,1,256]{3,2,1,0:T(1,128)S(1)}, f32[3,64,1024]{2,1,0:T(8,128)S(1)}, bf16[1536,128]{1,0:T(8,128)(2,1)S(1)}) custom-call(f32[32,12]{1,0:T(8,128)S(1)} %convert_element_type.41.table, f32[3,3,256,256]{3,2,1,0:T(8,128)S(1)} %bias.1, bf16[5,4,256,128]{3,2,1,0:T(8,128)(2,1)S(1)} %get-tuple-element.80.qkv, ...), custom_call_target="tpu_custom_call" | custom-call | flops 6442450944 | bytes 8388608 | tf_op jit(solution)/shard_map/attn_fwd/pallas_call | solution.py:49
  76.9 5.4 %collective-permute-done.17.a2 = bf16[1536,128]{1,0:T(8,128)(2,1)S(1)} collective-permute-done((bf16[1536,128]{1,0:T(8,128)(2,1)S(1)}, bf16[1536,128]{1,0:T(8,128)(2,1)S(1)}, u32[]{:S(2)}, u32[]{:S(2)}) %collective-permute-start.17) | collective-permute-done | bytes 393248 | tf_op jit(solution)/shard_map/ppermute | solution.py:630
  82.3 1.5 collective-permute-start.23
  86.5 5.6 %collective-permute-done.23.p5 = bf16[576,256]{1,0:T(8,128)(2,1)S(1)} collective-permute-done((bf16[576,256]{1,0:T(8,128)(2,1)S(1)}, bf16[576,256]{1,0:T(8,128)(2,1)S(1)}, u32[]{:S(2)}, u32[]{:S(2)}) %collective-permute-start.23) | collective-permute-done | bytes 294944 | tf_op jit(solution)/shard_map/ppermute | solution.py:630
  92.8 5.2 %collective-permute-done.25.p7 = bf16[576,256]{1,0:T(8,128)(2,1)S(1)} collective-permute-done((bf16[576,256]{1,0:T(8,128)(2,1)S(1)}, bf16[576,256]{1,0:T(8,128)(2,1)S(1)}, u32[]{:S(2)}, u32[]{:S(2)}) %collective-permute-start.25) | collective-permute-done | bytes 294944 | tf_op jit(solution)/shard_map/ppermute | solution.py:630
  107.3 17.8 %ffn.1 = (bf16[4,256,768]{2,1,0:T(8,128)(2,1)}, bf16[768,768]{1,0:T(8,128)(2,1)}, bf16[4,256,768]{2,1,0:T(8,128)(2,1)}, bf16[4,256,768]{2,1,0:T(8,128)(2,1)}, bf...) custom-call(bf16[1536,128]{1,0:T(8,128)(2,1)S(1)} %get-tuple-element, ...), custom_call_target="tpu_custom_call" | custom-call | flops 6039797760 | bytes 16777216 | tf_op jit(solution)/shard_map/ffn/pallas_call | solution.py:49
  127.7 5.1 %ffn_dw.1 = (bf16[4,576,256]{2,1,0:T(8,128)(2,1)S(1)}, bf16[4,576,256]{2,1,0:T(8,128)(2,1)S(1)}) custom-call(bf16[1024,768]{1,0:T(8,128)(2,1)S(1)} %bitcast.52, bf16[1024,1024]{1,0:T(8,128)(2,1)} %bitcast.54, bf16[1024,512]{1,0:T(8,128)(2,1)S(1)} %bitcast.53, bf16[1024,768]{1,0:T(8,128)(2,1)} %bitcast.55), custom_call_target="tpu_custom_call" | custom-call | flops 2415919104 | bytes 12582912 | tf_op jit(solution)/shard_map/ffn_dw/pallas_call | solution.py:49
  134.5 10.6 %collective-permute-done.32.rx = bf16[256,768]{1,0:T(8,128)(2,1)S(1)} collective-permute-done((bf16[256,768]{1,0:T(8,128)(2,1)S(1)}, bf16[256,768]{1,0:T(8,128)(2,1)S(1)}, u32[]{:S(2)}, u32[]{:S(2)}) %collective-permute-start.32) | collective-permute-done | bytes 393248 | tf_op jit(solution)/shard_map/ppermute | solution.py:630
  145.1 3.1 %mid.1 = (f32[256,768]{1,0:T(8,128)S(1)}, bf16[384,128]{1,0:T(8,128)(2,1)S(1)}, bf16[384,128]{1,0:T(8,128)(2,1)S(1)}, bf16[384,128]{1,0:T(8,128)(2,1)S(1)}, bf16...) custom-call(bf16[2,256,768]{2,1,0:T(8,128)(2,1)S(1)} %copy-done.2, ...), custom_call_target="tpu_custom_call" | custom-call | flops 603979776 | bytes 8388608 | tf_op jit(solution)/shard_map/mid/pallas_call | solution.py:49
  149.0 12.3 %collective-permute-done.46 = bf16[4,576,256]{2,1,0:T(8,128)(2,1)S(1)} collective-permute-done((bf16[4,576,256]{2,1,0:T(8,128)(2,1)S(1)}, bf16[4,576,256]{2,1,0:T(8,128)(2,1)S(1)}, u32[]{:S(2)}, u32[]{:S(2)}) %collective-permute-start.46) | collective-permute-done | bytes 1179680 | tf_op jit(solution)/shard_map/ppermute | solution.py:630
  161.4 1.7 collective-permute-start.47
  166.0 2.8 %collective-permute-done.34.g2 = bf16[384,128]{1,0:T(8,128)(2,1)S(1)} collective-permute-done((bf16[384,128]{1,0:T(8,128)(2,1)S(1)}, bf16[384,128]{1,0:T(8,128)(2,1)S(1)}, u32[]{:S(2)}, u32[]{:S(2)}) %collective-permute-start.34) | collective-permute-done | bytes 98336 | tf_op jit(solution)/shard_map/ppermute | solution.py:630
  170.1 15.1 %attn_bwd.1 = (bf16[4,256,640]{2,1,0:T(8,128)(2,1)S(1)}, bf16[2,256,768]{2,1,0:T(8,128)(2,1)S(1)}, bf16[2,256,768]{2,1,0:T(8,128)(2,1)S(1)}, f32[32,128]{1,0:T(8,128)S(1)}) custom-call(bf16[5,4,256,128]{3,2,1,0:T(8,128)(2,1)} %copy-done.41, bf16[3,4,4,256,256]{4,3,2,1,0:T(8,128)(2,1)} %get-tuple-element.93.prob, ...), custom_call_target="tpu_custom_call" | custom-call | flops 12884901888 | bytes 12582912 | tf_op jit(solution)/shard_map/attn_bwd/pallas_call | solution.py:49
  187.1 2.5 attn_dw.1
  190.5 15.2 %collective-permute-done.48.along = bf16[576,256]{1,0:T(8,128)(2,1)S(1)} collective-permute-done((bf16[576,256]{1,0:T(8,128)(2,1)S(1)}, bf16[576,256]{1,0:T(8,128)(2,1)S(1)}, u32[]{:S(2)}, u32[]{:S(2)}) %collective-permute-start.48) | collective-permute-done | bytes 294944 | tf_op jit(solution)/shard_map/ppermute | solution.py:630
  213.1 7.2 %collective-permute-done.37 = bf16[256,768]{1,0:T(8,128)(2,1)S(1)} collective-permute-done((bf16[256,768]{1,0:T(8,128)(2,1)S(1)}, bf16[256,768]{1,0:T(8,128)(2,1)S(1)}, u32[]{:S(2)}, u32[]{:S(2)}) %collective-permute-start.37) | collective-permute-done | bytes 393248 | tf_op jit(solution)/shard_map/ppermute | solution.py:630
  220.8 10.5 %collective-permute-done.42.got = bf16[736,128]{1,0:T(8,128)(2,1)S(1)} collective-permute-done((bf16[736,128]{1,0:T(8,128)(2,1)S(1)}, bf16[736,128]{1,0:T(8,128)(2,1)S(1)}, u32[]{:S(2)}, u32[]{:S(2)}) %collective-permute-start.42) | collective-permute-done | bytes 188448 | tf_op jit(solution)/shard_map/ppermute | solution.py:630
  235.0 2.2 collective-permute-done.44.b2
  (205 shorter events, 67.3 us)
Async XLA Ops:
  7.2 92.4 %all-gather.2.cloned.1.call-start = ((), (), s32[]{:S(2)}) async-start(), calls=%async_computation | async-start | bytes 1216512 | tf_op jit(solution)/shard_map/all_gather | solution.py:665
  7.9 12.8 %collective-permute-start.1 = (bf16[256,768]{1,0:T(8,128)(2,1)}, bf16[256,768]{1,0:T(8,128)(2,1)S(1)}, u32[]{:S(2)}, u32[]{:S(2)}) collective-permute-start(bf16[256,768]{1,0:T(8,128)(2,1)} %bitcast.42), channel_id=1, source_target_pairs={{0,2},{1,3},{2,0},{3,1},{4,6},{5,7},{6,4},{7,5},{8,10},{9,11},{10,... | collective-permute-start | bytes 1179656 | tf_op jit(solution)/shard_map/ppermute | solution.py:630
  18.6 27.7 %collective-permute-start = (bf16[256,768]{1,0:T(8,128)(2,1)}, bf16[256,768]{1,0:T(8,128)(2,1)S(1)}, u32[]{:S(2)}, u32[]{:S(2)}) collective-permute-start(bf16[256,768]{1,0:T(8,128)(2,1)} %bitcast.43), channel_id=1, source_target_pairs={{0,1},{1,0},{2,3},{3,2},{4,5},{5,4},{6,7},{7,6},{8,9},{9,8},{10,11... | collective-permute-start | bytes 1179656 | tf_op jit(solution)/shard_map/ppermute | solution.py:630
  20.8 26.1 %collective-permute-start.2 = (bf16[256,768]{1,0:T(8,128)(2,1)S(1)}, bf16[256,768]{1,0:T(8,128)(2,1)S(1)}, u32[]{:S(2)}, u32[]{:S(2)}) collective-permute-start(bf16[256,768]{1,0:T(8,128)(2,1)S(1)} %collective-permute-done.1.t2), channel_id=1, source_target_pairs={{0,1},{1,0},{2,3},{3,2},{4,5},{5,4},{6,7},{7,6},{8,9},{9,8},{10,11... | collective-permute-start | bytes 1179656 | tf_op jit(solution)/shard_map/ppermute | solution.py:630
  24.4 10.1 %collective-permute-start.7 = (bf16[96,640]{1,0:T(8,128)(2,1)S(1)}, bf16[96,640]{1,0:T(8,128)(2,1)S(1)}, u32[]{:S(2)}, u32[]{:S(2)}) collective-permute-start(bf16[96,640]{1,0:T(8,128)(2,1)S(1)} %get-tuple-element.79.p0), channel_id=1, source_target_pairs={{0,16},{1,17},{2,18},{3,19},{4,20},{5,21},{6,22},{7,23},{8,24},{9,... | collective-permute-start | bytes 368648 | tf_op jit(solution)/shard_map/ppermute | solution.py:630
  44.2 13.4 %collective-permute-start.13 = (s32[1,256]{1,0:T(1,128)S(1)}, s32[1,256]{1,0:T(1,128)S(1)}, u32[]{:S(2)}, u32[]{:S(2)}) collective-permute-start(s32[1,256]{1,0:T(1,128)S(1)} %copy-done.38), channel_id=1, source_target_pairs={{0,1},{1,0},{2,3},{3,2},{4,5},{5,4},{6,7},{7,6},{8,9},{9,8},{10,11... | collective-permute-start | bytes 3080 | tf_op jit(solution)/shard_map/ppermute | solution.py:630
  46.0 30.4 %collective-permute-start.27 = (bf16[256,768]{1,0:T(8,128)(2,1)S(1)}, bf16[256,768]{1,0:T(8,128)(2,1)S(1)}, u32[]{:S(2)}, u32[]{:S(2)}) collective-permute-start(bf16[256,768]{1,0:T(8,128)(2,1)S(1)} %bitcast.47), channel_id=1, source_target_pairs={{0,2},{1,3},{2,0},{3,1},{4,6},{5,7},{6,4},{7,5},{8,10},{9,11},{10,... | collective-permute-start | bytes 1179656 | tf_op jit(solution)/shard_map/ppermute | solution.py:630
  46.3 30.1 %collective-permute-start.26 = (bf16[256,768]{1,0:T(8,128)(2,1)S(1)}, bf16[256,768]{1,0:T(8,128)(2,1)S(1)}, u32[]{:S(2)}, u32[]{:S(2)}) collective-permute-start(bf16[256,768]{1,0:T(8,128)(2,1)S(1)} %bitcast.48), channel_id=1, source_target_pairs={{0,1},{1,0},{2,3},{3,2},{4,5},{5,4},{6,7},{7,6},{8,9},{9,8},{10,11... | collective-permute-start | bytes 1179656 | tf_op jit(solution)/shard_map/ppermute | solution.py:630
  46.8 11.5 %collective-permute-start.15 = (s32[1,256]{1,0:T(1,128)S(1)}, s32[1,256]{1,0:T(1,128)S(1)}, u32[]{:S(2)}, u32[]{:S(2)}) collective-permute-start(s32[1,256]{1,0:T(1,128)S(1)} %collective-permute-done.14.s2), channel_id=1, source_target_pairs={{0,1},{1,0},{2,3},{3,2},{4,5},{5,4},{6,7},{7,6},{8,9},{9,8},{10,11... | collective-permute-start | bytes 3080 | tf_op jit(solution)/shard_map/ppermute | solution.py:630
  46.8 24.9 %collective-permute-start.20 = (bf16[576,256]{1,0:T(8,128)(2,1)S(1)}, bf16[576,256]{1,0:T(8,128)(2,1)S(1)}, u32[]{:S(2)}, u32[]{:S(2)}) collective-permute-start(bf16[576,256]{1,0:T(8,128)(2,1)S(1)} %get-tuple-element.83.p0), channel_id=1, source_target_pairs={{0,16},{1,17},{2,18},{3,19},{4,20},{5,21},{6,22},{7,23},{8,24},{9,... | collective-permute-start | bytes 884744 | tf_op jit(solution)/shard_map/ppermute | solution.py:630
  57.6 15.6 %collective-permute-start.19 = (bf16[576,256]{1,0:T(8,128)(2,1)S(1)}, bf16[576,256]{1,0:T(8,128)(2,1)S(1)}, u32[]{:S(2)}, u32[]{:S(2)}) collective-permute-start(bf16[576,256]{1,0:T(8,128)(2,1)S(1)} %get-tuple-element.83.p0), channel_id=1, source_target_pairs={{0,8},{1,9},{2,10},{3,11},{4,12},{5,13},{6,14},{7,15},{8,0},{9,1},... | collective-permute-start | bytes 884744 | tf_op jit(solution)/shard_map/ppermute | solution.py:630
  58.3 16.1 %collective-permute-start.22 = (bf16[576,256]{1,0:T(8,128)(2,1)S(1)}, bf16[576,256]{1,0:T(8,128)(2,1)S(1)}, u32[]{:S(2)}, u32[]{:S(2)}) collective-permute-start(bf16[576,256]{1,0:T(8,128)(2,1)S(1)} %get-tuple-element.83.p0), channel_id=1, source_target_pairs={{0,4},{1,5},{2,6},{3,7},{4,0},{5,1},{6,2},{7,3},{8,12},{9,13},{10,... | collective-permute-start | bytes 884744 | tf_op jit(solution)/shard_map/ppermute | solution.py:630
  71.8 10.5 %collective-permute-start.17 = (bf16[1536,128]{1,0:T(8,128)(2,1)S(1)}, bf16[1536,128]{1,0:T(8,128)(2,1)S(1)}, u32[]{:S(2)}, u32[]{:S(2)}) collective-permute-start(bf16[1536,128]{1,0:T(8,128)(2,1)S(1)} %get-tuple-element.81.a0), channel_id=1, source_target_pairs={{0,2},{1,3},{2,0},{3,1},{4,6},{5,7},{6,4},{7,5},{8,10},{9,11},{10,... | collective-permute-start | bytes 1179656 | tf_op jit(solution)/shard_map/ppermute | solution.py:630
  75.1 9.4 %collective-permute-start.24 = (bf16[576,256]{1,0:T(8,128)(2,1)S(1)}, bf16[576,256]{1,0:T(8,128)(2,1)S(1)}, u32[]{:S(2)}, u32[]{:S(2)}) collective-permute-start(bf16[576,256]{1,0:T(8,128)(2,1)S(1)} %collective-permute-done.20.p2), channel_id=1, source_target_pairs={{0,4},{1,5},{2,6},{3,7},{4,0},{5,1},{6,2},{7,3},{8,12},{9,13},{10,... | collective-permute-start | bytes 884744 | tf_op jit(solution)/shard_map/ppermute | solution.py:630
  76.4 16.5 %collective-permute-start.28 = (bf16[256,768]{1,0:T(8,128)(2,1)S(1)}, bf16[256,768]{1,0:T(8,128)(2,1)S(1)}, u32[]{:S(2)}, u32[]{:S(2)}) collective-permute-start(bf16[256,768]{1,0:T(8,128)(2,1)S(1)} %collective-permute-done.27.c2), channel_id=1, source_target_pairs={{0,1},{1,0},{2,3},{3,2},{4,5},{5,4},{6,7},{7,6},{8,9},{9,8},{10,11... | collective-permute-start | bytes 1179656 | tf_op jit(solution)/shard_map/ppermute | solution.py:630
  76.4 22.4 %collective-permute-start.16 = (bf16[1536,128]{1,0:T(8,128)(2,1)S(1)}, bf16[1536,128]{1,0:T(8,128)(2,1)S(1)}, u32[]{:S(2)}, u32[]{:S(2)}) collective-permute-start(bf16[1536,128]{1,0:T(8,128)(2,1)S(1)} %get-tuple-element.81.a0), channel_id=1, source_target_pairs={{0,1},{1,0},{2,3},{3,2},{4,5},{5,4},{6,7},{7,6},{8,9},{9,8},{10,11... | collective-permute-start | bytes 1179656 | tf_op jit(solution)/shard_map/ppermute | solution.py:630
  82.3 16.5 %collective-permute-start.18 = (bf16[1536,128]{1,0:T(8,128)(2,1)S(1)}, bf16[1536,128]{1,0:T(8,128)(2,1)S(1)}, u32[]{:S(2)}, u32[]{:S(2)}) collective-permute-start(bf16[1536,128]{1,0:T(8,128)(2,1)S(1)} %collective-permute-done.17.a2), channel_id=1, source_target_pairs={{0,1},{1,0},{2,3},{3,2},{4,5},{5,4},{6,7},{7,6},{8,9},{9,8},{10,11... | collective-permute-start | bytes 1179656 | tf_op jit(solution)/shard_map/ppermute | solution.py:630
  82.3 9.8 %collective-permute-start.23 = (bf16[576,256]{1,0:T(8,128)(2,1)S(1)}, bf16[576,256]{1,0:T(8,128)(2,1)S(1)}, u32[]{:S(2)}, u32[]{:S(2)}) collective-permute-start(bf16[576,256]{1,0:T(8,128)(2,1)S(1)} %collective-permute-done.19.p1), channel_id=1, source_target_pairs={{0,4},{1,5},{2,6},{3,7},{4,0},{5,1},{6,2},{7,3},{8,12},{9,13},{10,... | collective-permute-start | bytes 884744 | tf_op jit(solution)/shard_map/ppermute | solution.py:630
  85.3 12.7 %collective-permute-start.25 = (bf16[576,256]{1,0:T(8,128)(2,1)S(1)}, bf16[576,256]{1,0:T(8,128)(2,1)S(1)}, u32[]{:S(2)}, u32[]{:S(2)}) collective-permute-start(bf16[576,256]{1,0:T(8,128)(2,1)S(1)} %collective-permute-done.21.p3), channel_id=1, source_target_pairs={{0,4},{1,5},{2,6},{3,7},{4,0},{5,1},{6,2},{7,3},{8,12},{9,13},{10,... | collective-permute-start | bytes 884744 | tf_op jit(solution)/shard_map/ppermute | solution.py:630
  132.8 28.4 %collective-permute-start.46 = (bf16[4,576,256]{2,1,0:T(8,128)(2,1)S(1)}, bf16[4,576,256]{2,1,0:T(8,128)(2,1)S(1)}, u32[]{:S(2)}, u32[]{:S(2)}) collective-permute-start(bf16[4,576,256]{2,1,0:T(8,128)(2,1)S(1)} %get-tuple-element.129), channel_id=1, source_target_pairs={{0,4},{1,5},{2,6},{3,7},{4,0},{5,1},{6,2},{7,3},{8,12},{9,13},{10,... | collective-permute-start | bytes 3538952 | tf_op jit(solution)/shard_map/ppermute | solution.py:630
  133.8 11.3 %collective-permute-start.32 = (bf16[256,768]{1,0:T(8,128)(2,1)S(1)}, bf16[256,768]{1,0:T(8,128)(2,1)S(1)}, u32[]{:S(2)}, u32[]{:S(2)}) collective-permute-start(bf16[256,768]{1,0:T(8,128)(2,1)S(1)} %fusion.13), channel_id=1, source_target_pairs={{0,2},{1,3},{2,0},{3,1},{4,6},{5,7},{6,4},{7,5},{8,10},{9,11},{10,... | collective-permute-start | bytes 1179656 | tf_op jit(solution)/shard_map/ppermute | solution.py:630
  148.2 15.8 %collective-permute-start.38 = (bf16[2,8,24,768]{3,2,1,0:T(8,128)(2,1)S(1)}, bf16[2,8,24,768]{3,2,1,0:T(8,128)(2,1)S(1)}, u32[]{:S(2)}, u32[]{:S(2)}) collective-permute-start(bf16[2,8,24,768]{3,2,1,0:T(8,128)(2,1)S(1)} %get-tuple-element.106), channel_id=1, source_target_pairs={{0,1},{1,0},{2,3},{3,2},{4,5},{5,4},{6,7},{7,6},{8,9},{9,8},{10,11... | collective-permute-start | bytes 1769480 | tf_op jit(solution)/shard_map/ppermute | solution.py:630
  148.4 37.7 %collective-permute-start.29 = (bf16[2,256,768]{2,1,0:T(8,128)(2,1)}, bf16[2,256,768]{2,1,0:T(8,128)(2,1)S(1)}, u32[]{:S(2)}, u32[]{:S(2)}) collective-permute-start(bf16[2,256,768]{2,1,0:T(8,128)(2,1)} %get-tuple-element.87), channel_id=1, source_target_pairs={{0,1},{1,0},{2,3},{3,2},{4,5},{5,4},{6,7},{7,6},{8,9},{9,8},{10,11... | collective-permute-start | bytes 2359304 | tf_op jit(solution)/shard_map/ppermute | solution.py:630
  161.4 28.6 %collective-permute-start.47 = (bf16[2,576,256]{2,1,0:T(8,128)(2,1)S(1)}, bf16[2,576,256]{2,1,0:T(8,128)(2,1)S(1)}, u32[]{:S(2)}, u32[]{:S(2)}) collective-permute-start(bf16[2,576,256]{2,1,0:T(8,128)(2,1)S(1)} %get-tuple-element.162), channel_id=1, source_target_pairs={{0,8},{1,9},{2,10},{3,11},{4,12},{5,13},{6,14},{7,15},{8,0},{9,1},... | collective-permute-start | bytes 1769480 | tf_op jit(solution)/shard_map/ppermute | solution.py:630
  165.0 22.0 %collective-permute-start.39 = (bf16[8,24,768]{2,1,0:T(8,128)(2,1)S(1)}, bf16[8,24,768]{2,1,0:T(8,128)(2,1)S(1)}, u32[]{:S(2)}, u32[]{:S(2)}) collective-permute-start(bf16[8,24,768]{2,1,0:T(8,128)(2,1)S(1)} %fusion.16), channel_id=1, source_target_pairs={{0,2},{1,3},{2,0},{3,1},{4,6},{5,7},{6,4},{7,5},{8,10},{9,11},{10,... | collective-permute-start | bytes 884744 | tf_op jit(solution)/shard_map/ppermute | solution.py:630
  185.1 22.6 %collective-permute-start.36 = (bf16[2,256,768]{2,1,0:T(8,128)(2,1)S(1)}, bf16[2,256,768]{2,1,0:T(8,128)(2,1)S(1)}, u32[]{:S(2)}, u32[]{:S(2)}) collective-permute-start(bf16[2,256,768]{2,1,0:T(8,128)(2,1)S(1)} %get-tuple-element.102), channel_id=1, source_target_pairs={{0,1},{1,0},{2,3},{3,2},{4,5},{5,4},{6,7},{7,6},{8,9},{9,8},{10,11... | collective-permute-start | bytes 2359304 | tf_op jit(solution)/shard_map/ppermute | solution.py:630
  186.1 23.8 %collective-permute-start.30 = (bf16[256,768]{1,0:T(8,128)(2,1)S(1)}, bf16[256,768]{1,0:T(8,128)(2,1)S(1)}, u32[]{:S(2)}, u32[]{:S(2)}) collective-permute-start(bf16[256,768]{1,0:T(8,128)(2,1)S(1)} %fusion.14), channel_id=1, source_target_pairs={{0,2},{1,3},{2,0},{3,1},{4,6},{5,7},{6,4},{7,5},{8,10},{9,11},{10,... | collective-permute-start | bytes 1179656 | tf_op jit(solution)/shard_map/ppermute | solution.py:630
  189.5 19.0 %collective-permute-start.40 = (bf16[2752,128]{1,0:T(8,128)(2,1)S(1)}, bf16[2752,128]{1,0:T(8,128)(2,1)S(1)}, u32[]{:S(2)}, u32[]{:S(2)}) collective-permute-start(bf16[2752,128]{1,0:T(8,128)(2,1)S(1)} %get-tuple-element.109), channel_id=1, source_target_pairs={{0,4},{1,5},{2,6},{3,7},{4,0},{5,1},{6,2},{7,3},{8,12},{9,13},{10,... | collective-permute-start | bytes 2113544 | tf_op jit(solution)/shard_map/ppermute | solution.py:630
  190.1 15.7 %collective-permute-start.48 = (bf16[576,256]{1,0:T(8,128)(2,1)S(1)}, bf16[576,256]{1,0:T(8,128)(2,1)S(1)}, u32[]{:S(2)}, u32[]{:S(2)}) collective-permute-start(bf16[576,256]{1,0:T(8,128)(2,1)S(1)} %fusion.15), channel_id=1, source_target_pairs={{0,16},{1,17},{2,18},{3,19},{4,20},{5,21},{6,22},{7,23},{8,24},{9,... | collective-permute-start | bytes 884744 | tf_op jit(solution)/shard_map/ppermute | solution.py:630
  208.5 11.7 %collective-permute-start.37 = (bf16[256,768]{1,0:T(8,128)(2,1)S(1)}, bf16[256,768]{1,0:T(8,128)(2,1)S(1)}, u32[]{:S(2)}, u32[]{:S(2)}) collective-permute-start(bf16[256,768]{1,0:T(8,128)(2,1)S(1)} %fusion.12), channel_id=1, source_target_pairs={{0,2},{1,3},{2,0},{3,1},{4,6},{5,7},{6,4},{7,5},{8,10},{9,11},{10,... | collective-permute-start | bytes 1179656 | tf_op jit(solution)/shard_map/ppermute | solution.py:630
  210.0 10.6 %collective-permute-start.41 = (bf16[1408,128]{1,0:T(8,128)(2,1)S(1)}, bf16[1408,128]{1,0:T(8,128)(2,1)S(1)}, u32[]{:S(2)}, u32[]{:S(2)}) collective-permute-start(bf16[1408,128]{1,0:T(8,128)(2,1)S(1)} %get-tuple-element.111), channel_id=1, source_target_pairs={{0,8},{1,9},{2,10},{3,11},{4,12},{5,13},{6,14},{7,15},{8,0},{9,1},... | collective-permute-start | bytes 1081352 | tf_op jit(solution)/shard_map/ppermute | solution.py:630
  220.7 10.6 %collective-permute-start.42 = (bf16[736,128]{1,0:T(8,128)(2,1)S(1)}, bf16[736,128]{1,0:T(8,128)(2,1)S(1)}, u32[]{:S(2)}, u32[]{:S(2)}) collective-permute-start(bf16[736,128]{1,0:T(8,128)(2,1)S(1)} %get-tuple-element.113), channel_id=1, source_target_pairs={{0,16},{1,17},{2,18},{3,19},{4,20},{5,21},{6,22},{7,23},{8,24},{9,... | collective-permute-start | bytes 565256 | tf_op jit(solution)/shard_map/ppermute | solution.py:630
  (68 other events, 332.2 us)
Sparse Core Ops, SparseCore 0:
  10.9 64.8 all-gather.1

commit v2 on v1

--- a/solution.py
+++ b/solution.py
@@ -43,19 +43,29 @@
     return jnp.where(relative > 0, NB // 2, 0) + jnp.where(distance < 8, distance, far)
 
 
-def call(kernel, out_shape, *args, scratch=(), smem=(), vmem=48, flops=0, nbytes=0, name=None):
+def call(
+    kernel, out_shape, *args, scratch=(), smem=(), held=(), after=(), vmem=8, cost=0, name=None
+):
     vspec = pl.BlockSpec(memory_space=pltpu.VMEM)
     sspec = pl.BlockSpec(memory_space=pltpu.SMEM)
+    aspec = pl.BlockSpec(memory_space=pl.ANY)
+    hspec = pl.BlockSpec(memory_space=pltpu.HBM)
+    skip = len(after)
+
+    def body(*refs):
+        kernel(*refs[skip:])
+
+    specs = [sspec if n in smem else hspec if n in held else vspec for n in range(len(args))]
     return pl.pallas_call(
-        kernel,
+        body,
         out_shape=out_shape,
-        in_specs=[sspec if n in smem else vspec for n in range(len(args))],
+        in_specs=[aspec] * skip + specs,
         out_specs=jax.tree.map(lambda _: vspec, out_shape),
         scratch_shapes=list(scratch),
         compiler_params=pltpu.CompilerParams(vmem_limit_bytes=vmem * MIB),
-        cost_estimate=pl.CostEstimate(flops=flops, bytes_accessed=nbytes, transcendentals=0),
+        cost_estimate=pl.CostEstimate(flops=cost * 1_150_000_000, bytes_accessed=0, transcendentals=0),
         name=name,
-    )(*args)
+    )(*after, *args)
 
 
 def sds(shape, dtype):
@@ -66,19 +76,36 @@
     return lax.broadcasted_iota(jnp.int32, (rows, 128), 1) < 64
 
 
-def prep_kernel(wq, wk, wv, wg, wu, g1, g2, s0, s1, s2, s3, slabs):
+def prep_kernel(
+    wq, wk, wv, wg, wu, g1, g2, s0, s1, s2, s3, gains, slabs, vq, vk, vv, vg, vu, sems
+):
     j_me = lax.axis_index("blk")
     rows = wq.shape[0]
+    pairs = ((wq, vq), (wk, vk), (wv, vv), (wg, vg), (wu, vu))
+    copies = [pltpu.make_async_copy(a, b, sems.at[n]) for n, (a, b) in enumerate(pairs)]
+    for copy in copies:
+        copy.start()
+    eye = lax.broadcasted_iota(jnp.int32, (rows, rows), 0) == lax.broadcasted_iota(
+        jnp.int32, (rows, rows), 1
+    )
+    columns = []
+    for n, ref in enumerate((g1, g2)):
+        row = jnp.broadcast_to(ref[...].astype(F32).reshape(1, rows), (rows, rows))
+        column = jnp.sum(jnp.where(eye, row, 0.0), axis=1, keepdims=True)
+        columns.append(column)
+        gains[n] = jnp.broadcast_to(column, (rows, 128))
     low = low_half(rows)
     lane = lax.broadcasted_iota(jnp.int32, (rows, 128), 1)
-    gains = jnp.where(lane == 64, g1[...], jnp.where(lane == 65, g2[...], 0.0))
+    spare = jnp.where(lane == 64, columns[0], jnp.where(lane == 65, columns[1], 0.0))
+    for copy in copies:
+        copy.wait()
 
     def tile(ref, index):
         return ref[:, 128 * index : 128 * index + 128].astype(F32)
 
     for j in range(TP):
         first, second = [], []
-        for ref in (wq, wk, wv):
+        for ref in (vq, vk, vv):
             at = 192 * j // 128
             a, b = tile(ref, at), tile(ref, at + 1)
             if j % 2:
@@ -88,9 +115,9 @@
             second.append(b)
         tiles = first + [
             jnp.where(low, second[0], pltpu.roll(second[1], 64, 1)),
-            jnp.where(low, second[2], gains),
+            jnp.where(low, second[2], spare),
         ]
-        for ref in (wg, wu):
+        for ref in (vg, vu):
             for t in range(4):
                 a = tile(ref, 4 * t + j // 2)
                 b = tile(ref, 4 * t + 2 + j // 2)
@@ -104,16 +131,64 @@
         ref[...] = slabs[k]
 
 
-def pack_kernel(s0, s1, s2, s3, wd, first, second, whole):
+def pack_kernel(s0, s1, s2, s3, wo, first, whole, vo, sem):
     j = lax.axis_index("blk")
     rows = s0.shape[0]
+    copy = pltpu.make_async_copy(wo, vo, sem)
+    copy.start()
     for k, ref in enumerate((s0, s1, s2, s3)):
-        whole[pl.ds(pl.multiple_of(rows * (j ^ k), 8), rows)] = ref[...].astype(F32)
-    first[...] = whole[:, 0:640].astype(BF16)
+        whole[pl.ds(pl.multiple_of(rows * (j ^ k), 8), rows)] = ref[:, 0:640].astype(F32)
+    first[0:96] = whole[...].astype(BF16)
+    copy.wait()
+    out = vo[...].astype(F32)
+    rest = [out[8 * n : 8 * n + 8, 640:768] for n in range(3)]
+    rest = jnp.concatenate(rest + [jnp.zeros((8, 256), F32)], axis=1)
+    first[96:128] = jnp.concatenate([out[:, 0:640], rest], axis=0).astype(BF16)
+
+
+def pack_more_kernel(s0, s1, s2, s3, wd, cot, seg, second, extra, whole, vd, sems):
+    j = lax.axis_index("blk")
+    rows = s0.shape[0]
+    pairs = ((wd, vd), (cot, extra.at[0:T]))
+    copies = [pltpu.make_async_copy(a, b, sems.at[n]) for n, (a, b) in enumerate(pairs)]
+    for copy in copies:
+        copy.start()
+    for k, ref in enumerate((s0, s1, s2, s3)):
+        whole[pl.ds(pl.multiple_of(rows * (j ^ k), 8), rows)] = ref[:, 640:1664].astype(F32)
     for n in range(4):
-        second[96 * n : 96 * n + 96] = whole[:, 640 + 256 * n : 896 + 256 * n].astype(BF16)
+        second[96 * n : 96 * n + 96] = whole[:, 256 * n : 256 * n + 256].astype(BF16)
+    ids = jnp.broadcast_to(seg[...], (16, T))
+    extra[T : T + 16, 0:T] = (ids // 2).astype(F32).astype(BF16)
+    extra[T : T + 16, T : 2 * T] = (ids % 2).astype(F32).astype(BF16)
+    extra[T : T + 16, 2 * T : 3 * T] = jnp.zeros((16, T), BF16)
+    for copy in copies:
+        copy.wait()
     for n in range(3):
-        second[384 + 64 * n : 448 + 64 * n] = wd[:, 256 * n : 256 * n + 256]
+        second[384 + 64 * n : 448 + 64 * n] = vd[:, 256 * n : 256 * n + 256]
+
+
+def stripes_kernel(p0, p1, p2, p3, p4, p5, p6, p7, out, whole):
+    dp = lax.axis_index("dp")
+    for n, ref in enumerate((p0, p1, p2, p3, p4, p5, p6, p7)):
+        at = pl.ds(pl.multiple_of(24 * (dp ^ piece_at(n)), 8), 24)
+        part = ref[96:128].astype(F32)
+        whole[at, 0:640] = part[0:24]
+        rest = [part[24:32, 128 * m : 128 * m + 128] for m in range(3)]
+        whole[at, 640:768] = jnp.concatenate(rest, axis=0)
+    out[...] = whole[...].astype(BF16)
+
+
+def out_weight_kernel(p0, p1, p2, p3, out, whole):
+    j = lax.axis_index("blk")
+    for k, ref in enumerate((p0, p1, p2, p3)):
+        rows = ref[...].astype(F32)
+        for d in range(8):
+            at = pl.multiple_of(24 * (TP * d + (j ^ k)), 8)
+            whole[pl.ds(at, 24)] = rows[24 * d : 24 * d + 24]
+    for k in range(TP):
+        at = pl.multiple_of(192 * (j ^ k), 64)
+        out[128 * k : 128 * k + 128] = whole[pl.ds(at, 128)].astype(BF16)
+        out[512 + 64 * k : 576 + 64 * k] = whole[pl.ds(at + 128, 64)].astype(BF16)
 
 
 def bias_kernel(table, out):
@@ -135,13 +210,15 @@
     return 2 * (n % 4) + n // 4
 
 
-def qkv_kernel(t0, t1, t2, t3, p0, p1, p2, p3, p4, p5, p6, p7, tok, n1, qkv, w, gains):
+def qkv_kernel(
+    t0, t1, t2, t3, p0, p1, p2, p3, p4, p5, p6, p7, tok, n1, qkv, w, gains
+):
     j = lax.axis_index("blk")
     dp = lax.axis_index("dp")
     for k, ref in enumerate((t0, t1, t2, t3)):
         tok[j ^ k] = ref[...]
     for n, ref in enumerate((p0, p1, p2, p3, p4, p5, p6, p7)):
-        w[pl.ds(pl.multiple_of(96 * (dp ^ piece_at(n)), 32), 96)] = ref[...]
+        w[pl.ds(pl.multiple_of(96 * (dp ^ piece_at(n)), 32), 96)] = ref[0:96]
     turned = jnp.transpose(w[:, 512:640].astype(F32))
     gains[...] = turned[64:72]
 
@@ -158,66 +235,63 @@
     lax.fori_loop(0, TP, body, 0)
 
 
-def attn_fwd_kernel(
-    table, bias, qkv, s0, s1, s2, s3, prob, inv_tot, out_t, att, segq, segk, qtm, vt, sc
-):
+def row_kernel(e0, e1, e2, e3, cot, segq, segk):
     j_me = lax.axis_index("blk")
-    for k, ref in enumerate((s0, s1, s2, s3)):
-        row = ref[...].astype(F32)
-        segq[j_me ^ k] = jnp.broadcast_to(row, (8, T))
-        col = jnp.transpose(jnp.broadcast_to(row, (128, T)))
+    for k, ref in enumerate((e0, e1, e2, e3)):
+        cot[j_me ^ k] = ref[0:T]
+        parts = ref[T : T + 16].astype(F32)
+        row = (2.0 * parts[:, 0:T] + parts[:, T : 2 * T])[0:8]
+        segq[j_me ^ k] = row
+        col = jnp.transpose(jnp.broadcast_to(row[0:1], (128, T)))
         segk[j_me ^ k, :, 0:128] = col
         segk[j_me ^ k, :, 128:256] = col
+
+
+def attn_fwd_kernel(h, table, bias, qkv, segq, segk, prob, inv_tot, out_t, qt, vt, sc):
+    j_me = lax.axis_index("blk")
     rows_low = lax.broadcasted_iota(jnp.int32, (128, T), 0) < 64
+    half = slice(64, 128) if h == 1 else slice(0, 64)
     for i in range(TP):
-        q0 = jnp.transpose(qkv[0, i].astype(F32))
-        q1 = jnp.transpose(pltpu.roll(qkv[3, i].astype(F32), 64, 1))
-        qtm[0, i] = jnp.where(rows_low, q0, 0.0).astype(BF16)
-        qtm[1, i] = jnp.where(rows_low, 0.0, q0).astype(BF16)
-        qtm[2, i] = jnp.where(rows_low, 0.0, q1).astype(BF16)
-        v0 = jnp.transpose(qkv[2, i].astype(F32)).astype(BF16)
-        v1 = jnp.transpose(qkv[4, i].astype(F32)).astype(BF16)
-        vt[0, :, T * i : T * i + T] = v0[0:64]
-        vt[1, :, T * i : T * i + T] = v0[64:128]
-        vt[2, :, T * i : T * i + T] = v1[0:64]
-
-    def head(h, carry):
-        tile = 1 + 2 * (h // 2)
-        far = (table[15, HT * j_me + h], table[31, HT * j_me + h])
-        for i in range(TP):
-            peak = jnp.full((1, T), MASKED, F32)
-            for j in range(TP):
-                s = dot(qkv[tile, j], qtm[h, i])
-                if abs(j - i) <= 1:
-                    s = s + bias[h, j - i + 1]
-                else:
-                    s = s + far[j > i]
-                if i in (0, TP - 1) or j in (0, TP - 1):
-                    s = jnp.where(segk[j] == segq[i, 0:1], s, MASKED)
-                sc[j] = s
-                peak = jnp.maximum(peak, jnp.max(s, axis=0, keepdims=True))
-            total = jnp.zeros((1, T), F32)
-            for j in range(TP):
-                p = jnp.exp(sc[j] - peak)
-                total = total + jnp.sum(p, axis=0, keepdims=True)
-                prob[h, i, j] = p.astype(BF16)
-            inv = 1.0 / total
-            inv_tot[h, i] = inv
-            o = dot(vt[h], prob[h, i].reshape(TP * T, T))
-            out_t[h, :, T * i : T * i + T] = o * inv
-        return carry
-
-    lax.fori_loop(0, HT, head, 0)
+        if h < 2:
+            q = jnp.transpose(qkv[0, i].astype(F32))
+        else:
+            q = jnp.transpose(pltpu.roll(qkv[3, i].astype(F32), 64, 1))
+        qt[i] = jnp.where(rows_low == (h == 0), q, 0.0).astype(BF16)
+        v = jnp.transpose(qkv[2 + 2 * (h // 2), i].astype(F32)).astype(BF16)
+        vt[:, T * i : T * i + T] = v[half]
+
+    tile = 1 + 2 * (h // 2)
+    far = (table[15, HT * j_me + h], table[31, HT * j_me + h])
+    for i in range(TP):
+        peak = jnp.full((1, T), MASKED, F32)
+        for j in range(TP):
+            s = dot(qkv[tile, j], qt[i])
+            if abs(j - i) <= 1:
+                s = s + bias[h, j - i + 1]
+            else:
+                s = s + far[j > i]
+            if i in (0, TP - 1) or j in (0, TP - 1):
+                s = jnp.where(segk[j] == segq[i, 0:1], s, MASKED)
+            sc[j] = s
+            peak = jnp.maximum(peak, jnp.max(s, axis=0, keepdims=True))
+        total = jnp.zeros((1, T), F32)
+        for j in range(TP):
+            p = jnp.exp(sc[j] - peak)
+            total = total + jnp.sum(p, axis=0, keepdims=True)
+            prob[i, j] = p.astype(BF16)
+        inv = 1.0 / total
+        inv_tot[i] = inv
+        out_t[:, T * i : T * i + T] = dot(vt[...], prob[i].reshape(TP * T, T)) * inv
+
+
+def join_kernel(o0, o1, o2, att):
     for b in range(TP):
-        both = jnp.concatenate(
-            [out_t[0, :, T * b : T * b + T], out_t[1, :, T * b : T * b + T]], axis=0
-        )
-        att[T * b : T * b + T, :] = jnp.transpose(both).astype(BF16)
+        at = slice(T * b, T * b + T)
+        both = jnp.concatenate([o0[:, at], o1[:, at]], axis=0)
+        att[at, :] = jnp.transpose(both).astype(BF16)
     for b in range(2):
-        both = jnp.concatenate(
-            [out_t[2, :, T * b : T * b + T], out_t[2, :, T * (b + 2) : T * (b + 2) + T]], axis=0
-        )
-        att[1024 + T * b : 1024 + T * b + T, :] = jnp.transpose(both).astype(BF16)
+        both = [o2[:, T * c : T * c + T] for c in (b, b + 2)]
+        att[1024 + T * b : 1280 + T * b, :] = jnp.transpose(jnp.concatenate(both, axis=0)).astype(BF16)
 
 
 def put_pair(keep, give, k, value):
@@ -230,23 +304,23 @@
         give[k // 2] = value
 
 
-def ffn_kernel(
-    a0, a1, a2, a3, wo, gains, p0, p1, p2, p3, p4, p5, p6, p7, tok, c0, c1, c2, c3,
-    attc, wop, cot, n2, hid, ggug, two_keep, two_give, lo_keep, lo_give, mixed_own, wgu, wd,
-):
-    j = lax.axis_index("blk")
+def units_kernel(p0, p1, p2, p3, p4, p5, p6, p7, wgu, wd):
     dp = lax.axis_index("dp")
     for n, ref in enumerate((p0, p1, p2, p3, p4, p5, p6, p7)):
         at = dp ^ piece_at(n)
+        rows = pl.ds(pl.multiple_of(96 * at, 32), 96)
         for m in range(4):
-            wgu[pl.ds(pl.multiple_of(96 * at, 32), 96), 256 * m : 256 * m + 256] = ref[96 * m : 96 * m + 96]
+            wgu[rows, 256 * m : 256 * m + 256] = ref[96 * m : 96 * m + 96]
+        rows = pl.ds(pl.multiple_of(64 * at, 64), 64)
         for m in range(3):
-            wd[pl.ds(pl.multiple_of(64 * at, 64), 64), 256 * m : 256 * m + 256] = ref[384 + 64 * m : 448 + 64 * m]
-    for k, ref in enumerate((c0, c1, c2, c3)):
-        cot[j ^ k] = ref[...]
-        at = pl.multiple_of(192 * (j ^ k), 64)
-        wop[128 * k : 128 * k + 128] = wo[pl.ds(at, 128)]
-        wop[512 + 64 * k : 512 + 64 * k + 64] = wo[pl.ds(at + 128, 64)]
+            wd[rows, 256 * m : 256 * m + 256] = ref[384 + 64 * m : 448 + 64 * m]
+
+
+def ffn_kernel(
+    a0, a1, a2, a3, gains, wop, wgu, wd, tok, cot,
+    attc, n2, hid, ggug, two_keep, two_give, lo_keep, lo_give, mixed_own,
+):
+    j = lax.axis_index("blk")
     low = low_half(T)
 
     def body(k, carry):
@@ -291,13 +365,13 @@
     lax.fori_loop(0, TP, body, 0)
 
 
-def mid_kernel(keep, rc, rx, mixed_own, cot_own, attc, wop, gains, mixed_grad, g0, g1, g2, g3, wo_keep, wo_give, dw):
+def mid_kernel(keep, rc, rx, mixed_own, cot, attc, wop, gains, mixed_grad, g0, g1, g2, g3, wo_keep, wo_one, wo_three, dw):
     j = lax.axis_index("blk")
     u = (keep[0].astype(F32) + rc[0].astype(F32) + rx[...].astype(F32)) * gains[1:2]
     mixed = mixed_own[...]
     rstd = lax.rsqrt(jnp.mean(mixed * mixed, axis=-1, keepdims=True) + EPSILON)
     n = mixed * rstd
-    mg = cot_own[...].astype(F32) + rstd * (u - n * jnp.mean(u * n, axis=-1, keepdims=True))
+    mg = cot[j].astype(F32) + rstd * (u - n * jnp.mean(u * n, axis=-1, keepdims=True))
     mixed_grad[...] = mg
     ml = mg.astype(BF16)
     ag = dot_nt(ml, wop[...])
@@ -317,16 +391,15 @@
         dw[pl.ds(at, 128)] = perm[128 * k : 128 * k + 128]
         dw[pl.ds(at + 128, 64)] = perm[512 + 64 * k : 512 + 64 * k + 64]
     for k in range(TP):
-        ref = wo_give if k % 2 else wo_keep
+        ref = (wo_keep.at[0], wo_one, wo_keep.at[1], wo_three)[k]
         for d in range(8):
             at = pl.multiple_of(24 * (TP * d + (j ^ k)), 8)
-            ref[k // 2, d] = dw[pl.ds(at, 24)].astype(BF16)
+            ref[d] = dw[pl.ds(at, 24)].astype(BF16)
 
 
 SLOTS = (0, 2, 1, 3)
-WO_ROWS = 32
-CHUNK = 5 * 96 + 6 * WO_ROWS
-TAIL = 64
+CHUNK = 5 * 96 + 6 * 24
+TAIL = 16
 
 
 def slots(body):
@@ -336,7 +409,7 @@
             body(give, slot, dp ^ (2 * z + give))
 
 
-def ffn_dw_kernel(n2, ggug, hid, cot, keep, give, dwgu, dwd):
+def ffn_dw_kernel(n2, ggug, hid, cot, y_keep, y_give, z_keep, z_give, dwgu, dwd):
     for m in range(2):
         at = slice(512 * m, 512 * m + 512)
         dwgu[:, at] = dot_tn(n2[...], ggug[:, at])
@@ -345,50 +418,60 @@
         dwd[:, at] = dot_tn(hid[...], cot[:, at])
 
     def put(g, slot, owner):
-        ref = give if g else keep
+        ref = y_give if g else y_keep
         a = pl.ds(pl.multiple_of(96 * owner, 32), 96)
-        for m in range(4):
+        for m in range(3):
             ref[slot, 96 * m : 96 * m + 96] = dwgu[a, 256 * m : 256 * m + 256].astype(BF16)
+        ref = z_give if slot > 1 else z_keep
+        slot = 2 * (slot % 2) + g
+        ref[slot, 0:96] = dwgu[a, 768:1024].astype(BF16)
         a = pl.ds(pl.multiple_of(64 * owner, 64), 64)
         for m in range(3):
-            ref[slot, 384 + 64 * m : 448 + 64 * m] = dwd[a, 256 * m : 256 * m + 256].astype(BF16)
+            ref[slot, 96 + 64 * m : 160 + 64 * m] = dwd[a, 256 * m : 256 * m + 256].astype(BF16)
 
     slots(put)
 
 
+def ffn_second_kernel(y_keep, y_got, z_keep, z_got, y_next, y_give, z_next, z_give):
+    for keep, got, rest, give in ((y_keep, y_got, y_next, y_give), (z_keep, z_got, z_next, z_give)):
+        rest[...] = (keep[0:2].astype(F32) + got[0:2].astype(F32)).astype(BF16)
+        give[...] = (keep[2:4].astype(F32) + got[2:4].astype(F32)).astype(BF16)
+
+
+def ffn_third_kernel(y_keep, y_got, z_keep, z_got, y_give, z_give):
+    y_give[...] = (y_keep[1].astype(F32) + y_got[1].astype(F32)).astype(BF16)
+    z_give[...] = (z_keep[1].astype(F32) + z_got[1].astype(F32)).astype(BF16)
+
+
 def split(x):
-    high = x.astype(BF16)
-    return high, (x - high.astype(F32)).astype(BF16)
-
-
-def attn_dw_kernel(n1, dqkv, wo_keep, wo_got, wo_along, table_grad, keep, give, dw, wo):
+    high = x.astype(BF16).astype(F32)
+    return jnp.concatenate([high, x - high], axis=0).astype(BF16)
+
+
+def attn_dw_kernel(n1, dqkv, wo_keep, wo_got, wo_along, table_grad, keep, give, dw, wo, chunk):
     for t in range(5):
         at = slice(128 * t, 128 * t + 128)
         dw[:, at] = dot_tn(n1[...], dqkv[:, at])
     for d in range(8):
-        wo[d] = wo_keep[0, d].astype(F32) + wo_got[0, d].astype(F32) + wo_along[d].astype(F32)
+        wo[d] = wo_keep[0, d].astype(F32) + wo_got[d].astype(F32) + wo_along[d].astype(F32)
 
     def put(g, slot, owner):
         ref = give if g else keep
-        base = CHUNK * slot
         a = pl.ds(pl.multiple_of(96 * owner, 32), 96)
         for t in range(5):
-            ref[base + 96 * t : base + 96 * t + 96] = dw[a, 128 * t : 128 * t + 128].astype(BF16)
-        base = base + 480
-        pad = jnp.zeros((WO_ROWS - 24, 128), F32)
+            chunk[96 * t : 96 * t + 96] = dw[a, 128 * t : 128 * t + 128]
         for t in range(6):
-            part = wo[owner, :, 128 * t : 128 * t + 128]
-            full = jnp.concatenate([part, pad], axis=0)
-            ref[base + WO_ROWS * t : base + WO_ROWS * t + WO_ROWS] = full.astype(BF16)
+            chunk[480 + 24 * t : 504 + 24 * t] = wo[owner, :, 128 * t : 128 * t + 128]
+        ref[CHUNK * slot : CHUNK * slot + CHUNK] = chunk[...].astype(BF16)
 
     slots(put)
     for ref in (keep, give):
-        for n, part in enumerate(split(table_grad[...])):
-            ref[4 * CHUNK + 32 * n : 4 * CHUNK + 32 * n + 32] = part
+        ref[4 * CHUNK : 4 * CHUNK + 16] = split(table_grad[...])
 
 
 def tail_of(ref, base):
-    return ref[base : base + 32].astype(F32) + ref[base + 32 : base + 64].astype(F32)
+    both = ref[base : base + 16].astype(F32)
+    return both[0:8] + both[8:16]
 
 
 def stage_kernel(n, keep, got, next_keep, next_give):
@@ -396,42 +479,34 @@
     for at, ref in ((0, next_keep), (half, next_give)):
         here = slice(at, at + half)
         ref[0:half] = (keep[here].astype(F32) + got[here].astype(F32)).astype(BF16)
-        parts = split(tail_of(keep, n * CHUNK) + tail_of(got, n * CHUNK))
-        for m, part in enumerate(parts):
-            ref[half + 32 * m : half + 32 * m + 32] = part
-
-
-def back_kernel(keep, got, dwo, b0, b1, b2, b3, total):
+        ref[half : half + 16] = split(tail_of(keep, n * CHUNK) + tail_of(got, n * CHUNK))
+
+
+def back_kernel(keep, got, yk, yg, ya, zk, zg, za, dwo, dwd, b0, b1, b2, b3, total, ffn):
     j = lax.axis_index("blk")
+    ffn[0:288] = yk[0].astype(F32) + yg[0].astype(F32) + ya[...].astype(F32)
+    ffn[288:576] = zk[0].astype(F32) + zg[0].astype(F32) + za[...].astype(F32)
+    for m in range(3):
+        dwd[:, 256 * m : 256 * m + 256] = ffn[384 + 64 * m : 448 + 64 * m]
     total[...] = keep[0:CHUNK].astype(F32) + got[0:CHUNK].astype(F32)
-    parts = split(tail_of(keep, CHUNK) + tail_of(got, CHUNK))
+    parts = split(tail_of(keep, CHUNK) + tail_of(got, CHUNK)).astype(F32)
+    parts = jnp.concatenate([parts, jnp.zeros((8, 128), F32)], axis=0).astype(BF16)
     for t in range(6):
-        at = 480 + WO_ROWS * t
+        at = 480 + 24 * t
         dwo[:, 128 * t : 128 * t + 128] = total[at : at + 24]
-    pad = jnp.zeros((8, 128), F32)
     for k, ref in enumerate((b0, b1, b2, b3)):
         for t in range(5):
             part = total[pl.ds(pl.multiple_of(96 * t + 24 * (j ^ k), 8), 24)]
-            ref[0:32, 128 * t : 128 * t + 128] = jnp.concatenate([part, pad], axis=0).astype(BF16)
-        for m, part in enumerate(parts):
-            ref[32:64, 128 * m : 128 * m + 128] = part
-        ref[32:64, 256:640] = jnp.zeros((32, 384), BF16)
-
-
-def ffn_back_kernel(keep, got, along, dwd, b0, b1, b2, b3, total):
-    j = lax.axis_index("blk")
-    total[...] = keep[0].astype(F32) + got[0].astype(F32) + along[...].astype(F32)
-    for m in range(3):
-        dwd[:, 256 * m : 256 * m + 256] = total[384 + 64 * m : 448 + 64 * m]
-    for k, ref in enumerate((b0, b1, b2, b3)):
+            ref[:, 128 * t : 128 * t + 128] = part.astype(BF16)
         for m in range(4):
-            part = total[pl.ds(pl.multiple_of(96 * m + 24 * (j ^ k), 8), 24)]
-            ref[:, 256 * m : 256 * m + 256] = part.astype(BF16)
+            part = ffn[pl.ds(pl.multiple_of(96 * m + 24 * (j ^ k), 8), 24)]
+            ref[:, 640 + 256 * m : 896 + 256 * m] = part.astype(BF16)
+        ref[:, 1664:1792] = parts
 
 
 def attn_bwd_kernel(
-    qkv, prob, inv_tot, out_t, g0, g1, g2, g3, w,
-    dqkv, one_keep, one_give, table_grad,
+    qkv, p0, p1, p2, v0, v1, v2, o0, o1, o2, g0, g1, g2, g3,
+    dqkv, table_grad,
     dotm, dom, qm, ktm, delta, dst, dq_acc, dk_acc, dv_acc, near, far,
 ):
     j_me = lax.axis_index("blk")
@@ -446,8 +521,8 @@
         second = jnp.concatenate([rest, pltpu.roll(rest, 64, 1)], axis=0)
         t0 = jnp.transpose(first)
         t1 = jnp.transpose(second)
-        t0 = t0 * jnp.where(rows_low, inv_tot[0, b], inv_tot[1, b])
-        t1 = jnp.where(rows_low, t1 * inv_tot[2, b], 0.0)
+        t0 = t0 * jnp.where(rows_low, v0[b], v1[b])
+        t1 = jnp.where(rows_low, t1 * v2[b], 0.0)
         t0, t1 = t0.astype(BF16), t1.astype(BF16)
         f0, f1 = t0.astype(F32), t1.astype(F32)
         dotm[0, b] = jnp.where(rows_low, f0, 0.0).astype(BF16)
@@ -463,7 +538,7 @@
         for h in range(HT):
             g = dotm[h, i].astype(F32)
             g = g[64:128] if h == 1 else g[0:64]
-            delta[h, i] = jnp.sum(out_t[h, :, at] * g, axis=0, keepdims=True)
+            delta[h, i] = jnp.sum((o0, o1, o2)[h][:, at] * g, axis=0, keepdims=True)
         q0 = qkv[0, i].astype(F32)
         turned = pltpu.roll(qkv[3, i].astype(F32), 64, 1)
         qm[0, i] = jnp.where(low, q0, 0.0).astype(BF16)
@@ -495,7 +570,7 @@
     hot_neg = bucket_of(-lane_id) == row_id
     hot_pos = bucket_of(128 - lane_id) == row_id
 
-    def head(h, carry):
+    for h, prob in enumerate((p0, p1, p2)):
         second = h // 2
         near[...] = jnp.zeros(near.shape, F32)
         far[...] = jnp.zeros(far.shape, F32)
@@ -504,7 +579,7 @@
             row_delta = delta[h, i]
             for j in range(TP):
                 dp = dot(qkv[2 + 2 * second, j], dotm[h, i])
-                ds = prob[h, i, j].astype(F32) * (dp - row_delta)
+                ds = prob[i, j].astype(F32) * (dp - row_delta)
                 dst[j] = ds.astype(BF16)
                 for a in range(2):
                     for c in range(2):
@@ -517,7 +592,7 @@
             d_all = dst[...].reshape(TP * T, T)
             dq_acc[second, :, at] += dot(ktm[h], d_all)
             dk_acc[second] += dot(d_all, qm[h, i])
-            dv_acc[second] += dot(prob[h, i].reshape(TP * T, T), dom[h, i])
+            dv_acc[second] += dot(prob[i].reshape(TP * T, T), dom[h, i])
         before, diagonal, after = near[0], near[1], near[2]
         neg = jnp.where(upper, diagonal, before)
         pos = jnp.where(upper, after, diagonal)
@@ -535,10 +610,8 @@
             + jnp.where(row_id == 31, far_pos, 0.0)
         )
         sums = jnp.sum(spread, axis=1, keepdims=True)
-        table_grad[...] += jnp.where(lane_id == HT * j_me + h, sums, 0.0)
-        return carry
-
-    lax.fori_loop(0, HT, head, 0)
+        sums = jnp.sum(jnp.where(lane_id == row_id, sums, 0.0), axis=0, keepdims=True)
+        table_grad[h : h + 1] = sums
     for i in range(TP):
         at = slice(T * i, T * i + T)
         dq0 = jnp.transpose(dq_acc[0, :, at])
@@ -549,9 +622,12 @@
         dqkv[i, :, 384:512] = (dq1 + dk_acc[1, at]).astype(BF16)
         dqkv[i, :, 512:640] = dv_acc[1, at].astype(BF16)
 
+
+def one_grad_kernel(dqkv, w, keep, give):
+    j = lax.axis_index("blk")
+
     def body(k, carry):
-        b = j_me ^ k
-        put_pair(one_keep, one_give, k, dot_nt(dqkv[b], w[...]).astype(BF16))
+        put_pair(keep, give, k, dot_nt(dqkv[j ^ k], w[...]).astype(BF16))
         return carry
 
     lax.fori_loop(0, TP, body, 0)
@@ -566,15 +642,28 @@
     return jnp.sum(total, axis=1, keepdims=True) / gain
 
 
-def attn_final_kernel(b0, b1, b2, b3, g1, wq, wk, wv, dq, dk, dv, gg1, table, src):
+def put_row(ref, wide):
+    rows = wide.shape[0]
+    row_id = lax.broadcasted_iota(jnp.int32, (rows, 128), 0)
+    eye = row_id == lax.broadcasted_iota(jnp.int32, (rows, 128), 1)
+    ref[...] = jnp.sum(jnp.where(eye, wide, 0.0), axis=0, keepdims=True)[:, 0:rows]
+
+
+def final_kernel(
+    b0, b1, b2, b3, gains, wq, wk, wv, wg, wu, dq, dk, dv, dg, du, gg1, gg2, table, src
+):
     j_me = lax.axis_index("blk")
     rows = wq.shape[0]
     low = low_half(rows)
-    sums = jnp.zeros((NB, 128), F32)
+    heads = jnp.zeros((128, 128), F32)
+    head_id = lax.broadcasted_iota(jnp.int32, (128, 128), 0)
     for k, ref in enumerate((b0, b1, b2, b3)):
-        src[j_me ^ k] = ref[0:32].astype(F32)
-        sums = sums + ref[32:64, 0:128].astype(F32) + ref[32:64, 128:256].astype(F32)
-    table[...] = sums
+        src[j_me ^ k] = ref[:, 0:1664].astype(F32)
+        parts = ref[:, 1664:1792].astype(F32)
+        for h in range(HT):
+            row = parts[h : h + 1] + parts[8 + h : 9 + h]
+            heads = jnp.where(head_id == HT * (j_me ^ k) + h, row, heads)
+    table[...] = jnp.transpose(heads)[0:NB, 0:H]
 
     def one(j, n):
         return src[j, 0:rows, 128 * n : 128 * n + 128]
@@ -593,30 +682,33 @@
                 jnp.where(low, rest[0], mid),
                 jnp.where(low, mid, pltpu.roll(rest[1], 64, 1)),
             ]
-        gain_grad = gain_grad + finish(parts, w, out, g1[...])
-    gg1[...] = gain_grad
-
-
-def ffn_final_kernel(b0, b1, b2, b3, g2, wg, wu, dg, du, gg2, src):
-    j_me = lax.axis_index("blk")
-    rows = wg.shape[0]
-    low = low_half(rows)
-    for k, ref in enumerate((b0, b1, b2, b3)):
-        src[j_me ^ k] = ref[...].astype(F32)
+        gain_grad = gain_grad + finish(parts, w, out, gains[0])
+    put_row(gg1, gain_grad)
     gain_grad = jnp.zeros((rows, 128), F32)
     for n, (w, out) in enumerate(((wg, dg), (wu, du))):
         parts = [None] * 16
         for t in range(4):
-            at = slice(512 * n + 128 * t, 512 * n + 128 * t + 128)
+            at = 5 + 4 * n + t
             for half in range(2):
-                a, b = src[2 * half, :, at], src[2 * half + 1, :, at]
+                a, b = one(2 * half, at), one(2 * half + 1, at)
                 parts[4 * t + half] = jnp.where(low, a, pltpu.roll(b, 64, 1))
                 parts[4 * t + 2 + half] = jnp.where(low, pltpu.roll(a, 64, 1), b)
-        gain_grad = gain_grad + finish(parts, w, out, g2[...])
-    gg2[...] = gain_grad
+        gain_grad = gain_grad + finish(parts, w, out, gains[1])
+    put_row(gg2, gain_grad)
+
+
+def close_kernel(keep, got, along, mixed_grad, tok, gains, tokens_grad):
+    x = tok[lax.axis_index("blk")].astype(F32)
+    rstd = lax.rsqrt(jnp.mean(x * x, axis=-1, keepdims=True) + EPSILON)
+    n = x * rstd
+    u = (keep[0].astype(F32) + got[0].astype(F32) + along[...].astype(F32)) * gains[0:1]
+    grad = rstd * (u - n * jnp.mean(u * n, axis=-1, keepdims=True))
+    tokens_grad[...] = mixed_grad[...] + grad
 
 
 AXES = ("dp", "blk")
+GATE = 0
+COST = {"qkv": 0, "attn_fwd": (0, 20, 20), "units": 30, "ffn": 0, "ffn_dw": 0, "mid": 20, "attn_bwd": 40, "one_grad": 40, "stage_y": 10, "stage_z": 10}
 
 
 def group_local(
@@ -626,130 +718,153 @@
 ):
     n_dev = n_dp * n_blk
 
+    def later(x, *others):
+        return lax.optimization_barrier((x,) + others)[0]
+
     def swap(x, mask):
         return lax.ppermute(x, AXES, [(d, d ^ mask) for d in range(n_dev)])
 
-    def share(x):
+    def share(x, *others):
         along = swap(x, 2)
-        return (x, swap(x, 1), along, swap(along, 1))
+        return (x, swap(x, 1), along, swap(later(along, *others), 1))
 
     def reduce_pair(keep, give):
         got = swap(give, 1)
         return got, swap(keep[1] + got[1], 2)
 
+    def round_one(x, late=None):
+        late = x if late is None else late
+        return lax.optimization_barrier((swap(x, 16), swap(late, 8), swap(late, 4)))
+
+    def round_two(state):
+        far, near, _ = state
+        return lax.optimization_barrier((swap(far, 8), swap(near, 4), swap(far, 4)))
+
+    def gathered(x, one, two):
+        far, near, other = one
+        last, near_y, far_y = two
+        return (x, near, far, last, other, near_y, far_y, swap(last, 4))
+
     tok_own, cot_own = tokens[0], cotangent[0]
-    rows = w_query.shape[0]
+    rows, ff = w_query.shape[0], w_gate.shape[1]
+    flat = TP * T
     table = rel_bias.astype(F32)
-    gain1 = jnp.broadcast_to(attn_gain.astype(F32)[:, None], (rows, 128))
-    gain2 = jnp.broadcast_to(ffn_gain.astype(F32)[:, None], (rows, 128))
-
-    def spread(x):
-        near, far = swap(x, 8), swap(x, 16)
-        last = swap(far, 8)
-        return (x, near, far, last) + tuple(swap(v, 4) for v in (x, near, far, last))
-
-    slabs = call(
-        prep_kernel, (sds((rows, 1664), BF16),) * TP,
-        w_query, w_key, w_value, w_gate, w_up, gain1, gain2, name="prep",
-        scratch=(pltpu.VMEM((TP, rows, 1664), BF16),),
+
+    toks_x, toks_c = swap(tok_own, 2), swap(tok_own, 1)
+    *slabs, gain_cols = call(
+        prep_kernel,
+        (sds((rows, 1664), BF16),) * TP + (sds((2, rows, 128), F32),),
+        w_query, w_key, w_value, w_gate, w_up, attn_gain, ffn_gain,
+        name="prep", vmem=60, held=(0, 1, 2, 3, 4),
+        scratch=(
+            pltpu.VMEM((TP, rows, 1664), BF16),
+            *(pltpu.VMEM((rows, D), BF16),) * 3,
+            *(pltpu.VMEM((rows, ff), BF16),) * 2,
+            pltpu.SemaphoreType.DMA((5,)),
+        ),
     )
     slabs = (slabs[0], swap(slabs[1], 1), swap(slabs[2], 2), swap(slabs[3], 3))
-    first, second = call(
-        pack_kernel, (sds((96, 640), BF16), sds((576, 256), BF16)),
-        *slabs, w_down, name="pack", scratch=(pltpu.VMEM((96, 1664), F32),),
-    )
-    toks = share(tok_own)
-    firsts = spread(first)
-    segs = share(segment_ids)
-    seconds = spread(second)
-    wo = lax.all_gather(w_attn_out, AXES, axis=0, tiled=True)
-    cots = share(cot_own)
-
     bias = call(bias_kernel, sds((HT, 3, T, T), F32), table, smem=(0,), name="bias")
+    first = call(
+        pack_kernel, sds((128, 640), BF16), *slabs, w_attn_out,
+        name="pack", vmem=60, held=(4,), after=(bias,),
+        scratch=(pltpu.VMEM((96, 640), F32), pltpu.VMEM((rows, D), BF16), pltpu.SemaphoreType.DMA),
+    )
+    second, extra = call(
+        pack_more_kernel, (sds((576, 256), BF16), sds((T + 16, D), BF16)),
+        *slabs, w_down, cot_own, segment_ids, name="pack_more", vmem=60, held=(4, 5), after=(first,),
+        scratch=(
+            pltpu.VMEM((96, 1024), F32), pltpu.VMEM((64, D), BF16), pltpu.SemaphoreType.DMA((2,)),
+        ),
+    )
+    first_one = round_one(first)
+    first_two = round_two(lax.optimization_barrier(first_one + (extra,))[:3])
+    firsts = gathered(first, first_one, first_two)
+    toks = (tok_own, toks_c, toks_x, swap(later(toks_x, *first_two), 1))
+    second_one = round_one(later(second, *first_one), later(second, *first_two))
+
     tok, n1, qkv, w_qkv, gains = call(
         qkv_kernel,
         (
             sds((TP, T, D), BF16), sds((TP, T, D), BF16), sds((5, TP, T, 128), BF16),
             sds((D, 640), BF16), sds((8, D), F32),
         ),
-        *toks, *firsts, name="qkv",
-        flops=2 * 1024 * 768 * 640, nbytes=8 * MIB,
-    )
-    prob, inv_tot, out_t, att = call(
-        attn_fwd_kernel,
-        (
-            sds((HT, TP, TP, T, T), BF16),
-            sds((HT, TP, 1, T), F32),
-            sds((HT, DH, TP * T), F32),
-            sds((1536, 128), BF16),
-        ),
-        table, bias, qkv, *segs, smem=(0,), name="attn_fwd",
-        scratch=(
-            pltpu.VMEM((TP, 8, T), F32),
-            pltpu.VMEM((TP, T, T), F32),
-            pltpu.VMEM((HT, TP, 128, T), BF16),
-            pltpu.VMEM((HT, DH, TP * T), BF16),
-            pltpu.VMEM((TP, T, T), F32),
-        ),
-        flops=8 * 1024 * 1024 * 768, nbytes=8 * MIB,
-    )
-    atts = share(att)
-    (
-        attc, wop, cot, n2, hid, ggug, two_keep, two_give, lo_keep, lo_give, mixed_own,
-    ) = call(
+        *toks, *firsts, name="qkv", vmem=16, cost=COST["qkv"],
+    )
+    extras = share(extra, gains)
+    cot, segq, segk = call(
+        row_kernel, (sds((TP, T, D), BF16), sds((TP, 8, T), F32), sds((TP, T, T), F32)),
+        *extras, name="row",
+    )
+    stripes = call(
+        stripes_kernel, sds((192, D), BF16), *firsts, name="stripes", after=(segq,),
+        scratch=(pltpu.VMEM((192, D), F32),),
+    )
+    stripes = share(stripes)
+    wop = call(
+        out_weight_kernel, sds((D, D), BF16), *stripes, name="out_weight",
+        scratch=(pltpu.VMEM((D, D), F32),),
+    )
+    heads = []
+    for h in range(HT):
+        heads.append(
+            call(
+                functools.partial(attn_fwd_kernel, h),
+                (sds((TP, TP, T, T), BF16), sds((TP, 1, T), F32), sds((DH, flat), F32)),
+                table, bias, qkv, segq, segk, smem=(0,), name="attn_fwd", vmem=14,
+                cost=COST["attn_fwd"][h], after=(heads[-1][1],) if heads else (),
+                scratch=(
+                    pltpu.VMEM((TP, 128, T), BF16),
+                    pltpu.VMEM((DH, flat), BF16),
+                    pltpu.VMEM((TP, T, T), F32),
+                ),
+            )
+        )
+    probs, inv_tots, out_ts = zip(*heads)
+    second_two = round_two(lax.optimization_barrier(second_one + (inv_tots[GATE],))[:3])
+    seconds = gathered(second, second_one, second_two)
+    att = call(join_kernel, sds((1536, 128), BF16), *out_ts, name="join")
+    atts = share(att, wop)
+    wgu, wd = call(
+        units_kernel, (sds((D, 1024), BF16), sds((512, D), BF16)), *seconds, name="units",
+        cost=COST["units"],
+    )
+    attc, n2, hid, ggug, two_keep, two_give, lo_keep, lo_give, mixed_own = call(
         ffn_kernel,
         (
-            sds((TP, T, D), BF16), sds((D, D), BF16), sds((TP, T, D), BF16), sds((TP, T, D), BF16),
+            sds((TP, T, D), BF16), sds((TP, T, D), BF16),
             sds((TP, T, 512), BF16), sds((TP, T, 1024), BF16),
             sds((2, T, D), BF16), sds((2, T, D), BF16), sds((2, T, D), BF16), sds((2, T, D), BF16),
             sds((T, D), F32),
         ),
-        *atts, wo, gains, *seconds, tok, *cots, name="ffn",
-        scratch=(pltpu.VMEM((D, 1024), BF16), pltpu.VMEM((512, D), BF16)),
-        flops=2 * 1024 * 768 * (768 + 512 * 6), nbytes=16 * MIB,
+        *atts, gains, wop, wgu, wd, tok, cot, name="ffn", vmem=30, cost=COST["ffn"],
     )
     two_c, two_x = reduce_pair(two_keep, two_give)
-    mixed_grad, g0, g1, g2, g3, wo_keep, wo_give = call(
+    y_keep, y_give, z_keep, z_give = call(
+        ffn_dw_kernel, (sds((4, 288, 256), BF16),) * 4,
+        n2.reshape(flat, D), ggug.reshape(flat, 1024), hid.reshape(flat, 512), cot.reshape(flat, D),
+        name="ffn_dw", vmem=20, cost=COST["ffn_dw"],
+        scratch=(pltpu.VMEM((D, 1024), F32), pltpu.VMEM((512, D), F32)),
+    )
+    y_got, z_got = swap(y_give, 4), swap(z_give, 8)
+    mixed_grad, g0, g1, g2, g3, wo_keep, *wo_gives = call(
         mid_kernel,
-        (sds((T, D), F32),) + (sds((384, 128), BF16),) * 4 + (sds((2, 8, 24, D), BF16),) * 2,
-        two_keep, two_c, two_x, mixed_own, cot_own, attc, wop, gains, name="mid",
-        scratch=(pltpu.VMEM((D, D), F32),),
-        flops=4 * 256 * 768 * 768, nbytes=8 * MIB,
+        (sds((T, D), F32),) + (sds((384, 128), BF16),) * 4
+        + (sds((2, 8, 24, D), BF16),) + (sds((8, 24, D), BF16),) * 2,
+        two_keep, two_c, two_x, mixed_own, cot, attc, wop, gains, name="mid", vmem=16,
+        after=(y_give,), scratch=(pltpu.VMEM((D, D), F32),), cost=COST["mid"],
     )
     g1, g2, g3 = swap(g1, 1), swap(g2, 2), swap(g3, 3)
-    wo_got, wo_along = reduce_pair(wo_keep, wo_give)
-    flat = TP * T
-    keep, give = call(
-        ffn_dw_kernel, (sds((4, 576, 256), BF16),) * 2,
-        n2.reshape(flat, D), ggug.reshape(flat, 1024), hid.reshape(flat, 512), cot.reshape(flat, D),
-        name="ffn_dw", scratch=(pltpu.VMEM((D, 1024), F32), pltpu.VMEM((512, D), F32)),
-        flops=2 * 1024 * 768 * 512 * 3, nbytes=12 * MIB,
-    )
-    got = swap(give, 4)
-    f_give = keep[2:] + got[2:]
-    f_keep = keep[:2] + got[:2]
-    got = swap(f_give, 8)
-    along = swap(f_keep[1] + got[1], 16)
-    dwd, *backs = call(
-        ffn_back_kernel, (sds((64, D), F32),) + (sds((rows, 1024), BF16),) * 4,
-        f_keep, got, along, name="ffn_back", scratch=(pltpu.VMEM((576, 256), F32),),
-    )
-    backs = (backs[0], swap(backs[1], 1), swap(backs[2], 2), swap(backs[3], 3))
-    ff = w_gate.shape[1]
-    dg, du, gg2 = call(
-        ffn_final_kernel, (sds((rows, ff), F32),) * 2 + (sds((rows, 128), F32),),
-        *backs, gain2, w_gate, w_up, name="ffn_final",
-        scratch=(pltpu.VMEM((TP, rows, 1024), F32),),
-    )
-    dqkv, one_keep, one_give, table_grad = call(
+    lo_c = swap(later(lo_give, mixed_grad), 1)
+    lo_x = swap(later(lo_keep[1] + lo_c[1], g1, g2, g3), 2)
+    layer_out = mixed_own + lo_keep[0].astype(F32) + lo_c[0].astype(F32) + lo_x.astype(F32)
+    wo_got = (swap(wo_gives[0], 1), swap(wo_gives[1], 1))
+    wo_along = swap(later(wo_keep[1] + wo_got[1], g1, g2, g3), 2)
+    dqkv, table_grad = call(
         attn_bwd_kernel,
-        (
-            sds((TP, T, 640), BF16),
-            sds((2, T, D), BF16),
-            sds((2, T, D), BF16),
-            sds((NB, 128), F32),
-        ),
-        qkv, prob, inv_tot, out_t, g0, g1, g2, g3, w_qkv, name="attn_bwd",
+        (sds((TP, T, 640), BF16), sds((8, 128), F32)),
+        qkv, *probs, *inv_tots, *out_ts, g0, g1, g2, g3, name="attn_bwd", vmem=26,
+        cost=COST["attn_bwd"], after=(y_got, z_got),
         scratch=(
             pltpu.VMEM((HT, TP, 128, T), BF16),
             pltpu.VMEM((HT, TP, T, 128), BF16),
@@ -763,47 +878,65 @@
             pltpu.VMEM((3, 128, 128), F32),
             pltpu.VMEM((2, 8, 128), F32),
         ),
-        flops=16 * 1024 * 1024 * 768, nbytes=12 * MIB,
-    )
-    one_c, one_x = reduce_pair(one_keep, one_give)
-    lo_c, lo_x = reduce_pair(lo_keep, lo_give)
-    layer_out = mixed_own + lo_keep[0].astype(F32) + lo_c[0].astype(F32) + lo_x.astype(F32)
+    )
 
     def chunks(n):
         return sds((n * CHUNK + TAIL, 128), BF16)
 
     keep, give = call(
         attn_dw_kernel, (chunks(4),) * 2,
-        n1.reshape(flat, D), dqkv.reshape(flat, 640), wo_keep, wo_got, wo_along, table_grad,
-        name="attn_dw", scratch=(pltpu.VMEM((D, 640), F32), pltpu.VMEM((8, 24, D), F32)),
-        flops=2 * 1024 * 768 * 640, nbytes=6 * MIB,
+        n1.reshape(flat, D), dqkv.reshape(flat, 640), wo_keep, wo_got[0], wo_along, table_grad,
+        name="attn_dw", vmem=16,
+        scratch=(
+            pltpu.VMEM((D, 640), F32), pltpu.VMEM((8, 24, D), F32), pltpu.VMEM((CHUNK, 128), F32),
+        ),
     )
     got = swap(give, 4)
+    y_keep, y_give, z_keep, z_give = call(
+        ffn_second_kernel, (sds((2, 288, 256), BF16),) * 4, y_keep, y_got, z_keep, z_got,
+        name="ffn_second", after=(give,),
+    )
+    y_got, z_got = swap(y_give, 8), swap(z_give, 16)
+    one_keep, one_give = call(
+        one_grad_kernel, (sds((2, T, D), BF16),) * 2, dqkv, w_qkv, name="one_grad", vmem=16,
+        after=(y_give,), cost=COST["one_grad"],
+    )
+    one_c, one_x = reduce_pair(one_keep, one_give)
+    tokens_grad = call(
+        close_kernel, sds((T, D), F32), one_keep, one_c, one_x, mixed_grad, tok, gains,
+        name="close", vmem=10,
+    )
+    y_give, z_give = call(
+        ffn_third_kernel, (sds((288, 256), BF16),) * 2, y_keep, y_got, z_keep, z_got,
+        name="ffn_third", after=(give,),
+    )
+    y_along, z_along = swap(y_give, 16), swap(z_give, 4)
     keep, give = call(
-        functools.partial(stage_kernel, 4), (chunks(2),) * 2, keep, got, name="stage_y"
+        functools.partial(stage_kernel, 4), (chunks(2),) * 2, keep, got, name="stage_y",
+        after=(y_give,), cost=COST["stage_y"],
     )
     got = swap(give, 8)
     keep, give = call(
-        functools.partial(stage_kernel, 2), (chunks(1),) * 2, keep, got, name="stage_z"
+        functools.partial(stage_kernel, 2), (chunks(1),) * 2, keep, got, name="stage_z",
+        after=(y_along, z_along), cost=COST["stage_z"],
     )
     got = swap(give, 16)
-    dwo, *backs = call(
-        back_kernel, (sds((rows, D), F32),) + (sds((64, 640), BF16),) * 4,
-        keep, got, name="back", scratch=(pltpu.VMEM((CHUNK, 128), F32),),
+    dwo, dwd, *backs = call(
+        back_kernel,
+        (sds((rows, D), F32), sds((64, D), F32)) + (sds((rows, 1792), BF16),) * 4,
+        keep, got, y_keep, y_got, y_along, z_keep, z_got, z_along, name="back", after=(tokens_grad,),
+        scratch=(pltpu.VMEM((CHUNK, 128), F32), pltpu.VMEM((576, 256), F32)),
     )
     backs = (backs[0], swap(backs[1], 1), swap(backs[2], 2), swap(backs[3], 3))
-    dq, dk, dv, gg1, table_sum = call(
-        attn_final_kernel,
-        (sds((rows, D), F32),) * 3 + (sds((rows, 128), F32), sds((NB, 128), F32)),
-        *backs, gain1, w_query, w_key, w_value, name="attn_final",
-        scratch=(pltpu.VMEM((TP, 32, 640), F32),),
-    )
-
-    x = tok_own.astype(F32)
-    rstd = lax.rsqrt(jnp.mean(x * x, axis=-1, keepdims=True) + EPSILON)
-    n = x * rstd
-    u = (one_keep[0].astype(F32) + one_c[0].astype(F32) + one_x.astype(F32)) * gains[0:1]
-    tokens_grad = mixed_grad + rstd * (u - n * jnp.mean(u * n, axis=-1, keepdims=True))
+    dq, dk, dv, dg, du, gg1, gg2, table_sum = call(
+        final_kernel,
+        (sds((rows, D), F32),) * 3
+        + (sds((rows, ff), F32),) * 2
+        + (sds((1, rows), F32), sds((1, rows), F32), sds((NB, H), F32)),
+        *backs, gain_cols, w_query, w_key, w_value, w_gate, w_up, name="final",
+        scratch=(pltpu.VMEM((TP, rows, 1664), F32),),
+    )
+
     return (
         layer_out.astype(BF16)[None],
         tokens_grad[None],
@@ -811,12 +944,12 @@
         dk,
         dv,
         dwo,
-        gg1[:, 0],
-        table_sum[:, :H],
+        gg1[0],
+        table_sum,
         dg,
         du,
         dwd,
-        gg2[:, 0],
+        gg2[0],
     )
 
 

time: 248 us -> 187 us (0.75)
  local copies, waits for them, and re-layouts: 30.3 us -> 5.57 us
  waiting for transfers between devices: 92.4 us -> 76.2 us
  between operations: 14.4 us -> 1.08 us
  Pallas kernels: 65.1 us -> 55.3 us
  starting transfers between devices: 42.1 us -> 47 us
    unnamed x96 -> x34, local copies, waits for them, and re-layouts: 27.6 us -> 5.57 us
    ppermute x52 -> x53, waiting for transfers between devices: 91.7 us -> 76.2 us  [swap(): return lax.ppermute(x, AXES, [(d, d ^ mask) for d in range(n_dev)])]
    pallas_call x16 -> x26, Pallas kernels: 65.1 us -> 55.3 us  [call(): pl.pallas_call(body, out_shape=out_shape, in_specs=[aspec] * skip + specs...]
    ppermute x52 -> x53, starting transfers between devices: 42 us -> 47 us  [swap(): return lax.ppermute(x, AXES, [(d, d ^ mask) for d in range(n_dev)])]
  transfers between devices with their start and end apart: 53 -> 53, of which waited for: 23 -> 25; matrix products, arithmetic and copies ran while one was open for 2% -> 1% of each run, Pallas kernels for 18% -> 20%
where the time goes in v2:
time: 187 us; the launch traced here: 186 us
  waiting for transfers between devices  76.2 us (41%)
  Pallas kernels  55.3 us (30%)
  starting transfers between devices  47 us (25%)
  local copies, waits for them, and re-layouts  5.57 us (3%)
    ppermute x53, waiting for transfers between devices, swap(): return lax.ppermute(x, AXES, [(d, d ^ mask) for d in range(n_dev)])  76.2 us
    pallas_call x26, Pallas kernels, call(): pl.pallas_call(body, out_shape=out_shape, in_specs=[aspec] * skip + specs...  55.3 us
    ppermute x53, starting transfers between devices, swap(): return lax.ppermute(x, AXES, [(d, d ^ mask) for d in range(n_dev)])  47 us
    unnamed x34, local copies, waits for them, and re-layouts  5.57 us
  transfers between devices with their start and end apart: 53, of which 25 were waited for; matrix products, arithmetic and copies ran while one was open for 1% of the time, Pallas kernels for 20%

profile of v2, /device:TPU:0, one launch (start us, length us, event | category | flops | bytes accessed | tf_op | source)
XLA Modules:
  0.0 186.3 jit_solution(2240075322789939183)
XLA Ops:
  0.6 2.6 %prep.1 = (bf16[24,1664]{1,0:T(8,128)(2,1)}, bf16[24,1664]{1,0:T(8,128)(2,1)}, bf16[24,1664]{1,0:T(8,128)(2,1)}, bf16[24,1664]{1,0:T(8,128)(2,1)}, f32[2,24,128]{2,1,0:T(8,128)}) custom-call(bf16[24,768]{1,0:T(8,128)(2,1)} %refs_5_.7, bf16[24,768]{1,0:T(8,128)(2,1)} %refs_6_.3, bf16[24,768]{1,0:T(8,128)(2,1)} %refs_7_.3, bf16[24,2048]{1,0:T(8,128)(2,1)} %refs_8_.1, ...), custom_call_target="tpu_custom_call" | custom-call | tf_op jit(solution)/shard_map/prep/pallas_call | solution.py:59
  3.8 2.6 %collective-permute-start.3 = (bf16[24,1664]{1,0:T(8,128)(2,1)}, bf16[24,1664]{1,0:T(8,128)(2,1)S(1)}, u32[]{:S(2)}, u32[]{:S(2)}) collective-permute-start(bf16[24,1664]{1,0:T(8,128)(2,1)} %get-tuple-element.115), channel_id=1, source_target_pairs={{0,2},{1,3},{2,0},{3,1},{4,6},{5,7},{6,4},{7,5},{8,10},{9,11},{10,... | collective-permute-start | bytes 239624 | tf_op jit(solution)/shard_map/ppermute | solution.py:725
  12.5 2.5 %pack.1.refs_0_.refs_4_.refs_1_ = bf16[128,640]{1,0:T(8,128)(2,1)} custom-call(f32[3,3,256,256]{3,2,1,0:T(8,128)} %copy-done, bf16[24,1664]{1,0:T(8,128)(2,1)} %get-tuple-element.113.refs_1_, bf16[24,1664]{1,0:T(8,128)(2,1)} %copy-done.13, bf16[24,1664]{1,0:T(8,128)(2,1)} %copy-done.14, bf16[24,1664]{1,0:T(8,128)(2,1)} %copy-done.15, bf16[24,768]{1,0:T(8,128)(2,1)} %refs_5_.5), custom_call_target="tpu_custom_call" | custom-call | tf_op jit(solution)/shard_map/pack/pallas_call | solution.py:59
  18.2 2.6 %collective-permute-start.5 = (bf16[128,640]{1,0:T(8,128)(2,1)}, bf16[128,640]{1,0:T(8,128)(2,1)S(1)}, u32[]{:S(2)}, u32[]{:S(2)}) collective-permute-start(bf16[128,640]{1,0:T(8,128)(2,1)} %pack.1.refs_0_.refs_4_.refs_1_), channel_id=1, source_target_pairs={{0,16},{1,17},{2,18},{3,19},{4,20},{5,21},{6,22},{7,23},{8,24},{9,... | collective-permute-start | bytes 491528 | tf_op jit(solution)/shard_map/ppermute | solution.py:725
  20.8 2.9 %pack_more.1 = (bf16[576,256]{1,0:T(8,128)(2,1)}, bf16[272,768]{1,0:T(8,128)(2,1)}) custom-call(bf16[128,640]{1,0:T(8,128)(2,1)} %pack.1.refs_0_.refs_4_.refs_1_, bf16[24,1664]{1,0:T(8,128)(2,1)} %get-tuple-element.113.refs_1_, bf16[24,1664]{1,0:T(8,128)(2,1)} %copy-done.13, bf16[24,1664]{1,0:T(8,128)(2,1)} %copy-done.14, bf16[24,1664]{1,0:T(8,128)(2,1)} %copy-done.15, ...), custom_call_target="tpu_custom_call" | custom-call | tf_op jit(solution)/shard_map/pack_more/pallas_call | solution.py:59
  23.7 2.4 %collective-permute-done.6.refs_5_.refs_2_ = bf16[128,640]{1,0:T(8,128)(2,1)S(1)} collective-permute-done((bf16[128,640]{1,0:T(8,128)(2,1)}, bf16[128,640]{1,0:T(8,128)(2,1)S(1)}, u32[]{:S(2)}, u32[]{:S(2)}) %collective-permute-start.6) | collective-permute-done | bytes 163872 | tf_op jit(solution)/shard_map/ppermute | solution.py:725
  26.1 2.4 %collective-permute-done.5.refs_6_.refs_3_ = bf16[128,640]{1,0:T(8,128)(2,1)S(1)} collective-permute-done((bf16[128,640]{1,0:T(8,128)(2,1)}, bf16[128,640]{1,0:T(8,128)(2,1)S(1)}, u32[]{:S(2)}, u32[]{:S(2)}) %collective-permute-start.5) | collective-permute-done | bytes 163872 | tf_op jit(solution)/shard_map/ppermute | solution.py:725
  36.6 5.9 %collective-permute-done.12.refs_11_.refs_8_ = bf16[128,640]{1,0:T(8,128)(2,1)S(1)} collective-permute-done((bf16[128,640]{1,0:T(8,128)(2,1)S(1)}, bf16[128,640]{1,0:T(8,128)(2,1)S(1)}, u32[]{:S(2)}, u32[]{:S(2)}) %collective-permute-start.12) | collective-permute-done | bytes 163872 | tf_op jit(solution)/shard_map/ppermute | solution.py:725
  43.4 2.7 %qkv.1 = (bf16[4,256,768]{2,1,0:T(8,128)(2,1)S(1)}, bf16[4,256,768]{2,1,0:T(8,128)(2,1)S(1)}, bf16[5,4,256,128]{3,2,1,0:T(8,128)(2,1)S(1)}, bf16[768,640]{1,0:T(8,128)(2,1)S(1)}, f32[8,768]{1,0:T(8,128)S(1)}) custom-call(bf16[256,768]{1,0:T(8,128)(2,1)S(1)} %bitcast.38, bf16[256,768]{1,0:T(8,128)(2,1)S(1)} %collective-permute-done.refs_1_, ...), custom_call_target="tpu_custom_call" | custom-call | tf_op jit(solution)/shard_map/qkv/pallas_call | solution.py:59
  49.8 13.3 %collective-permute-done.22.refs_2_ = bf16[576,256]{1,0:T(8,128)(2,1)S(1)} collective-permute-done((bf16[576,256]{1,0:T(8,128)(2,1)}, bf16[576,256]{1,0:T(8,128)(2,1)S(1)}, u32[]{:S(2)}, u32[]{:S(2)}) %collective-permute-start.22) | collective-permute-done | bytes 294944 | tf_op jit(solution)/shard_map/ppermute | solution.py:725
  63.3 3.5 %attn_fwd.3 = (bf16[4,4,256,256]{3,2,1,0:T(8,128)(2,1)S(1)}, f32[4,1,256]{2,1,0:T(1,128)S(1)}, f32[64,1024]{1,0:T(8,128)S(1)}) custom-call(f32[32,12]{1,0:T(8,128)S(1)} %convert_element_type.21.refs_0_.refs_1_, f32[3,3,256,256]{3,2,1,0:T(8,128)S(1)} %copy-done.1, bf16[5,4,256,128]{3,2,1,0:T(8,128)(2,1)S(1)} %get-tuple-element.127.refs_2_.refs_3_, ...), custom_call_target="tpu_custom_call" | custom-call | tf_op jit(solution)/shard_map/attn_fwd/pallas_call | solution.py:59
  68.0 3.5 %attn_fwd.4 = (bf16[4,4,256,256]{3,2,1,0:T(8,128)(2,1)S(1)}, f32[4,1,256]{2,1,0:T(1,128)S(1)}, f32[64,1024]{1,0:T(8,128)S(1)}) custom-call(f32[4,1,256]{2,1,0:T(1,128)S(1)} %get-tuple-element.133.refs_0_.refs_6_, f32[32,12]{1,0:T(8,128)S(1)} %convert_element_type.21.refs_0_.refs_1_, f32[3,3,256,256]{3,2,1,0:T(8,128)S(1)} %copy-done.1, ...), custom_call_target="tpu_custom_call" | custom-call | flops 23000000512 | tf_op jit(solution)/shard_map/attn_fwd/pallas_call | solution.py:59
  71.5 2.2 %collective-permute-start.19 = (bf16[192,768]{1,0:T(8,128)(2,1)S(1)}, bf16[192,768]{1,0:T(8,128)(2,1)S(1)}, u32[]{:S(2)}, u32[]{:S(2)}) collective-permute-start(bf16[192,768]{1,0:T(8,128)(2,1)S(1)} %stripes.1.refs_0_), channel_id=1, source_target_pairs={{0,2},{1,3},{2,0},{3,1},{4,6},{5,7},{6,4},{7,5},{8,10},{9,11},{10,... | collective-permute-start | bytes 884744 | tf_op jit(solution)/shard_map/ppermute | solution.py:725
  75.2 3.5 %attn_fwd.5 = (bf16[4,4,256,256]{3,2,1,0:T(8,128)(2,1)S(1)}, f32[4,1,256]{2,1,0:T(1,128)S(1)}, f32[64,1024]{1,0:T(8,128)S(1)}) custom-call(f32[4,1,256]{2,1,0:T(1,128)S(1)} %get-tuple-element.135.refs_0_.refs_7_, f32[32,12]{1,0:T(8,128)S(1)} %convert_element_type.21.refs_0_.refs_1_, f32[3,3,256,256]{3,2,1,0:T(8,128)S(1)} %copy-done.1, ...), custom_call_target="tpu_custom_call" | custom-call | flops 23000000512 | tf_op jit(solution)/shard_map/attn_fwd/pallas_call | solution.py:59
  83.6 5.0 %collective-permute-done.17.refs_2_ = bf16[1536,128]{1,0:T(8,128)(2,1)S(1)} collective-permute-done((bf16[1536,128]{1,0:T(8,128)(2,1)S(1)}, bf16[1536,128]{1,0:T(8,128)(2,1)S(1)}, u32[]{:S(2)}, u32[]{:S(2)}) %collective-permute-start.17) | collective-permute-done | bytes 393248 | tf_op jit(solution)/shard_map/ppermute | solution.py:725
  88.6 2.6 %collective-permute-done.28.refs_7_ = bf16[576,256]{1,0:T(8,128)(2,1)S(1)} collective-permute-done((bf16[576,256]{1,0:T(8,128)(2,1)S(1)}, bf16[576,256]{1,0:T(8,128)(2,1)S(1)}, u32[]{:S(2)}, u32[]{:S(2)}) %collective-permute-start.28) | collective-permute-done | bytes 294944 | tf_op jit(solution)/shard_map/ppermute | solution.py:725
  91.4 11.3 %ffn.1 = (bf16[4,256,768]{2,1,0:T(8,128)(2,1)S(1)}, bf16[4,256,768]{2,1,0:T(8,128)(2,1)S(1)}, bf16[4,256,512]{2,1,0:T(8,128)(2,1)S(1)}, bf16[4,256,1024]{2,1,0:T...) custom-call(bf16[1536,128]{1,0:T(8,128)(2,1)S(1)} %join.1.refs_0_, ...), custom_call_target="tpu_custom_call" | custom-call | tf_op jit(solution)/shard_map/ffn/pallas_call | solution.py:59
  102.8 2.3 %collective-permute-done.29.refs_2_ = bf16[2,256,768]{2,1,0:T(8,128)(2,1)S(1)} collective-permute-done((bf16[2,256,768]{2,1,0:T(8,128)(2,1)S(1)}, bf16[2,256,768]{2,1,0:T(8,128)(2,1)S(1)}, u32[]{:S(2)}, u32[]{:S(2)}) %collective-permute-start.29) | collective-permute-done | bytes 786464 | tf_op jit(solution)/shard_map/ppermute | solution.py:725
  105.1 1.8 collective-permute-start.30
  106.9 2.9 %ffn_dw.1 = (bf16[4,288,256]{2,1,0:T(8,128)(2,1)S(1)}, bf16[4,288,256]{2,1,0:T(8,128)(2,1)S(1)}, bf16[4,288,256]{2,1,0:T(8,128)(2,1)S(1)}, bf16[4,288,256]{2,1,0:T(8,128)(2,1)S(1)}) custom-call(bf16[1024,768]{1,0:T(8,128)(2,1)S(1)} %bitcast.33, bf16[1024,1024]{1,0:T(8,128)(2,1)S(1)} %bitcast.31, bf16[1024,512]{1,0:T(8,128)(2,1)S(1)} %bitcast.35, ...), custom_call_target="tpu_custom_call" | custom-call | tf_op jit(solution)/shard_map/ffn_dw/pallas_call | solution.py:59
  111.9 4.4 %collective-permute-done.30.refs_3_ = bf16[256,768]{1,0:T(8,128)(2,1)S(1)} collective-permute-done((bf16[256,768]{1,0:T(8,128)(2,1)S(1)}, bf16[256,768]{1,0:T(8,128)(2,1)S(1)}, u32[]{:S(2)}, u32[]{:S(2)}) %collective-permute-start.30) | collective-permute-done | bytes 393248 | tf_op jit(solution)/shard_map/ppermute | solution.py:725
  121.3 1.8 collective-permute-done.33.refs_14_
  123.1 2.0 %collective-permute-done.34.refs_15_ = bf16[384,128]{1,0:T(8,128)(2,1)S(1)} collective-permute-done((bf16[384,128]{1,0:T(8,128)(2,1)S(1)}, bf16[384,128]{1,0:T(8,128)(2,1)S(1)}, u32[]{:S(2)}, u32[]{:S(2)}) %collective-permute-start.34) | collective-permute-done | bytes 98336 | tf_op jit(solution)/shard_map/ppermute | solution.py:725
  126.2 7.3 %attn_bwd.1 = (bf16[4,256,640]{2,1,0:T(8,128)(2,1)S(1)}, f32[8,128]{1,0:T(8,128)S(1)}) custom-call(bf16[4,288,256]{2,1,0:T(8,128)(2,1)S(1)} %collective-permute-done.36.refs_0_.refs_2_, bf16[4,288,256]{2,1,0:T(8,128)(2,1)S(1)} %collective-permute-done.37.refs_1_.refs_4_, bf16[5,4,256,128]{3,2,1,0:T(8,128)(2,1)S(1)} %get-tuple-element.127.refs_2_.refs_3_, ...), custom_call_target="tpu_custom_call" | custom-call | flops 46000001024 | tf_op jit(solution)/shard_map/attn_bwd/pallas_call | solution.py:59
  134.2 2.5 %attn_dw.1 = (bf16[2512,128]{1,0:T(8,128)(2,1)S(1)}, bf16[2512,128]{1,0:T(8,128)(2,1)S(1)}) custom-call(bf16[1024,768]{1,0:T(8,128)(2,1)S(1)} %bitcast.32, bf16[1024,640]{1,0:T(8,128)(2,1)S(1)} %bitcast.34, bf16[2,8,24,768]{3,2,1,0:T(8,128)(2,1)S(1)} %get-tuple-element.177.refs_2_, bf16[8,24,768]{2,1,0:T(8,128)(2,1)S(1)} %collective-permute-done.38.refs_3_, ...), custom_call_target="tpu_custom_call" | custom-call | tf_op jit(solution)/shard_map/attn_dw/pallas_call | solution.py:59
  138.7 2.6 %collective-permute-start.44 = (bf16[2,288,256]{2,1,0:T(8,128)(2,1)S(1)}, bf16[2,288,256]{2,1,0:T(8,128)(2,1)S(1)}, u32[]{:S(2)}, u32[]{:S(2)}) collective-permute-start(bf16[2,288,256]{2,1,0:T(8,128)(2,1)S(1)} %get-tuple-element.191), channel_id=1, source_target_pairs={{0,16},{1,17},{2,18},{3,19},{4,20},{5,21},{6,22},{7,23},{8,24},{9,... | collective-permute-start | bytes 884744 | tf_op jit(solution)/shard_map/ppermute | solution.py:725
  141.8 2.2 %one_grad.1 = (bf16[2,256,768]{2,1,0:T(8,128)(2,1)S(1)}, bf16[2,256,768]{2,1,0:T(8,128)(2,1)S(1)}) custom-call(bf16[2,288,256]{2,1,0:T(8,128)(2,1)S(1)} %get-tuple-element.185.refs_0_, bf16[4,256,640]{2,1,0:T(8,128)(2,1)S(1)} %get-tuple-element.176.refs_1_, bf16[768,640]{1,0:T(8,128)(2,1)S(1)} %get-tuple-element.186.refs_2_), custom_call_target="tpu_custom_call" | custom-call | flops 46000001024 | tf_op jit(solution)/shard_map/one_grad/pallas_call | solution.py:59
  144.0 10.5 %collective-permute-done.44.refs_4_.refs_7_ = bf16[2,288,256]{2,1,0:T(8,128)(2,1)S(1)} collective-permute-done((bf16[2,288,256]{2,1,0:T(8,128)(2,1)S(1)}, bf16[2,288,256]{2,1,0:T(8,128)(2,1)S(1)}, u32[]{:S(2)}, u32[]{:S(2)}) %collective-permute-start.44) | collective-permute-done | bytes 294944 | tf_op jit(solution)/shard_map/ppermute | solution.py:725
  161.1 3.3 %collective-permute-done.46.refs_1_.refs_8_ = bf16[288,256]{1,0:T(8,128)(2,1)S(1)} collective-permute-done((bf16[288,256]{1,0:T(8,128)(2,1)S(1)}, bf16[288,256]{1,0:T(8,128)(2,1)S(1)}, u32[]{:S(2)}, u32[]{:S(2)}) %collective-permute-start.46) | collective-permute-done | bytes 147488 | tf_op jit(solution)/shard_map/ppermute | solution.py:725
  165.6 1.9 %collective-permute-done.48.refs_3_ = bf16[1264,128]{1,0:T(8,128)(2,1)S(1)} collective-permute-done((bf16[1264,128]{1,0:T(8,128)(2,1)S(1)}, bf16[1264,128]{1,0:T(8,128)(2,1)S(1)}, u32[]{:S(2)}, u32[]{:S(2)}) %collective-permute-start.48) | collective-permute-done | bytes 323616 | tf_op jit(solution)/shard_map/ppermute | solution.py:725
  169.0 5.5 %collective-permute-done.42.refs_2_ = bf16[256,768]{1,0:T(8,128)(2,1)S(1)} collective-permute-done((bf16[256,768]{1,0:T(8,128)(2,1)S(1)}, bf16[256,768]{1,0:T(8,128)(2,1)S(1)}, u32[]{:S(2)}, u32[]{:S(2)}) %collective-permute-start.42) | collective-permute-done | bytes 393248 | tf_op jit(solution)/shard_map/ppermute | solution.py:725
  180.7 2.6 %collective-permute-done.51.refs_2_ = bf16[24,1792]{1,0:T(8,128)(2,1)S(1)} collective-permute-done((bf16[24,1792]{1,0:T(8,128)(2,1)S(1)}, bf16[24,1792]{1,0:T(8,128)(2,1)S(1)}, u32[]{:S(2)}, u32[]{:S(2)}) %collective-permute-start.51) | collective-permute-done | bytes 86048 | tf_op jit(solution)/shard_map/ppermute | solution.py:725
  (140 shorter events, 60.1 us)
Async XLA Ops:
  3.3 8.6 %collective-permute-start.2 = (bf16[24,1664]{1,0:T(8,128)(2,1)}, bf16[24,1664]{1,0:T(8,128)(2,1)S(1)}, u32[]{:S(2)}, u32[]{:S(2)}) collective-permute-start(bf16[24,1664]{1,0:T(8,128)(2,1)} %get-tuple-element.114), channel_id=1, source_target_pairs={{0,1},{1,0},{2,3},{3,2},{4,5},{5,4},{6,7},{7,6},{8,9},{9,8},{10,11... | collective-permute-start | bytes 239624 | tf_op jit(solution)/shard_map/ppermute | solution.py:725
  6.4 29.4 %collective-permute-start.1 = (bf16[256,768]{1,0:T(8,128)(2,1)}, bf16[256,768]{1,0:T(8,128)(2,1)S(1)}, u32[]{:S(2)}, u32[]{:S(2)}) collective-permute-start(bf16[256,768]{1,0:T(8,128)(2,1)} %bitcast.36), channel_id=1, source_target_pairs={{0,2},{1,3},{2,0},{3,1},{4,6},{5,7},{6,4},{7,5},{8,10},{9,11},{10,... | collective-permute-start | bytes 1179656 | tf_op jit(solution)/shard_map/ppermute | solution.py:725
  15.0 8.7 %collective-permute-start.7 = (bf16[128,640]{1,0:T(8,128)(2,1)}, bf16[128,640]{1,0:T(8,128)(2,1)S(1)}, u32[]{:S(2)}, u32[]{:S(2)}) collective-permute-start(bf16[128,640]{1,0:T(8,128)(2,1)} %pack.1.refs_0_.refs_4_.refs_1_), channel_id=1, source_target_pairs={{0,4},{1,5},{2,6},{3,7},{4,0},{5,1},{6,2},{7,3},{8,12},{9,13},{10,... | collective-permute-start | bytes 491528 | tf_op jit(solution)/shard_map/ppermute | solution.py:725
  16.6 9.5 %collective-permute-start.6 = (bf16[128,640]{1,0:T(8,128)(2,1)}, bf16[128,640]{1,0:T(8,128)(2,1)S(1)}, u32[]{:S(2)}, u32[]{:S(2)}) collective-permute-start(bf16[128,640]{1,0:T(8,128)(2,1)} %pack.1.refs_0_.refs_4_.refs_1_), channel_id=1, source_target_pairs={{0,8},{1,9},{2,10},{3,11},{4,12},{5,13},{6,14},{7,15},{8,0},{9,1},... | collective-permute-start | bytes 491528 | tf_op jit(solution)/shard_map/ppermute | solution.py:725
  18.2 10.3 %collective-permute-start.5 = (bf16[128,640]{1,0:T(8,128)(2,1)}, bf16[128,640]{1,0:T(8,128)(2,1)S(1)}, u32[]{:S(2)}, u32[]{:S(2)}) collective-permute-start(bf16[128,640]{1,0:T(8,128)(2,1)} %pack.1.refs_0_.refs_4_.refs_1_), channel_id=1, source_target_pairs={{0,16},{1,17},{2,18},{3,19},{4,20},{5,21},{6,22},{7,23},{8,24},{9,... | collective-permute-start | bytes 491528 | tf_op jit(solution)/shard_map/ppermute | solution.py:725
  31.0 15.2 %collective-permute-start.14 = (bf16[272,768]{1,0:T(8,128)(2,1)}, bf16[272,768]{1,0:T(8,128)(2,1)S(1)}, u32[]{:S(2)}, u32[]{:S(2)}) collective-permute-start(bf16[272,768]{1,0:T(8,128)(2,1)} %get-tuple-element.120.refs_0_), channel_id=1, source_target_pairs={{0,2},{1,3},{2,0},{3,1},{4,6},{5,7},{6,4},{7,5},{8,10},{9,11},{10,... | collective-permute-start | bytes 1253384 | tf_op jit(solution)/shard_map/ppermute | solution.py:725
  36.4 26.7 %collective-permute-start.13 = (bf16[272,768]{1,0:T(8,128)(2,1)}, bf16[272,768]{1,0:T(8,128)(2,1)S(1)}, u32[]{:S(2)}, u32[]{:S(2)}) collective-permute-start(bf16[272,768]{1,0:T(8,128)(2,1)} %get-tuple-element.120.refs_0_), channel_id=1, source_target_pairs={{0,1},{1,0},{2,3},{3,2},{4,5},{5,4},{6,7},{7,6},{8,9},{9,8},{10,11... | collective-permute-start | bytes 1253384 | tf_op jit(solution)/shard_map/ppermute | solution.py:725
  46.1 16.9 %collective-permute-start.15 = (bf16[272,768]{1,0:T(8,128)(2,1)S(1)}, bf16[272,768]{1,0:T(8,128)(2,1)S(1)}, u32[]{:S(2)}, u32[]{:S(2)}) collective-permute-start(bf16[272,768]{1,0:T(8,128)(2,1)S(1)} %collective-permute-done.14.refs_2_), channel_id=1, source_target_pairs={{0,1},{1,0},{2,3},{3,2},{4,5},{5,4},{6,7},{7,6},{8,9},{9,8},{10,11... | collective-permute-start | bytes 1253384 | tf_op jit(solution)/shard_map/ppermute | solution.py:725
  46.2 16.9 %collective-permute-start.22 = (bf16[576,256]{1,0:T(8,128)(2,1)}, bf16[576,256]{1,0:T(8,128)(2,1)S(1)}, u32[]{:S(2)}, u32[]{:S(2)}) collective-permute-start(bf16[576,256]{1,0:T(8,128)(2,1)} %get-tuple-element.140.refs_0_), channel_id=1, source_target_pairs={{0,16},{1,17},{2,18},{3,19},{4,20},{5,21},{6,22},{7,23},{8,24},{9,... | collective-permute-start | bytes 884744 | tf_op jit(solution)/shard_map/ppermute | solution.py:725
  47.7 15.3 %collective-permute-start.24 = (bf16[576,256]{1,0:T(8,128)(2,1)}, bf16[576,256]{1,0:T(8,128)(2,1)S(1)}, u32[]{:S(2)}, u32[]{:S(2)}) collective-permute-start(bf16[576,256]{1,0:T(8,128)(2,1)} %get-tuple-element.140.refs_0_), channel_id=1, source_target_pairs={{0,4},{1,5},{2,6},{3,7},{4,0},{5,1},{6,2},{7,3},{8,12},{9,13},{10,... | collective-permute-start | bytes 884744 | tf_op jit(solution)/shard_map/ppermute | solution.py:725
  48.2 14.8 %collective-permute-start.23 = (bf16[576,256]{1,0:T(8,128)(2,1)}, bf16[576,256]{1,0:T(8,128)(2,1)S(1)}, u32[]{:S(2)}, u32[]{:S(2)}) collective-permute-start(bf16[576,256]{1,0:T(8,128)(2,1)} %get-tuple-element.140.refs_0_), channel_id=1, source_target_pairs={{0,8},{1,9},{2,10},{3,11},{4,12},{5,13},{6,14},{7,15},{8,0},{9,1},... | collective-permute-start | bytes 884744 | tf_op jit(solution)/shard_map/ppermute | solution.py:725
  66.8 15.0 %collective-permute-start.27 = (bf16[576,256]{1,0:T(8,128)(2,1)S(1)}, bf16[576,256]{1,0:T(8,128)(2,1)S(1)}, u32[]{:S(2)}, u32[]{:S(2)}) collective-permute-start(bf16[576,256]{1,0:T(8,128)(2,1)S(1)} %collective-permute-done.22.refs_2_), channel_id=1, source_target_pairs={{0,4},{1,5},{2,6},{3,7},{4,0},{5,1},{6,2},{7,3},{8,12},{9,13},{10,... | collective-permute-start | bytes 884744 | tf_op jit(solution)/shard_map/ppermute | solution.py:725
  67.8 14.0 %collective-permute-start.25 = (bf16[576,256]{1,0:T(8,128)(2,1)S(1)}, bf16[576,256]{1,0:T(8,128)(2,1)S(1)}, u32[]{:S(2)}, u32[]{:S(2)}) collective-permute-start(bf16[576,256]{1,0:T(8,128)(2,1)S(1)} %collective-permute-done.22.refs_2_), channel_id=1, source_target_pairs={{0,8},{1,9},{2,10},{3,11},{4,12},{5,13},{6,14},{7,15},{8,0},{9,1},... | collective-permute-start | bytes 884744 | tf_op jit(solution)/shard_map/ppermute | solution.py:725
  71.5 8.8 %collective-permute-start.19 = (bf16[192,768]{1,0:T(8,128)(2,1)S(1)}, bf16[192,768]{1,0:T(8,128)(2,1)S(1)}, u32[]{:S(2)}, u32[]{:S(2)}) collective-permute-start(bf16[192,768]{1,0:T(8,128)(2,1)S(1)} %stripes.1.refs_0_), channel_id=1, source_target_pairs={{0,2},{1,3},{2,0},{3,1},{4,6},{5,7},{6,4},{7,5},{8,10},{9,11},{10,... | collective-permute-start | bytes 884744 | tf_op jit(solution)/shard_map/ppermute | solution.py:725
  73.7 8.1 %collective-permute-start.26 = (bf16[576,256]{1,0:T(8,128)(2,1)S(1)}, bf16[576,256]{1,0:T(8,128)(2,1)S(1)}, u32[]{:S(2)}, u32[]{:S(2)}) collective-permute-start(bf16[576,256]{1,0:T(8,128)(2,1)S(1)} %collective-permute-done.23.refs_1_), channel_id=1, source_target_pairs={{0,4},{1,5},{2,6},{3,7},{4,0},{5,1},{6,2},{7,3},{8,12},{9,13},{10,... | collective-permute-start | bytes 884744 | tf_op jit(solution)/shard_map/ppermute | solution.py:725
  79.0 9.6 %collective-permute-start.17 = (bf16[1536,128]{1,0:T(8,128)(2,1)S(1)}, bf16[1536,128]{1,0:T(8,128)(2,1)S(1)}, u32[]{:S(2)}, u32[]{:S(2)}) collective-permute-start(bf16[1536,128]{1,0:T(8,128)(2,1)S(1)} %join.1.refs_0_), channel_id=1, source_target_pairs={{0,2},{1,3},{2,0},{3,1},{4,6},{5,7},{6,4},{7,5},{8,10},{9,11},{10,... | collective-permute-start | bytes 1179656 | tf_op jit(solution)/shard_map/ppermute | solution.py:725
  81.8 9.4 %collective-permute-start.28 = (bf16[576,256]{1,0:T(8,128)(2,1)S(1)}, bf16[576,256]{1,0:T(8,128)(2,1)S(1)}, u32[]{:S(2)}, u32[]{:S(2)}) collective-permute-start(bf16[576,256]{1,0:T(8,128)(2,1)S(1)} %collective-permute-done.25.refs_3_), channel_id=1, source_target_pairs={{0,4},{1,5},{2,6},{3,7},{4,0},{5,1},{6,2},{7,3},{8,12},{9,13},{10,... | collective-permute-start | bytes 884744 | tf_op jit(solution)/shard_map/ppermute | solution.py:725
  83.2 8.2 %collective-permute-start.16 = (bf16[1536,128]{1,0:T(8,128)(2,1)S(1)}, bf16[1536,128]{1,0:T(8,128)(2,1)S(1)}, u32[]{:S(2)}, u32[]{:S(2)}) collective-permute-start(bf16[1536,128]{1,0:T(8,128)(2,1)S(1)} %join.1.refs_0_), channel_id=1, source_target_pairs={{0,1},{1,0},{2,3},{3,2},{4,5},{5,4},{6,7},{7,6},{8,9},{9,8},{10,11... | collective-permute-start | bytes 1179656 | tf_op jit(solution)/shard_map/ppermute | solution.py:725
  105.1 11.2 %collective-permute-start.30 = (bf16[256,768]{1,0:T(8,128)(2,1)S(1)}, bf16[256,768]{1,0:T(8,128)(2,1)S(1)}, u32[]{:S(2)}, u32[]{:S(2)}) collective-permute-start(bf16[256,768]{1,0:T(8,128)(2,1)S(1)} %fusion.5), channel_id=1, source_target_pairs={{0,2},{1,3},{2,0},{3,1},{4,6},{5,7},{6,4},{7,5},{8,10},{9,11},{10,... | collective-permute-start | bytes 1179656 | tf_op jit(solution)/shard_map/ppermute | solution.py:725
  109.8 16.3 %collective-permute-start.37 = (bf16[4,288,256]{2,1,0:T(8,128)(2,1)S(1)}, bf16[4,288,256]{2,1,0:T(8,128)(2,1)S(1)}, u32[]{:S(2)}, u32[]{:S(2)}) collective-permute-start(bf16[4,288,256]{2,1,0:T(8,128)(2,1)S(1)} %get-tuple-element.170), channel_id=1, source_target_pairs={{0,8},{1,9},{2,10},{3,11},{4,12},{5,13},{6,14},{7,15},{8,0},{9,1},... | collective-permute-start | bytes 1769480 | tf_op jit(solution)/shard_map/ppermute | solution.py:725
  111.3 14.9 %collective-permute-start.36 = (bf16[4,288,256]{2,1,0:T(8,128)(2,1)S(1)}, bf16[4,288,256]{2,1,0:T(8,128)(2,1)S(1)}, u32[]{:S(2)}, u32[]{:S(2)}) collective-permute-start(bf16[4,288,256]{2,1,0:T(8,128)(2,1)S(1)} %get-tuple-element.159.refs_0_), channel_id=1, source_target_pairs={{0,4},{1,5},{2,6},{3,7},{4,0},{5,1},{6,2},{7,3},{8,12},{9,13},{10,... | collective-permute-start | bytes 1769480 | tf_op jit(solution)/shard_map/ppermute | solution.py:725
  120.8 12.7 %collective-permute-start.38 = (bf16[8,24,768]{2,1,0:T(8,128)(2,1)S(1)}, bf16[8,24,768]{2,1,0:T(8,128)(2,1)S(1)}, u32[]{:S(2)}, u32[]{:S(2)}) collective-permute-start(bf16[8,24,768]{2,1,0:T(8,128)(2,1)S(1)} %get-tuple-element.178), channel_id=1, source_target_pairs={{0,1},{1,0},{2,3},{3,2},{4,5},{5,4},{6,7},{7,6},{8,9},{9,8},{10,11... | collective-permute-start | bytes 884744 | tf_op jit(solution)/shard_map/ppermute | solution.py:725
  123.1 33.4 %collective-permute-start.31 = (bf16[2,256,768]{2,1,0:T(8,128)(2,1)S(1)}, bf16[2,256,768]{2,1,0:T(8,128)(2,1)S(1)}, u32[]{:S(2)}, u32[]{:S(2)}) collective-permute-start(bf16[2,256,768]{2,1,0:T(8,128)(2,1)S(1)} %get-tuple-element.164), channel_id=1, source_target_pairs={{0,1},{1,0},{2,3},{3,2},{4,5},{5,4},{6,7},{7,6},{8,9},{9,8},{10,11... | collective-permute-start | bytes 2359304 | tf_op jit(solution)/shard_map/ppermute | solution.py:725
  125.1 9.1 %collective-permute-start.40 = (bf16[8,24,768]{2,1,0:T(8,128)(2,1)S(1)}, bf16[8,24,768]{2,1,0:T(8,128)(2,1)S(1)}, u32[]{:S(2)}, u32[]{:S(2)}) collective-permute-start(bf16[8,24,768]{2,1,0:T(8,128)(2,1)S(1)} %bitcast_add_fusion), channel_id=1, source_target_pairs={{0,2},{1,3},{2,0},{3,1},{4,6},{5,7},{6,4},{7,5},{8,10},{9,11},{10,... | collective-permute-start | bytes 884744 | tf_op jit(solution)/shard_map/ppermute | solution.py:725
  136.7 19.2 %collective-permute-start.47 = (bf16[2512,128]{1,0:T(8,128)(2,1)S(1)}, bf16[2512,128]{1,0:T(8,128)(2,1)S(1)}, u32[]{:S(2)}, u32[]{:S(2)}) collective-permute-start(bf16[2512,128]{1,0:T(8,128)(2,1)S(1)} %get-tuple-element.182.refs_0_), channel_id=1, source_target_pairs={{0,4},{1,5},{2,6},{3,7},{4,0},{5,1},{6,2},{7,3},{8,12},{9,13},{10,... | collective-permute-start | bytes 1929224 | tf_op jit(solution)/shard_map/ppermute | solution.py:725
  138.7 15.9 %collective-permute-start.44 = (bf16[2,288,256]{2,1,0:T(8,128)(2,1)S(1)}, bf16[2,288,256]{2,1,0:T(8,128)(2,1)S(1)}, u32[]{:S(2)}, u32[]{:S(2)}) collective-permute-start(bf16[2,288,256]{2,1,0:T(8,128)(2,1)S(1)} %get-tuple-element.191), channel_id=1, source_target_pairs={{0,16},{1,17},{2,18},{3,19},{4,20},{5,21},{6,22},{7,23},{8,24},{9,... | collective-permute-start | bytes 884744 | tf_op jit(solution)/shard_map/ppermute | solution.py:725
  141.3 14.5 %collective-permute-start.43 = (bf16[2,288,256]{2,1,0:T(8,128)(2,1)S(1)}, bf16[2,288,256]{2,1,0:T(8,128)(2,1)S(1)}, u32[]{:S(2)}, u32[]{:S(2)}) collective-permute-start(bf16[2,288,256]{2,1,0:T(8,128)(2,1)S(1)} %get-tuple-element.185.refs_0_), channel_id=1, source_target_pairs={{0,8},{1,9},{2,10},{3,11},{4,12},{5,13},{6,14},{7,15},{8,0},{9,1},... | collective-permute-start | bytes 884744 | tf_op jit(solution)/shard_map/ppermute | solution.py:725
  144.0 16.3 %collective-permute-start.41 = (bf16[2,256,768]{2,1,0:T(8,128)(2,1)S(1)}, bf16[2,256,768]{2,1,0:T(8,128)(2,1)S(1)}, u32[]{:S(2)}, u32[]{:S(2)}) collective-permute-start(bf16[2,256,768]{2,1,0:T(8,128)(2,1)S(1)} %get-tuple-element.188), channel_id=1, source_target_pairs={{0,1},{1,0},{2,3},{3,2},{4,5},{5,4},{6,7},{7,6},{8,9},{9,8},{10,11... | collective-permute-start | bytes 2359304 | tf_op jit(solution)/shard_map/ppermute | solution.py:725
  156.0 11.5 %collective-permute-start.48 = (bf16[1264,128]{1,0:T(8,128)(2,1)S(1)}, bf16[1264,128]{1,0:T(8,128)(2,1)S(1)}, u32[]{:S(2)}, u32[]{:S(2)}) collective-permute-start(bf16[1264,128]{1,0:T(8,128)(2,1)S(1)} %get-tuple-element.196), channel_id=1, source_target_pairs={{0,8},{1,9},{2,10},{3,11},{4,12},{5,13},{6,14},{7,15},{8,0},{9,1},... | collective-permute-start | bytes 970760 | tf_op jit(solution)/shard_map/ppermute | solution.py:725
  156.5 23.3 %collective-permute-start.35 = (bf16[256,768]{1,0:T(8,128)(2,1)S(1)}, bf16[256,768]{1,0:T(8,128)(2,1)S(1)}, u32[]{:S(2)}, u32[]{:S(2)}) collective-permute-start(bf16[256,768]{1,0:T(8,128)(2,1)S(1)} %fusion.4), channel_id=1, source_target_pairs={{0,2},{1,3},{2,0},{3,1},{4,6},{5,7},{6,4},{7,5},{8,10},{9,11},{10,... | collective-permute-start | bytes 1179656 | tf_op jit(solution)/shard_map/ppermute | solution.py:725
  160.3 14.2 %collective-permute-start.42 = (bf16[256,768]{1,0:T(8,128)(2,1)S(1)}, bf16[256,768]{1,0:T(8,128)(2,1)S(1)}, u32[]{:S(2)}, u32[]{:S(2)}) collective-permute-start(bf16[256,768]{1,0:T(8,128)(2,1)S(1)} %fusion.3), channel_id=1, source_target_pairs={{0,2},{1,3},{2,0},{3,1},{4,6},{5,7},{6,4},{7,5},{8,10},{9,11},{10,... | collective-permute-start | bytes 1179656 | tf_op jit(solution)/shard_map/ppermute | solution.py:725
  167.6 8.3 %collective-permute-start.49 = (bf16[640,128]{1,0:T(8,128)(2,1)S(1)}, bf16[640,128]{1,0:T(8,128)(2,1)S(1)}, u32[]{:S(2)}, u32[]{:S(2)}) collective-permute-start(bf16[640,128]{1,0:T(8,128)(2,1)S(1)} %get-tuple-element.198), channel_id=1, source_target_pairs={{0,16},{1,17},{2,18},{3,19},{4,20},{5,21},{6,22},{7,23},{8,24},{9,... | collective-permute-start | bytes 491528 | tf_op jit(solution)/shard_map/ppermute | solution.py:725
  (37 other events, 230.2 us)

commit v3 on v2

--- a/solution.py
+++ b/solution.py
@@ -77,11 +77,11 @@
 
 
 def prep_kernel(
-    wq, wk, wv, wg, wu, g1, g2, s0, s1, s2, s3, gains, slabs, vq, vk, vv, vg, vu, sems
+    wq, wk, wv, wg, wu, tok, seg, g1, g2, s0, s1, s2, s3, ts, gains, slabs, vq, vk, vv, vg, vu, sems
 ):
     j_me = lax.axis_index("blk")
     rows = wq.shape[0]
-    pairs = ((wq, vq), (wk, vk), (wv, vv), (wg, vg), (wu, vu))
+    pairs = ((wq, vq), (wk, vk), (wv, vv), (wg, vg), (wu, vu), (tok, ts.at[0:T]))
     copies = [pltpu.make_async_copy(a, b, sems.at[n]) for n, (a, b) in enumerate(pairs)]
     for copy in copies:
         copy.start()
@@ -94,6 +94,10 @@
         column = jnp.sum(jnp.where(eye, row, 0.0), axis=1, keepdims=True)
         columns.append(column)
         gains[n] = jnp.broadcast_to(column, (rows, 128))
+    ids = jnp.broadcast_to(seg[...], (16, T))
+    ts[T : T + 16, 0:T] = (ids // 2).astype(F32).astype(BF16)
+    ts[T : T + 16, T : 2 * T] = (ids % 2).astype(F32).astype(BF16)
+    ts[T : T + 16, 2 * T : 3 * T] = jnp.zeros((16, T), BF16)
     low = low_half(rows)
     lane = lax.broadcasted_iota(jnp.int32, (rows, 128), 1)
     spare = jnp.where(lane == 64, columns[0], jnp.where(lane == 65, columns[1], 0.0))
@@ -146,23 +150,16 @@
     first[96:128] = jnp.concatenate([out[:, 0:640], rest], axis=0).astype(BF16)
 
 
-def pack_more_kernel(s0, s1, s2, s3, wd, cot, seg, second, extra, whole, vd, sems):
+def pack_more_kernel(s0, s1, s2, s3, wd, second, whole, vd, sem):
     j = lax.axis_index("blk")
     rows = s0.shape[0]
-    pairs = ((wd, vd), (cot, extra.at[0:T]))
-    copies = [pltpu.make_async_copy(a, b, sems.at[n]) for n, (a, b) in enumerate(pairs)]
-    for copy in copies:
-        copy.start()
+    copy = pltpu.make_async_copy(wd, vd, sem)
+    copy.start()
     for k, ref in enumerate((s0, s1, s2, s3)):
         whole[pl.ds(pl.multiple_of(rows * (j ^ k), 8), rows)] = ref[:, 640:1664].astype(F32)
     for n in range(4):
         second[96 * n : 96 * n + 96] = whole[:, 256 * n : 256 * n + 256].astype(BF16)
-    ids = jnp.broadcast_to(seg[...], (16, T))
-    extra[T : T + 16, 0:T] = (ids // 2).astype(F32).astype(BF16)
-    extra[T : T + 16, T : 2 * T] = (ids % 2).astype(F32).astype(BF16)
-    extra[T : T + 16, 2 * T : 3 * T] = jnp.zeros((16, T), BF16)
-    for copy in copies:
-        copy.wait()
+    copy.wait()
     for n in range(3):
         second[384 + 64 * n : 448 + 64 * n] = vd[:, 256 * n : 256 * n + 256]
 
@@ -201,7 +198,7 @@
         for h in range(HT):
             row = jnp.zeros((8, 512), F32)
             for b in range(NB):
-                row = jnp.where(bucket == b, table[b, HT * j + h], row)
+                row = jnp.where(bucket == b, table[HT * j + h, b], row)
             wide = jnp.broadcast_to(row[0:1], (T, 512))
             out[h, n] = pltpu.roll(wide, 0, 1, stride=1, stride_axis=0)[:, :T]
 
@@ -211,12 +208,18 @@
 
 
 def qkv_kernel(
-    t0, t1, t2, t3, p0, p1, p2, p3, p4, p5, p6, p7, tok, n1, qkv, w, gains
+    t0, t1, t2, t3, p0, p1, p2, p3, p4, p5, p6, p7, tok, n1, qkv, w, gains, segq, segk
 ):
     j = lax.axis_index("blk")
     dp = lax.axis_index("dp")
     for k, ref in enumerate((t0, t1, t2, t3)):
-        tok[j ^ k] = ref[...]
+        tok[j ^ k] = ref[0:T]
+        parts = ref[T : T + 16].astype(F32)
+        row = (2.0 * parts[:, 0:T] + parts[:, T : 2 * T])[0:8]
+        segq[j ^ k] = row
+        col = jnp.transpose(jnp.broadcast_to(row[0:1], (128, T)))
+        segk[j ^ k, :, 0:128] = col
+        segk[j ^ k, :, 128:256] = col
     for n, ref in enumerate((p0, p1, p2, p3, p4, p5, p6, p7)):
         w[pl.ds(pl.multiple_of(96 * (dp ^ piece_at(n)), 32), 96)] = ref[0:96]
     turned = jnp.transpose(w[:, 512:640].astype(F32))
@@ -233,18 +236,6 @@
         return carry
 
     lax.fori_loop(0, TP, body, 0)
-
-
-def row_kernel(e0, e1, e2, e3, cot, segq, segk):
-    j_me = lax.axis_index("blk")
-    for k, ref in enumerate((e0, e1, e2, e3)):
-        cot[j_me ^ k] = ref[0:T]
-        parts = ref[T : T + 16].astype(F32)
-        row = (2.0 * parts[:, 0:T] + parts[:, T : 2 * T])[0:8]
-        segq[j_me ^ k] = row
-        col = jnp.transpose(jnp.broadcast_to(row[0:1], (128, T)))
-        segk[j_me ^ k, :, 0:128] = col
-        segk[j_me ^ k, :, 128:256] = col
 
 
 def attn_fwd_kernel(h, table, bias, qkv, segq, segk, prob, inv_tot, out_t, qt, vt, sc):
@@ -261,7 +252,7 @@
         vt[:, T * i : T * i + T] = v[half]
 
     tile = 1 + 2 * (h // 2)
-    far = (table[15, HT * j_me + h], table[31, HT * j_me + h])
+    far = (table[HT * j_me + h, 15], table[HT * j_me + h, 31])
     for i in range(TP):
         peak = jnp.full((1, T), MASKED, F32)
         for j in range(TP):
@@ -317,34 +308,30 @@
 
 
 def ffn_kernel(
-    a0, a1, a2, a3, gains, wop, wgu, wd, tok, cot,
-    attc, n2, hid, ggug, two_keep, two_give, lo_keep, lo_give, mixed_own,
+    ks, a0, a1, a2, a3, gains, wop, wgu, wd, tok, c0, c1,
+    n2, hid, ggug, keep, give, attc, mixed_own,
 ):
     j = lax.axis_index("blk")
     low = low_half(T)
-
-    def body(k, carry):
+    refs = (a0, a1, a2, a3)
+    for m, k in enumerate(ks):
         b = j ^ k
         half = b // 2
-        refs = (a0, a1, a2, a3)
         for n, ref in enumerate(refs):
-            attc[b, :, 128 * n : 128 * n + 128] = ref[pl.ds(pl.multiple_of(b * T, T), T)]
+            attc[m, :, 128 * n : 128 * n + 128] = ref[pl.ds(pl.multiple_of(b * T, T), T)]
         rest = [
             ref[pl.ds(pl.multiple_of(1024 + (b % 2) * T, T), T)].astype(F32) for ref in refs
         ]
         for n in range(2):
             lo = pltpu.roll(rest[2 * n], 64 * half, 1)
             hi = pltpu.roll(rest[2 * n + 1], 64 * (1 - half), 1)
-            attc[b, :, 512 + 128 * n : 640 + 128 * n] = jnp.where(low, lo, hi).astype(BF16)
-        mixed = tok[b].astype(F32) + dot(attc[b], wop[...])
-
-        @pl.when(k == 0)
-        def _():
+            attc[m, :, 512 + 128 * n : 640 + 128 * n] = jnp.where(low, lo, hi).astype(BF16)
+        mixed = tok[b].astype(F32) + dot(attc[m], wop[...])
+        if k == 0:
             mixed_own[...] = mixed
-
         rstd = lax.rsqrt(jnp.mean(mixed * mixed, axis=-1, keepdims=True) + EPSILON)
         n = (mixed * rstd * gains[1:2]).astype(BF16)
-        n2[b] = n
+        n2[m] = n
         gate = dot(n, wgu[:, 0:512])
         up = dot(n, wgu[:, 512:1024])
         c = 0.7978845608028654
@@ -352,26 +339,20 @@
         th = jnp.tanh(c * gate * (1.0 + 0.044715 * sq))
         act = 0.5 * gate * (1.0 + th)
         slope = 0.5 * (1.0 + th) + 0.5 * gate * (1.0 - th * th) * (c * (1.0 + 3 * 0.044715 * sq))
-        hidden = (act * up).astype(BF16)
-        hid[b] = hidden
-        hg = dot_nt(cot[b], wd[...])
-        ggug[b, :, 0:512] = (hg * up * slope).astype(BF16)
-        ggug[b, :, 512:1024] = (hg * act).astype(BF16)
-        two = dot_nt(ggug[b], wgu[...]).astype(BF16)
-        put_pair(two_keep, two_give, k, two)
-        put_pair(lo_keep, lo_give, k, dot(hidden, wd[...]).astype(BF16))
-        return carry
-
-    lax.fori_loop(0, TP, body, 0)
+        hid[m] = (act * up).astype(BF16)
+        hg = dot_nt((c0, c1)[m][...], wd[...])
+        ggug[m, :, 0:512] = (hg * up * slope).astype(BF16)
+        ggug[m, :, 512:1024] = (hg * act).astype(BF16)
+        (keep, give)[m][...] = dot_nt(ggug[m], wgu[...]).astype(BF16)
 
 
 def mid_kernel(keep, rc, rx, mixed_own, cot, attc, wop, gains, mixed_grad, g0, g1, g2, g3, wo_keep, wo_one, wo_three, dw):
     j = lax.axis_index("blk")
-    u = (keep[0].astype(F32) + rc[0].astype(F32) + rx[...].astype(F32)) * gains[1:2]
+    u = (keep[...].astype(F32) + rc[...].astype(F32) + rx[...].astype(F32)) * gains[1:2]
     mixed = mixed_own[...]
     rstd = lax.rsqrt(jnp.mean(mixed * mixed, axis=-1, keepdims=True) + EPSILON)
     n = mixed * rstd
-    mg = cot[j].astype(F32) + rstd * (u - n * jnp.mean(u * n, axis=-1, keepdims=True))
+    mg = cot[...].astype(F32) + rstd * (u - n * jnp.mean(u * n, axis=-1, keepdims=True))
     mixed_grad[...] = mg
     ml = mg.astype(BF16)
     ag = dot_nt(ml, wop[...])
@@ -385,7 +366,7 @@
         else:
             v = jnp.where(low, pltpu.roll(top, 64, 1), bottom)
         ref[256:384] = v.astype(BF16)
-    perm = dot_tn(attc[j], ml)
+    perm = dot_tn(attc[0], ml)
     for k in range(TP):
         at = pl.multiple_of(192 * (j ^ k), 64)
         dw[pl.ds(at, 128)] = perm[128 * k : 128 * k + 128]
@@ -398,7 +379,8 @@
 
 
 SLOTS = (0, 2, 1, 3)
-CHUNK = 5 * 96 + 6 * 24
+FIRST = 3 * 96
+SECOND = 2 * 96 + 6 * 24
 TAIL = 16
 
 
@@ -409,13 +391,23 @@
             body(give, slot, dp ^ (2 * z + give))
 
 
-def ffn_dw_kernel(n2, ggug, hid, cot, y_keep, y_give, z_keep, z_give, dwgu, dwd):
+def ffn_dw_kernel(
+    na, ga, ha, nb, gb, hb, c0, c1, c2, c3, wd, y_keep, y_give, z_keep, z_give, lo_keep, lo_give, dwgu, dwd
+):
     for m in range(2):
         at = slice(512 * m, 512 * m + 512)
-        dwgu[:, at] = dot_tn(n2[...], ggug[:, at])
+        dwgu[:, at] = dot_tn(na[...], ga[:, at]) + dot_tn(nb[...], gb[:, at])
     for m in range(3):
         at = slice(256 * m, 256 * m + 256)
-        dwd[:, at] = dot_tn(hid[...], cot[:, at])
+        dwd[:, at] = (
+            dot_tn(ha[0:T], c2[:, at])
+            + dot_tn(ha[T : 2 * T], c3[:, at])
+            + dot_tn(hb[0:T], c0[:, at])
+            + dot_tn(hb[T : 2 * T], c1[:, at])
+        )
+    for n, ref in enumerate((hb, ha)):
+        lo_keep[n] = dot(ref[0:T], wd[...]).astype(BF16)
+        lo_give[n] = dot(ref[T : 2 * T], wd[...]).astype(BF16)
 
     def put(g, slot, owner):
         ref = y_give if g else y_keep
@@ -448,8 +440,23 @@
     return jnp.concatenate([high, x - high], axis=0).astype(BF16)
 
 
-def attn_dw_kernel(n1, dqkv, wo_keep, wo_got, wo_along, table_grad, keep, give, dw, wo, chunk):
-    for t in range(5):
+def first_dw_kernel(n1, dqkv, keep, give, dw):
+    for t in range(3):
+        at = slice(128 * t, 128 * t + 128)
+        dw[:, at] = dot_tn(n1[...], dqkv[:, at])
+
+    def put(g, slot, owner):
+        ref = give if g else keep
+        a = pl.ds(pl.multiple_of(96 * owner, 32), 96)
+        for t in range(3):
+            at = FIRST * slot + 96 * t
+            ref[at : at + 96] = dw[a, 128 * t : 128 * t + 128].astype(BF16)
+
+    slots(put)
+
+
+def second_dw_kernel(n1, dqkv, wo_keep, wo_got, wo_along, ta, tb, keep, give, dw, wo, chunk):
+    for t in range(2):
         at = slice(128 * t, 128 * t + 128)
         dw[:, at] = dot_tn(n1[...], dqkv[:, at])
     for d in range(8):
@@ -458,15 +465,15 @@
     def put(g, slot, owner):
         ref = give if g else keep
         a = pl.ds(pl.multiple_of(96 * owner, 32), 96)
-        for t in range(5):
+        for t in range(2):
             chunk[96 * t : 96 * t + 96] = dw[a, 128 * t : 128 * t + 128]
         for t in range(6):
-            chunk[480 + 24 * t : 504 + 24 * t] = wo[owner, :, 128 * t : 128 * t + 128]
-        ref[CHUNK * slot : CHUNK * slot + CHUNK] = chunk[...].astype(BF16)
+            chunk[192 + 24 * t : 216 + 24 * t] = wo[owner, :, 128 * t : 128 * t + 128]
+        ref[SECOND * slot : SECOND * slot + SECOND] = chunk[...].astype(BF16)
 
     slots(put)
     for ref in (keep, give):
-        ref[4 * CHUNK : 4 * CHUNK + 16] = split(table_grad[...])
+        ref[4 * SECOND : 4 * SECOND + 16] = split(ta[...] + tb[...])
 
 
 def tail_of(ref, base):
@@ -474,22 +481,24 @@
     return both[0:8] + both[8:16]
 
 
-def stage_kernel(n, keep, got, next_keep, next_give):
-    half = n // 2 * CHUNK
+def stage_kernel(n, chunk, keep, got, next_keep, next_give):
+    half = n // 2 * chunk
     for at, ref in ((0, next_keep), (half, next_give)):
         here = slice(at, at + half)
         ref[0:half] = (keep[here].astype(F32) + got[here].astype(F32)).astype(BF16)
-        ref[half : half + 16] = split(tail_of(keep, n * CHUNK) + tail_of(got, n * CHUNK))
-
-
-def back_kernel(keep, got, yk, yg, ya, zk, zg, za, dwo, dwd, b0, b1, b2, b3, total, ffn):
+        if chunk == SECOND:
+            ref[half : half + 16] = split(tail_of(keep, n * chunk) + tail_of(got, n * chunk))
+
+
+def back_kernel(ka, ga, kb, gb, yk, yg, ya, zk, zg, za, dwo, dwd, b0, b1, b2, b3, total, ffn):
     j = lax.axis_index("blk")
     ffn[0:288] = yk[0].astype(F32) + yg[0].astype(F32) + ya[...].astype(F32)
     ffn[288:576] = zk[0].astype(F32) + zg[0].astype(F32) + za[...].astype(F32)
     for m in range(3):
         dwd[:, 256 * m : 256 * m + 256] = ffn[384 + 64 * m : 448 + 64 * m]
-    total[...] = keep[0:CHUNK].astype(F32) + got[0:CHUNK].astype(F32)
-    parts = split(tail_of(keep, CHUNK) + tail_of(got, CHUNK)).astype(F32)
+    total[0:FIRST] = ka[...].astype(F32) + ga[...].astype(F32)
+    total[FIRST : FIRST + SECOND] = kb[0:SECOND].astype(F32) + gb[0:SECOND].astype(F32)
+    parts = split(tail_of(kb, SECOND) + tail_of(gb, SECOND)).astype(F32)
     parts = jnp.concatenate([parts, jnp.zeros((8, 128), F32)], axis=0).astype(BF16)
     for t in range(6):
         at = 480 + 24 * t
@@ -504,51 +513,47 @@
         ref[:, 1664:1792] = parts
 
 
-def attn_bwd_kernel(
-    qkv, p0, p1, p2, v0, v1, v2, o0, o1, o2, g0, g1, g2, g3,
-    dqkv, table_grad,
-    dotm, dom, qm, ktm, delta, dst, dq_acc, dk_acc, dv_acc, near, far,
-):
+def attn_bwd_kernel(second, *refs):
+    count = 1 if second else 2
+    heads = range(HT - 1, HT) if second else range(2)
+    qkv, refs = refs[0], refs[1:]
+    probs, refs = refs[:count], refs[count:]
+    invs, refs = refs[:count], refs[count:]
+    outs, refs = refs[:count], refs[count:]
+    (g0, g1, g2, g3, dqkv, table_grad,
+     dotm, dom, qm, ktm, delta, dst, dq_acc, dk_acc, dv_acc, near, far) = refs
     j_me = lax.axis_index("blk")
     low = low_half(T)
-    low_short = low_half(128)
     rows_low = lax.broadcasted_iota(jnp.int32, (128, T), 0) < 64
 
     for k, ref in enumerate((g0, g1, g2, g3)):
         b = j_me ^ k
-        first = ref[0:256].astype(F32)
-        rest = ref[256:384].astype(F32)
-        second = jnp.concatenate([rest, pltpu.roll(rest, 64, 1)], axis=0)
-        t0 = jnp.transpose(first)
-        t1 = jnp.transpose(second)
-        t0 = t0 * jnp.where(rows_low, v0[b], v1[b])
-        t1 = jnp.where(rows_low, t1 * v2[b], 0.0)
-        t0, t1 = t0.astype(BF16), t1.astype(BF16)
-        f0, f1 = t0.astype(F32), t1.astype(F32)
-        dotm[0, b] = jnp.where(rows_low, f0, 0.0).astype(BF16)
-        dotm[1, b] = jnp.where(rows_low, 0.0, f0).astype(BF16)
-        dotm[2, b] = t1
-        back = jnp.transpose(f0)
-        dom[0, b] = jnp.where(low, back, 0.0).astype(BF16)
-        dom[1, b] = jnp.where(low, 0.0, back).astype(BF16)
-        dom[2, b] = jnp.transpose(f1).astype(BF16)
+        if second:
+            rest = ref[256:384].astype(F32)
+            rows = jnp.concatenate([rest, pltpu.roll(rest, 64, 1)], axis=0)
+            turned = jnp.where(rows_low, jnp.transpose(rows) * invs[0][b], 0.0)
+        else:
+            turned = jnp.transpose(ref[0:256].astype(F32))
+            turned = turned * jnp.where(rows_low, invs[0][b], invs[1][b])
+        turned = turned.astype(BF16).astype(F32)
+        back = jnp.transpose(turned)
+        for n in range(count):
+            dotm[n, b] = jnp.where(rows_low == (n == 0), turned, 0.0).astype(BF16)
+            dom[n, b] = jnp.where(low == (n == 0), back, 0.0).astype(BF16)
 
     for i in range(TP):
         at = slice(T * i, T * i + T)
-        for h in range(HT):
-            g = dotm[h, i].astype(F32)
-            g = g[64:128] if h == 1 else g[0:64]
-            delta[h, i] = jnp.sum((o0, o1, o2)[h][:, at] * g, axis=0, keepdims=True)
-        q0 = qkv[0, i].astype(F32)
-        turned = pltpu.roll(qkv[3, i].astype(F32), 64, 1)
-        qm[0, i] = jnp.where(low, q0, 0.0).astype(BF16)
-        qm[1, i] = jnp.where(low, 0.0, q0).astype(BF16)
-        qm[2, i] = jnp.where(low, 0.0, turned).astype(BF16)
-        k0 = jnp.transpose(qkv[1, i].astype(F32))
-        k1 = jnp.transpose(turned)
-        ktm[0, :, at] = jnp.where(rows_low, k0, 0.0).astype(BF16)
-        ktm[1, :, at] = jnp.where(rows_low, 0.0, k0).astype(BF16)
-        ktm[2, :, at] = jnp.where(rows_low, k1, 0.0).astype(BF16)
+        if second:
+            q = pltpu.roll(qkv[3, i].astype(F32), 64, 1)
+            keys = jnp.transpose(q)
+        else:
+            q = qkv[0, i].astype(F32)
+            keys = jnp.transpose(qkv[1, i].astype(F32))
+        for n in range(count):
+            g = dotm[n, i].astype(F32)[64 * n : 64 * n + 64]
+            delta[n, i] = jnp.sum(outs[n][:, at] * g, axis=0, keepdims=True)
+            qm[n, i] = jnp.where(low == (n == 0 and not second), q, 0.0).astype(BF16)
+            ktm[n, :, at] = jnp.where(rows_low == (n == 0), keys, 0.0).astype(BF16)
 
     dq_acc[...] = jnp.zeros(dq_acc.shape, F32)
     dk_acc[...] = jnp.zeros(dk_acc.shape, F32)
@@ -570,15 +575,14 @@
     hot_neg = bucket_of(-lane_id) == row_id
     hot_pos = bucket_of(128 - lane_id) == row_id
 
-    for h, prob in enumerate((p0, p1, p2)):
-        second = h // 2
+    for n, prob in enumerate(probs):
         near[...] = jnp.zeros(near.shape, F32)
         far[...] = jnp.zeros(far.shape, F32)
         for i in range(TP):
             at = slice(T * i, T * i + T)
-            row_delta = delta[h, i]
+            row_delta = delta[n, i]
             for j in range(TP):
-                dp = dot(qkv[2 + 2 * second, j], dotm[h, i])
+                dp = dot(qkv[2 + 2 * second, j], dotm[n, i])
                 ds = prob[i, j].astype(F32) * (dp - row_delta)
                 dst[j] = ds.astype(BF16)
                 for a in range(2):
@@ -590,9 +594,9 @@
                         else:
                             far[int(gap > 0)] += jnp.sum(part.reshape(16, 8, 128), axis=0)
             d_all = dst[...].reshape(TP * T, T)
-            dq_acc[second, :, at] += dot(ktm[h], d_all)
-            dk_acc[second] += dot(d_all, qm[h, i])
-            dv_acc[second] += dot(prob[i].reshape(TP * T, T), dom[h, i])
+            dq_acc[:, at] += dot(ktm[n], d_all)
+            dk_acc[...] += dot(d_all, qm[n, i])
+            dv_acc[...] += dot(prob[i].reshape(TP * T, T), dom[n, i])
         before, diagonal, after = near[0], near[1], near[2]
         neg = jnp.where(upper, diagonal, before)
         pos = jnp.where(upper, after, diagonal)
@@ -611,23 +615,25 @@
         )
         sums = jnp.sum(spread, axis=1, keepdims=True)
         sums = jnp.sum(jnp.where(lane_id == row_id, sums, 0.0), axis=0, keepdims=True)
+        h = heads[n]
         table_grad[h : h + 1] = sums
     for i in range(TP):
         at = slice(T * i, T * i + T)
-        dq0 = jnp.transpose(dq_acc[0, :, at])
-        dq1 = jnp.transpose(dq_acc[1, :, at])
-        dqkv[i, :, 0:128] = dq0.astype(BF16)
-        dqkv[i, :, 128:256] = dk_acc[0, at].astype(BF16)
-        dqkv[i, :, 256:384] = dv_acc[0, at].astype(BF16)
-        dqkv[i, :, 384:512] = (dq1 + dk_acc[1, at]).astype(BF16)
-        dqkv[i, :, 512:640] = dv_acc[1, at].astype(BF16)
-
-
-def one_grad_kernel(dqkv, w, keep, give):
+        dq = jnp.transpose(dq_acc[:, at])
+        if second:
+            parts = (dq + dk_acc[at], dv_acc[at])
+        else:
+            parts = (dq, dk_acc[at], dv_acc[at])
+        for n, part in enumerate(parts):
+            dqkv[i, :, 128 * n : 128 * n + 128] = part.astype(BF16)
+
+
+def one_grad_kernel(da, db, w, keep, give):
     j = lax.axis_index("blk")
 
     def body(k, carry):
-        put_pair(keep, give, k, dot_nt(dqkv[j ^ k], w[...]).astype(BF16))
+        total = dot_nt(da[j ^ k], w[:, 0:384]) + dot_nt(db[j ^ k], w[:, 384:640])
+        put_pair(keep, give, k, total.astype(BF16))
         return carry
 
     lax.fori_loop(0, TP, body, 0)
@@ -663,7 +669,7 @@
         for h in range(HT):
             row = parts[h : h + 1] + parts[8 + h : 9 + h]
             heads = jnp.where(head_id == HT * (j_me ^ k) + h, row, heads)
-    table[...] = jnp.transpose(heads)[0:NB, 0:H]
+    table[...] = heads[0:H, 0:NB]
 
     def one(j, n):
         return src[j, 0:rows, 128 * n : 128 * n + 128]
@@ -707,8 +713,7 @@
 
 
 AXES = ("dp", "blk")
-GATE = 0
-COST = {"qkv": 0, "attn_fwd": (0, 20, 20), "units": 30, "ffn": 0, "ffn_dw": 0, "mid": 20, "attn_bwd": 40, "one_grad": 40, "stage_y": 10, "stage_z": 10}
+COST = {"qkv": 0, "attn_fwd": (0, 0, 0), "units": 15, "ffn": 0, "ffn_dw": 0, "mid": 20, "attn_bwd": (0, 10), "one_grad": 40, "stage_y": 10, "stage_z": 10}
 
 
 def group_local(
@@ -732,69 +737,69 @@
         got = swap(give, 1)
         return got, swap(keep[1] + got[1], 2)
 
-    def round_one(x, late=None):
-        late = x if late is None else late
-        return lax.optimization_barrier((swap(x, 16), swap(late, 8), swap(late, 4)))
-
-    def round_two(state):
-        far, near, _ = state
+    def round_one(x):
+        return lax.optimization_barrier((swap(x, 16), swap(x, 8), swap(x, 4)))
+
+    def round_two(far, near):
         return lax.optimization_barrier((swap(far, 8), swap(near, 4), swap(far, 4)))
 
-    def gathered(x, one, two):
+    def gathered(x, one, two, *others):
         far, near, other = one
         last, near_y, far_y = two
-        return (x, near, far, last, other, near_y, far_y, swap(last, 4))
+        return (x, near, far, last, other, near_y, far_y, swap(later(last, *others), 4))
 
     tok_own, cot_own = tokens[0], cotangent[0]
     rows, ff = w_query.shape[0], w_gate.shape[1]
     flat = TP * T
-    table = rel_bias.astype(F32)
-
-    toks_x, toks_c = swap(tok_own, 2), swap(tok_own, 1)
-    *slabs, gain_cols = call(
+    table = rel_bias.astype(F32).T
+
+    *slabs, tok_seg, gain_cols = call(
         prep_kernel,
-        (sds((rows, 1664), BF16),) * TP + (sds((2, rows, 128), F32),),
-        w_query, w_key, w_value, w_gate, w_up, attn_gain, ffn_gain,
-        name="prep", vmem=60, held=(0, 1, 2, 3, 4),
+        (sds((rows, 1664), BF16),) * TP + (sds((T + 16, D), BF16), sds((2, rows, 128), F32)),
+        w_query, w_key, w_value, w_gate, w_up, tok_own, segment_ids, attn_gain, ffn_gain,
+        name="prep", vmem=60, held=(0, 1, 2, 3, 4, 5),
         scratch=(
             pltpu.VMEM((TP, rows, 1664), BF16),
             *(pltpu.VMEM((rows, D), BF16),) * 3,
             *(pltpu.VMEM((rows, ff), BF16),) * 2,
-            pltpu.SemaphoreType.DMA((5,)),
+            pltpu.SemaphoreType.DMA((6,)),
         ),
     )
+    toks_x, toks_c = swap(tok_seg, 2), swap(tok_seg, 1)
     slabs = (slabs[0], swap(slabs[1], 1), swap(slabs[2], 2), swap(slabs[3], 3))
-    bias = call(bias_kernel, sds((HT, 3, T, T), F32), table, smem=(0,), name="bias")
     first = call(
         pack_kernel, sds((128, 640), BF16), *slabs, w_attn_out,
-        name="pack", vmem=60, held=(4,), after=(bias,),
+        name="pack", vmem=60, held=(4,),
         scratch=(pltpu.VMEM((96, 640), F32), pltpu.VMEM((rows, D), BF16), pltpu.SemaphoreType.DMA),
     )
-    second, extra = call(
-        pack_more_kernel, (sds((576, 256), BF16), sds((T + 16, D), BF16)),
-        *slabs, w_down, cot_own, segment_ids, name="pack_more", vmem=60, held=(4, 5), after=(first,),
-        scratch=(
-            pltpu.VMEM((96, 1024), F32), pltpu.VMEM((64, D), BF16), pltpu.SemaphoreType.DMA((2,)),
-        ),
+    second = call(
+        pack_more_kernel, sds((576, 256), BF16), *slabs, w_down,
+        name="pack_more", vmem=60, held=(4,), after=(first,),
+        scratch=(pltpu.VMEM((96, 1024), F32), pltpu.VMEM((64, D), BF16), pltpu.SemaphoreType.DMA),
     )
     first_one = round_one(first)
-    first_two = round_two(lax.optimization_barrier(first_one + (extra,))[:3])
-    firsts = gathered(first, first_one, first_two)
-    toks = (tok_own, toks_c, toks_x, swap(later(toks_x, *first_two), 1))
-    second_one = round_one(later(second, *first_one), later(second, *first_two))
-
-    tok, n1, qkv, w_qkv, gains = call(
+    bias = call(
+        bias_kernel, sds((HT, 3, T, T), F32), table, smem=(0,), name="bias", after=(second,)
+    )
+    far, near = lax.optimization_barrier(first_one + (second, bias))[:2]
+    first_two = round_two(far, near)
+    toks_r = swap(later(toks_x, *first_two), 1)
+    firsts = gathered(first, first_one, first_two, *())
+    toks = (tok_seg, toks_c, toks_x, toks_r)
+    cots_x = swap(later(cot_own, *first_one), 2)
+    second_one = (
+        swap(later(second, *first_one), 16),
+        swap(later(second, *first_two), 8),
+        swap(later(second, *first_two), 4),
+    )
+
+    tok, n1, qkv, w_qkv, gains, segq, segk = call(
         qkv_kernel,
         (
             sds((TP, T, D), BF16), sds((TP, T, D), BF16), sds((5, TP, T, 128), BF16),
-            sds((D, 640), BF16), sds((8, D), F32),
+            sds((D, 640), BF16), sds((8, D), F32), sds((TP, 8, T), F32), sds((TP, T, T), F32),
         ),
         *toks, *firsts, name="qkv", vmem=16, cost=COST["qkv"],
-    )
-    extras = share(extra, gains)
-    cot, segq, segk = call(
-        row_kernel, (sds((TP, T, D), BF16), sds((TP, 8, T), F32), sds((TP, T, T), F32)),
-        *extras, name="row",
     )
     stripes = call(
         stripes_kernel, sds((192, D), BF16), *firsts, name="stripes", after=(segq,),
@@ -812,7 +817,7 @@
                 functools.partial(attn_fwd_kernel, h),
                 (sds((TP, TP, T, T), BF16), sds((TP, 1, T), F32), sds((DH, flat), F32)),
                 table, bias, qkv, segq, segk, smem=(0,), name="attn_fwd", vmem=14,
-                cost=COST["attn_fwd"][h], after=(heads[-1][1],) if heads else (),
+                cost=COST["attn_fwd"][h], after=(heads[-1][1],) if heads else (cots_x,),
                 scratch=(
                     pltpu.VMEM((TP, 128, T), BF16),
                     pltpu.VMEM((DH, flat), BF16),
@@ -821,7 +826,9 @@
             )
         )
     probs, inv_tots, out_ts = zip(*heads)
-    second_two = round_two(lax.optimization_barrier(second_one + (inv_tots[GATE],))[:3])
+    cots = (cot_own, swap(later(cot_own, inv_tots[0]), 1), cots_x, swap(later(cots_x, inv_tots[0]), 1))
+    far, near = lax.optimization_barrier(second_one + (inv_tots[0],))[:2]
+    second_two = round_two(far, near)
     seconds = gathered(second, second_one, second_two)
     att = call(join_kernel, sds((1536, 128), BF16), *out_ts, name="join")
     atts = share(att, wop)
@@ -829,21 +836,28 @@
         units_kernel, (sds((D, 1024), BF16), sds((512, D), BF16)), *seconds, name="units",
         cost=COST["units"],
     )
-    attc, n2, hid, ggug, two_keep, two_give, lo_keep, lo_give, mixed_own = call(
-        ffn_kernel,
-        (
-            sds((TP, T, D), BF16), sds((TP, T, D), BF16),
-            sds((TP, T, 512), BF16), sds((TP, T, 1024), BF16),
-            sds((2, T, D), BF16), sds((2, T, D), BF16), sds((2, T, D), BF16), sds((2, T, D), BF16),
-            sds((T, D), F32),
-        ),
-        *atts, gains, wop, wgu, wd, tok, cot, name="ffn", vmem=30, cost=COST["ffn"],
-    )
-    two_c, two_x = reduce_pair(two_keep, two_give)
-    y_keep, y_give, z_keep, z_give = call(
-        ffn_dw_kernel, (sds((4, 288, 256), BF16),) * 4,
-        n2.reshape(flat, D), ggug.reshape(flat, 1024), hid.reshape(flat, 512), cot.reshape(flat, D),
-        name="ffn_dw", vmem=20, cost=COST["ffn_dw"],
+
+    def ffn(ks, *after):
+        return call(
+            functools.partial(ffn_kernel, ks),
+            (
+                sds((2, T, D), BF16), sds((2, T, 512), BF16), sds((2, T, 1024), BF16),
+                sds((T, D), BF16), sds((T, D), BF16), sds((2, T, D), BF16), sds((T, D), F32),
+            ),
+            *atts, gains, wop, wgu, wd, tok, cots[ks[0]], cots[ks[1]], name="ffn", vmem=24,
+            cost=COST["ffn"], after=after,
+        )
+
+    n2_a, hid_a, ggug_a, keep, give, _, _ = ffn((2, 3))
+    two_x = keep + swap(give, 1)
+    n2_b, hid_b, ggug_b, two_keep, give, attc, mixed_own = ffn((0, 1), two_x)
+    two_x = swap(two_x, 2)
+    two_c = swap(give, 1)
+    y_keep, y_give, z_keep, z_give, lo_keep, lo_give = call(
+        ffn_dw_kernel, (sds((4, 288, 256), BF16),) * 4 + (sds((2, T, D), BF16),) * 2,
+        n2_a.reshape(2 * T, D), ggug_a.reshape(2 * T, 1024), hid_a.reshape(2 * T, 512),
+        n2_b.reshape(2 * T, D), ggug_b.reshape(2 * T, 1024), hid_b.reshape(2 * T, 512),
+        *cots, wd, name="ffn_dw", vmem=20, cost=COST["ffn_dw"],
         scratch=(pltpu.VMEM((D, 1024), F32), pltpu.VMEM((512, D), F32)),
     )
     y_got, z_got = swap(y_give, 4), swap(z_give, 8)
@@ -851,88 +865,105 @@
         mid_kernel,
         (sds((T, D), F32),) + (sds((384, 128), BF16),) * 4
         + (sds((2, 8, 24, D), BF16),) + (sds((8, 24, D), BF16),) * 2,
-        two_keep, two_c, two_x, mixed_own, cot, attc, wop, gains, name="mid", vmem=16,
+        two_keep, two_c, two_x, mixed_own, cot_own, attc, wop, gains, name="mid", vmem=16,
         after=(y_give,), scratch=(pltpu.VMEM((D, D), F32),), cost=COST["mid"],
     )
     g1, g2, g3 = swap(g1, 1), swap(g2, 2), swap(g3, 3)
     lo_c = swap(later(lo_give, mixed_grad), 1)
-    lo_x = swap(later(lo_keep[1] + lo_c[1], g1, g2, g3), 2)
-    layer_out = mixed_own + lo_keep[0].astype(F32) + lo_c[0].astype(F32) + lo_x.astype(F32)
+    lo_sum = lo_keep[1] + lo_c[1]
     wo_got = (swap(wo_gives[0], 1), swap(wo_gives[1], 1))
     wo_along = swap(later(wo_keep[1] + wo_got[1], g1, g2, g3), 2)
-    dqkv, table_grad = call(
-        attn_bwd_kernel,
-        (sds((TP, T, 640), BF16), sds((8, 128), F32)),
-        qkv, *probs, *inv_tots, *out_ts, g0, g1, g2, g3, name="attn_bwd", vmem=26,
-        cost=COST["attn_bwd"], after=(y_got, z_got),
-        scratch=(
-            pltpu.VMEM((HT, TP, 128, T), BF16),
-            pltpu.VMEM((HT, TP, T, 128), BF16),
-            pltpu.VMEM((HT, TP, T, 128), BF16),
-            pltpu.VMEM((HT, 128, TP * T), BF16),
-            pltpu.VMEM((HT, TP, 1, T), F32),
-            pltpu.VMEM((TP, T, T), BF16),
-            pltpu.VMEM((2, 128, TP * T), F32),
-            pltpu.VMEM((2, TP * T, 128), F32),
-            pltpu.VMEM((2, TP * T, 128), F32),
-            pltpu.VMEM((3, 128, 128), F32),
-            pltpu.VMEM((2, 8, 128), F32),
-        ),
-    )
-
-    def chunks(n):
-        return sds((n * CHUNK + TAIL, 128), BF16)
-
-    keep, give = call(
-        attn_dw_kernel, (chunks(4),) * 2,
-        n1.reshape(flat, D), dqkv.reshape(flat, 640), wo_keep, wo_got[0], wo_along, table_grad,
-        name="attn_dw", vmem=16,
-        scratch=(
-            pltpu.VMEM((D, 640), F32), pltpu.VMEM((8, 24, D), F32), pltpu.VMEM((CHUNK, 128), F32),
-        ),
-    )
-    got = swap(give, 4)
+
+    def attn_bwd(second, *after):
+        mine = slice(2, 3) if second else slice(0, 2)
+        count = 1 if second else 2
+        return call(
+            functools.partial(attn_bwd_kernel, second),
+            (sds((TP, T, 256 if second else 384), BF16), sds((8, 128), F32)),
+            qkv, *probs[mine], *inv_tots[mine], *out_ts[mine], g0, g1, g2, g3,
+            name="attn_bwd", vmem=22, cost=COST["attn_bwd"][second], after=after,
+            scratch=(
+                pltpu.VMEM((count, TP, 128, T), BF16),
+                pltpu.VMEM((count, TP, T, 128), BF16),
+                pltpu.VMEM((count, TP, T, 128), BF16),
+                pltpu.VMEM((count, 128, TP * T), BF16),
+                pltpu.VMEM((count, TP, 1, T), F32),
+                pltpu.VMEM((TP, T, T), BF16),
+                pltpu.VMEM((128, TP * T), F32),
+                pltpu.VMEM((TP * T, 128), F32),
+                pltpu.VMEM((TP * T, 128), F32),
+                pltpu.VMEM((3, 128, 128), F32),
+                pltpu.VMEM((2, 8, 128), F32),
+            ),
+        )
+
+    def chunks(n, chunk):
+        return sds((n * chunk + (TAIL if chunk == SECOND else 0), 128), BF16)
+
+    def stage(n, chunk, keep, got, name, *after):
+        return call(
+            functools.partial(stage_kernel, n, chunk), (chunks(n // 2, chunk),) * 2, keep, got,
+            name=name, after=after, cost=COST[name],
+        )
+
+    da, ta = attn_bwd(0)
+    a_keep, a_give = call(
+        first_dw_kernel, (chunks(4, FIRST),) * 2, n1.reshape(flat, D), da.reshape(flat, 384),
+        name="first_dw", vmem=12, scratch=(pltpu.VMEM((D, 384), F32),),
+    )
+    a_got = swap(a_give, 4)
     y_keep, y_give, z_keep, z_give = call(
         ffn_second_kernel, (sds((2, 288, 256), BF16),) * 4, y_keep, y_got, z_keep, z_got,
-        name="ffn_second", after=(give,),
+        name="ffn_second", after=(a_give,),
     )
     y_got, z_got = swap(y_give, 8), swap(z_give, 16)
+    db, tb = attn_bwd(1, y_give, *())
+    b_keep, b_give = call(
+        second_dw_kernel, (chunks(4, SECOND),) * 2,
+        n1.reshape(flat, D), db.reshape(flat, 256), wo_keep, wo_got[0], wo_along, ta, tb,
+        name="second_dw", vmem=12,
+        scratch=(
+            pltpu.VMEM((D, 256), F32), pltpu.VMEM((8, 24, D), F32), pltpu.VMEM((SECOND, 128), F32),
+        ),
+    )
+    b_got = swap(b_give, 4)
     one_keep, one_give = call(
-        one_grad_kernel, (sds((2, T, D), BF16),) * 2, dqkv, w_qkv, name="one_grad", vmem=16,
-        after=(y_give,), cost=COST["one_grad"],
+        one_grad_kernel, (sds((2, T, D), BF16),) * 2, da, db, w_qkv, name="one_grad", vmem=16,
+        after=(b_give,), cost=COST["one_grad"],
     )
     one_c, one_x = reduce_pair(one_keep, one_give)
+    a_keep, a_give = stage(4, FIRST, a_keep, a_got, "stage_y", b_give)
+    a_got = swap(a_give, 8)
+    y_give, z_give = call(
+        ffn_third_kernel, (sds((288, 256), BF16),) * 2, y_keep, y_got, z_keep, z_got,
+        name="ffn_third", after=(a_give,),
+    )
+    y_along, z_along = swap(y_give, 16), swap(z_give, 4)
+    b_keep, b_give = stage(4, SECOND, b_keep, b_got, "stage_y", *(y_give,))
+    b_got = swap(b_give, 8)
+    a_keep, a_give = stage(2, FIRST, a_keep, a_got, "stage_z", b_give)
+    a_got = swap(a_give, 16)
+    b_keep, b_give = stage(2, SECOND, b_keep, b_got, "stage_z", *(a_give,))
+    b_got = swap(b_give, 16)
+    lo_x = swap(later(lo_sum, one_c), 2)
+    layer_out = mixed_own + lo_keep[0].astype(F32) + lo_c[0].astype(F32) + lo_x.astype(F32)
     tokens_grad = call(
         close_kernel, sds((T, D), F32), one_keep, one_c, one_x, mixed_grad, tok, gains,
-        name="close", vmem=10,
-    )
-    y_give, z_give = call(
-        ffn_third_kernel, (sds((288, 256), BF16),) * 2, y_keep, y_got, z_keep, z_got,
-        name="ffn_third", after=(give,),
-    )
-    y_along, z_along = swap(y_give, 16), swap(z_give, 4)
-    keep, give = call(
-        functools.partial(stage_kernel, 4), (chunks(2),) * 2, keep, got, name="stage_y",
-        after=(y_give,), cost=COST["stage_y"],
-    )
-    got = swap(give, 8)
-    keep, give = call(
-        functools.partial(stage_kernel, 2), (chunks(1),) * 2, keep, got, name="stage_z",
-        after=(y_along, z_along), cost=COST["stage_z"],
-    )
-    got = swap(give, 16)
+        name="close", vmem=10, after=(a_got,),
+    )
     dwo, dwd, *backs = call(
         back_kernel,
         (sds((rows, D), F32), sds((64, D), F32)) + (sds((rows, 1792), BF16),) * 4,
-        keep, got, y_keep, y_got, y_along, z_keep, z_got, z_along, name="back", after=(tokens_grad,),
-        scratch=(pltpu.VMEM((CHUNK, 128), F32), pltpu.VMEM((576, 256), F32)),
+        a_keep, a_got, b_keep, b_got, y_keep, y_got, y_along, z_keep, z_got, z_along,
+        name="back", after=(tokens_grad,),
+        scratch=(pltpu.VMEM((FIRST + SECOND, 128), F32), pltpu.VMEM((576, 256), F32)),
     )
     backs = (backs[0], swap(backs[1], 1), swap(backs[2], 2), swap(backs[3], 3))
     dq, dk, dv, dg, du, gg1, gg2, table_sum = call(
         final_kernel,
         (sds((rows, D), F32),) * 3
         + (sds((rows, ff), F32),) * 2
-        + (sds((1, rows), F32), sds((1, rows), F32), sds((NB, H), F32)),
+        + (sds((1, rows), F32), sds((1, rows), F32), sds((H, NB), F32)),
         *backs, gain_cols, w_query, w_key, w_value, w_gate, w_up, name="final",
         scratch=(pltpu.VMEM((TP, rows, 1664), F32),),
     )
@@ -945,7 +976,7 @@
         dv,
         dwo,
         gg1[0],
-        table_sum,
+        table_sum.T,
         dg,
         du,
         dwd,

time: 187 us -> 169 us (0.904); the launches traced: 186 us -> 166 us
  waiting for transfers between devices: 76.2 us -> 51.9 us
  starting transfers between devices: 47 us -> 53.6 us
  local copies, waits for them, and re-layouts: 5.57 us -> 1.8 us
    ppermute x53 -> x57, waiting for transfers between devices: 76.2 us -> 51.9 us  [swap(): return lax.ppermute(x, AXES, [(d, d ^ mask) for d in range(n_dev)])]
    ppermute x53 -> x57, starting transfers between devices: 47 us -> 53.6 us  [swap(): return lax.ppermute(x, AXES, [(d, d ^ mask) for d in range(n_dev)])]
    unnamed x34 -> x26, local copies, waits for them, and re-layouts: 5.57 us -> 1.8 us
    pallas_call x26 -> x30, Pallas kernels: 55.3 us -> 55.4 us  [call(): pl.pallas_call(body, out_shape=out_shape, in_specs=[aspec] * skip + specs...]
  transfers between devices with their start and end apart: 53 -> 57, of which waited for: 25 -> 23; matrix products, arithmetic and copies ran while one was open for 1% -> 1% of each run, Pallas kernels for 20% -> 28%
where the time goes in v3:
time: 169 us; the launch traced here: 166 us
  Pallas kernels  55.4 us (33%)
  starting transfers between devices  53.6 us (32%)
  waiting for transfers between devices  51.9 us (31%)
  other arithmetic  1.89 us (1%)
  local copies, waits for them, and re-layouts  1.8 us (1%)
    pallas_call x30, Pallas kernels, call(): pl.pallas_call(body, out_shape=out_shape, in_specs=[aspec] * skip + specs...  55.4 us
    ppermute x57, starting transfers between devices, swap(): return lax.ppermute(x, AXES, [(d, d ^ mask) for d in range(n_dev)])  53.6 us
    ppermute x57, waiting for transfers between devices, swap(): return lax.ppermute(x, AXES, [(d, d ^ mask) for d in range(n_dev)])  51.9 us
  transfers between devices with their start and end apart: 57, of which 23 were waited for; matrix products, arithmetic and copies ran while one was open for 1% of the time, Pallas kernels for 28%

profile of v3, /device:TPU:0, one launch (start us, length us, event | category | flops | bytes accessed | tf_op | source)
XLA Modules:
  0.0 166.0 jit_solution(4217400463970263071)
XLA Ops:
  0.6 3.0 %prep.1 = (bf16[24,1664]{1,0:T(8,128)(2,1)}, bf16[24,1664]{1,0:T(8,128)(2,1)}, bf16[24,1664]{1,0:T(8,128)(2,1)}, bf16[24,1664]{1,0:T(8,128)(2,1)}, bf16[272,768]{1,0:T(8,128)(2,1)}, /*index=5*/f32[2,24,128]{2,1,0:T(8,128)}) custom-call(bf16[24,768]{1,0:T(8,128)(2,1)} %refs_5_.3, bf16[24,768]{1,0:T(8,128)(2,1)} %refs_6_.3, bf16[24,768]{1,0:T(8,128)(2,1)} %refs_7_.3, ...), custom_call_target="tpu_custom_call" | custom-call | tf_op jit(solution)/shard_map/prep/pallas_call | solution.py:59
  4.1 2.6 %collective-permute-start.1 = (bf16[24,1664]{1,0:T(8,128)(2,1)}, bf16[24,1664]{1,0:T(8,128)(2,1)S(1)}, u32[]{:S(2)}, u32[]{:S(2)}) collective-permute-start(bf16[24,1664]{1,0:T(8,128)(2,1)} %get-tuple-element.125), channel_id=1, source_target_pairs={{0,2},{1,3},{2,0},{3,1},{4,6},{5,7},{6,4},{7,5},{8,10},{9,11},{10,... | collective-permute-start | bytes 239624 | tf_op jit(solution)/shard_map/ppermute | solution.py:730
  12.1 2.4 %pack.1.refs_0_.refs_4_.refs_1_ = bf16[128,640]{1,0:T(8,128)(2,1)} custom-call(bf16[24,1664]{1,0:T(8,128)(2,1)} %get-tuple-element.123.refs_0_.refs_1_, bf16[24,1664]{1,0:T(8,128)(2,1)} %copy-done.10, bf16[24,1664]{1,0:T(8,128)(2,1)} %copy-done.11, bf16[24,1664]{1,0:T(8,128)(2,1)} %copy-done.12, bf16[24,768]{1,0:T(8,128)(2,1)} %refs_4_.3), custom_call_target="tpu_custom_call" | custom-call | tf_op jit(solution)/shard_map/pack/pallas_call | solution.py:59
  17.9 2.6 %collective-permute-start.3 = (bf16[128,640]{1,0:T(8,128)(2,1)}, bf16[128,640]{1,0:T(8,128)(2,1)S(1)}, u32[]{:S(2)}, u32[]{:S(2)}) collective-permute-start(bf16[128,640]{1,0:T(8,128)(2,1)} %pack.1.refs_0_.refs_4_.refs_1_), channel_id=1, source_target_pairs={{0,16},{1,17},{2,18},{3,19},{4,20},{5,21},{6,22},{7,23},{8,24},{9,... | collective-permute-start | bytes 491528 | tf_op jit(solution)/shard_map/ppermute | solution.py:730
  21.1 2.7 %pack_more.1.refs_0_ = bf16[576,256]{1,0:T(8,128)(2,1)} custom-call(bf16[128,640]{1,0:T(8,128)(2,1)} %pack.1.refs_0_.refs_4_.refs_1_, bf16[24,1664]{1,0:T(8,128)(2,1)} %get-tuple-element.123.refs_0_.refs_1_, bf16[24,1664]{1,0:T(8,128)(2,1)} %copy-done.10, bf16[24,1664]{1,0:T(8,128)(2,1)} %copy-done.11, bf16[24,1664]{1,0:T(8,128)(2,1)} %copy-done.12, ...), custom_call_target="tpu_custom_call" | custom-call | tf_op jit(solution)/shard_map/pack_more/pallas_call | solution.py:59
  26.1 2.4 %collective-permute-done.3.refs_6_.refs_3_ = bf16[128,640]{1,0:T(8,128)(2,1)S(1)} collective-permute-done((bf16[128,640]{1,0:T(8,128)(2,1)}, bf16[128,640]{1,0:T(8,128)(2,1)S(1)}, u32[]{:S(2)}, u32[]{:S(2)}) %collective-permute-start.3) | collective-permute-done | bytes 163872 | tf_op jit(solution)/shard_map/ppermute | solution.py:730
  30.9 2.9 %collective-permute-done.10.refs_9_.refs_6_ = bf16[128,640]{1,0:T(8,128)(2,1)S(1)} collective-permute-done((bf16[128,640]{1,0:T(8,128)(2,1)S(1)}, bf16[128,640]{1,0:T(8,128)(2,1)S(1)}, u32[]{:S(2)}, u32[]{:S(2)}) %collective-permute-start.10) | collective-permute-done | bytes 163872 | tf_op jit(solution)/shard_map/ppermute | solution.py:730
  33.8 2.4 %collective-permute-done.11.refs_10_.refs_7_ = bf16[128,640]{1,0:T(8,128)(2,1)S(1)} collective-permute-done((bf16[128,640]{1,0:T(8,128)(2,1)S(1)}, bf16[128,640]{1,0:T(8,128)(2,1)S(1)}, u32[]{:S(2)}, u32[]{:S(2)}) %collective-permute-start.11) | collective-permute-done | bytes 163872 | tf_op jit(solution)/shard_map/ppermute | solution.py:730
  38.0 2.2 %collective-permute-start.21 = (bf16[576,256]{1,0:T(8,128)(2,1)}, bf16[576,256]{1,0:T(8,128)(2,1)S(1)}, u32[]{:S(2)}, u32[]{:S(2)}) collective-permute-start(bf16[576,256]{1,0:T(8,128)(2,1)} %pack_more.1.refs_0_), channel_id=1, source_target_pairs={{0,16},{1,17},{2,18},{3,19},{4,20},{5,21},{6,22},{7,23},{8,24},{9,... | collective-permute-start | bytes 884744 | tf_op jit(solution)/shard_map/ppermute | solution.py:730
  41.8 2.4 %collective-permute-start.20 = (bf16[576,256]{1,0:T(8,128)(2,1)}, bf16[576,256]{1,0:T(8,128)(2,1)S(1)}, u32[]{:S(2)}, u32[]{:S(2)}) collective-permute-start(bf16[576,256]{1,0:T(8,128)(2,1)} %pack_more.1.refs_0_), channel_id=1, source_target_pairs={{0,8},{1,9},{2,10},{3,11},{4,12},{5,13},{6,14},{7,15},{8,0},{9,1},... | collective-permute-start | bytes 884744 | tf_op jit(solution)/shard_map/ppermute | solution.py:730
  44.2 2.8 %qkv.1 = (bf16[4,256,768]{2,1,0:T(8,128)(2,1)S(1)}, bf16[4,256,768]{2,1,0:T(8,128)(2,1)S(1)}, bf16[5,4,256,128]{3,2,1,0:T(8,128)(2,1)S(1)}, bf16[768,640]{1,0:T(...) custom-call(bf16[272,768]{1,0:T(8,128)(2,1)S(1)} %copy-done.3, ...), custom_call_target="tpu_custom_call" | custom-call | tf_op jit(solution)/shard_map/qkv/pallas_call | solution.py:59
  48.2 3.3 %attn_fwd.3 = (bf16[4,4,256,256]{3,2,1,0:T(8,128)(2,1)S(1)}, f32[4,1,256]{2,1,0:T(1,128)S(1)}, f32[64,1024]{1,0:T(8,128)S(1)}) custom-call(bf16[256,768]{1,0:T(8,128)(2,1)S(1)} %collective-permute-done.6.refs_0_.refs_9_.refs_8_, f32[12,32]{1,0:T(8,128)S(1)} %convert_bitcast_fusion.refs_1_, f32[3,3,256,256]{3,2,1,0:T(8,128)S(1)} %bias.1.refs_2_, ...), custom_call_target="tpu_custom_call" | custom-call | tf_op jit(solution)/shard_map/attn_fwd/pallas_call | solution.py:59
  51.5 3.2 %collective-permute-done.21.refs_2_ = bf16[576,256]{1,0:T(8,128)(2,1)S(1)} collective-permute-done((bf16[576,256]{1,0:T(8,128)(2,1)}, bf16[576,256]{1,0:T(8,128)(2,1)S(1)}, u32[]{:S(2)}, u32[]{:S(2)}) %collective-permute-start.21) | collective-permute-done | bytes 294944 | tf_op jit(solution)/shard_map/ppermute | solution.py:730
  57.9 3.3 %attn_fwd.4 = (bf16[4,4,256,256]{3,2,1,0:T(8,128)(2,1)S(1)}, f32[4,1,256]{2,1,0:T(1,128)S(1)}, f32[64,1024]{1,0:T(8,128)S(1)}) custom-call(f32[4,1,256]{2,1,0:T(1,128)S(1)} %get-tuple-element.142.refs_0_.refs_3_, f32[12,32]{1,0:T(8,128)S(1)} %convert_bitcast_fusion.refs_1_, f32[3,3,256,256]{3,2,1,0:T(8,128)S(1)} %bias.1.refs_2_, ...), custom_call_target="tpu_custom_call" | custom-call | tf_op jit(solution)/shard_map/attn_fwd/pallas_call | solution.py:59
  61.2 3.4 %attn_fwd.5 = (bf16[4,4,256,256]{3,2,1,0:T(8,128)(2,1)S(1)}, f32[4,1,256]{2,1,0:T(1,128)S(1)}, f32[64,1024]{1,0:T(8,128)S(1)}) custom-call(f32[4,1,256]{2,1,0:T(1,128)S(1)} %get-tuple-element.144.refs_0_.refs_4_, f32[12,32]{1,0:T(8,128)S(1)} %convert_bitcast_fusion.refs_1_, f32[3,3,256,256]{3,2,1,0:T(8,128)S(1)} %bias.1.refs_2_, ...), custom_call_target="tpu_custom_call" | custom-call | tf_op jit(solution)/shard_map/attn_fwd/pallas_call | solution.py:59
  65.9 3.3 %collective-permute-done.25.refs_6_ = bf16[576,256]{1,0:T(8,128)(2,1)S(1)} collective-permute-done((bf16[576,256]{1,0:T(8,128)(2,1)S(1)}, bf16[576,256]{1,0:T(8,128)(2,1)S(1)}, u32[]{:S(2)}, u32[]{:S(2)}) %collective-permute-start.25) | collective-permute-done | bytes 294944 | tf_op jit(solution)/shard_map/ppermute | solution.py:730
  71.5 2.9 %collective-permute-done.15.refs_2_.refs_3_ = bf16[1536,128]{1,0:T(8,128)(2,1)S(1)} collective-permute-done((bf16[1536,128]{1,0:T(8,128)(2,1)S(1)}, bf16[1536,128]{1,0:T(8,128)(2,1)S(1)}, u32[]{:S(2)}, u32[]{:S(2)}) %collective-permute-start.15) | collective-permute-done | bytes 393248 | tf_op jit(solution)/shard_map/ppermute | solution.py:730
  74.4 1.8 %collective-permute-done.26.refs_7_ = bf16[576,256]{1,0:T(8,128)(2,1)S(1)} collective-permute-done((bf16[576,256]{1,0:T(8,128)(2,1)S(1)}, bf16[576,256]{1,0:T(8,128)(2,1)S(1)}, u32[]{:S(2)}, u32[]{:S(2)}) %collective-permute-start.26) | collective-permute-done | bytes 294944 | tf_op jit(solution)/shard_map/ppermute | solution.py:730
  77.4 4.8 %ffn.2 = (bf16[2,256,768]{2,1,0:T(8,128)(2,1)S(1)}, bf16[2,256,512]{2,1,0:T(8,128)(2,1)S(1)}, bf16[2,256,1024]{2,1,0:T(8,128)(2,1)S(1)}, bf16[256,768]{1,0:T(8,1...) custom-call(bf16[1536,128]{1,0:T(8,128)(2,1)S(1)} %join.1.refs_0_.refs_1_, ...), custom_call_target="tpu_custom_call" | custom-call | tf_op jit(solution)/shard_map/ffn/pallas_call | solution.py:59
  84.8 4.4 %ffn.3 = (bf16[2,256,768]{2,1,0:T(8,128)(2,1)S(1)}, bf16[2,256,512]{2,1,0:T(8,128)(2,1)S(1)}, bf16[2,256,1024]{2,1,0:T(8,128)(2,1)S(1)}, bf16[256,768]{1,0:T(8,1...) custom-call(bf16[256,768]{1,0:T(8,128)(2,1)S(1)} %add.27.refs_0_, ...), custom_call_target="tpu_custom_call" | custom-call | tf_op jit(solution)/shard_map/ffn/pallas_call | solution.py:59
  89.3 3.8 %ffn_dw.1 = (bf16[4,288,256]{2,1,0:T(8,128)(2,1)S(1)}, bf16[4,288,256]{2,1,0:T(8,128)(2,1)S(1)}, bf16[4,288,256]{2,1,0:T(8,128)(2,1)S(1)}, bf16[4,288,256]{2,1,0...) custom-call(bf16[512,768]{1,0:T(8,128)(2,1)S(1)} %bitcast.43, ...), custom_call_target="tpu_custom_call" | custom-call | tf_op jit(solution)/shard_map/ffn_dw/pallas_call | solution.py:59
  100.5 3.1 %collective-permute-done.34.refs_9_.refs_7_ = bf16[384,128]{1,0:T(8,128)(2,1)S(1)} collective-permute-done((bf16[384,128]{1,0:T(8,128)(2,1)S(1)}, bf16[384,128]{1,0:T(8,128)(2,1)S(1)}, u32[]{:S(2)}, u32[]{:S(2)}) %collective-permute-start.34) | collective-permute-done | bytes 98336 | tf_op jit(solution)/shard_map/ppermute | solution.py:730
  105.3 5.4 %attn_bwd.2 = (bf16[4,256,384]{2,1,0:T(8,128)(2,1)S(1)}, f32[8,128]{1,0:T(8,128)S(1)}) custom-call(bf16[5,4,256,128]{3,2,1,0:T(8,128)(2,1)S(1)} %get-tuple-element.138.refs_3_.refs_0_.refs_1_, bf16[4,4,256,256]{3,2,1,0:T(8,128)(2,1)S(1)} %get-tuple-element.178.refs_1_, bf16[4,4,256,256]{3,2,1,0:T(8,128)(2,1)S(1)} %get-tuple-element.179.refs_2_, ...), custom_call_target="tpu_custom_call" | custom-call | tf_op jit(solution)/shard_map/attn_bwd/pallas_call | solution.py:59
  115.5 2.9 %attn_bwd.3 = (bf16[4,256,256]{2,1,0:T(8,128)(2,1)S(1)}, f32[8,128]{1,0:T(8,128)S(1)}) custom-call(bf16[2,288,256]{2,1,0:T(8,128)(2,1)S(1)} %get-tuple-element.189.refs_0_, bf16[5,4,256,128]{3,2,1,0:T(8,128)(2,1)S(1)} %get-tuple-element.138.refs_3_.refs_0_.refs_1_, bf16[4,4,256,256]{3,2,1,0:T(8,128)(2,1)S(1)} %get-tuple-element.190.refs_2_, ...), custom_call_target="tpu_custom_call" | custom-call | flops 11500000256 | tf_op jit(solution)/shard_map/attn_bwd/pallas_call | solution.py:59
  118.4 3.2 %collective-permute-start.45 = (bf16[2,288,256]{2,1,0:T(8,128)(2,1)S(1)}, bf16[2,288,256]{2,1,0:T(8,128)(2,1)S(1)}, u32[]{:S(2)}, u32[]{:S(2)}) collective-permute-start(bf16[2,288,256]{2,1,0:T(8,128)(2,1)S(1)} %get-tuple-element.207), channel_id=1, source_target_pairs={{0,16},{1,17},{2,18},{3,19},{4,20},{5,21},{6,22},{7,23},{8,24},{9,... | collective-permute-start | bytes 884744 | tf_op jit(solution)/shard_map/ppermute | solution.py:730
  124.9 2.2 %one_grad.1 = (bf16[2,256,768]{2,1,0:T(8,128)(2,1)S(1)}, bf16[2,256,768]{2,1,0:T(8,128)(2,1)S(1)}) custom-call(bf16[1360,128]{1,0:T(8,128)(2,1)S(1)} %get-tuple-element.199.refs_0_, bf16[4,256,384]{2,1,0:T(8,128)(2,1)S(1)} %get-tuple-element.184.refs_1_, bf16[4,256,256]{2,1,0:T(8,128)(2,1)S(1)} %get-tuple-element.192.refs_2_, ...), custom_call_target="tpu_custom_call" | custom-call | flops 46000001024 | tf_op jit(solution)/shard_map/one_grad/pallas_call | solution.py:59
  128.6 5.8 %collective-permute-done.45.refs_4_.refs_9_ = bf16[2,288,256]{2,1,0:T(8,128)(2,1)S(1)} collective-permute-done((bf16[2,288,256]{2,1,0:T(8,128)(2,1)S(1)}, bf16[2,288,256]{2,1,0:T(8,128)(2,1)S(1)}, u32[]{:S(2)}, u32[]{:S(2)}) %collective-permute-start.45) | collective-permute-done | bytes 294944 | tf_op jit(solution)/shard_map/ppermute | solution.py:730
  135.6 4.1 %collective-permute-start.50 = (bf16[688,128]{1,0:T(8,128)(2,1)S(1)}, bf16[688,128]{1,0:T(8,128)(2,1)S(1)}, u32[]{:S(2)}, u32[]{:S(2)}) collective-permute-start(bf16[688,128]{1,0:T(8,128)(2,1)S(1)} %get-tuple-element.210.refs_0_), channel_id=1, source_target_pairs={{0,8},{1,9},{2,10},{3,11},{4,12},{5,13},{6,14},{7,15},{8,0},{9,1},... | collective-permute-start | bytes 528392 | tf_op jit(solution)/shard_map/ppermute | solution.py:730
  140.8 7.1 %collective-permute-done.50.refs_2_ = bf16[688,128]{1,0:T(8,128)(2,1)S(1)} collective-permute-done((bf16[688,128]{1,0:T(8,128)(2,1)S(1)}, bf16[688,128]{1,0:T(8,128)(2,1)S(1)}, u32[]{:S(2)}, u32[]{:S(2)}) %collective-permute-start.50) | collective-permute-done | bytes 176160 | tf_op jit(solution)/shard_map/ppermute | solution.py:730
  149.8 2.1 %collective-permute-done.49.refs_3_ = bf16[256,768]{1,0:T(8,128)(2,1)S(1)} collective-permute-done((bf16[256,768]{1,0:T(8,128)(2,1)S(1)}, bf16[256,768]{1,0:T(8,128)(2,1)S(1)}, u32[]{:S(2)}, u32[]{:S(2)}) %collective-permute-start.49) | collective-permute-done | bytes 393248 | tf_op jit(solution)/shard_map/ppermute | solution.py:730
  153.2 2.6 %collective-permute-done.51.refs_4_ = bf16[352,128]{1,0:T(8,128)(2,1)S(1)} collective-permute-done((bf16[352,128]{1,0:T(8,128)(2,1)S(1)}, bf16[352,128]{1,0:T(8,128)(2,1)S(1)}, u32[]{:S(2)}, u32[]{:S(2)}) %collective-permute-start.51) | collective-permute-done | bytes 90144 | tf_op jit(solution)/shard_map/ppermute | solution.py:730
  160.8 2.6 %collective-permute-done.55.refs_2_ = bf16[24,1792]{1,0:T(8,128)(2,1)S(1)} collective-permute-done((bf16[24,1792]{1,0:T(8,128)(2,1)S(1)}, bf16[24,1792]{1,0:T(8,128)(2,1)S(1)}, u32[]{:S(2)}, u32[]{:S(2)}) %collective-permute-start.55) | collective-permute-done | bytes 86048 | tf_op jit(solution)/shard_map/ppermute | solution.py:730
  (144 shorter events, 61.0 us)
Async XLA Ops:
  6.8 29.9 %collective-permute-start.8 = (bf16[272,768]{1,0:T(8,128)(2,1)}, bf16[272,768]{1,0:T(8,128)(2,1)S(1)}, u32[]{:S(2)}, u32[]{:S(2)}) collective-permute-start(bf16[272,768]{1,0:T(8,128)(2,1)} %get-tuple-element.131.refs_0_), channel_id=1, source_target_pairs={{0,2},{1,3},{2,0},{3,1},{4,6},{5,7},{6,4},{7,5},{8,10},{9,11},{10,... | collective-permute-start | bytes 1253384 | tf_op jit(solution)/shard_map/ppermute | solution.py:730
  8.5 31.8 %collective-permute-start.7 = (bf16[272,768]{1,0:T(8,128)(2,1)}, bf16[272,768]{1,0:T(8,128)(2,1)S(1)}, u32[]{:S(2)}, u32[]{:S(2)}) collective-permute-start(bf16[272,768]{1,0:T(8,128)(2,1)} %get-tuple-element.131.refs_0_), channel_id=1, source_target_pairs={{0,1},{1,0},{2,3},{3,2},{4,5},{5,4},{6,7},{7,6},{8,9},{9,8},{10,11... | collective-permute-start | bytes 1253384 | tf_op jit(solution)/shard_map/ppermute | solution.py:730
  14.5 10.7 %collective-permute-start.5 = (bf16[128,640]{1,0:T(8,128)(2,1)}, bf16[128,640]{1,0:T(8,128)(2,1)S(1)}, u32[]{:S(2)}, u32[]{:S(2)}) collective-permute-start(bf16[128,640]{1,0:T(8,128)(2,1)} %pack.1.refs_0_.refs_4_.refs_1_), channel_id=1, source_target_pairs={{0,4},{1,5},{2,6},{3,7},{4,0},{5,1},{6,2},{7,3},{8,12},{9,13},{10,... | collective-permute-start | bytes 491528 | tf_op jit(solution)/shard_map/ppermute | solution.py:730
  16.3 9.8 %collective-permute-start.4 = (bf16[128,640]{1,0:T(8,128)(2,1)}, bf16[128,640]{1,0:T(8,128)(2,1)S(1)}, u32[]{:S(2)}, u32[]{:S(2)}) collective-permute-start(bf16[128,640]{1,0:T(8,128)(2,1)} %pack.1.refs_0_.refs_4_.refs_1_), channel_id=1, source_target_pairs={{0,8},{1,9},{2,10},{3,11},{4,12},{5,13},{6,14},{7,15},{8,0},{9,1},... | collective-permute-start | bytes 491528 | tf_op jit(solution)/shard_map/ppermute | solution.py:730
  17.9 10.6 %collective-permute-start.3 = (bf16[128,640]{1,0:T(8,128)(2,1)}, bf16[128,640]{1,0:T(8,128)(2,1)S(1)}, u32[]{:S(2)}, u32[]{:S(2)}) collective-permute-start(bf16[128,640]{1,0:T(8,128)(2,1)} %pack.1.refs_0_.refs_4_.refs_1_), channel_id=1, source_target_pairs={{0,16},{1,17},{2,18},{3,19},{4,20},{5,21},{6,22},{7,23},{8,24},{9,... | collective-permute-start | bytes 491528 | tf_op jit(solution)/shard_map/ppermute | solution.py:730
  36.7 11.5 %collective-permute-start.6 = (bf16[256,768]{1,0:T(8,128)(2,1)S(1)}, bf16[256,768]{1,0:T(8,128)(2,1)S(1)}, u32[]{:S(2)}, u32[]{:S(2)}) collective-permute-start(bf16[256,768]{1,0:T(8,128)(2,1)S(1)} %bitcast.36), channel_id=1, source_target_pairs={{0,2},{1,3},{2,0},{3,1},{4,6},{5,7},{6,4},{7,5},{8,10},{9,11},{10,... | collective-permute-start | bytes 1179656 | tf_op jit(solution)/shard_map/ppermute | solution.py:730
  38.0 16.6 %collective-permute-start.21 = (bf16[576,256]{1,0:T(8,128)(2,1)}, bf16[576,256]{1,0:T(8,128)(2,1)S(1)}, u32[]{:S(2)}, u32[]{:S(2)}) collective-permute-start(bf16[576,256]{1,0:T(8,128)(2,1)} %pack_more.1.refs_0_), channel_id=1, source_target_pairs={{0,16},{1,17},{2,18},{3,19},{4,20},{5,21},{6,22},{7,23},{8,24},{9,... | collective-permute-start | bytes 884744 | tf_op jit(solution)/shard_map/ppermute | solution.py:730
  40.2 14.4 %collective-permute-start.22 = (bf16[576,256]{1,0:T(8,128)(2,1)}, bf16[576,256]{1,0:T(8,128)(2,1)S(1)}, u32[]{:S(2)}, u32[]{:S(2)}) collective-permute-start(bf16[576,256]{1,0:T(8,128)(2,1)} %pack_more.1.refs_0_), channel_id=1, source_target_pairs={{0,4},{1,5},{2,6},{3,7},{4,0},{5,1},{6,2},{7,3},{8,12},{9,13},{10,... | collective-permute-start | bytes 884744 | tf_op jit(solution)/shard_map/ppermute | solution.py:730
  41.8 13.9 %collective-permute-start.20 = (bf16[576,256]{1,0:T(8,128)(2,1)}, bf16[576,256]{1,0:T(8,128)(2,1)S(1)}, u32[]{:S(2)}, u32[]{:S(2)}) collective-permute-start(bf16[576,256]{1,0:T(8,128)(2,1)} %pack_more.1.refs_0_), channel_id=1, source_target_pairs={{0,8},{1,9},{2,10},{3,11},{4,12},{5,13},{6,14},{7,15},{8,0},{9,1},... | collective-permute-start | bytes 884744 | tf_op jit(solution)/shard_map/ppermute | solution.py:730
  47.2 18.2 %collective-permute-start.17 = (bf16[192,768]{1,0:T(8,128)(2,1)S(1)}, bf16[192,768]{1,0:T(8,128)(2,1)S(1)}, u32[]{:S(2)}, u32[]{:S(2)}) collective-permute-start(bf16[192,768]{1,0:T(8,128)(2,1)S(1)} %stripes.1.refs_0_), channel_id=1, source_target_pairs={{0,2},{1,3},{2,0},{3,1},{4,6},{5,7},{6,4},{7,5},{8,10},{9,11},{10,... | collective-permute-start | bytes 884744 | tf_op jit(solution)/shard_map/ppermute | solution.py:730
  55.7 9.9 %collective-permute-start.24 = (bf16[576,256]{1,0:T(8,128)(2,1)S(1)}, bf16[576,256]{1,0:T(8,128)(2,1)S(1)}, u32[]{:S(2)}, u32[]{:S(2)}) collective-permute-start(bf16[576,256]{1,0:T(8,128)(2,1)S(1)} %collective-permute-done.20.refs_1_), channel_id=1, source_target_pairs={{0,4},{1,5},{2,6},{3,7},{4,0},{5,1},{6,2},{7,3},{8,12},{9,13},{10,... | collective-permute-start | bytes 884744 | tf_op jit(solution)/shard_map/ppermute | solution.py:730
  56.2 13.0 %collective-permute-start.25 = (bf16[576,256]{1,0:T(8,128)(2,1)S(1)}, bf16[576,256]{1,0:T(8,128)(2,1)S(1)}, u32[]{:S(2)}, u32[]{:S(2)}) collective-permute-start(bf16[576,256]{1,0:T(8,128)(2,1)S(1)} %collective-permute-done.21.refs_2_), channel_id=1, source_target_pairs={{0,4},{1,5},{2,6},{3,7},{4,0},{5,1},{6,2},{7,3},{8,12},{9,13},{10,... | collective-permute-start | bytes 884744 | tf_op jit(solution)/shard_map/ppermute | solution.py:730
  57.7 11.5 %collective-permute-start.23 = (bf16[576,256]{1,0:T(8,128)(2,1)S(1)}, bf16[576,256]{1,0:T(8,128)(2,1)S(1)}, u32[]{:S(2)}, u32[]{:S(2)}) collective-permute-start(bf16[576,256]{1,0:T(8,128)(2,1)S(1)} %collective-permute-done.21.refs_2_), channel_id=1, source_target_pairs={{0,8},{1,9},{2,10},{3,11},{4,12},{5,13},{6,14},{7,15},{8,0},{9,1},... | collective-permute-start | bytes 884744 | tf_op jit(solution)/shard_map/ppermute | solution.py:730
  64.8 9.6 %collective-permute-start.15 = (bf16[1536,128]{1,0:T(8,128)(2,1)S(1)}, bf16[1536,128]{1,0:T(8,128)(2,1)S(1)}, u32[]{:S(2)}, u32[]{:S(2)}) collective-permute-start(bf16[1536,128]{1,0:T(8,128)(2,1)S(1)} %join.1.refs_0_.refs_1_), channel_id=1, source_target_pairs={{0,2},{1,3},{2,0},{3,1},{4,6},{5,7},{6,4},{7,5},{8,10},{9,11},{10,... | collective-permute-start | bytes 1179656 | tf_op jit(solution)/shard_map/ppermute | solution.py:730
  84.1 12.3 %collective-permute-start.31 = (bf16[256,768]{1,0:T(8,128)(2,1)S(1)}, bf16[256,768]{1,0:T(8,128)(2,1)S(1)}, u32[]{:S(2)}, u32[]{:S(2)}) collective-permute-start(bf16[256,768]{1,0:T(8,128)(2,1)S(1)} %add.27.refs_0_), channel_id=1, source_target_pairs={{0,2},{1,3},{2,0},{3,1},{4,6},{5,7},{6,4},{7,5},{8,10},{9,11},{10,... | collective-permute-start | bytes 1179656 | tf_op jit(solution)/shard_map/ppermute | solution.py:730
  93.1 19.1 %collective-permute-start.37 = (bf16[4,288,256]{2,1,0:T(8,128)(2,1)S(1)}, bf16[4,288,256]{2,1,0:T(8,128)(2,1)S(1)}, u32[]{:S(2)}, u32[]{:S(2)}) collective-permute-start(bf16[4,288,256]{2,1,0:T(8,128)(2,1)S(1)} %get-tuple-element.188), channel_id=1, source_target_pairs={{0,8},{1,9},{2,10},{3,11},{4,12},{5,13},{6,14},{7,15},{8,0},{9,1},... | collective-permute-start | bytes 1769480 | tf_op jit(solution)/shard_map/ppermute | solution.py:730
  94.8 18.1 %collective-permute-start.36 = (bf16[4,288,256]{2,1,0:T(8,128)(2,1)S(1)}, bf16[4,288,256]{2,1,0:T(8,128)(2,1)S(1)}, u32[]{:S(2)}, u32[]{:S(2)}) collective-permute-start(bf16[4,288,256]{2,1,0:T(8,128)(2,1)S(1)} %get-tuple-element.171.refs_0_), channel_id=1, source_target_pairs={{0,4},{1,5},{2,6},{3,7},{4,0},{5,1},{6,2},{7,3},{8,12},{9,13},{10,... | collective-permute-start | bytes 1769480 | tf_op jit(solution)/shard_map/ppermute | solution.py:730
  97.7 17.0 %collective-permute-start.39 = (bf16[8,24,768]{2,1,0:T(8,128)(2,1)S(1)}, bf16[8,24,768]{2,1,0:T(8,128)(2,1)S(1)}, u32[]{:S(2)}, u32[]{:S(2)}) collective-permute-start(bf16[8,24,768]{2,1,0:T(8,128)(2,1)S(1)} %get-tuple-element.195), channel_id=1, source_target_pairs={{0,1},{1,0},{2,3},{3,2},{4,5},{5,4},{6,7},{7,6},{8,9},{9,8},{10,11... | collective-permute-start | bytes 884744 | tf_op jit(solution)/shard_map/ppermute | solution.py:730
  103.6 14.8 %collective-permute-start.38 = (bf16[8,24,768]{2,1,0:T(8,128)(2,1)S(1)}, bf16[8,24,768]{2,1,0:T(8,128)(2,1)S(1)}, u32[]{:S(2)}, u32[]{:S(2)}) collective-permute-start(bf16[8,24,768]{2,1,0:T(8,128)(2,1)S(1)} %get-tuple-element.194), channel_id=1, source_target_pairs={{0,1},{1,0},{2,3},{3,2},{4,5},{5,4},{6,7},{7,6},{8,9},{9,8},{10,11... | collective-permute-start | bytes 884744 | tf_op jit(solution)/shard_map/ppermute | solution.py:730
  104.6 30.8 %collective-permute-start.32 = (bf16[2,256,768]{2,1,0:T(8,128)(2,1)S(1)}, bf16[2,256,768]{2,1,0:T(8,128)(2,1)S(1)}, u32[]{:S(2)}, u32[]{:S(2)}) collective-permute-start(bf16[2,256,768]{2,1,0:T(8,128)(2,1)S(1)} %get-tuple-element.176), channel_id=1, source_target_pairs={{0,1},{1,0},{2,3},{3,2},{4,5},{5,4},{6,7},{7,6},{8,9},{9,8},{10,11... | collective-permute-start | bytes 2359304 | tf_op jit(solution)/shard_map/ppermute | solution.py:730
  112.1 15.0 %collective-permute-start.43 = (bf16[1152,128]{1,0:T(8,128)(2,1)S(1)}, bf16[1152,128]{1,0:T(8,128)(2,1)S(1)}, u32[]{:S(2)}, u32[]{:S(2)}) collective-permute-start(bf16[1152,128]{1,0:T(8,128)(2,1)S(1)} %get-tuple-element.185.refs_0_), channel_id=1, source_target_pairs={{0,4},{1,5},{2,6},{3,7},{4,0},{5,1},{6,2},{7,3},{8,12},{9,13},{10,... | collective-permute-start | bytes 884744 | tf_op jit(solution)/shard_map/ppermute | solution.py:730
  113.2 21.2 %collective-permute-start.44 = (bf16[2,288,256]{2,1,0:T(8,128)(2,1)S(1)}, bf16[2,288,256]{2,1,0:T(8,128)(2,1)S(1)}, u32[]{:S(2)}, u32[]{:S(2)}) collective-permute-start(bf16[2,288,256]{2,1,0:T(8,128)(2,1)S(1)} %get-tuple-element.189.refs_0_), channel_id=1, source_target_pairs={{0,8},{1,9},{2,10},{3,11},{4,12},{5,13},{6,14},{7,15},{8,0},{9,1},... | collective-permute-start | bytes 884744 | tf_op jit(solution)/shard_map/ppermute | solution.py:730
  114.7 8.4 %collective-permute-start.40 = (bf16[8,24,768]{2,1,0:T(8,128)(2,1)S(1)}, bf16[8,24,768]{2,1,0:T(8,128)(2,1)S(1)}, u32[]{:S(2)}, u32[]{:S(2)}) collective-permute-start(bf16[8,24,768]{2,1,0:T(8,128)(2,1)S(1)} %bitcast_add_fusion), channel_id=1, source_target_pairs={{0,2},{1,3},{2,0},{3,1},{4,6},{5,7},{6,4},{7,5},{8,10},{9,11},{10,... | collective-permute-start | bytes 884744 | tf_op jit(solution)/shard_map/ppermute | solution.py:730
  118.4 16.0 %collective-permute-start.45 = (bf16[2,288,256]{2,1,0:T(8,128)(2,1)S(1)}, bf16[2,288,256]{2,1,0:T(8,128)(2,1)S(1)}, u32[]{:S(2)}, u32[]{:S(2)}) collective-permute-start(bf16[2,288,256]{2,1,0:T(8,128)(2,1)S(1)} %get-tuple-element.207), channel_id=1, source_target_pairs={{0,16},{1,17},{2,18},{3,19},{4,20},{5,21},{6,22},{7,23},{8,24},{9,... | collective-permute-start | bytes 884744 | tf_op jit(solution)/shard_map/ppermute | solution.py:730
  124.3 11.2 %collective-permute-start.46 = (bf16[1360,128]{1,0:T(8,128)(2,1)S(1)}, bf16[1360,128]{1,0:T(8,128)(2,1)S(1)}, u32[]{:S(2)}, u32[]{:S(2)}) collective-permute-start(bf16[1360,128]{1,0:T(8,128)(2,1)S(1)} %get-tuple-element.199.refs_0_), channel_id=1, source_target_pairs={{0,4},{1,5},{2,6},{3,7},{4,0},{5,1},{6,2},{7,3},{8,12},{9,13},{10,... | collective-permute-start | bytes 1044488 | tf_op jit(solution)/shard_map/ppermute | solution.py:730
  127.2 12.5 %collective-permute-start.47 = (bf16[576,128]{1,0:T(8,128)(2,1)S(1)}, bf16[576,128]{1,0:T(8,128)(2,1)S(1)}, u32[]{:S(2)}, u32[]{:S(2)}) collective-permute-start(bf16[576,128]{1,0:T(8,128)(2,1)S(1)} %get-tuple-element.204.refs_0_), channel_id=1, source_target_pairs={{0,8},{1,9},{2,10},{3,11},{4,12},{5,13},{6,14},{7,15},{8,0},{9,1},... | collective-permute-start | bytes 442376 | tf_op jit(solution)/shard_map/ppermute | solution.py:730
  134.5 18.7 %collective-permute-start.53 = (bf16[288,256]{1,0:T(8,128)(2,1)S(1)}, bf16[288,256]{1,0:T(8,128)(2,1)S(1)}, u32[]{:S(2)}, u32[]{:S(2)}) collective-permute-start(bf16[288,256]{1,0:T(8,128)(2,1)S(1)} %get-tuple-element.218), channel_id=1, source_target_pairs={{0,4},{1,5},{2,6},{3,7},{4,0},{5,1},{6,2},{7,3},{8,12},{9,13},{10,... | collective-permute-start | bytes 442376 | tf_op jit(solution)/shard_map/ppermute | solution.py:730
  135.4 17.8 %collective-permute-start.52 = (bf16[288,256]{1,0:T(8,128)(2,1)S(1)}, bf16[288,256]{1,0:T(8,128)(2,1)S(1)}, u32[]{:S(2)}, u32[]{:S(2)}) collective-permute-start(bf16[288,256]{1,0:T(8,128)(2,1)S(1)} %get-tuple-element.208.refs_0_), channel_id=1, source_target_pairs={{0,16},{1,17},{2,18},{3,19},{4,20},{5,21},{6,22},{7,23},{8,24},{9,... | collective-permute-start | bytes 442376 | tf_op jit(solution)/shard_map/ppermute | solution.py:730
  135.6 12.3 %collective-permute-start.50 = (bf16[688,128]{1,0:T(8,128)(2,1)S(1)}, bf16[688,128]{1,0:T(8,128)(2,1)S(1)}, u32[]{:S(2)}, u32[]{:S(2)}) collective-permute-start(bf16[688,128]{1,0:T(8,128)(2,1)S(1)} %get-tuple-element.210.refs_0_), channel_id=1, source_target_pairs={{0,8},{1,9},{2,10},{3,11},{4,12},{5,13},{6,14},{7,15},{8,0},{9,1},... | collective-permute-start | bytes 528392 | tf_op jit(solution)/shard_map/ppermute | solution.py:730
  139.7 9.1 %collective-permute-start.48 = (bf16[288,128]{1,0:T(8,128)(2,1)S(1)}, bf16[288,128]{1,0:T(8,128)(2,1)S(1)}, u32[]{:S(2)}, u32[]{:S(2)}) collective-permute-start(bf16[288,128]{1,0:T(8,128)(2,1)S(1)} %get-tuple-element.212.refs_0_), channel_id=1, source_target_pairs={{0,16},{1,17},{2,18},{3,19},{4,20},{5,21},{6,22},{7,23},{8,24},{9,... | collective-permute-start | bytes 221192 | tf_op jit(solution)/shard_map/ppermute | solution.py:730
  139.9 12.0 %collective-permute-start.49 = (bf16[256,768]{1,0:T(8,128)(2,1)S(1)}, bf16[256,768]{1,0:T(8,128)(2,1)S(1)}, u32[]{:S(2)}, u32[]{:S(2)}) collective-permute-start(bf16[256,768]{1,0:T(8,128)(2,1)S(1)} %fusion.3), channel_id=1, source_target_pairs={{0,2},{1,3},{2,0},{3,1},{4,6},{5,7},{6,4},{7,5},{8,10},{9,11},{10,... | collective-permute-start | bytes 1179656 | tf_op jit(solution)/shard_map/ppermute | solution.py:730
  147.9 12.0 %collective-permute-start.42 = (bf16[256,768]{1,0:T(8,128)(2,1)S(1)}, bf16[256,768]{1,0:T(8,128)(2,1)S(1)}, u32[]{:S(2)}, u32[]{:S(2)}) collective-permute-start(bf16[256,768]{1,0:T(8,128)(2,1)S(1)} %fusion.4), channel_id=1, source_target_pairs={{0,2},{1,3},{2,0},{3,1},{4,6},{5,7},{6,4},{7,5},{8,10},{9,11},{10,... | collective-permute-start | bytes 1179656 | tf_op jit(solution)/shard_map/ppermute | solution.py:730
  (38 other events, 236.2 us)

commit v4 on v3

--- a/solution.py
+++ b/solution.py
@@ -490,27 +490,35 @@
             ref[half : half + 16] = split(tail_of(keep, n * chunk) + tail_of(got, n * chunk))
 
 
-def back_kernel(ka, ga, kb, gb, yk, yg, ya, zk, zg, za, dwo, dwd, b0, b1, b2, b3, total, ffn):
+def first_back_kernel(ka, ga, yk, yg, ya, zk, zg, za, dwd, b0, b1, b2, b3, total, ffn):
     j = lax.axis_index("blk")
     ffn[0:288] = yk[0].astype(F32) + yg[0].astype(F32) + ya[...].astype(F32)
     ffn[288:576] = zk[0].astype(F32) + zg[0].astype(F32) + za[...].astype(F32)
     for m in range(3):
         dwd[:, 256 * m : 256 * m + 256] = ffn[384 + 64 * m : 448 + 64 * m]
-    total[0:FIRST] = ka[...].astype(F32) + ga[...].astype(F32)
-    total[FIRST : FIRST + SECOND] = kb[0:SECOND].astype(F32) + gb[0:SECOND].astype(F32)
-    parts = split(tail_of(kb, SECOND) + tail_of(gb, SECOND)).astype(F32)
-    parts = jnp.concatenate([parts, jnp.zeros((8, 128), F32)], axis=0).astype(BF16)
-    for t in range(6):
-        at = 480 + 24 * t
-        dwo[:, 128 * t : 128 * t + 128] = total[at : at + 24]
+    total[...] = ka[...].astype(F32) + ga[...].astype(F32)
     for k, ref in enumerate((b0, b1, b2, b3)):
-        for t in range(5):
+        for t in range(3):
             part = total[pl.ds(pl.multiple_of(96 * t + 24 * (j ^ k), 8), 24)]
             ref[:, 128 * t : 128 * t + 128] = part.astype(BF16)
         for m in range(4):
             part = ffn[pl.ds(pl.multiple_of(96 * m + 24 * (j ^ k), 8), 24)]
-            ref[:, 640 + 256 * m : 896 + 256 * m] = part.astype(BF16)
-        ref[:, 1664:1792] = parts
+            ref[:, 384 + 256 * m : 640 + 256 * m] = part.astype(BF16)
+
+
+def second_back_kernel(kb, gb, dwo, b0, b1, b2, b3, total):
+    j = lax.axis_index("blk")
+    total[...] = kb[0:SECOND].astype(F32) + gb[0:SECOND].astype(F32)
+    parts = split(tail_of(kb, SECOND) + tail_of(gb, SECOND)).astype(F32)
+    parts = jnp.concatenate([parts, jnp.zeros((8, 128), F32)], axis=0).astype(BF16)
+    for t in range(6):
+        at = 192 + 24 * t
+        dwo[:, 128 * t : 128 * t + 128] = total[at : at + 24]
+    for k, ref in enumerate((b0, b1, b2, b3)):
+        for t in range(2):
+            part = total[pl.ds(pl.multiple_of(96 * t + 24 * (j ^ k), 8), 24)]
+            ref[:, 128 * t : 128 * t + 128] = part.astype(BF16)
+        ref[:, 256:384] = parts
 
 
 def attn_bwd_kernel(second, *refs):
@@ -655,26 +663,44 @@
     ref[...] = jnp.sum(jnp.where(eye, wide, 0.0), axis=0, keepdims=True)[:, 0:rows]
 
 
-def final_kernel(
-    b0, b1, b2, b3, gains, wq, wk, wv, wg, wu, dq, dk, dv, dg, du, gg1, gg2, table, src
+def first_final_kernel(b0, b1, b2, b3, gains, wg, wu, dg, du, gg2, src):
+    j_me = lax.axis_index("blk")
+    low = low_half(wg.shape[0])
+    for k, ref in enumerate((b0, b1, b2, b3)):
+        src[j_me ^ k] = ref[:, 384:1408].astype(F32)
+    gain_grad = 0.0
+    for n, (w, out) in enumerate(((wg, dg), (wu, du))):
+        parts = [None] * 16
+        for t in range(4):
+            at = slice(512 * n + 128 * t, 512 * n + 128 * t + 128)
+            for half in range(2):
+                a, b = src[2 * half, :, at], src[2 * half + 1, :, at]
+                parts[4 * t + half] = jnp.where(low, a, pltpu.roll(b, 64, 1))
+                parts[4 * t + 2 + half] = jnp.where(low, pltpu.roll(a, 64, 1), b)
+        gain_grad = gain_grad + finish(parts, w, out, gains[1])
+    put_row(gg2, gain_grad)
+
+
+def second_final_kernel(
+    a0, a1, a2, a3, b0, b1, b2, b3, gains, wq, wk, wv, dq, dk, dv, gg1, table, src
 ):
     j_me = lax.axis_index("blk")
-    rows = wq.shape[0]
-    low = low_half(rows)
+    low = low_half(wq.shape[0])
     heads = jnp.zeros((128, 128), F32)
     head_id = lax.broadcasted_iota(jnp.int32, (128, 128), 0)
-    for k, ref in enumerate((b0, b1, b2, b3)):
-        src[j_me ^ k] = ref[:, 0:1664].astype(F32)
-        parts = ref[:, 1664:1792].astype(F32)
+    for k, (first, second) in enumerate(zip((a0, a1, a2, a3), (b0, b1, b2, b3))):
+        src[j_me ^ k, :, 0:384] = first[:, 0:384].astype(F32)
+        src[j_me ^ k, :, 384:640] = second[:, 0:256].astype(F32)
+        parts = second[:, 256:384].astype(F32)
         for h in range(HT):
             row = parts[h : h + 1] + parts[8 + h : 9 + h]
             heads = jnp.where(head_id == HT * (j_me ^ k) + h, row, heads)
     table[...] = heads[0:H, 0:NB]
 
     def one(j, n):
-        return src[j, 0:rows, 128 * n : 128 * n + 128]
-
-    gain_grad = jnp.zeros((rows, 128), F32)
+        return src[j, :, 128 * n : 128 * n + 128]
+
+    gain_grad = 0.0
     for n, (w, out) in enumerate(((wq, dq), (wk, dk), (wv, dv))):
         parts = []
         for j in range(0, TP, 2):
@@ -690,20 +716,10 @@
             ]
         gain_grad = gain_grad + finish(parts, w, out, gains[0])
     put_row(gg1, gain_grad)
-    gain_grad = jnp.zeros((rows, 128), F32)
-    for n, (w, out) in enumerate(((wg, dg), (wu, du))):
-        parts = [None] * 16
-        for t in range(4):
-            at = 5 + 4 * n + t
-            for half in range(2):
-                a, b = one(2 * half, at), one(2 * half + 1, at)
-                parts[4 * t + half] = jnp.where(low, a, pltpu.roll(b, 64, 1))
-                parts[4 * t + 2 + half] = jnp.where(low, pltpu.roll(a, 64, 1), b)
-        gain_grad = gain_grad + finish(parts, w, out, gains[1])
-    put_row(gg2, gain_grad)
-
-
-def close_kernel(keep, got, along, mixed_grad, tok, gains, tokens_grad):
+
+
+def close_kernel(keep, got, along, mixed_grad, tok, gains, tokens_grad, mark):
+    mark[...] = jnp.zeros((8, 128), F32)
     x = tok[lax.axis_index("blk")].astype(F32)
     rstd = lax.rsqrt(jnp.mean(x * x, axis=-1, keepdims=True) + EPSILON)
     n = x * rstd
@@ -713,7 +729,7 @@
 
 
 AXES = ("dp", "blk")
-COST = {"qkv": 0, "attn_fwd": (0, 0, 0), "units": 15, "ffn": 0, "ffn_dw": 0, "mid": 20, "attn_bwd": (0, 10), "one_grad": 40, "stage_y": 10, "stage_z": 10}
+COST = {"qkv": 0, "attn_fwd": (0, 0, 0), "units": 15, "ffn": 0, "ffn_dw": 0, "mid": 0, "attn_bwd": (0, 10), "one_grad": 40, "stage_y": 0, "stage_z": 10, "first_back": 0}
 
 
 def group_local(
@@ -786,7 +802,6 @@
     toks_r = swap(later(toks_x, *first_two), 1)
     firsts = gathered(first, first_one, first_two, *())
     toks = (tok_seg, toks_c, toks_x, toks_r)
-    cots_x = swap(later(cot_own, *first_one), 2)
     second_one = (
         swap(later(second, *first_one), 16),
         swap(later(second, *first_two), 8),
@@ -810,6 +825,7 @@
         out_weight_kernel, sds((D, D), BF16), *stripes, name="out_weight",
         scratch=(pltpu.VMEM((D, D), F32),),
     )
+    cots_x = swap(later(cot_own, *(gains,)), 2)
     heads = []
     for h in range(HT):
         heads.append(
@@ -817,7 +833,7 @@
                 functools.partial(attn_fwd_kernel, h),
                 (sds((TP, TP, T, T), BF16), sds((TP, 1, T), F32), sds((DH, flat), F32)),
                 table, bias, qkv, segq, segk, smem=(0,), name="attn_fwd", vmem=14,
-                cost=COST["attn_fwd"][h], after=(heads[-1][1],) if heads else (cots_x,),
+                cost=COST["attn_fwd"][h], after=((heads[-1][1],) if heads else ()) + ((cots_x,) if h == 2 else ()),
                 scratch=(
                     pltpu.VMEM((TP, 128, T), BF16),
                     pltpu.VMEM((DH, flat), BF16),
@@ -869,10 +885,11 @@
         after=(y_give,), scratch=(pltpu.VMEM((D, D), F32),), cost=COST["mid"],
     )
     g1, g2, g3 = swap(g1, 1), swap(g2, 2), swap(g3, 3)
-    lo_c = swap(later(lo_give, mixed_grad), 1)
+    wo_got = (swap(wo_gives[0], 1), swap(wo_gives[1], 1))
+    lo_c = swap(later(lo_give, *()), 1)
     lo_sum = lo_keep[1] + lo_c[1]
-    wo_got = (swap(wo_gives[0], 1), swap(wo_gives[1], 1))
-    wo_along = swap(later(wo_keep[1] + wo_got[1], g1, g2, g3), 2)
+    wo_sum = later(wo_keep[1] + wo_got[1], g1, g2, g3)
+    wo_along = swap(wo_sum, 2)
 
     def attn_bwd(second, *after):
         mine = slice(2, 3) if second else slice(0, 2)
@@ -906,7 +923,7 @@
             name=name, after=after, cost=COST[name],
         )
 
-    da, ta = attn_bwd(0)
+    da, ta = attn_bwd(0, *(wo_sum,))
     a_keep, a_give = call(
         first_dw_kernel, (chunks(4, FIRST),) * 2, n1.reshape(flat, D), da.reshape(flat, 384),
         name="first_dw", vmem=12, scratch=(pltpu.VMEM((D, 384), F32),),
@@ -917,7 +934,7 @@
         name="ffn_second", after=(a_give,),
     )
     y_got, z_got = swap(y_give, 8), swap(z_give, 16)
-    db, tb = attn_bwd(1, y_give, *())
+    db, tb = attn_bwd(1, y_give, *(lo_sum,))
     b_keep, b_give = call(
         second_dw_kernel, (chunks(4, SECOND),) * 2,
         n1.reshape(flat, D), db.reshape(flat, 256), wo_keep, wo_got[0], wo_along, ta, tb,
@@ -931,7 +948,9 @@
         one_grad_kernel, (sds((2, T, D), BF16),) * 2, da, db, w_qkv, name="one_grad", vmem=16,
         after=(b_give,), cost=COST["one_grad"],
     )
-    one_c, one_x = reduce_pair(one_keep, one_give)
+    lo_x = swap(later(lo_sum, *()), 2)
+    one_c = swap(one_give, 1)
+    one_x = swap(later(one_keep[1] + one_c[1], *(lo_x,)), 2)
     a_keep, a_give = stage(4, FIRST, a_keep, a_got, "stage_y", b_give)
     a_got = swap(a_give, 8)
     y_give, z_give = call(
@@ -945,29 +964,34 @@
     a_got = swap(a_give, 16)
     b_keep, b_give = stage(2, SECOND, b_keep, b_got, "stage_z", *(a_give,))
     b_got = swap(b_give, 16)
-    lo_x = swap(later(lo_sum, one_c), 2)
     layer_out = mixed_own + lo_keep[0].astype(F32) + lo_c[0].astype(F32) + lo_x.astype(F32)
-    tokens_grad = call(
-        close_kernel, sds((T, D), F32), one_keep, one_c, one_x, mixed_grad, tok, gains,
+    tokens_grad, mark = call(
+        close_kernel, (sds((T, D), F32), sds((8, 128), F32)), one_keep, one_c, one_x, mixed_grad, tok, gains,
         name="close", vmem=10, after=(a_got,),
     )
-    dwo, dwd, *backs = call(
-        back_kernel,
-        (sds((rows, D), F32), sds((64, D), F32)) + (sds((rows, 1792), BF16),) * 4,
-        a_keep, a_got, b_keep, b_got, y_keep, y_got, y_along, z_keep, z_got, z_along,
-        name="back", after=(tokens_grad,),
-        scratch=(pltpu.VMEM((FIRST + SECOND, 128), F32), pltpu.VMEM((576, 256), F32)),
-    )
-    backs = (backs[0], swap(backs[1], 1), swap(backs[2], 2), swap(backs[3], 3))
-    dq, dk, dv, dg, du, gg1, gg2, table_sum = call(
-        final_kernel,
-        (sds((rows, D), F32),) * 3
-        + (sds((rows, ff), F32),) * 2
-        + (sds((1, rows), F32), sds((1, rows), F32), sds((H, NB), F32)),
-        *backs, gain_cols, w_query, w_key, w_value, w_gate, w_up, name="final",
-        scratch=(pltpu.VMEM((TP, rows, 1664), F32),),
-    )
-
+    dwd, *backs = call(
+        first_back_kernel, (sds((64, D), F32),) + (sds((rows, 1408), BF16),) * 4,
+        a_keep, a_got, y_keep, y_got, y_along, z_keep, z_got, z_along,
+        name="first_back", after=(b_give,), cost=COST["first_back"],
+        scratch=(pltpu.VMEM((FIRST, 128), F32), pltpu.VMEM((576, 256), F32)),
+    )
+    firsts = (backs[0], swap(backs[1], 1), swap(backs[2], 2), swap(backs[3], 3))
+    dwo, *backs = call(
+        second_back_kernel, (sds((rows, D), F32),) + (sds((rows, 384), BF16),) * 4, b_keep, b_got,
+        name="second_back", after=(mark, *firsts[1:]), scratch=(pltpu.VMEM((SECOND, 128), F32),),
+    )
+    seconds = (backs[0], swap(backs[1], 1), swap(backs[2], 2), swap(backs[3], 3))
+    dg, du, gg2 = call(
+        first_final_kernel, (sds((rows, ff), F32),) * 2 + (sds((1, rows), F32),),
+        *firsts, gain_cols, w_gate, w_up, name="first_final",
+        scratch=(pltpu.VMEM((TP, rows, 1024), F32),),
+    )
+    dq, dk, dv, gg1, table_sum = call(
+        second_final_kernel,
+        (sds((rows, D), F32),) * 3 + (sds((1, rows), F32), sds((H, NB), F32)),
+        *firsts, *seconds, gain_cols, w_query, w_key, w_value, name="second_final", after=(gg2,),
+        scratch=(pltpu.VMEM((TP, rows, 640), F32),),
+    )
     return (
         layer_out.astype(BF16)[None],
         tokens_grad[None],

time: 169 us -> 164 us (0.970)
  waiting for transfers between devices: 51.9 us -> 40.9 us
  starting transfers between devices: 53.6 us -> 58.8 us
    ppermute x57 -> x60, waiting for transfers between devices: 51.9 us -> 40.9 us  [swap(): return lax.ppermute(x, AXES, [(d, d ^ mask) for d in range(n_dev)])]
    ppermute x57 -> x60, starting transfers between devices: 53.6 us -> 58.8 us  [swap(): return lax.ppermute(x, AXES, [(d, d ^ mask) for d in range(n_dev)])]
    pallas_call x30 -> x32, Pallas kernels: 55.4 us -> 56.4 us  [call(): pl.pallas_call(body, out_shape=out_shape, in_specs=[aspec] * skip + specs...]
  transfers between devices with their start and end apart: 57 -> 60, of which waited for: 23 -> 24; matrix products, arithmetic and copies ran while one was open for 1% -> 1% of each run, Pallas kernels for 28% -> 29%
where the time goes in v4:
time: 164 us; the launch traced here: 161 us
  starting transfers between devices  58.8 us (36%)
  Pallas kernels  56.4 us (34%)
  waiting for transfers between devices  40.9 us (25%)
  other arithmetic  1.9 us (1%)
    ppermute x60, starting transfers between devices, swap(): return lax.ppermute(x, AXES, [(d, d ^ mask) for d in range(n_dev)])  58.8 us
    pallas_call x32, Pallas kernels, call(): pl.pallas_call(body, out_shape=out_shape, in_specs=[aspec] * skip + specs...  56.4 us
    ppermute x60, waiting for transfers between devices, swap(): return lax.ppermute(x, AXES, [(d, d ^ mask) for d in range(n_dev)])  40.9 us
  transfers between devices with their start and end apart: 60, of which 24 were waited for; matrix products, arithmetic and copies ran while one was open for 1% of the time, Pallas kernels for 29%

profile of v4, /device:TPU:0, one launch (start us, length us, event | category | flops | bytes accessed | tf_op | source)
XLA Modules:
  0.0 160.9 jit_solution(15426388476461997892)
XLA Ops:
  0.6 3.0 %prep.1 = (bf16[24,1664]{1,0:T(8,128)(2,1)}, bf16[24,1664]{1,0:T(8,128)(2,1)}, bf16[24,1664]{1,0:T(8,128)(2,1)}, bf16[24,1664]{1,0:T(8,128)(2,1)}, bf16[272,768]{1,0:T(8,128)(2,1)}, /*index=5*/f32[2,24,128]{2,1,0:T(8,128)}) custom-call(bf16[24,768]{1,0:T(8,128)(2,1)} %refs_10_.1, bf16[24,768]{1,0:T(8,128)(2,1)} %refs_11_.1, bf16[24,768]{1,0:T(8,128)(2,1)} %refs_12_.1, ...), custom_call_target="tpu_custom_call" | custom-call | tf_op jit(solution)/shard_map/prep/pallas_call | solution.py:59
  4.1 2.6 %collective-permute-start.1 = (bf16[24,1664]{1,0:T(8,128)(2,1)}, bf16[24,1664]{1,0:T(8,128)(2,1)S(1)}, u32[]{:S(2)}, u32[]{:S(2)}) collective-permute-start(bf16[24,1664]{1,0:T(8,128)(2,1)} %get-tuple-element.130), channel_id=1, source_target_pairs={{0,2},{1,3},{2,0},{3,1},{4,6},{5,7},{6,4},{7,5},{8,10},{9,11},{10,... | collective-permute-start | bytes 239624 | tf_op jit(solution)/shard_map/ppermute | solution.py:746
  12.1 2.4 %pack.1.refs_0_.refs_4_.refs_1_ = bf16[128,640]{1,0:T(8,128)(2,1)} custom-call(bf16[24,1664]{1,0:T(8,128)(2,1)} %get-tuple-element.128.refs_0_.refs_1_, bf16[24,1664]{1,0:T(8,128)(2,1)} %copy-done.10, bf16[24,1664]{1,0:T(8,128)(2,1)} %copy-done.11, bf16[24,1664]{1,0:T(8,128)(2,1)} %copy-done.12, bf16[24,768]{1,0:T(8,128)(2,1)} %refs_4_.3), custom_call_target="tpu_custom_call" | custom-call | tf_op jit(solution)/shard_map/pack/pallas_call | solution.py:59
  17.9 2.6 %collective-permute-start.5 = (bf16[128,640]{1,0:T(8,128)(2,1)}, bf16[128,640]{1,0:T(8,128)(2,1)S(1)}, u32[]{:S(2)}, u32[]{:S(2)}) collective-permute-start(bf16[128,640]{1,0:T(8,128)(2,1)} %pack.1.refs_0_.refs_4_.refs_1_), channel_id=1, source_target_pairs={{0,16},{1,17},{2,18},{3,19},{4,20},{5,21},{6,22},{7,23},{8,24},{9,... | collective-permute-start | bytes 491528 | tf_op jit(solution)/shard_map/ppermute | solution.py:746
  21.1 2.7 %pack_more.1.refs_0_ = bf16[576,256]{1,0:T(8,128)(2,1)} custom-call(bf16[128,640]{1,0:T(8,128)(2,1)} %pack.1.refs_0_.refs_4_.refs_1_, bf16[24,1664]{1,0:T(8,128)(2,1)} %get-tuple-element.128.refs_0_.refs_1_, bf16[24,1664]{1,0:T(8,128)(2,1)} %copy-done.10, bf16[24,1664]{1,0:T(8,128)(2,1)} %copy-done.11, bf16[24,1664]{1,0:T(8,128)(2,1)} %copy-done.12, ...), custom_call_target="tpu_custom_call" | custom-call | tf_op jit(solution)/shard_map/pack_more/pallas_call | solution.py:59
  26.1 2.4 %collective-permute-done.5.refs_6_.refs_3_ = bf16[128,640]{1,0:T(8,128)(2,1)S(1)} collective-permute-done((bf16[128,640]{1,0:T(8,128)(2,1)}, bf16[128,640]{1,0:T(8,128)(2,1)S(1)}, u32[]{:S(2)}, u32[]{:S(2)}) %collective-permute-start.5) | collective-permute-done | bytes 163872 | tf_op jit(solution)/shard_map/ppermute | solution.py:746
  30.9 2.9 %collective-permute-done.9.refs_9_.refs_6_ = bf16[128,640]{1,0:T(8,128)(2,1)S(1)} collective-permute-done((bf16[128,640]{1,0:T(8,128)(2,1)S(1)}, bf16[128,640]{1,0:T(8,128)(2,1)S(1)}, u32[]{:S(2)}, u32[]{:S(2)}) %collective-permute-start.9) | collective-permute-done | bytes 163872 | tf_op jit(solution)/shard_map/ppermute | solution.py:746
  36.3 1.8 %collective-permute-start.21 = (bf16[576,256]{1,0:T(8,128)(2,1)}, bf16[576,256]{1,0:T(8,128)(2,1)S(1)}, u32[]{:S(2)}, u32[]{:S(2)}) collective-permute-start(bf16[576,256]{1,0:T(8,128)(2,1)} %pack_more.1.refs_0_), channel_id=1, source_target_pairs={{0,16},{1,17},{2,18},{3,19},{4,20},{5,21},{6,22},{7,23},{8,24},{9,... | collective-permute-start | bytes 884744 | tf_op jit(solution)/shard_map/ppermute | solution.py:746
  39.7 2.5 %collective-permute-start.20 = (bf16[576,256]{1,0:T(8,128)(2,1)}, bf16[576,256]{1,0:T(8,128)(2,1)S(1)}, u32[]{:S(2)}, u32[]{:S(2)}) collective-permute-start(bf16[576,256]{1,0:T(8,128)(2,1)} %pack_more.1.refs_0_), channel_id=1, source_target_pairs={{0,8},{1,9},{2,10},{3,11},{4,12},{5,13},{6,14},{7,15},{8,0},{9,1},... | collective-permute-start | bytes 884744 | tf_op jit(solution)/shard_map/ppermute | solution.py:746
  42.8 2.8 %qkv.1 = (bf16[4,256,768]{2,1,0:T(8,128)(2,1)S(1)}, bf16[4,256,768]{2,1,0:T(8,128)(2,1)S(1)}, bf16[5,4,256,128]{3,2,1,0:T(8,128)(2,1)S(1)}, bf16[768,640]{1,0:T(...) custom-call(bf16[272,768]{1,0:T(8,128)(2,1)S(1)} %copy-done.2, ...), custom_call_target="tpu_custom_call" | custom-call | tf_op jit(solution)/shard_map/qkv/pallas_call | solution.py:59
  47.9 3.3 %attn_fwd.3 = (bf16[4,4,256,256]{3,2,1,0:T(8,128)(2,1)S(1)}, f32[4,1,256]{2,1,0:T(1,128)S(1)}, f32[64,1024]{1,0:T(8,128)S(1)}) custom-call(f32[12,32]{1,0:T(8,128)S(1)} %convert_bitcast_fusion.refs_1_.refs_0_.refs_2_, f32[3,3,256,256]{3,2,1,0:T(8,128)S(1)} %bias.1.refs_1_.refs_2_.refs_3_, ...), custom_call_target="tpu_custom_call" | custom-call | tf_op jit(solution)/shard_map/attn_fwd/pallas_call | solution.py:59
  56.1 3.3 %attn_fwd.4 = (bf16[4,4,256,256]{3,2,1,0:T(8,128)(2,1)S(1)}, f32[4,1,256]{2,1,0:T(1,128)S(1)}, f32[64,1024]{1,0:T(8,128)S(1)}) custom-call(f32[4,1,256]{2,1,0:T(1,128)S(1)} %get-tuple-element.146.refs_0_.refs_4_, f32[12,32]{1,0:T(8,128)S(1)} %convert_bitcast_fusion.refs_1_.refs_0_.refs_2_, f32[3,3,256,256]{3,2,1,0:T(8,128)S(1)} %bias.1.refs_1_.refs_2_.refs_3_, ...), custom_call_target="tpu_custom_call" | custom-call | tf_op jit(solution)/shard_map/attn_fwd/pallas_call | solution.py:59
  59.4 3.4 %attn_fwd.5 = (bf16[4,4,256,256]{3,2,1,0:T(8,128)(2,1)S(1)}, f32[4,1,256]{2,1,0:T(1,128)S(1)}, f32[64,1024]{1,0:T(8,128)S(1)}) custom-call(f32[4,1,256]{2,1,0:T(1,128)S(1)} %get-tuple-element.148.refs_0_.refs_5_, bf16[256,768]{1,0:T(8,128)(2,1)S(1)} %collective-permute-done.13.refs_1_.refs_9_.refs_8_, ...), custom_call_target="tpu_custom_call" | custom-call | tf_op jit(solution)/shard_map/attn_fwd/pallas_call | solution.py:59
  63.0 1.9 %collective-permute-start.15 = (bf16[1536,128]{1,0:T(8,128)(2,1)S(1)}, bf16[1536,128]{1,0:T(8,128)(2,1)S(1)}, u32[]{:S(2)}, u32[]{:S(2)}) collective-permute-start(bf16[1536,128]{1,0:T(8,128)(2,1)S(1)} %join.1.refs_0_.refs_1_), channel_id=1, source_target_pairs={{0,2},{1,3},{2,0},{3,1},{4,6},{5,7},{6,4},{7,5},{8,10},{9,11},{10,... | collective-permute-start | bytes 1179656 | tf_op jit(solution)/shard_map/ppermute | solution.py:746
  65.4 2.2 %collective-permute-done.25.refs_6_ = bf16[576,256]{1,0:T(8,128)(2,1)S(1)} collective-permute-done((bf16[576,256]{1,0:T(8,128)(2,1)S(1)}, bf16[576,256]{1,0:T(8,128)(2,1)S(1)}, u32[]{:S(2)}, u32[]{:S(2)}) %collective-permute-start.25) | collective-permute-done | bytes 294944 | tf_op jit(solution)/shard_map/ppermute | solution.py:746
  69.9 2.7 %collective-permute-done.15.refs_2_.refs_3_ = bf16[1536,128]{1,0:T(8,128)(2,1)S(1)} collective-permute-done((bf16[1536,128]{1,0:T(8,128)(2,1)S(1)}, bf16[1536,128]{1,0:T(8,128)(2,1)S(1)}, u32[]{:S(2)}, u32[]{:S(2)}) %collective-permute-start.15) | collective-permute-done | bytes 393248 | tf_op jit(solution)/shard_map/ppermute | solution.py:746
  72.6 2.0 %collective-permute-done.26.refs_7_ = bf16[576,256]{1,0:T(8,128)(2,1)S(1)} collective-permute-done((bf16[576,256]{1,0:T(8,128)(2,1)S(1)}, bf16[576,256]{1,0:T(8,128)(2,1)S(1)}, u32[]{:S(2)}, u32[]{:S(2)}) %collective-permute-start.26) | collective-permute-done | bytes 294944 | tf_op jit(solution)/shard_map/ppermute | solution.py:746
  75.8 4.8 %ffn.2 = (bf16[2,256,768]{2,1,0:T(8,128)(2,1)S(1)}, bf16[2,256,512]{2,1,0:T(8,128)(2,1)S(1)}, bf16[2,256,1024]{2,1,0:T(8,128)(2,1)S(1)}, bf16[256,768]{1,0:T(8,1...) custom-call(bf16[1536,128]{1,0:T(8,128)(2,1)S(1)} %join.1.refs_0_.refs_1_, ...), custom_call_target="tpu_custom_call" | custom-call | tf_op jit(solution)/shard_map/ffn/pallas_call | solution.py:59
  84.3 4.2 %ffn.3 = (bf16[2,256,768]{2,1,0:T(8,128)(2,1)S(1)}, bf16[2,256,512]{2,1,0:T(8,128)(2,1)S(1)}, bf16[2,256,1024]{2,1,0:T(8,128)(2,1)S(1)}, bf16[256,768]{1,0:T(8,1...) custom-call(bf16[256,768]{1,0:T(8,128)(2,1)S(1)} %add.26.refs_0_, ...), custom_call_target="tpu_custom_call" | custom-call | tf_op jit(solution)/shard_map/ffn/pallas_call | solution.py:59
  88.6 3.8 %ffn_dw.1 = (bf16[4,288,256]{2,1,0:T(8,128)(2,1)S(1)}, bf16[4,288,256]{2,1,0:T(8,128)(2,1)S(1)}, bf16[4,288,256]{2,1,0:T(8,128)(2,1)S(1)}, bf16[4,288,256]{2,1,0...) custom-call(bf16[512,768]{1,0:T(8,128)(2,1)S(1)} %bitcast.42, ...), custom_call_target="tpu_custom_call" | custom-call | tf_op jit(solution)/shard_map/ffn_dw/pallas_call | solution.py:59
  100.5 4.1 %collective-permute-done.36.refs_10_.refs_8_ = bf16[384,128]{1,0:T(8,128)(2,1)S(1)} collective-permute-done((bf16[384,128]{1,0:T(8,128)(2,1)S(1)}, bf16[384,128]{1,0:T(8,128)(2,1)S(1)}, u32[]{:S(2)}, u32[]{:S(2)}) %collective-permute-start.36) | collective-permute-done | bytes 98336 | tf_op jit(solution)/shard_map/ppermute | solution.py:746
  106.1 5.4 %attn_bwd.2 = (bf16[4,256,384]{2,1,0:T(8,128)(2,1)S(1)}, f32[8,128]{1,0:T(8,128)S(1)}) custom-call(bf16[8,24,768]{2,1,0:T(8,128)(2,1)S(1)} %bitcast_add_fusion.refs_0_, bf16[5,4,256,128]{3,2,1,0:T(8,128)(2,1)S(1)} %get-tuple-element.142.refs_2_.refs_3_.refs_4_.refs_1_, bf16[4,4,256,256]{3,2,1,0:T(8,128)(2,1)S(1)} %get-tuple-element.187.refs_2_, ...), custom_call_target="tpu_custom_call" | custom-call | tf_op jit(solution)/shard_map/attn_bwd/pallas_call | solution.py:59
  113.8 3.1 %collective-permute-start.44 = (bf16[2,288,256]{2,1,0:T(8,128)(2,1)S(1)}, bf16[2,288,256]{2,1,0:T(8,128)(2,1)S(1)}, u32[]{:S(2)}, u32[]{:S(2)}) collective-permute-start(bf16[2,288,256]{2,1,0:T(8,128)(2,1)S(1)} %get-tuple-element.207), channel_id=1, source_target_pairs={{0,16},{1,17},{2,18},{3,19},{4,20},{5,21},{6,22},{7,23},{8,24},{9,... | collective-permute-start | bytes 884744 | tf_op jit(solution)/shard_map/ppermute | solution.py:746
  118.2 2.9 %attn_bwd.3 = (bf16[4,256,256]{2,1,0:T(8,128)(2,1)S(1)}, f32[8,128]{1,0:T(8,128)S(1)}) custom-call(bf16[2,288,256]{2,1,0:T(8,128)(2,1)S(1)} %get-tuple-element.195.refs_0_, bf16[256,768]{1,0:T(8,128)(2,1)S(1)} %fusion.4.refs_1_, bf16[5,4,256,128]{3,2,1,0:T(8,128)(2,1)S(1)} %get-tuple-element.142.refs_2_.refs_3_.refs_4_.refs_1_, ...), custom_call_target="tpu_custom_call" | custom-call | flops 11500000256 | tf_op jit(solution)/shard_map/attn_bwd/pallas_call | solution.py:59
  124.0 2.1 %collective-permute-start.46 = (bf16[576,128]{1,0:T(8,128)(2,1)S(1)}, bf16[576,128]{1,0:T(8,128)(2,1)S(1)}, u32[]{:S(2)}, u32[]{:S(2)}) collective-permute-start(bf16[576,128]{1,0:T(8,128)(2,1)S(1)} %get-tuple-element.204.refs_0_), channel_id=1, source_target_pairs={{0,8},{1,9},{2,10},{3,11},{4,12},{5,13},{6,14},{7,15},{8,0},{9,1},... | collective-permute-start | bytes 442376 | tf_op jit(solution)/shard_map/ppermute | solution.py:746
  126.1 2.2 %one_grad.1 = (bf16[2,256,768]{2,1,0:T(8,128)(2,1)S(1)}, bf16[2,256,768]{2,1,0:T(8,128)(2,1)S(1)}) custom-call(bf16[1360,128]{1,0:T(8,128)(2,1)S(1)} %get-tuple-element.202.refs_0_, bf16[4,256,384]{2,1,0:T(8,128)(2,1)S(1)} %get-tuple-element.190.refs_1_, bf16[4,256,256]{2,1,0:T(8,128)(2,1)S(1)} %get-tuple-element.198.refs_2_, ...), custom_call_target="tpu_custom_call" | custom-call | flops 46000001024 | tf_op jit(solution)/shard_map/one_grad/pallas_call | solution.py:59
  128.3 2.0 %collective-permute-done.44.refs_4_.refs_7_ = bf16[2,288,256]{2,1,0:T(8,128)(2,1)S(1)} collective-permute-done((bf16[2,288,256]{2,1,0:T(8,128)(2,1)S(1)}, bf16[2,288,256]{2,1,0:T(8,128)(2,1)S(1)}, u32[]{:S(2)}, u32[]{:S(2)}) %collective-permute-start.44) | collective-permute-done | bytes 294944 | tf_op jit(solution)/shard_map/ppermute | solution.py:746
  130.7 4.0 %collective-permute-start.52 = (bf16[288,256]{1,0:T(8,128)(2,1)S(1)}, bf16[288,256]{1,0:T(8,128)(2,1)S(1)}, u32[]{:S(2)}, u32[]{:S(2)}) collective-permute-start(bf16[288,256]{1,0:T(8,128)(2,1)S(1)} %get-tuple-element.222), channel_id=1, source_target_pairs={{0,4},{1,5},{2,6},{3,7},{4,0},{5,1},{6,2},{7,3},{8,12},{9,13},{10,... | collective-permute-start | bytes 442376 | tf_op jit(solution)/shard_map/ppermute | solution.py:746
  137.0 2.9 %collective-permute-start.47 = (bf16[288,128]{1,0:T(8,128)(2,1)S(1)}, bf16[288,128]{1,0:T(8,128)(2,1)S(1)}, u32[]{:S(2)}, u32[]{:S(2)}) collective-permute-start(bf16[288,128]{1,0:T(8,128)(2,1)S(1)} %get-tuple-element.212.refs_0_), channel_id=1, source_target_pairs={{0,16},{1,17},{2,18},{3,19},{4,20},{5,21},{6,22},{7,23},{8,24},{9,... | collective-permute-start | bytes 221192 | tf_op jit(solution)/shard_map/ppermute | solution.py:746
  141.3 4.0 %collective-permute-done.50.refs_2_ = bf16[688,128]{1,0:T(8,128)(2,1)S(1)} collective-permute-done((bf16[688,128]{1,0:T(8,128)(2,1)S(1)}, bf16[688,128]{1,0:T(8,128)(2,1)S(1)}, u32[]{:S(2)}, u32[]{:S(2)}) %collective-permute-start.50) | collective-permute-done | bytes 176160 | tf_op jit(solution)/shard_map/ppermute | solution.py:746
  146.4 2.0 %collective-permute-start.54 = (bf16[24,1408]{1,0:T(8,128)(2,1)S(1)}, bf16[24,1408]{1,0:T(8,128)(2,1)S(1)}, u32[]{:S(2)}, u32[]{:S(2)}) collective-permute-start(bf16[24,1408]{1,0:T(8,128)(2,1)S(1)} %get-tuple-element.225), channel_id=1, source_target_pairs={{0,2},{1,3},{2,0},{3,1},{4,6},{5,7},{6,4},{7,5},{8,10},{9,11},{10,... | collective-permute-start | bytes 202760 | tf_op jit(solution)/shard_map/ppermute | solution.py:746
  148.6 3.3 %collective-permute-done.49.refs_3_ = bf16[256,768]{1,0:T(8,128)(2,1)S(1)} collective-permute-done((bf16[256,768]{1,0:T(8,128)(2,1)S(1)}, bf16[256,768]{1,0:T(8,128)(2,1)S(1)}, u32[]{:S(2)}, u32[]{:S(2)}) %collective-permute-start.49) | collective-permute-done | bytes 393248 | tf_op jit(solution)/shard_map/ppermute | solution.py:746
  (152 shorter events, 64.1 us)
Async XLA Ops:
  6.8 29.0 %collective-permute-start.4 = (bf16[272,768]{1,0:T(8,128)(2,1)}, bf16[272,768]{1,0:T(8,128)(2,1)S(1)}, u32[]{:S(2)}, u32[]{:S(2)}) collective-permute-start(bf16[272,768]{1,0:T(8,128)(2,1)} %get-tuple-element.132.refs_0_), channel_id=1, source_target_pairs={{0,2},{1,3},{2,0},{3,1},{4,6},{5,7},{6,4},{7,5},{8,10},{9,11},{10,... | collective-permute-start | bytes 1253384 | tf_op jit(solution)/shard_map/ppermute | solution.py:746
  14.5 10.7 %collective-permute-start.7 = (bf16[128,640]{1,0:T(8,128)(2,1)}, bf16[128,640]{1,0:T(8,128)(2,1)S(1)}, u32[]{:S(2)}, u32[]{:S(2)}) collective-permute-start(bf16[128,640]{1,0:T(8,128)(2,1)} %pack.1.refs_0_.refs_4_.refs_1_), channel_id=1, source_target_pairs={{0,4},{1,5},{2,6},{3,7},{4,0},{5,1},{6,2},{7,3},{8,12},{9,13},{10,... | collective-permute-start | bytes 491528 | tf_op jit(solution)/shard_map/ppermute | solution.py:746
  16.3 9.8 %collective-permute-start.6 = (bf16[128,640]{1,0:T(8,128)(2,1)}, bf16[128,640]{1,0:T(8,128)(2,1)S(1)}, u32[]{:S(2)}, u32[]{:S(2)}) collective-permute-start(bf16[128,640]{1,0:T(8,128)(2,1)} %pack.1.refs_0_.refs_4_.refs_1_), channel_id=1, source_target_pairs={{0,8},{1,9},{2,10},{3,11},{4,12},{5,13},{6,14},{7,15},{8,0},{9,1},... | collective-permute-start | bytes 491528 | tf_op jit(solution)/shard_map/ppermute | solution.py:746
  17.9 10.6 %collective-permute-start.5 = (bf16[128,640]{1,0:T(8,128)(2,1)}, bf16[128,640]{1,0:T(8,128)(2,1)S(1)}, u32[]{:S(2)}, u32[]{:S(2)}) collective-permute-start(bf16[128,640]{1,0:T(8,128)(2,1)} %pack.1.refs_0_.refs_4_.refs_1_), channel_id=1, source_target_pairs={{0,16},{1,17},{2,18},{3,19},{4,20},{5,21},{6,22},{7,23},{8,24},{9,... | collective-permute-start | bytes 491528 | tf_op jit(solution)/shard_map/ppermute | solution.py:746
  30.9 8.8 %collective-permute-start.3 = (bf16[272,768]{1,0:T(8,128)(2,1)S(1)}, bf16[272,768]{1,0:T(8,128)(2,1)S(1)}, u32[]{:S(2)}, u32[]{:S(2)}) collective-permute-start(bf16[272,768]{1,0:T(8,128)(2,1)S(1)} %copy-done.2), channel_id=1, source_target_pairs={{0,1},{1,0},{2,3},{3,2},{4,5},{5,4},{6,7},{7,6},{8,9},{9,8},{10,11... | collective-permute-start | bytes 1253384 | tf_op jit(solution)/shard_map/ppermute | solution.py:746
  36.3 16.7 %collective-permute-start.21 = (bf16[576,256]{1,0:T(8,128)(2,1)}, bf16[576,256]{1,0:T(8,128)(2,1)S(1)}, u32[]{:S(2)}, u32[]{:S(2)}) collective-permute-start(bf16[576,256]{1,0:T(8,128)(2,1)} %pack_more.1.refs_0_), channel_id=1, source_target_pairs={{0,16},{1,17},{2,18},{3,19},{4,20},{5,21},{6,22},{7,23},{8,24},{9,... | collective-permute-start | bytes 884744 | tf_op jit(solution)/shard_map/ppermute | solution.py:746
  38.1 14.8 %collective-permute-start.22 = (bf16[576,256]{1,0:T(8,128)(2,1)}, bf16[576,256]{1,0:T(8,128)(2,1)S(1)}, u32[]{:S(2)}, u32[]{:S(2)}) collective-permute-start(bf16[576,256]{1,0:T(8,128)(2,1)} %pack_more.1.refs_0_), channel_id=1, source_target_pairs={{0,4},{1,5},{2,6},{3,7},{4,0},{5,1},{6,2},{7,3},{8,12},{9,13},{10,... | collective-permute-start | bytes 884744 | tf_op jit(solution)/shard_map/ppermute | solution.py:746
  39.7 14.4 %collective-permute-start.20 = (bf16[576,256]{1,0:T(8,128)(2,1)}, bf16[576,256]{1,0:T(8,128)(2,1)S(1)}, u32[]{:S(2)}, u32[]{:S(2)}) collective-permute-start(bf16[576,256]{1,0:T(8,128)(2,1)} %pack_more.1.refs_0_), channel_id=1, source_target_pairs={{0,8},{1,9},{2,10},{3,11},{4,12},{5,13},{6,14},{7,15},{8,0},{9,1},... | collective-permute-start | bytes 884744 | tf_op jit(solution)/shard_map/ppermute | solution.py:746
  45.7 13.7 %collective-permute-start.13 = (bf16[256,768]{1,0:T(8,128)(2,1)S(1)}, bf16[256,768]{1,0:T(8,128)(2,1)S(1)}, u32[]{:S(2)}, u32[]{:S(2)}) collective-permute-start(bf16[256,768]{1,0:T(8,128)(2,1)S(1)} %bitcast.35), channel_id=1, source_target_pairs={{0,2},{1,3},{2,0},{3,1},{4,6},{5,7},{6,4},{7,5},{8,10},{9,11},{10,... | collective-permute-start | bytes 1179656 | tf_op jit(solution)/shard_map/ppermute | solution.py:746
  47.5 17.4 %collective-permute-start.17 = (bf16[192,768]{1,0:T(8,128)(2,1)S(1)}, bf16[192,768]{1,0:T(8,128)(2,1)S(1)}, u32[]{:S(2)}, u32[]{:S(2)}) collective-permute-start(bf16[192,768]{1,0:T(8,128)(2,1)S(1)} %stripes.1.refs_0_), channel_id=1, source_target_pairs={{0,2},{1,3},{2,0},{3,1},{4,6},{5,7},{6,4},{7,5},{8,10},{9,11},{10,... | collective-permute-start | bytes 884744 | tf_op jit(solution)/shard_map/ppermute | solution.py:746
  54.1 10.8 %collective-permute-start.24 = (bf16[576,256]{1,0:T(8,128)(2,1)S(1)}, bf16[576,256]{1,0:T(8,128)(2,1)S(1)}, u32[]{:S(2)}, u32[]{:S(2)}) collective-permute-start(bf16[576,256]{1,0:T(8,128)(2,1)S(1)} %collective-permute-done.20.refs_1_), channel_id=1, source_target_pairs={{0,4},{1,5},{2,6},{3,7},{4,0},{5,1},{6,2},{7,3},{8,12},{9,13},{10,... | collective-permute-start | bytes 884744 | tf_op jit(solution)/shard_map/ppermute | solution.py:746
  54.6 13.0 %collective-permute-start.25 = (bf16[576,256]{1,0:T(8,128)(2,1)S(1)}, bf16[576,256]{1,0:T(8,128)(2,1)S(1)}, u32[]{:S(2)}, u32[]{:S(2)}) collective-permute-start(bf16[576,256]{1,0:T(8,128)(2,1)S(1)} %collective-permute-done.21.refs_2_), channel_id=1, source_target_pairs={{0,4},{1,5},{2,6},{3,7},{4,0},{5,1},{6,2},{7,3},{8,12},{9,13},{10,... | collective-permute-start | bytes 884744 | tf_op jit(solution)/shard_map/ppermute | solution.py:746
  56.1 11.5 %collective-permute-start.23 = (bf16[576,256]{1,0:T(8,128)(2,1)S(1)}, bf16[576,256]{1,0:T(8,128)(2,1)S(1)}, u32[]{:S(2)}, u32[]{:S(2)}) collective-permute-start(bf16[576,256]{1,0:T(8,128)(2,1)S(1)} %collective-permute-done.21.refs_2_), channel_id=1, source_target_pairs={{0,8},{1,9},{2,10},{3,11},{4,12},{5,13},{6,14},{7,15},{8,0},{9,1},... | collective-permute-start | bytes 884744 | tf_op jit(solution)/shard_map/ppermute | solution.py:746
  63.0 9.7 %collective-permute-start.15 = (bf16[1536,128]{1,0:T(8,128)(2,1)S(1)}, bf16[1536,128]{1,0:T(8,128)(2,1)S(1)}, u32[]{:S(2)}, u32[]{:S(2)}) collective-permute-start(bf16[1536,128]{1,0:T(8,128)(2,1)S(1)} %join.1.refs_0_.refs_1_), channel_id=1, source_target_pairs={{0,2},{1,3},{2,0},{3,1},{4,6},{5,7},{6,4},{7,5},{8,10},{9,11},{10,... | collective-permute-start | bytes 1179656 | tf_op jit(solution)/shard_map/ppermute | solution.py:746
  82.5 13.3 %collective-permute-start.33 = (bf16[256,768]{1,0:T(8,128)(2,1)S(1)}, bf16[256,768]{1,0:T(8,128)(2,1)S(1)}, u32[]{:S(2)}, u32[]{:S(2)}) collective-permute-start(bf16[256,768]{1,0:T(8,128)(2,1)S(1)} %add.26.refs_0_), channel_id=1, source_target_pairs={{0,2},{1,3},{2,0},{3,1},{4,6},{5,7},{6,4},{7,5},{8,10},{9,11},{10,... | collective-permute-start | bytes 1179656 | tf_op jit(solution)/shard_map/ppermute | solution.py:746
  92.3 24.5 %collective-permute-start.30 = (bf16[2,256,768]{2,1,0:T(8,128)(2,1)S(1)}, bf16[2,256,768]{2,1,0:T(8,128)(2,1)S(1)}, u32[]{:S(2)}, u32[]{:S(2)}) collective-permute-start(bf16[2,256,768]{2,1,0:T(8,128)(2,1)S(1)} %get-tuple-element.175), channel_id=1, source_target_pairs={{0,1},{1,0},{2,3},{3,2},{4,5},{5,4},{6,7},{7,6},{8,9},{9,8},{10,11... | collective-permute-start | bytes 2359304 | tf_op jit(solution)/shard_map/ppermute | solution.py:746
  92.9 20.1 %collective-permute-start.39 = (bf16[4,288,256]{2,1,0:T(8,128)(2,1)S(1)}, bf16[4,288,256]{2,1,0:T(8,128)(2,1)S(1)}, u32[]{:S(2)}, u32[]{:S(2)}) collective-permute-start(bf16[4,288,256]{2,1,0:T(8,128)(2,1)S(1)} %get-tuple-element.194), channel_id=1, source_target_pairs={{0,8},{1,9},{2,10},{3,11},{4,12},{5,13},{6,14},{7,15},{8,0},{9,1},... | collective-permute-start | bytes 1769480 | tf_op jit(solution)/shard_map/ppermute | solution.py:746
  94.3 19.2 %collective-permute-start.38 = (bf16[4,288,256]{2,1,0:T(8,128)(2,1)S(1)}, bf16[4,288,256]{2,1,0:T(8,128)(2,1)S(1)}, u32[]{:S(2)}, u32[]{:S(2)}) collective-permute-start(bf16[4,288,256]{2,1,0:T(8,128)(2,1)S(1)} %get-tuple-element.177.refs_0_), channel_id=1, source_target_pairs={{0,4},{1,5},{2,6},{3,7},{4,0},{5,1},{6,2},{7,3},{8,12},{9,13},{10,... | collective-permute-start | bytes 1769480 | tf_op jit(solution)/shard_map/ppermute | solution.py:746
  104.6 16.5 %collective-permute-start.40 = (bf16[8,24,768]{2,1,0:T(8,128)(2,1)S(1)}, bf16[8,24,768]{2,1,0:T(8,128)(2,1)S(1)}, u32[]{:S(2)}, u32[]{:S(2)}) collective-permute-start(bf16[8,24,768]{2,1,0:T(8,128)(2,1)S(1)} %get-tuple-element.199), channel_id=1, source_target_pairs={{0,1},{1,0},{2,3},{3,2},{4,5},{5,4},{6,7},{7,6},{8,9},{9,8},{10,11... | collective-permute-start | bytes 884744 | tf_op jit(solution)/shard_map/ppermute | solution.py:746
  105.1 17.0 %collective-permute-start.41 = (bf16[8,24,768]{2,1,0:T(8,128)(2,1)S(1)}, bf16[8,24,768]{2,1,0:T(8,128)(2,1)S(1)}, u32[]{:S(2)}, u32[]{:S(2)}) collective-permute-start(bf16[8,24,768]{2,1,0:T(8,128)(2,1)S(1)} %bitcast_add_fusion.refs_0_), channel_id=1, source_target_pairs={{0,2},{1,3},{2,0},{3,1},{4,6},{5,7},{6,4},{7,5},{8,10},{9,11},{10,... | collective-permute-start | bytes 884744 | tf_op jit(solution)/shard_map/ppermute | solution.py:746
  113.0 10.9 %collective-permute-start.42 = (bf16[1152,128]{1,0:T(8,128)(2,1)S(1)}, bf16[1152,128]{1,0:T(8,128)(2,1)S(1)}, u32[]{:S(2)}, u32[]{:S(2)}) collective-permute-start(bf16[1152,128]{1,0:T(8,128)(2,1)S(1)} %get-tuple-element.191.refs_0_), channel_id=1, source_target_pairs={{0,4},{1,5},{2,6},{3,7},{4,0},{5,1},{6,2},{7,3},{8,12},{9,13},{10,... | collective-permute-start | bytes 884744 | tf_op jit(solution)/shard_map/ppermute | solution.py:746
  113.8 16.6 %collective-permute-start.44 = (bf16[2,288,256]{2,1,0:T(8,128)(2,1)S(1)}, bf16[2,288,256]{2,1,0:T(8,128)(2,1)S(1)}, u32[]{:S(2)}, u32[]{:S(2)}) collective-permute-start(bf16[2,288,256]{2,1,0:T(8,128)(2,1)S(1)} %get-tuple-element.207), channel_id=1, source_target_pairs={{0,16},{1,17},{2,18},{3,19},{4,20},{5,21},{6,22},{7,23},{8,24},{9,... | collective-permute-start | bytes 884744 | tf_op jit(solution)/shard_map/ppermute | solution.py:746
  116.9 13.8 %collective-permute-start.43 = (bf16[2,288,256]{2,1,0:T(8,128)(2,1)S(1)}, bf16[2,288,256]{2,1,0:T(8,128)(2,1)S(1)}, u32[]{:S(2)}, u32[]{:S(2)}) collective-permute-start(bf16[2,288,256]{2,1,0:T(8,128)(2,1)S(1)} %get-tuple-element.195.refs_0_), channel_id=1, source_target_pairs={{0,8},{1,9},{2,10},{3,11},{4,12},{5,13},{6,14},{7,15},{8,0},{9,1},... | collective-permute-start | bytes 884744 | tf_op jit(solution)/shard_map/ppermute | solution.py:746
  121.1 18.9 %collective-permute-start.31 = (bf16[256,768]{1,0:T(8,128)(2,1)S(1)}, bf16[256,768]{1,0:T(8,128)(2,1)S(1)}, u32[]{:S(2)}, u32[]{:S(2)}) collective-permute-start(bf16[256,768]{1,0:T(8,128)(2,1)S(1)} %fusion.4.refs_1_), channel_id=1, source_target_pairs={{0,2},{1,3},{2,0},{3,1},{4,6},{5,7},{6,4},{7,5},{8,10},{9,11},{10,... | collective-permute-start | bytes 1179656 | tf_op jit(solution)/shard_map/ppermute | solution.py:746
  123.3 11.4 %collective-permute-start.45 = (bf16[1360,128]{1,0:T(8,128)(2,1)S(1)}, bf16[1360,128]{1,0:T(8,128)(2,1)S(1)}, u32[]{:S(2)}, u32[]{:S(2)}) collective-permute-start(bf16[1360,128]{1,0:T(8,128)(2,1)S(1)} %get-tuple-element.202.refs_0_), channel_id=1, source_target_pairs={{0,4},{1,5},{2,6},{3,7},{4,0},{5,1},{6,2},{7,3},{8,12},{9,13},{10,... | collective-permute-start | bytes 1044488 | tf_op jit(solution)/shard_map/ppermute | solution.py:746
  124.0 10.8 %collective-permute-start.46 = (bf16[576,128]{1,0:T(8,128)(2,1)S(1)}, bf16[576,128]{1,0:T(8,128)(2,1)S(1)}, u32[]{:S(2)}, u32[]{:S(2)}) collective-permute-start(bf16[576,128]{1,0:T(8,128)(2,1)S(1)} %get-tuple-element.204.refs_0_), channel_id=1, source_target_pairs={{0,8},{1,9},{2,10},{3,11},{4,12},{5,13},{6,14},{7,15},{8,0},{9,1},... | collective-permute-start | bytes 442376 | tf_op jit(solution)/shard_map/ppermute | solution.py:746
  130.7 14.8 %collective-permute-start.52 = (bf16[288,256]{1,0:T(8,128)(2,1)S(1)}, bf16[288,256]{1,0:T(8,128)(2,1)S(1)}, u32[]{:S(2)}, u32[]{:S(2)}) collective-permute-start(bf16[288,256]{1,0:T(8,128)(2,1)S(1)} %get-tuple-element.222), channel_id=1, source_target_pairs={{0,4},{1,5},{2,6},{3,7},{4,0},{5,1},{6,2},{7,3},{8,12},{9,13},{10,... | collective-permute-start | bytes 442376 | tf_op jit(solution)/shard_map/ppermute | solution.py:746
  134.7 10.9 %collective-permute-start.51 = (bf16[288,256]{1,0:T(8,128)(2,1)S(1)}, bf16[288,256]{1,0:T(8,128)(2,1)S(1)}, u32[]{:S(2)}, u32[]{:S(2)}) collective-permute-start(bf16[288,256]{1,0:T(8,128)(2,1)S(1)} %get-tuple-element.208.refs_0_), channel_id=1, source_target_pairs={{0,16},{1,17},{2,18},{3,19},{4,20},{5,21},{6,22},{7,23},{8,24},{9,... | collective-permute-start | bytes 442376 | tf_op jit(solution)/shard_map/ppermute | solution.py:746
  134.8 10.4 %collective-permute-start.50 = (bf16[688,128]{1,0:T(8,128)(2,1)S(1)}, bf16[688,128]{1,0:T(8,128)(2,1)S(1)}, u32[]{:S(2)}, u32[]{:S(2)}) collective-permute-start(bf16[688,128]{1,0:T(8,128)(2,1)S(1)} %get-tuple-element.210.refs_0_), channel_id=1, source_target_pairs={{0,8},{1,9},{2,10},{3,11},{4,12},{5,13},{6,14},{7,15},{8,0},{9,1},... | collective-permute-start | bytes 528392 | tf_op jit(solution)/shard_map/ppermute | solution.py:746
  137.0 8.6 %collective-permute-start.47 = (bf16[288,128]{1,0:T(8,128)(2,1)S(1)}, bf16[288,128]{1,0:T(8,128)(2,1)S(1)}, u32[]{:S(2)}, u32[]{:S(2)}) collective-permute-start(bf16[288,128]{1,0:T(8,128)(2,1)S(1)} %get-tuple-element.212.refs_0_), channel_id=1, source_target_pairs={{0,16},{1,17},{2,18},{3,19},{4,20},{5,21},{6,22},{7,23},{8,24},{9,... | collective-permute-start | bytes 221192 | tf_op jit(solution)/shard_map/ppermute | solution.py:746
  140.0 11.9 %collective-permute-start.49 = (bf16[256,768]{1,0:T(8,128)(2,1)S(1)}, bf16[256,768]{1,0:T(8,128)(2,1)S(1)}, u32[]{:S(2)}, u32[]{:S(2)}) collective-permute-start(bf16[256,768]{1,0:T(8,128)(2,1)S(1)} %fusion.3), channel_id=1, source_target_pairs={{0,2},{1,3},{2,0},{3,1},{4,6},{5,7},{6,4},{7,5},{8,10},{9,11},{10,... | collective-permute-start | bytes 1179656 | tf_op jit(solution)/shard_map/ppermute | solution.py:746
  145.3 8.0 %collective-permute-start.56 = (bf16[352,128]{1,0:T(8,128)(2,1)S(1)}, bf16[352,128]{1,0:T(8,128)(2,1)S(1)}, u32[]{:S(2)}, u32[]{:S(2)}) collective-permute-start(bf16[352,128]{1,0:T(8,128)(2,1)S(1)} %get-tuple-element.220.refs_0_), channel_id=1, source_target_pairs={{0,16},{1,17},{2,18},{3,19},{4,20},{5,21},{6,22},{7,23},{8,24},{9,... | collective-permute-start | bytes 270344 | tf_op jit(solution)/shard_map/ppermute | solution.py:746
  (41 other events, 224.1 us)

commit v5 on v4

--- a/solution.py
+++ b/solution.py
@@ -663,7 +663,8 @@
     ref[...] = jnp.sum(jnp.where(eye, wide, 0.0), axis=0, keepdims=True)[:, 0:rows]
 
 
-def first_final_kernel(b0, b1, b2, b3, gains, wg, wu, dg, du, gg2, src):
+def first_final_kernel(b0, b1, b2, b3, gains, wg, wu, dg, du, gg2, mark, src):
+    mark[...] = jnp.zeros((8, 128), F32)
     j_me = lax.axis_index("blk")
     low = low_half(wg.shape[0])
     for k, ref in enumerate((b0, b1, b2, b3)):
@@ -785,12 +786,12 @@
     slabs = (slabs[0], swap(slabs[1], 1), swap(slabs[2], 2), swap(slabs[3], 3))
     first = call(
         pack_kernel, sds((128, 640), BF16), *slabs, w_attn_out,
-        name="pack", vmem=60, held=(4,),
+        name="pack", vmem=30, held=(4,),
         scratch=(pltpu.VMEM((96, 640), F32), pltpu.VMEM((rows, D), BF16), pltpu.SemaphoreType.DMA),
     )
     second = call(
         pack_more_kernel, sds((576, 256), BF16), *slabs, w_down,
-        name="pack_more", vmem=60, held=(4,), after=(first,),
+        name="pack_more", vmem=30, held=(4,), after=(first,),
         scratch=(pltpu.VMEM((96, 1024), F32), pltpu.VMEM((64, D), BF16), pltpu.SemaphoreType.DMA),
     )
     first_one = round_one(first)
@@ -842,7 +843,7 @@
             )
         )
     probs, inv_tots, out_ts = zip(*heads)
-    cots = (cot_own, swap(later(cot_own, inv_tots[0]), 1), cots_x, swap(later(cots_x, inv_tots[0]), 1))
+    cots = (cot_own, swap(later(cot_own, inv_tots[2]), 1), cots_x, swap(later(cots_x, inv_tots[2]), 1))
     far, near = lax.optimization_barrier(second_one + (inv_tots[0],))[:2]
     second_two = round_two(far, near)
     seconds = gathered(second, second_one, second_two)
@@ -877,17 +878,17 @@
         scratch=(pltpu.VMEM((D, 1024), F32), pltpu.VMEM((512, D), F32)),
     )
     y_got, z_got = swap(y_give, 4), swap(z_give, 8)
+    lo_c = swap(later(lo_give, *()), 1)
+    lo_sum = lo_keep[1] + lo_c[1]
     mixed_grad, g0, g1, g2, g3, wo_keep, *wo_gives = call(
         mid_kernel,
         (sds((T, D), F32),) + (sds((384, 128), BF16),) * 4
         + (sds((2, 8, 24, D), BF16),) + (sds((8, 24, D), BF16),) * 2,
         two_keep, two_c, two_x, mixed_own, cot_own, attc, wop, gains, name="mid", vmem=16,
-        after=(y_give,), scratch=(pltpu.VMEM((D, D), F32),), cost=COST["mid"],
+        after=(y_give, *()), scratch=(pltpu.VMEM((D, D), F32),), cost=COST["mid"],
     )
     g1, g2, g3 = swap(g1, 1), swap(g2, 2), swap(g3, 3)
     wo_got = (swap(wo_gives[0], 1), swap(wo_gives[1], 1))
-    lo_c = swap(later(lo_give, *()), 1)
-    lo_sum = lo_keep[1] + lo_c[1]
     wo_sum = later(wo_keep[1] + wo_got[1], g1, g2, g3)
     wo_along = swap(wo_sum, 2)
 
@@ -948,7 +949,7 @@
         one_grad_kernel, (sds((2, T, D), BF16),) * 2, da, db, w_qkv, name="one_grad", vmem=16,
         after=(b_give,), cost=COST["one_grad"],
     )
-    lo_x = swap(later(lo_sum, *()), 2)
+    lo_x = swap(later(lo_sum, *(db,)), 2)
     one_c = swap(one_give, 1)
     one_x = swap(later(one_keep[1] + one_c[1], *(lo_x,)), 2)
     a_keep, a_give = stage(4, FIRST, a_keep, a_got, "stage_y", b_give)
@@ -981,15 +982,16 @@
         name="second_back", after=(mark, *firsts[1:]), scratch=(pltpu.VMEM((SECOND, 128), F32),),
     )
     seconds = (backs[0], swap(backs[1], 1), swap(backs[2], 2), swap(backs[3], 3))
-    dg, du, gg2 = call(
-        first_final_kernel, (sds((rows, ff), F32),) * 2 + (sds((1, rows), F32),),
+    dg, du, gg2, mark = call(
+        first_final_kernel,
+        (sds((rows, ff), F32),) * 2 + (sds((1, rows), F32), sds((8, 128), F32)),
         *firsts, gain_cols, w_gate, w_up, name="first_final",
         scratch=(pltpu.VMEM((TP, rows, 1024), F32),),
     )
     dq, dk, dv, gg1, table_sum = call(
         second_final_kernel,
         (sds((rows, D), F32),) * 3 + (sds((1, rows), F32), sds((H, NB), F32)),
-        *firsts, *seconds, gain_cols, w_query, w_key, w_value, name="second_final", after=(gg2,),
+        *firsts, *seconds, gain_cols, w_query, w_key, w_value, name="second_final", after=(mark,),
         scratch=(pltpu.VMEM((TP, rows, 640), F32),),
     )
     return (

time: 164 us -> 161 us (0.982)
  Pallas kernels: 56.4 us -> 50.8 us
    pallas_call x32, Pallas kernels: 56.4 us -> 50.8 us  [call(): pl.pallas_call(body, out_shape=out_shape, in_specs=[aspec] * skip + specs...]
  transfers between devices with their start and end apart: 60 -> 60, of which waited for: 24 -> 24; matrix products, arithmetic and copies ran while one was open for 1% -> 1% of each run, Pallas kernels for 29% -> 26%
where the time goes in v5:
time: 161 us; the launch traced here: 158 us
  starting transfers between devices  59.1 us (37%)
  Pallas kernels  50.8 us (32%)
  waiting for transfers between devices  41.9 us (26%)
  local copies, waits for them, and re-layouts  2.59 us (2%)
  other arithmetic  1.86 us (1%)
    ppermute x60, starting transfers between devices, swap(): return lax.ppermute(x, AXES, [(d, d ^ mask) for d in range(n_dev)])  59.1 us
    pallas_call x32, Pallas kernels, call(): pl.pallas_call(body, out_shape=out_shape, in_specs=[aspec] * skip + specs...  50.8 us
    ppermute x60, waiting for transfers between devices, swap(): return lax.ppermute(x, AXES, [(d, d ^ mask) for d in range(n_dev)])  41.9 us
  transfers between devices with their start and end apart: 60, of which 24 were waited for; matrix products, arithmetic and copies ran while one was open for 1% of the time, Pallas kernels for 26%

profile of v5, /device:TPU:0, one launch (start us, length us, event | category | flops | bytes accessed | tf_op | source)
XLA Modules:
  0.0 157.8 jit_solution(1900020526519955819)
XLA Ops:
  0.6 3.0 %prep.1 = (bf16[24,1664]{1,0:T(8,128)(2,1)}, bf16[24,1664]{1,0:T(8,128)(2,1)}, bf16[24,1664]{1,0:T(8,128)(2,1)}, bf16[24,1664]{1,0:T(8,128)(2,1)}, bf16[272,768]{1,0:T(8,128)(2,1)}, /*index=5*/f32[2,24,128]{2,1,0:T(8,128)}) custom-call(bf16[24,768]{1,0:T(8,128)(2,1)} %refs_10_.1, bf16[24,768]{1,0:T(8,128)(2,1)} %refs_11_.1, bf16[24,768]{1,0:T(8,128)(2,1)} %refs_12_.1, ...), custom_call_target="tpu_custom_call" | custom-call | tf_op jit(solution)/shard_map/prep/pallas_call | solution.py:59
  4.1 2.6 %collective-permute-start.1 = (bf16[24,1664]{1,0:T(8,128)(2,1)}, bf16[24,1664]{1,0:T(8,128)(2,1)S(1)}, u32[]{:S(2)}, u32[]{:S(2)}) collective-permute-start(bf16[24,1664]{1,0:T(8,128)(2,1)} %get-tuple-element.132), channel_id=1, source_target_pairs={{0,2},{1,3},{2,0},{3,1},{4,6},{5,7},{6,4},{7,5},{8,10},{9,11},{10,... | collective-permute-start | bytes 239624 | tf_op jit(solution)/shard_map/ppermute | solution.py:747
  16.5 2.6 %collective-permute-start.5 = (bf16[128,640]{1,0:T(8,128)(2,1)S(1)}, bf16[128,640]{1,0:T(8,128)(2,1)S(1)}, u32[]{:S(2)}, u32[]{:S(2)}) collective-permute-start(bf16[128,640]{1,0:T(8,128)(2,1)S(1)} %pack.1.refs_0_.refs_4_.refs_1_), channel_id=1, source_target_pairs={{0,16},{1,17},{2,18},{3,19},{4,20},{5,21},{6,22},{7,23},{8,24},{9,... | collective-permute-start | bytes 491528 | tf_op jit(solution)/shard_map/ppermute | solution.py:747
  22.2 2.3 %collective-permute-done.6.refs_5_.refs_2_ = bf16[128,640]{1,0:T(8,128)(2,1)S(1)} collective-permute-done((bf16[128,640]{1,0:T(8,128)(2,1)S(1)}, bf16[128,640]{1,0:T(8,128)(2,1)S(1)}, u32[]{:S(2)}, u32[]{:S(2)}) %collective-permute-start.6) | collective-permute-done | bytes 163872 | tf_op jit(solution)/shard_map/ppermute | solution.py:747
  24.5 2.4 %collective-permute-done.5.refs_6_.refs_3_ = bf16[128,640]{1,0:T(8,128)(2,1)S(1)} collective-permute-done((bf16[128,640]{1,0:T(8,128)(2,1)S(1)}, bf16[128,640]{1,0:T(8,128)(2,1)S(1)}, u32[]{:S(2)}, u32[]{:S(2)}) %collective-permute-start.5) | collective-permute-done | bytes 163872 | tf_op jit(solution)/shard_map/ppermute | solution.py:747
  29.3 2.8 %collective-permute-done.9.refs_9_.refs_6_ = bf16[128,640]{1,0:T(8,128)(2,1)S(1)} collective-permute-done((bf16[128,640]{1,0:T(8,128)(2,1)S(1)}, bf16[128,640]{1,0:T(8,128)(2,1)S(1)}, u32[]{:S(2)}, u32[]{:S(2)}) %collective-permute-start.9) | collective-permute-done | bytes 163872 | tf_op jit(solution)/shard_map/ppermute | solution.py:747
  34.7 1.9 %collective-permute-start.21 = (bf16[576,256]{1,0:T(8,128)(2,1)S(1)}, bf16[576,256]{1,0:T(8,128)(2,1)S(1)}, u32[]{:S(2)}, u32[]{:S(2)}) collective-permute-start(bf16[576,256]{1,0:T(8,128)(2,1)S(1)} %pack_more.1.refs_0_), channel_id=1, source_target_pairs={{0,16},{1,17},{2,18},{3,19},{4,20},{5,21},{6,22},{7,23},{8,24},{9,... | collective-permute-start | bytes 884744 | tf_op jit(solution)/shard_map/ppermute | solution.py:747
  38.1 2.5 %collective-permute-start.20 = (bf16[576,256]{1,0:T(8,128)(2,1)S(1)}, bf16[576,256]{1,0:T(8,128)(2,1)S(1)}, u32[]{:S(2)}, u32[]{:S(2)}) collective-permute-start(bf16[576,256]{1,0:T(8,128)(2,1)S(1)} %pack_more.1.refs_0_), channel_id=1, source_target_pairs={{0,8},{1,9},{2,10},{3,11},{4,12},{5,13},{6,14},{7,15},{8,0},{9,1},... | collective-permute-start | bytes 884744 | tf_op jit(solution)/shard_map/ppermute | solution.py:747
  41.2 2.8 %qkv.1 = (bf16[4,256,768]{2,1,0:T(8,128)(2,1)S(1)}, bf16[4,256,768]{2,1,0:T(8,128)(2,1)S(1)}, bf16[5,4,256,128]{3,2,1,0:T(8,128)(2,1)S(1)}, bf16[768,640]{1,0:T(...) custom-call(bf16[272,768]{1,0:T(8,128)(2,1)S(1)} %copy-done.1, ...), custom_call_target="tpu_custom_call" | custom-call | tf_op jit(solution)/shard_map/qkv/pallas_call | solution.py:59
  46.3 3.3 %attn_fwd.3 = (bf16[4,4,256,256]{3,2,1,0:T(8,128)(2,1)S(1)}, f32[4,1,256]{2,1,0:T(1,128)S(1)}, f32[64,1024]{1,0:T(8,128)S(1)}) custom-call(f32[12,32]{1,0:T(8,128)S(1)} %convert_bitcast_fusion.refs_1_.refs_0_.refs_2_, f32[3,3,256,256]{3,2,1,0:T(8,128)S(1)} %bias.1.refs_1_.refs_2_.refs_3_, ...), custom_call_target="tpu_custom_call" | custom-call | tf_op jit(solution)/shard_map/attn_fwd/pallas_call | solution.py:59
  54.3 3.3 %attn_fwd.4 = (bf16[4,4,256,256]{3,2,1,0:T(8,128)(2,1)S(1)}, f32[4,1,256]{2,1,0:T(1,128)S(1)}, f32[64,1024]{1,0:T(8,128)S(1)}) custom-call(f32[4,1,256]{2,1,0:T(1,128)S(1)} %get-tuple-element.148.refs_0_.refs_4_, f32[12,32]{1,0:T(8,128)S(1)} %convert_bitcast_fusion.refs_1_.refs_0_.refs_2_, f32[3,3,256,256]{3,2,1,0:T(8,128)S(1)} %bias.1.refs_1_.refs_2_.refs_3_, ...), custom_call_target="tpu_custom_call" | custom-call | tf_op jit(solution)/shard_map/attn_fwd/pallas_call | solution.py:59
  57.6 3.4 %attn_fwd.5 = (bf16[4,4,256,256]{3,2,1,0:T(8,128)(2,1)S(1)}, f32[4,1,256]{2,1,0:T(1,128)S(1)}, f32[64,1024]{1,0:T(8,128)S(1)}) custom-call(f32[4,1,256]{2,1,0:T(1,128)S(1)} %get-tuple-element.150.refs_0_.refs_5_, bf16[256,768]{1,0:T(8,128)(2,1)S(1)} %collective-permute-done.13.refs_1_.refs_9_.refs_8_, ...), custom_call_target="tpu_custom_call" | custom-call | tf_op jit(solution)/shard_map/attn_fwd/pallas_call | solution.py:59
  61.2 1.9 %collective-permute-start.15 = (bf16[1536,128]{1,0:T(8,128)(2,1)S(1)}, bf16[1536,128]{1,0:T(8,128)(2,1)S(1)}, u32[]{:S(2)}, u32[]{:S(2)}) collective-permute-start(bf16[1536,128]{1,0:T(8,128)(2,1)S(1)} %join.1.refs_0_.refs_1_), channel_id=1, source_target_pairs={{0,2},{1,3},{2,0},{3,1},{4,6},{5,7},{6,4},{7,5},{8,10},{9,11},{10,... | collective-permute-start | bytes 1179656 | tf_op jit(solution)/shard_map/ppermute | solution.py:747
  63.7 2.1 %collective-permute-done.25.refs_6_ = bf16[576,256]{1,0:T(8,128)(2,1)S(1)} collective-permute-done((bf16[576,256]{1,0:T(8,128)(2,1)S(1)}, bf16[576,256]{1,0:T(8,128)(2,1)S(1)}, u32[]{:S(2)}, u32[]{:S(2)}) %collective-permute-start.25) | collective-permute-done | bytes 294944 | tf_op jit(solution)/shard_map/ppermute | solution.py:747
  68.1 2.8 %collective-permute-done.15.refs_2_.refs_3_ = bf16[1536,128]{1,0:T(8,128)(2,1)S(1)} collective-permute-done((bf16[1536,128]{1,0:T(8,128)(2,1)S(1)}, bf16[1536,128]{1,0:T(8,128)(2,1)S(1)}, u32[]{:S(2)}, u32[]{:S(2)}) %collective-permute-start.15) | collective-permute-done | bytes 393248 | tf_op jit(solution)/shard_map/ppermute | solution.py:747
  70.9 2.0 %collective-permute-done.26.refs_7_ = bf16[576,256]{1,0:T(8,128)(2,1)S(1)} collective-permute-done((bf16[576,256]{1,0:T(8,128)(2,1)S(1)}, bf16[576,256]{1,0:T(8,128)(2,1)S(1)}, u32[]{:S(2)}, u32[]{:S(2)}) %collective-permute-start.26) | collective-permute-done | bytes 294944 | tf_op jit(solution)/shard_map/ppermute | solution.py:747
  73.1 5.0 %ffn.2 = (bf16[2,256,768]{2,1,0:T(8,128)(2,1)S(1)}, bf16[2,256,512]{2,1,0:T(8,128)(2,1)S(1)}, bf16[2,256,1024]{2,1,0:T(8,128)(2,1)S(1)}, bf16[256,768]{1,0:T(8,1...) custom-call(bf16[1536,128]{1,0:T(8,128)(2,1)S(1)} %join.1.refs_0_.refs_1_, ...), custom_call_target="tpu_custom_call" | custom-call | tf_op jit(solution)/shard_map/ffn/pallas_call | solution.py:59
  79.9 1.9 %collective-permute-start.32 = (bf16[256,768]{1,0:T(8,128)(2,1)S(1)}, bf16[256,768]{1,0:T(8,128)(2,1)S(1)}, u32[]{:S(2)}, u32[]{:S(2)}) collective-permute-start(bf16[256,768]{1,0:T(8,128)(2,1)S(1)} %add.26.refs_0_), channel_id=1, source_target_pairs={{0,2},{1,3},{2,0},{3,1},{4,6},{5,7},{6,4},{7,5},{8,10},{9,11},{10,... | collective-permute-start | bytes 1179656 | tf_op jit(solution)/shard_map/ppermute | solution.py:747
  81.8 4.3 %ffn.3 = (bf16[2,256,768]{2,1,0:T(8,128)(2,1)S(1)}, bf16[2,256,512]{2,1,0:T(8,128)(2,1)S(1)}, bf16[2,256,1024]{2,1,0:T(8,128)(2,1)S(1)}, bf16[256,768]{1,0:T(8,1...) custom-call(bf16[256,768]{1,0:T(8,128)(2,1)S(1)} %add.26.refs_0_, ...), custom_call_target="tpu_custom_call" | custom-call | tf_op jit(solution)/shard_map/ffn/pallas_call | solution.py:59
  86.2 3.8 %ffn_dw.1 = (bf16[4,288,256]{2,1,0:T(8,128)(2,1)S(1)}, bf16[4,288,256]{2,1,0:T(8,128)(2,1)S(1)}, bf16[4,288,256]{2,1,0:T(8,128)(2,1)S(1)}, bf16[4,288,256]{2,1,0...) custom-call(bf16[512,768]{1,0:T(8,128)(2,1)S(1)} %bitcast.42, ...), custom_call_target="tpu_custom_call" | custom-call | tf_op jit(solution)/shard_map/ffn_dw/pallas_call | solution.py:59
  98.2 4.1 %collective-permute-done.35.refs_10_.refs_8_ = bf16[384,128]{1,0:T(8,128)(2,1)S(1)} collective-permute-done((bf16[384,128]{1,0:T(8,128)(2,1)S(1)}, bf16[384,128]{1,0:T(8,128)(2,1)S(1)}, u32[]{:S(2)}, u32[]{:S(2)}) %collective-permute-start.35) | collective-permute-done | bytes 98336 | tf_op jit(solution)/shard_map/ppermute | solution.py:747
  103.8 5.4 %attn_bwd.2 = (bf16[4,256,384]{2,1,0:T(8,128)(2,1)S(1)}, f32[8,128]{1,0:T(8,128)S(1)}) custom-call(bf16[8,24,768]{2,1,0:T(8,128)(2,1)S(1)} %bitcast_add_fusion.refs_0_, bf16[5,4,256,128]{3,2,1,0:T(8,128)(2,1)S(1)} %get-tuple-element.144.refs_2_.refs_3_.refs_4_.refs_1_, bf16[4,4,256,256]{3,2,1,0:T(8,128)(2,1)S(1)} %get-tuple-element.190.refs_2_, ...), custom_call_target="tpu_custom_call" | custom-call | tf_op jit(solution)/shard_map/attn_bwd/pallas_call | solution.py:59
  111.4 3.2 %collective-permute-start.44 = (bf16[2,288,256]{2,1,0:T(8,128)(2,1)S(1)}, bf16[2,288,256]{2,1,0:T(8,128)(2,1)S(1)}, u32[]{:S(2)}, u32[]{:S(2)}) collective-permute-start(bf16[2,288,256]{2,1,0:T(8,128)(2,1)S(1)} %get-tuple-element.210), channel_id=1, source_target_pairs={{0,16},{1,17},{2,18},{3,19},{4,20},{5,21},{6,22},{7,23},{8,24},{9,... | collective-permute-start | bytes 884744 | tf_op jit(solution)/shard_map/ppermute | solution.py:747
  115.8 2.9 %attn_bwd.3 = (bf16[4,256,256]{2,1,0:T(8,128)(2,1)S(1)}, f32[8,128]{1,0:T(8,128)S(1)}) custom-call(bf16[2,288,256]{2,1,0:T(8,128)(2,1)S(1)} %get-tuple-element.198.refs_0_, bf16[256,768]{1,0:T(8,128)(2,1)S(1)} %fusion.4.refs_1_, bf16[5,4,256,128]{3,2,1,0:T(8,128)(2,1)S(1)} %get-tuple-element.144.refs_2_.refs_3_.refs_4_.refs_1_, ...), custom_call_target="tpu_custom_call" | custom-call | flops 11500000256 | tf_op jit(solution)/shard_map/attn_bwd/pallas_call | solution.py:59
  121.7 2.1 %collective-permute-start.46 = (bf16[576,128]{1,0:T(8,128)(2,1)S(1)}, bf16[576,128]{1,0:T(8,128)(2,1)S(1)}, u32[]{:S(2)}, u32[]{:S(2)}) collective-permute-start(bf16[576,128]{1,0:T(8,128)(2,1)S(1)} %get-tuple-element.207.refs_0_), channel_id=1, source_target_pairs={{0,8},{1,9},{2,10},{3,11},{4,12},{5,13},{6,14},{7,15},{8,0},{9,1},... | collective-permute-start | bytes 442376 | tf_op jit(solution)/shard_map/ppermute | solution.py:747
  123.8 2.2 %one_grad.1 = (bf16[2,256,768]{2,1,0:T(8,128)(2,1)S(1)}, bf16[2,256,768]{2,1,0:T(8,128)(2,1)S(1)}) custom-call(bf16[1360,128]{1,0:T(8,128)(2,1)S(1)} %get-tuple-element.205.refs_0_, bf16[4,256,384]{2,1,0:T(8,128)(2,1)S(1)} %get-tuple-element.193.refs_1_, bf16[4,256,256]{2,1,0:T(8,128)(2,1)S(1)} %get-tuple-element.200.refs_2_, ...), custom_call_target="tpu_custom_call" | custom-call | flops 46000001024 | tf_op jit(solution)/shard_map/one_grad/pallas_call | solution.py:59
  125.9 2.0 %collective-permute-done.44.refs_4_.refs_7_ = bf16[2,288,256]{2,1,0:T(8,128)(2,1)S(1)} collective-permute-done((bf16[2,288,256]{2,1,0:T(8,128)(2,1)S(1)}, bf16[2,288,256]{2,1,0:T(8,128)(2,1)S(1)}, u32[]{:S(2)}, u32[]{:S(2)}) %collective-permute-start.44) | collective-permute-done | bytes 294944 | tf_op jit(solution)/shard_map/ppermute | solution.py:747
  128.5 3.7 %collective-permute-start.52 = (bf16[288,256]{1,0:T(8,128)(2,1)S(1)}, bf16[288,256]{1,0:T(8,128)(2,1)S(1)}, u32[]{:S(2)}, u32[]{:S(2)}) collective-permute-start(bf16[288,256]{1,0:T(8,128)(2,1)S(1)} %get-tuple-element.225), channel_id=1, source_target_pairs={{0,4},{1,5},{2,6},{3,7},{4,0},{5,1},{6,2},{7,3},{8,12},{9,13},{10,... | collective-permute-start | bytes 442376 | tf_op jit(solution)/shard_map/ppermute | solution.py:747
  134.5 2.9 %collective-permute-start.47 = (bf16[288,128]{1,0:T(8,128)(2,1)S(1)}, bf16[288,128]{1,0:T(8,128)(2,1)S(1)}, u32[]{:S(2)}, u32[]{:S(2)}) collective-permute-start(bf16[288,128]{1,0:T(8,128)(2,1)S(1)} %get-tuple-element.215.refs_0_), channel_id=1, source_target_pairs={{0,16},{1,17},{2,18},{3,19},{4,20},{5,21},{6,22},{7,23},{8,24},{9,... | collective-permute-start | bytes 221192 | tf_op jit(solution)/shard_map/ppermute | solution.py:747
  138.9 4.0 %collective-permute-done.50.refs_2_ = bf16[688,128]{1,0:T(8,128)(2,1)S(1)} collective-permute-done((bf16[688,128]{1,0:T(8,128)(2,1)S(1)}, bf16[688,128]{1,0:T(8,128)(2,1)S(1)}, u32[]{:S(2)}, u32[]{:S(2)}) %collective-permute-start.50) | collective-permute-done | bytes 176160 | tf_op jit(solution)/shard_map/ppermute | solution.py:747
  144.1 1.9 %collective-permute-start.54 = (bf16[24,1408]{1,0:T(8,128)(2,1)S(1)}, bf16[24,1408]{1,0:T(8,128)(2,1)S(1)}, u32[]{:S(2)}, u32[]{:S(2)}) collective-permute-start(bf16[24,1408]{1,0:T(8,128)(2,1)S(1)} %get-tuple-element.228), channel_id=1, source_target_pairs={{0,2},{1,3},{2,0},{3,1},{4,6},{5,7},{6,4},{7,5},{8,10},{9,11},{10,... | collective-permute-start | bytes 202760 | tf_op jit(solution)/shard_map/ppermute | solution.py:747
  146.2 3.0 %collective-permute-done.49.refs_3_ = bf16[256,768]{1,0:T(8,128)(2,1)S(1)} collective-permute-done((bf16[256,768]{1,0:T(8,128)(2,1)S(1)}, bf16[256,768]{1,0:T(8,128)(2,1)S(1)}, u32[]{:S(2)}, u32[]{:S(2)}) %collective-permute-start.49) | collective-permute-done | bytes 393248 | tf_op jit(solution)/shard_map/ppermute | solution.py:747
  (148 shorter events, 62.4 us)
Async XLA Ops:
  6.8 27.4 %collective-permute-start.4 = (bf16[272,768]{1,0:T(8,128)(2,1)}, bf16[272,768]{1,0:T(8,128)(2,1)S(1)}, u32[]{:S(2)}, u32[]{:S(2)}) collective-permute-start(bf16[272,768]{1,0:T(8,128)(2,1)} %get-tuple-element.134.refs_0_), channel_id=1, source_target_pairs={{0,2},{1,3},{2,0},{3,1},{4,6},{5,7},{6,4},{7,5},{8,10},{9,11},{10,... | collective-permute-start | bytes 1253384 | tf_op jit(solution)/shard_map/ppermute | solution.py:747
  13.2 9.0 %collective-permute-start.7 = (bf16[128,640]{1,0:T(8,128)(2,1)S(1)}, bf16[128,640]{1,0:T(8,128)(2,1)S(1)}, u32[]{:S(2)}, u32[]{:S(2)}) collective-permute-start(bf16[128,640]{1,0:T(8,128)(2,1)S(1)} %pack.1.refs_0_.refs_4_.refs_1_), channel_id=1, source_target_pairs={{0,4},{1,5},{2,6},{3,7},{4,0},{5,1},{6,2},{7,3},{8,12},{9,13},{10,... | collective-permute-start | bytes 491528 | tf_op jit(solution)/shard_map/ppermute | solution.py:747
  14.9 9.6 %collective-permute-start.6 = (bf16[128,640]{1,0:T(8,128)(2,1)S(1)}, bf16[128,640]{1,0:T(8,128)(2,1)S(1)}, u32[]{:S(2)}, u32[]{:S(2)}) collective-permute-start(bf16[128,640]{1,0:T(8,128)(2,1)S(1)} %pack.1.refs_0_.refs_4_.refs_1_), channel_id=1, source_target_pairs={{0,8},{1,9},{2,10},{3,11},{4,12},{5,13},{6,14},{7,15},{8,0},{9,1},... | collective-permute-start | bytes 491528 | tf_op jit(solution)/shard_map/ppermute | solution.py:747
  16.5 10.4 %collective-permute-start.5 = (bf16[128,640]{1,0:T(8,128)(2,1)S(1)}, bf16[128,640]{1,0:T(8,128)(2,1)S(1)}, u32[]{:S(2)}, u32[]{:S(2)}) collective-permute-start(bf16[128,640]{1,0:T(8,128)(2,1)S(1)} %pack.1.refs_0_.refs_4_.refs_1_), channel_id=1, source_target_pairs={{0,16},{1,17},{2,18},{3,19},{4,20},{5,21},{6,22},{7,23},{8,24},{9,... | collective-permute-start | bytes 491528 | tf_op jit(solution)/shard_map/ppermute | solution.py:747
  29.3 8.8 %collective-permute-start.3 = (bf16[272,768]{1,0:T(8,128)(2,1)S(1)}, bf16[272,768]{1,0:T(8,128)(2,1)S(1)}, u32[]{:S(2)}, u32[]{:S(2)}) collective-permute-start(bf16[272,768]{1,0:T(8,128)(2,1)S(1)} %copy-done.1), channel_id=1, source_target_pairs={{0,1},{1,0},{2,3},{3,2},{4,5},{5,4},{6,7},{7,6},{8,9},{9,8},{10,11... | collective-permute-start | bytes 1253384 | tf_op jit(solution)/shard_map/ppermute | solution.py:747
  34.7 16.5 %collective-permute-start.21 = (bf16[576,256]{1,0:T(8,128)(2,1)S(1)}, bf16[576,256]{1,0:T(8,128)(2,1)S(1)}, u32[]{:S(2)}, u32[]{:S(2)}) collective-permute-start(bf16[576,256]{1,0:T(8,128)(2,1)S(1)} %pack_more.1.refs_0_), channel_id=1, source_target_pairs={{0,16},{1,17},{2,18},{3,19},{4,20},{5,21},{6,22},{7,23},{8,24},{9,... | collective-permute-start | bytes 884744 | tf_op jit(solution)/shard_map/ppermute | solution.py:747
  36.6 14.6 %collective-permute-start.22 = (bf16[576,256]{1,0:T(8,128)(2,1)S(1)}, bf16[576,256]{1,0:T(8,128)(2,1)S(1)}, u32[]{:S(2)}, u32[]{:S(2)}) collective-permute-start(bf16[576,256]{1,0:T(8,128)(2,1)S(1)} %pack_more.1.refs_0_), channel_id=1, source_target_pairs={{0,4},{1,5},{2,6},{3,7},{4,0},{5,1},{6,2},{7,3},{8,12},{9,13},{10,... | collective-permute-start | bytes 884744 | tf_op jit(solution)/shard_map/ppermute | solution.py:747
  38.1 14.1 %collective-permute-start.20 = (bf16[576,256]{1,0:T(8,128)(2,1)S(1)}, bf16[576,256]{1,0:T(8,128)(2,1)S(1)}, u32[]{:S(2)}, u32[]{:S(2)}) collective-permute-start(bf16[576,256]{1,0:T(8,128)(2,1)S(1)} %pack_more.1.refs_0_), channel_id=1, source_target_pairs={{0,8},{1,9},{2,10},{3,11},{4,12},{5,13},{6,14},{7,15},{8,0},{9,1},... | collective-permute-start | bytes 884744 | tf_op jit(solution)/shard_map/ppermute | solution.py:747
  44.1 13.5 %collective-permute-start.13 = (bf16[256,768]{1,0:T(8,128)(2,1)S(1)}, bf16[256,768]{1,0:T(8,128)(2,1)S(1)}, u32[]{:S(2)}, u32[]{:S(2)}) collective-permute-start(bf16[256,768]{1,0:T(8,128)(2,1)S(1)} %bitcast.35), channel_id=1, source_target_pairs={{0,2},{1,3},{2,0},{3,1},{4,6},{5,7},{6,4},{7,5},{8,10},{9,11},{10,... | collective-permute-start | bytes 1179656 | tf_op jit(solution)/shard_map/ppermute | solution.py:747
  45.9 17.3 %collective-permute-start.17 = (bf16[192,768]{1,0:T(8,128)(2,1)S(1)}, bf16[192,768]{1,0:T(8,128)(2,1)S(1)}, u32[]{:S(2)}, u32[]{:S(2)}) collective-permute-start(bf16[192,768]{1,0:T(8,128)(2,1)S(1)} %stripes.1.refs_0_), channel_id=1, source_target_pairs={{0,2},{1,3},{2,0},{3,1},{4,6},{5,7},{6,4},{7,5},{8,10},{9,11},{10,... | collective-permute-start | bytes 884744 | tf_op jit(solution)/shard_map/ppermute | solution.py:747
  52.2 10.9 %collective-permute-start.24 = (bf16[576,256]{1,0:T(8,128)(2,1)S(1)}, bf16[576,256]{1,0:T(8,128)(2,1)S(1)}, u32[]{:S(2)}, u32[]{:S(2)}) collective-permute-start(bf16[576,256]{1,0:T(8,128)(2,1)S(1)} %collective-permute-done.20.refs_1_), channel_id=1, source_target_pairs={{0,4},{1,5},{2,6},{3,7},{4,0},{5,1},{6,2},{7,3},{8,12},{9,13},{10,... | collective-permute-start | bytes 884744 | tf_op jit(solution)/shard_map/ppermute | solution.py:747
  52.7 13.0 %collective-permute-start.25 = (bf16[576,256]{1,0:T(8,128)(2,1)S(1)}, bf16[576,256]{1,0:T(8,128)(2,1)S(1)}, u32[]{:S(2)}, u32[]{:S(2)}) collective-permute-start(bf16[576,256]{1,0:T(8,128)(2,1)S(1)} %collective-permute-done.21.refs_2_), channel_id=1, source_target_pairs={{0,4},{1,5},{2,6},{3,7},{4,0},{5,1},{6,2},{7,3},{8,12},{9,13},{10,... | collective-permute-start | bytes 884744 | tf_op jit(solution)/shard_map/ppermute | solution.py:747
  54.3 11.5 %collective-permute-start.23 = (bf16[576,256]{1,0:T(8,128)(2,1)S(1)}, bf16[576,256]{1,0:T(8,128)(2,1)S(1)}, u32[]{:S(2)}, u32[]{:S(2)}) collective-permute-start(bf16[576,256]{1,0:T(8,128)(2,1)S(1)} %collective-permute-done.21.refs_2_), channel_id=1, source_target_pairs={{0,8},{1,9},{2,10},{3,11},{4,12},{5,13},{6,14},{7,15},{8,0},{9,1},... | collective-permute-start | bytes 884744 | tf_op jit(solution)/shard_map/ppermute | solution.py:747
  61.2 9.7 %collective-permute-start.15 = (bf16[1536,128]{1,0:T(8,128)(2,1)S(1)}, bf16[1536,128]{1,0:T(8,128)(2,1)S(1)}, u32[]{:S(2)}, u32[]{:S(2)}) collective-permute-start(bf16[1536,128]{1,0:T(8,128)(2,1)S(1)} %join.1.refs_0_.refs_1_), channel_id=1, source_target_pairs={{0,2},{1,3},{2,0},{3,1},{4,6},{5,7},{6,4},{7,5},{8,10},{9,11},{10,... | collective-permute-start | bytes 1179656 | tf_op jit(solution)/shard_map/ppermute | solution.py:747
  79.9 13.6 %collective-permute-start.32 = (bf16[256,768]{1,0:T(8,128)(2,1)S(1)}, bf16[256,768]{1,0:T(8,128)(2,1)S(1)}, u32[]{:S(2)}, u32[]{:S(2)}) collective-permute-start(bf16[256,768]{1,0:T(8,128)(2,1)S(1)} %add.26.refs_0_), channel_id=1, source_target_pairs={{0,2},{1,3},{2,0},{3,1},{4,6},{5,7},{6,4},{7,5},{8,10},{9,11},{10,... | collective-permute-start | bytes 1179656 | tf_op jit(solution)/shard_map/ppermute | solution.py:747
  90.0 24.6 %collective-permute-start.30 = (bf16[2,256,768]{2,1,0:T(8,128)(2,1)S(1)}, bf16[2,256,768]{2,1,0:T(8,128)(2,1)S(1)}, u32[]{:S(2)}, u32[]{:S(2)}) collective-permute-start(bf16[2,256,768]{2,1,0:T(8,128)(2,1)S(1)} %get-tuple-element.178), channel_id=1, source_target_pairs={{0,1},{1,0},{2,3},{3,2},{4,5},{5,4},{6,7},{7,6},{8,9},{9,8},{10,11... | collective-permute-start | bytes 2359304 | tf_op jit(solution)/shard_map/ppermute | solution.py:747
  90.5 20.1 %collective-permute-start.38 = (bf16[4,288,256]{2,1,0:T(8,128)(2,1)S(1)}, bf16[4,288,256]{2,1,0:T(8,128)(2,1)S(1)}, u32[]{:S(2)}, u32[]{:S(2)}) collective-permute-start(bf16[4,288,256]{2,1,0:T(8,128)(2,1)S(1)} %get-tuple-element.197), channel_id=1, source_target_pairs={{0,8},{1,9},{2,10},{3,11},{4,12},{5,13},{6,14},{7,15},{8,0},{9,1},... | collective-permute-start | bytes 1769480 | tf_op jit(solution)/shard_map/ppermute | solution.py:747
  92.0 19.2 %collective-permute-start.37 = (bf16[4,288,256]{2,1,0:T(8,128)(2,1)S(1)}, bf16[4,288,256]{2,1,0:T(8,128)(2,1)S(1)}, u32[]{:S(2)}, u32[]{:S(2)}) collective-permute-start(bf16[4,288,256]{2,1,0:T(8,128)(2,1)S(1)} %get-tuple-element.180.refs_0_), channel_id=1, source_target_pairs={{0,4},{1,5},{2,6},{3,7},{4,0},{5,1},{6,2},{7,3},{8,12},{9,13},{10,... | collective-permute-start | bytes 1769480 | tf_op jit(solution)/shard_map/ppermute | solution.py:747
  102.3 16.4 %collective-permute-start.40 = (bf16[8,24,768]{2,1,0:T(8,128)(2,1)S(1)}, bf16[8,24,768]{2,1,0:T(8,128)(2,1)S(1)}, u32[]{:S(2)}, u32[]{:S(2)}) collective-permute-start(bf16[8,24,768]{2,1,0:T(8,128)(2,1)S(1)} %get-tuple-element.202), channel_id=1, source_target_pairs={{0,1},{1,0},{2,3},{3,2},{4,5},{5,4},{6,7},{7,6},{8,9},{9,8},{10,11... | collective-permute-start | bytes 884744 | tf_op jit(solution)/shard_map/ppermute | solution.py:747
  102.8 17.0 %collective-permute-start.41 = (bf16[8,24,768]{2,1,0:T(8,128)(2,1)S(1)}, bf16[8,24,768]{2,1,0:T(8,128)(2,1)S(1)}, u32[]{:S(2)}, u32[]{:S(2)}) collective-permute-start(bf16[8,24,768]{2,1,0:T(8,128)(2,1)S(1)} %bitcast_add_fusion.refs_0_), channel_id=1, source_target_pairs={{0,2},{1,3},{2,0},{3,1},{4,6},{5,7},{6,4},{7,5},{8,10},{9,11},{10,... | collective-permute-start | bytes 884744 | tf_op jit(solution)/shard_map/ppermute | solution.py:747
  110.7 10.9 %collective-permute-start.42 = (bf16[1152,128]{1,0:T(8,128)(2,1)S(1)}, bf16[1152,128]{1,0:T(8,128)(2,1)S(1)}, u32[]{:S(2)}, u32[]{:S(2)}) collective-permute-start(bf16[1152,128]{1,0:T(8,128)(2,1)S(1)} %get-tuple-element.194.refs_0_), channel_id=1, source_target_pairs={{0,4},{1,5},{2,6},{3,7},{4,0},{5,1},{6,2},{7,3},{8,12},{9,13},{10,... | collective-permute-start | bytes 884744 | tf_op jit(solution)/shard_map/ppermute | solution.py:747
  111.4 16.5 %collective-permute-start.44 = (bf16[2,288,256]{2,1,0:T(8,128)(2,1)S(1)}, bf16[2,288,256]{2,1,0:T(8,128)(2,1)S(1)}, u32[]{:S(2)}, u32[]{:S(2)}) collective-permute-start(bf16[2,288,256]{2,1,0:T(8,128)(2,1)S(1)} %get-tuple-element.210), channel_id=1, source_target_pairs={{0,16},{1,17},{2,18},{3,19},{4,20},{5,21},{6,22},{7,23},{8,24},{9,... | collective-permute-start | bytes 884744 | tf_op jit(solution)/shard_map/ppermute | solution.py:747
  114.6 13.8 %collective-permute-start.43 = (bf16[2,288,256]{2,1,0:T(8,128)(2,1)S(1)}, bf16[2,288,256]{2,1,0:T(8,128)(2,1)S(1)}, u32[]{:S(2)}, u32[]{:S(2)}) collective-permute-start(bf16[2,288,256]{2,1,0:T(8,128)(2,1)S(1)} %get-tuple-element.198.refs_0_), channel_id=1, source_target_pairs={{0,8},{1,9},{2,10},{3,11},{4,12},{5,13},{6,14},{7,15},{8,0},{9,1},... | collective-permute-start | bytes 884744 | tf_op jit(solution)/shard_map/ppermute | solution.py:747
  118.7 18.8 %collective-permute-start.39 = (bf16[256,768]{1,0:T(8,128)(2,1)S(1)}, bf16[256,768]{1,0:T(8,128)(2,1)S(1)}, u32[]{:S(2)}, u32[]{:S(2)}) collective-permute-start(bf16[256,768]{1,0:T(8,128)(2,1)S(1)} %fusion.4.refs_1_), channel_id=1, source_target_pairs={{0,2},{1,3},{2,0},{3,1},{4,6},{5,7},{6,4},{7,5},{8,10},{9,11},{10,... | collective-permute-start | bytes 1179656 | tf_op jit(solution)/shard_map/ppermute | solution.py:747
  120.9 11.3 %collective-permute-start.45 = (bf16[1360,128]{1,0:T(8,128)(2,1)S(1)}, bf16[1360,128]{1,0:T(8,128)(2,1)S(1)}, u32[]{:S(2)}, u32[]{:S(2)}) collective-permute-start(bf16[1360,128]{1,0:T(8,128)(2,1)S(1)} %get-tuple-element.205.refs_0_), channel_id=1, source_target_pairs={{0,4},{1,5},{2,6},{3,7},{4,0},{5,1},{6,2},{7,3},{8,12},{9,13},{10,... | collective-permute-start | bytes 1044488 | tf_op jit(solution)/shard_map/ppermute | solution.py:747
  121.7 10.7 %collective-permute-start.46 = (bf16[576,128]{1,0:T(8,128)(2,1)S(1)}, bf16[576,128]{1,0:T(8,128)(2,1)S(1)}, u32[]{:S(2)}, u32[]{:S(2)}) collective-permute-start(bf16[576,128]{1,0:T(8,128)(2,1)S(1)} %get-tuple-element.207.refs_0_), channel_id=1, source_target_pairs={{0,8},{1,9},{2,10},{3,11},{4,12},{5,13},{6,14},{7,15},{8,0},{9,1},... | collective-permute-start | bytes 442376 | tf_op jit(solution)/shard_map/ppermute | solution.py:747
  128.5 14.8 %collective-permute-start.52 = (bf16[288,256]{1,0:T(8,128)(2,1)S(1)}, bf16[288,256]{1,0:T(8,128)(2,1)S(1)}, u32[]{:S(2)}, u32[]{:S(2)}) collective-permute-start(bf16[288,256]{1,0:T(8,128)(2,1)S(1)} %get-tuple-element.225), channel_id=1, source_target_pairs={{0,4},{1,5},{2,6},{3,7},{4,0},{5,1},{6,2},{7,3},{8,12},{9,13},{10,... | collective-permute-start | bytes 442376 | tf_op jit(solution)/shard_map/ppermute | solution.py:747
  132.2 11.0 %collective-permute-start.51 = (bf16[288,256]{1,0:T(8,128)(2,1)S(1)}, bf16[288,256]{1,0:T(8,128)(2,1)S(1)}, u32[]{:S(2)}, u32[]{:S(2)}) collective-permute-start(bf16[288,256]{1,0:T(8,128)(2,1)S(1)} %get-tuple-element.211.refs_0_), channel_id=1, source_target_pairs={{0,16},{1,17},{2,18},{3,19},{4,20},{5,21},{6,22},{7,23},{8,24},{9,... | collective-permute-start | bytes 442376 | tf_op jit(solution)/shard_map/ppermute | solution.py:747
  132.4 10.5 %collective-permute-start.50 = (bf16[688,128]{1,0:T(8,128)(2,1)S(1)}, bf16[688,128]{1,0:T(8,128)(2,1)S(1)}, u32[]{:S(2)}, u32[]{:S(2)}) collective-permute-start(bf16[688,128]{1,0:T(8,128)(2,1)S(1)} %get-tuple-element.213.refs_0_), channel_id=1, source_target_pairs={{0,8},{1,9},{2,10},{3,11},{4,12},{5,13},{6,14},{7,15},{8,0},{9,1},... | collective-permute-start | bytes 528392 | tf_op jit(solution)/shard_map/ppermute | solution.py:747
  134.5 8.8 %collective-permute-start.47 = (bf16[288,128]{1,0:T(8,128)(2,1)S(1)}, bf16[288,128]{1,0:T(8,128)(2,1)S(1)}, u32[]{:S(2)}, u32[]{:S(2)}) collective-permute-start(bf16[288,128]{1,0:T(8,128)(2,1)S(1)} %get-tuple-element.215.refs_0_), channel_id=1, source_target_pairs={{0,16},{1,17},{2,18},{3,19},{4,20},{5,21},{6,22},{7,23},{8,24},{9,... | collective-permute-start | bytes 221192 | tf_op jit(solution)/shard_map/ppermute | solution.py:747
  137.5 11.7 %collective-permute-start.49 = (bf16[256,768]{1,0:T(8,128)(2,1)S(1)}, bf16[256,768]{1,0:T(8,128)(2,1)S(1)}, u32[]{:S(2)}, u32[]{:S(2)}) collective-permute-start(bf16[256,768]{1,0:T(8,128)(2,1)S(1)} %fusion.3), channel_id=1, source_target_pairs={{0,2},{1,3},{2,0},{3,1},{4,6},{5,7},{6,4},{7,5},{8,10},{9,11},{10,... | collective-permute-start | bytes 1179656 | tf_op jit(solution)/shard_map/ppermute | solution.py:747
  142.9 7.7 %collective-permute-start.56 = (bf16[352,128]{1,0:T(8,128)(2,1)S(1)}, bf16[352,128]{1,0:T(8,128)(2,1)S(1)}, u32[]{:S(2)}, u32[]{:S(2)}) collective-permute-start(bf16[352,128]{1,0:T(8,128)(2,1)S(1)} %get-tuple-element.223.refs_0_), channel_id=1, source_target_pairs={{0,16},{1,17},{2,18},{3,19},{4,20},{5,21},{6,22},{7,23},{8,24},{9,... | collective-permute-start | bytes 270344 | tf_op jit(solution)/shard_map/ppermute | solution.py:747
  (39 other events, 196.5 us)

commit v6 on v5

--- a/solution.py
+++ b/solution.py
@@ -755,7 +755,8 @@
         return got, swap(keep[1] + got[1], 2)
 
     def round_one(x):
-        return lax.optimization_barrier((swap(x, 16), swap(x, 8), swap(x, 4)))
+        other, near, far = lax.optimization_barrier((swap(x, 4), swap(x, 8), swap(x, 16)))
+        return far, near, other
 
     def round_two(far, near):
         return lax.optimization_barrier((swap(far, 8), swap(near, 4), swap(far, 4)))
@@ -798,7 +799,7 @@
     bias = call(
         bias_kernel, sds((HT, 3, T, T), F32), table, smem=(0,), name="bias", after=(second,)
     )
-    far, near = lax.optimization_barrier(first_one + (second, bias))[:2]
+    near, far = lax.optimization_barrier((*first_one[::-1], second, bias))[1:3]
     first_two = round_two(far, near)
     toks_r = swap(later(toks_x, *first_two), 1)
     firsts = gathered(first, first_one, first_two, *())
@@ -888,7 +889,7 @@
         after=(y_give, *()), scratch=(pltpu.VMEM((D, D), F32),), cost=COST["mid"],
     )
     g1, g2, g3 = swap(g1, 1), swap(g2, 2), swap(g3, 3)
-    wo_got = (swap(wo_gives[0], 1), swap(wo_gives[1], 1))
+    wo_got = (swap(later(wo_gives[0], g1), 1), swap(later(wo_gives[1], g1), 1))
     wo_sum = later(wo_keep[1] + wo_got[1], g1, g2, g3)
     wo_along = swap(wo_sum, 2)
 

time: 161 us -> 160 us (level)
  starting transfers between devices: 59.1 us -> 54.9 us
  waiting for transfers between devices: 41.9 us -> 44.9 us
    ppermute x60, starting transfers between devices: 59.1 us -> 54.9 us  [swap(): return lax.ppermute(x, AXES, [(d, d ^ mask) for d in range(n_dev)])]
    ppermute x60, waiting for transfers between devices: 41.9 us -> 44.9 us  [swap(): return lax.ppermute(x, AXES, [(d, d ^ mask) for d in range(n_dev)])]
  transfers between devices with their start and end apart: 60 -> 60, of which waited for: 24 -> 25; matrix products, arithmetic and copies ran while one was open for 1% -> 1% of each run, Pallas kernels for 26% -> 26%
where the time goes in v6:
time: 160 us; the launch traced here: 156 us
  starting transfers between devices  54.9 us (34%)
  Pallas kernels  50.8 us (32%)
  waiting for transfers between devices  44.9 us (28%)
  local copies, waits for them, and re-layouts  2.58 us (2%)
  other arithmetic  1.86 us (1%)
    ppermute x60, starting transfers between devices, swap(): return lax.ppermute(x, AXES, [(d, d ^ mask) for d in range(n_dev)])  54.9 us
    pallas_call x32, Pallas kernels, call(): pl.pallas_call(body, out_shape=out_shape, in_specs=[aspec] * skip + specs...  50.8 us
    ppermute x60, waiting for transfers between devices, swap(): return lax.ppermute(x, AXES, [(d, d ^ mask) for d in range(n_dev)])  44.9 us
  transfers between devices with their start and end apart: 60, of which 25 were waited for; matrix products, arithmetic and copies ran while one was open for 1% of the time, Pallas kernels for 26%

profile of v6, /device:TPU:0, one launch (start us, length us, event | category | flops | bytes accessed | tf_op | source)
XLA Modules:
  0.0 156.5 jit_solution(2654315334308689470)
XLA Ops:
  0.6 3.0 %prep.1 = (bf16[24,1664]{1,0:T(8,128)(2,1)}, bf16[24,1664]{1,0:T(8,128)(2,1)}, bf16[24,1664]{1,0:T(8,128)(2,1)}, bf16[24,1664]{1,0:T(8,128)(2,1)}, bf16[272,768]{1,0:T(8,128)(2,1)}, /*index=5*/f32[2,24,128]{2,1,0:T(8,128)}) custom-call(bf16[24,768]{1,0:T(8,128)(2,1)} %refs_10_.1, bf16[24,768]{1,0:T(8,128)(2,1)} %refs_11_.1, bf16[24,768]{1,0:T(8,128)(2,1)} %refs_12_.1, ...), custom_call_target="tpu_custom_call" | custom-call | tf_op jit(solution)/shard_map/prep/pallas_call | solution.py:59
  4.1 2.6 %collective-permute-start.1 = (bf16[24,1664]{1,0:T(8,128)(2,1)}, bf16[24,1664]{1,0:T(8,128)(2,1)S(1)}, u32[]{:S(2)}, u32[]{:S(2)}) collective-permute-start(bf16[24,1664]{1,0:T(8,128)(2,1)} %get-tuple-element.134), channel_id=1, source_target_pairs={{0,2},{1,3},{2,0},{3,1},{4,6},{5,7},{6,4},{7,5},{8,10},{9,11},{10,... | collective-permute-start | bytes 239624 | tf_op jit(solution)/shard_map/ppermute | solution.py:747
  13.2 2.8 %collective-permute-start.7 = (bf16[128,640]{1,0:T(8,128)(2,1)S(1)}, bf16[128,640]{1,0:T(8,128)(2,1)S(1)}, u32[]{:S(2)}, u32[]{:S(2)}) collective-permute-start(bf16[128,640]{1,0:T(8,128)(2,1)S(1)} %pack.1.refs_0_.refs_4_.refs_1_), channel_id=1, source_target_pairs={{0,16},{1,17},{2,18},{3,19},{4,20},{5,21},{6,22},{7,23},{8,24},{9,... | collective-permute-start | bytes 491528 | tf_op jit(solution)/shard_map/ppermute | solution.py:747
  22.2 2.1 %collective-permute-done.7.refs_6_.refs_3_ = bf16[128,640]{1,0:T(8,128)(2,1)S(1)} collective-permute-done((bf16[128,640]{1,0:T(8,128)(2,1)S(1)}, bf16[128,640]{1,0:T(8,128)(2,1)S(1)}, u32[]{:S(2)}, u32[]{:S(2)}) %collective-permute-start.7) | collective-permute-done | bytes 163872 | tf_op jit(solution)/shard_map/ppermute | solution.py:747
  28.0 3.6 %collective-permute-done.9.refs_9_.refs_6_ = bf16[128,640]{1,0:T(8,128)(2,1)S(1)} collective-permute-done((bf16[128,640]{1,0:T(8,128)(2,1)S(1)}, bf16[128,640]{1,0:T(8,128)(2,1)S(1)}, u32[]{:S(2)}, u32[]{:S(2)}) %collective-permute-start.9) | collective-permute-done | bytes 163872 | tf_op jit(solution)/shard_map/ppermute | solution.py:747
  31.7 1.9 %collective-permute-done.10.refs_10_.refs_7_ = bf16[128,640]{1,0:T(8,128)(2,1)S(1)} collective-permute-done((bf16[128,640]{1,0:T(8,128)(2,1)S(1)}, bf16[128,640]{1,0:T(8,128)(2,1)S(1)}, u32[]{:S(2)}, u32[]{:S(2)}) %collective-permute-start.10) | collective-permute-done | bytes 163872 | tf_op jit(solution)/shard_map/ppermute | solution.py:747
  37.2 2.9 %collective-permute-start.20 = (bf16[576,256]{1,0:T(8,128)(2,1)S(1)}, bf16[576,256]{1,0:T(8,128)(2,1)S(1)}, u32[]{:S(2)}, u32[]{:S(2)}) collective-permute-start(bf16[576,256]{1,0:T(8,128)(2,1)S(1)} %pack_more.1.refs_0_), channel_id=1, source_target_pairs={{0,8},{1,9},{2,10},{3,11},{4,12},{5,13},{6,14},{7,15},{8,0},{9,1},... | collective-permute-start | bytes 884744 | tf_op jit(solution)/shard_map/ppermute | solution.py:747
  40.7 2.8 %qkv.1 = (bf16[4,256,768]{2,1,0:T(8,128)(2,1)S(1)}, bf16[4,256,768]{2,1,0:T(8,128)(2,1)S(1)}, bf16[5,4,256,128]{3,2,1,0:T(8,128)(2,1)S(1)}, bf16[768,640]{1,0:T(...) custom-call(bf16[272,768]{1,0:T(8,128)(2,1)S(1)} %copy-done.1, ...), custom_call_target="tpu_custom_call" | custom-call | tf_op jit(solution)/shard_map/qkv/pallas_call | solution.py:59
  43.5 2.0 %collective-permute-start.13 = (bf16[256,768]{1,0:T(8,128)(2,1)S(1)}, bf16[256,768]{1,0:T(8,128)(2,1)S(1)}, u32[]{:S(2)}, u32[]{:S(2)}) collective-permute-start(bf16[256,768]{1,0:T(8,128)(2,1)S(1)} %bitcast.35), channel_id=1, source_target_pairs={{0,2},{1,3},{2,0},{3,1},{4,6},{5,7},{6,4},{7,5},{8,10},{9,11},{10,... | collective-permute-start | bytes 1179656 | tf_op jit(solution)/shard_map/ppermute | solution.py:747
  45.8 3.3 %attn_fwd.3 = (bf16[4,4,256,256]{3,2,1,0:T(8,128)(2,1)S(1)}, f32[4,1,256]{2,1,0:T(1,128)S(1)}, f32[64,1024]{1,0:T(8,128)S(1)}) custom-call(f32[12,32]{1,0:T(8,128)S(1)} %convert_bitcast_fusion.refs_1_.refs_0_.refs_2_, f32[3,3,256,256]{3,2,1,0:T(8,128)S(1)} %bias.1.refs_1_.refs_2_.refs_3_, ...), custom_call_target="tpu_custom_call" | custom-call | tf_op jit(solution)/shard_map/attn_fwd/pallas_call | solution.py:59
  49.1 2.4 %collective-permute-done.21.refs_2_ = bf16[576,256]{1,0:T(8,128)(2,1)S(1)} collective-permute-done((bf16[576,256]{1,0:T(8,128)(2,1)S(1)}, bf16[576,256]{1,0:T(8,128)(2,1)S(1)}, u32[]{:S(2)}, u32[]{:S(2)}) %collective-permute-start.21) | collective-permute-done | bytes 294944 | tf_op jit(solution)/shard_map/ppermute | solution.py:747
  54.1 3.3 %attn_fwd.4 = (bf16[4,4,256,256]{3,2,1,0:T(8,128)(2,1)S(1)}, f32[4,1,256]{2,1,0:T(1,128)S(1)}, f32[64,1024]{1,0:T(8,128)S(1)}) custom-call(f32[4,1,256]{2,1,0:T(1,128)S(1)} %get-tuple-element.150.refs_0_.refs_4_, f32[12,32]{1,0:T(8,128)S(1)} %convert_bitcast_fusion.refs_1_.refs_0_.refs_2_, f32[3,3,256,256]{3,2,1,0:T(8,128)S(1)} %bias.1.refs_1_.refs_2_.refs_3_, ...), custom_call_target="tpu_custom_call" | custom-call | tf_op jit(solution)/shard_map/attn_fwd/pallas_call | solution.py:59
  57.5 3.4 %attn_fwd.5 = (bf16[4,4,256,256]{3,2,1,0:T(8,128)(2,1)S(1)}, f32[4,1,256]{2,1,0:T(1,128)S(1)}, f32[64,1024]{1,0:T(8,128)S(1)}) custom-call(f32[4,1,256]{2,1,0:T(1,128)S(1)} %get-tuple-element.152.refs_0_.refs_5_, bf16[256,768]{1,0:T(8,128)(2,1)S(1)} %collective-permute-done.13.refs_1_.refs_9_.refs_8_, ...), custom_call_target="tpu_custom_call" | custom-call | tf_op jit(solution)/shard_map/attn_fwd/pallas_call | solution.py:59
  61.1 2.1 %collective-permute-start.15 = (bf16[1536,128]{1,0:T(8,128)(2,1)S(1)}, bf16[1536,128]{1,0:T(8,128)(2,1)S(1)}, u32[]{:S(2)}, u32[]{:S(2)}) collective-permute-start(bf16[1536,128]{1,0:T(8,128)(2,1)S(1)} %join.1.refs_0_.refs_1_), channel_id=1, source_target_pairs={{0,2},{1,3},{2,0},{3,1},{4,6},{5,7},{6,4},{7,5},{8,10},{9,11},{10,... | collective-permute-start | bytes 1179656 | tf_op jit(solution)/shard_map/ppermute | solution.py:747
  63.6 2.4 %collective-permute-done.25.refs_6_ = bf16[576,256]{1,0:T(8,128)(2,1)S(1)} collective-permute-done((bf16[576,256]{1,0:T(8,128)(2,1)S(1)}, bf16[576,256]{1,0:T(8,128)(2,1)S(1)}, u32[]{:S(2)}, u32[]{:S(2)}) %collective-permute-start.25) | collective-permute-done | bytes 294944 | tf_op jit(solution)/shard_map/ppermute | solution.py:747
  68.5 2.5 %collective-permute-done.15.refs_2_.refs_3_ = bf16[1536,128]{1,0:T(8,128)(2,1)S(1)} collective-permute-done((bf16[1536,128]{1,0:T(8,128)(2,1)S(1)}, bf16[1536,128]{1,0:T(8,128)(2,1)S(1)}, u32[]{:S(2)}, u32[]{:S(2)}) %collective-permute-start.15) | collective-permute-done | bytes 393248 | tf_op jit(solution)/shard_map/ppermute | solution.py:747
  70.9 2.0 %collective-permute-done.26.refs_7_ = bf16[576,256]{1,0:T(8,128)(2,1)S(1)} collective-permute-done((bf16[576,256]{1,0:T(8,128)(2,1)S(1)}, bf16[576,256]{1,0:T(8,128)(2,1)S(1)}, u32[]{:S(2)}, u32[]{:S(2)}) %collective-permute-start.26) | collective-permute-done | bytes 294944 | tf_op jit(solution)/shard_map/ppermute | solution.py:747
  73.2 5.0 %ffn.2 = (bf16[2,256,768]{2,1,0:T(8,128)(2,1)S(1)}, bf16[2,256,512]{2,1,0:T(8,128)(2,1)S(1)}, bf16[2,256,1024]{2,1,0:T(8,128)(2,1)S(1)}, bf16[256,768]{1,0:T(8,1...) custom-call(bf16[1536,128]{1,0:T(8,128)(2,1)S(1)} %join.1.refs_0_.refs_1_, ...), custom_call_target="tpu_custom_call" | custom-call | tf_op jit(solution)/shard_map/ffn/pallas_call | solution.py:59
  80.0 2.3 %collective-permute-start.32 = (bf16[256,768]{1,0:T(8,128)(2,1)S(1)}, bf16[256,768]{1,0:T(8,128)(2,1)S(1)}, u32[]{:S(2)}, u32[]{:S(2)}) collective-permute-start(bf16[256,768]{1,0:T(8,128)(2,1)S(1)} %add.26.refs_0_), channel_id=1, source_target_pairs={{0,2},{1,3},{2,0},{3,1},{4,6},{5,7},{6,4},{7,5},{8,10},{9,11},{10,... | collective-permute-start | bytes 1179656 | tf_op jit(solution)/shard_map/ppermute | solution.py:747
  82.3 4.3 %ffn.3 = (bf16[2,256,768]{2,1,0:T(8,128)(2,1)S(1)}, bf16[2,256,512]{2,1,0:T(8,128)(2,1)S(1)}, bf16[2,256,1024]{2,1,0:T(8,128)(2,1)S(1)}, bf16[256,768]{1,0:T(8,1...) custom-call(bf16[256,768]{1,0:T(8,128)(2,1)S(1)} %add.26.refs_0_, ...), custom_call_target="tpu_custom_call" | custom-call | tf_op jit(solution)/shard_map/ffn/pallas_call | solution.py:59
  86.7 3.8 %ffn_dw.1 = (bf16[4,288,256]{2,1,0:T(8,128)(2,1)S(1)}, bf16[4,288,256]{2,1,0:T(8,128)(2,1)S(1)}, bf16[4,288,256]{2,1,0:T(8,128)(2,1)S(1)}, bf16[4,288,256]{2,1,0...) custom-call(bf16[512,768]{1,0:T(8,128)(2,1)S(1)} %bitcast.42, ...), custom_call_target="tpu_custom_call" | custom-call | tf_op jit(solution)/shard_map/ffn_dw/pallas_call | solution.py:59
  98.2 3.1 %collective-permute-done.35.refs_10_.refs_8_ = bf16[384,128]{1,0:T(8,128)(2,1)S(1)} collective-permute-done((bf16[384,128]{1,0:T(8,128)(2,1)S(1)}, bf16[384,128]{1,0:T(8,128)(2,1)S(1)}, u32[]{:S(2)}, u32[]{:S(2)}) %collective-permute-start.35) | collective-permute-done | bytes 98336 | tf_op jit(solution)/shard_map/ppermute | solution.py:747
  103.8 5.4 %attn_bwd.2 = (bf16[4,256,384]{2,1,0:T(8,128)(2,1)S(1)}, f32[8,128]{1,0:T(8,128)S(1)}) custom-call(bf16[8,24,768]{2,1,0:T(8,128)(2,1)S(1)} %bitcast_add_fusion.refs_0_, bf16[5,4,256,128]{3,2,1,0:T(8,128)(2,1)S(1)} %get-tuple-element.146.refs_2_.refs_3_.refs_4_.refs_1_, bf16[4,4,256,256]{3,2,1,0:T(8,128)(2,1)S(1)} %get-tuple-element.193.refs_2_, ...), custom_call_target="tpu_custom_call" | custom-call | tf_op jit(solution)/shard_map/attn_bwd/pallas_call | solution.py:59
  112.1 3.3 %collective-permute-start.44 = (bf16[2,288,256]{2,1,0:T(8,128)(2,1)S(1)}, bf16[2,288,256]{2,1,0:T(8,128)(2,1)S(1)}, u32[]{:S(2)}, u32[]{:S(2)}) collective-permute-start(bf16[2,288,256]{2,1,0:T(8,128)(2,1)S(1)} %get-tuple-element.214), channel_id=1, source_target_pairs={{0,16},{1,17},{2,18},{3,19},{4,20},{5,21},{6,22},{7,23},{8,24},{9,... | collective-permute-start | bytes 884744 | tf_op jit(solution)/shard_map/ppermute | solution.py:747
  115.5 2.9 %attn_bwd.3 = (bf16[4,256,256]{2,1,0:T(8,128)(2,1)S(1)}, f32[8,128]{1,0:T(8,128)S(1)}) custom-call(bf16[2,288,256]{2,1,0:T(8,128)(2,1)S(1)} %get-tuple-element.201.refs_0_, bf16[256,768]{1,0:T(8,128)(2,1)S(1)} %fusion.4.refs_1_, bf16[5,4,256,128]{3,2,1,0:T(8,128)(2,1)S(1)} %get-tuple-element.146.refs_2_.refs_3_.refs_4_.refs_1_, ...), custom_call_target="tpu_custom_call" | custom-call | flops 11500000256 | tf_op jit(solution)/shard_map/attn_bwd/pallas_call | solution.py:59
  122.5 2.2 %one_grad.1 = (bf16[2,256,768]{2,1,0:T(8,128)(2,1)S(1)}, bf16[2,256,768]{2,1,0:T(8,128)(2,1)S(1)}) custom-call(bf16[1360,128]{1,0:T(8,128)(2,1)S(1)} %get-tuple-element.209.refs_0_, bf16[4,256,384]{2,1,0:T(8,128)(2,1)S(1)} %get-tuple-element.196.refs_1_, bf16[4,256,256]{2,1,0:T(8,128)(2,1)S(1)} %get-tuple-element.203.refs_2_, ...), custom_call_target="tpu_custom_call" | custom-call | flops 46000001024 | tf_op jit(solution)/shard_map/one_grad/pallas_call | solution.py:59
  124.7 4.2 %collective-permute-done.44.refs_4_.refs_7_ = bf16[2,288,256]{2,1,0:T(8,128)(2,1)S(1)} collective-permute-done((bf16[2,288,256]{2,1,0:T(8,128)(2,1)S(1)}, bf16[2,288,256]{2,1,0:T(8,128)(2,1)S(1)}, u32[]{:S(2)}, u32[]{:S(2)}) %collective-permute-start.44) | collective-permute-done | bytes 294944 | tf_op jit(solution)/shard_map/ppermute | solution.py:747
  128.9 2.7 %collective-permute-done.43.refs_2_.refs_4_ = bf16[2,288,256]{2,1,0:T(8,128)(2,1)S(1)} collective-permute-done((bf16[2,288,256]{2,1,0:T(8,128)(2,1)S(1)}, bf16[2,288,256]{2,1,0:T(8,128)(2,1)S(1)}, u32[]{:S(2)}, u32[]{:S(2)}) %collective-permute-start.43) | collective-permute-done | bytes 294944 | tf_op jit(solution)/shard_map/ppermute | solution.py:747
  132.0 1.8 %collective-permute-done.46.refs_2_ = bf16[576,128]{1,0:T(8,128)(2,1)S(1)} collective-permute-done((bf16[576,128]{1,0:T(8,128)(2,1)S(1)}, bf16[576,128]{1,0:T(8,128)(2,1)S(1)}, u32[]{:S(2)}, u32[]{:S(2)}) %collective-permute-start.46) | collective-permute-done | bytes 147488 | tf_op jit(solution)/shard_map/ppermute | solution.py:747
  134.8 2.2 %collective-permute-start.47 = (bf16[288,128]{1,0:T(8,128)(2,1)S(1)}, bf16[288,128]{1,0:T(8,128)(2,1)S(1)}, u32[]{:S(2)}, u32[]{:S(2)}) collective-permute-start(bf16[288,128]{1,0:T(8,128)(2,1)S(1)} %get-tuple-element.219.refs_0_), channel_id=1, source_target_pairs={{0,16},{1,17},{2,18},{3,19},{4,20},{5,21},{6,22},{7,23},{8,24},{9,... | collective-permute-start | bytes 221192 | tf_op jit(solution)/shard_map/ppermute | solution.py:747
  137.3 5.3 %collective-permute-done.50.refs_2_ = bf16[688,128]{1,0:T(8,128)(2,1)S(1)} collective-permute-done((bf16[688,128]{1,0:T(8,128)(2,1)S(1)}, bf16[688,128]{1,0:T(8,128)(2,1)S(1)}, u32[]{:S(2)}, u32[]{:S(2)}) %collective-permute-start.50) | collective-permute-done | bytes 176160 | tf_op jit(solution)/shard_map/ppermute | solution.py:747
  146.2 2.2 %collective-permute-done.49.refs_3_ = bf16[256,768]{1,0:T(8,128)(2,1)S(1)} collective-permute-done((bf16[256,768]{1,0:T(8,128)(2,1)S(1)}, bf16[256,768]{1,0:T(8,128)(2,1)S(1)}, u32[]{:S(2)}, u32[]{:S(2)}) %collective-permute-start.49) | collective-permute-done | bytes 393248 | tf_op jit(solution)/shard_map/ppermute | solution.py:747
  (148 shorter events, 59.5 us)
Async XLA Ops:
  6.8 26.8 %collective-permute-start.4 = (bf16[272,768]{1,0:T(8,128)(2,1)}, bf16[272,768]{1,0:T(8,128)(2,1)S(1)}, u32[]{:S(2)}, u32[]{:S(2)}) collective-permute-start(bf16[272,768]{1,0:T(8,128)(2,1)} %get-tuple-element.136.refs_0_), channel_id=1, source_target_pairs={{0,2},{1,3},{2,0},{3,1},{4,6},{5,7},{6,4},{7,5},{8,10},{9,11},{10,... | collective-permute-start | bytes 1253384 | tf_op jit(solution)/shard_map/ppermute | solution.py:747
  13.2 11.2 %collective-permute-start.7 = (bf16[128,640]{1,0:T(8,128)(2,1)S(1)}, bf16[128,640]{1,0:T(8,128)(2,1)S(1)}, u32[]{:S(2)}, u32[]{:S(2)}) collective-permute-start(bf16[128,640]{1,0:T(8,128)(2,1)S(1)} %pack.1.refs_0_.refs_4_.refs_1_), channel_id=1, source_target_pairs={{0,16},{1,17},{2,18},{3,19},{4,20},{5,21},{6,22},{7,23},{8,24},{9,... | collective-permute-start | bytes 491528 | tf_op jit(solution)/shard_map/ppermute | solution.py:747
  16.0 8.5 %collective-permute-start.6 = (bf16[128,640]{1,0:T(8,128)(2,1)S(1)}, bf16[128,640]{1,0:T(8,128)(2,1)S(1)}, u32[]{:S(2)}, u32[]{:S(2)}) collective-permute-start(bf16[128,640]{1,0:T(8,128)(2,1)S(1)} %pack.1.refs_0_.refs_4_.refs_1_), channel_id=1, source_target_pairs={{0,8},{1,9},{2,10},{3,11},{4,12},{5,13},{6,14},{7,15},{8,0},{9,1},... | collective-permute-start | bytes 491528 | tf_op jit(solution)/shard_map/ppermute | solution.py:747
  26.1 7.5 %collective-permute-start.10 = (bf16[128,640]{1,0:T(8,128)(2,1)S(1)}, bf16[128,640]{1,0:T(8,128)(2,1)S(1)}, u32[]{:S(2)}, u32[]{:S(2)}) collective-permute-start(bf16[128,640]{1,0:T(8,128)(2,1)S(1)} %collective-permute-done.7.refs_6_.refs_3_), channel_id=1, source_target_pairs={{0,4},{1,5},{2,6},{3,7},{4,0},{5,1},{6,2},{7,3},{8,12},{9,13},{10,... | collective-permute-start | bytes 491528 | tf_op jit(solution)/shard_map/ppermute | solution.py:747
  28.0 9.1 %collective-permute-start.3 = (bf16[272,768]{1,0:T(8,128)(2,1)S(1)}, bf16[272,768]{1,0:T(8,128)(2,1)S(1)}, u32[]{:S(2)}, u32[]{:S(2)}) collective-permute-start(bf16[272,768]{1,0:T(8,128)(2,1)S(1)} %copy-done.1), channel_id=1, source_target_pairs={{0,1},{1,0},{2,3},{3,2},{4,5},{5,4},{6,7},{7,6},{8,9},{9,8},{10,11... | collective-permute-start | bytes 1253384 | tf_op jit(solution)/shard_map/ppermute | solution.py:747
  35.1 16.4 %collective-permute-start.21 = (bf16[576,256]{1,0:T(8,128)(2,1)S(1)}, bf16[576,256]{1,0:T(8,128)(2,1)S(1)}, u32[]{:S(2)}, u32[]{:S(2)}) collective-permute-start(bf16[576,256]{1,0:T(8,128)(2,1)S(1)} %pack_more.1.refs_0_), channel_id=1, source_target_pairs={{0,16},{1,17},{2,18},{3,19},{4,20},{5,21},{6,22},{7,23},{8,24},{9,... | collective-permute-start | bytes 884744 | tf_op jit(solution)/shard_map/ppermute | solution.py:747
  36.7 14.8 %collective-permute-start.22 = (bf16[576,256]{1,0:T(8,128)(2,1)S(1)}, bf16[576,256]{1,0:T(8,128)(2,1)S(1)}, u32[]{:S(2)}, u32[]{:S(2)}) collective-permute-start(bf16[576,256]{1,0:T(8,128)(2,1)S(1)} %pack_more.1.refs_0_), channel_id=1, source_target_pairs={{0,4},{1,5},{2,6},{3,7},{4,0},{5,1},{6,2},{7,3},{8,12},{9,13},{10,... | collective-permute-start | bytes 884744 | tf_op jit(solution)/shard_map/ppermute | solution.py:747
  37.2 14.6 %collective-permute-start.20 = (bf16[576,256]{1,0:T(8,128)(2,1)S(1)}, bf16[576,256]{1,0:T(8,128)(2,1)S(1)}, u32[]{:S(2)}, u32[]{:S(2)}) collective-permute-start(bf16[576,256]{1,0:T(8,128)(2,1)S(1)} %pack_more.1.refs_0_), channel_id=1, source_target_pairs={{0,8},{1,9},{2,10},{3,11},{4,12},{5,13},{6,14},{7,15},{8,0},{9,1},... | collective-permute-start | bytes 884744 | tf_op jit(solution)/shard_map/ppermute | solution.py:747
  43.5 14.0 %collective-permute-start.13 = (bf16[256,768]{1,0:T(8,128)(2,1)S(1)}, bf16[256,768]{1,0:T(8,128)(2,1)S(1)}, u32[]{:S(2)}, u32[]{:S(2)}) collective-permute-start(bf16[256,768]{1,0:T(8,128)(2,1)S(1)} %bitcast.35), channel_id=1, source_target_pairs={{0,2},{1,3},{2,0},{3,1},{4,6},{5,7},{6,4},{7,5},{8,10},{9,11},{10,... | collective-permute-start | bytes 1179656 | tf_op jit(solution)/shard_map/ppermute | solution.py:747
  45.6 17.6 %collective-permute-start.17 = (bf16[192,768]{1,0:T(8,128)(2,1)S(1)}, bf16[192,768]{1,0:T(8,128)(2,1)S(1)}, u32[]{:S(2)}, u32[]{:S(2)}) collective-permute-start(bf16[192,768]{1,0:T(8,128)(2,1)S(1)} %stripes.1.refs_0_), channel_id=1, source_target_pairs={{0,2},{1,3},{2,0},{3,1},{4,6},{5,7},{6,4},{7,5},{8,10},{9,11},{10,... | collective-permute-start | bytes 884744 | tf_op jit(solution)/shard_map/ppermute | solution.py:747
  51.8 11.3 %collective-permute-start.24 = (bf16[576,256]{1,0:T(8,128)(2,1)S(1)}, bf16[576,256]{1,0:T(8,128)(2,1)S(1)}, u32[]{:S(2)}, u32[]{:S(2)}) collective-permute-start(bf16[576,256]{1,0:T(8,128)(2,1)S(1)} %collective-permute-done.20.refs_1_), channel_id=1, source_target_pairs={{0,4},{1,5},{2,6},{3,7},{4,0},{5,1},{6,2},{7,3},{8,12},{9,13},{10,... | collective-permute-start | bytes 884744 | tf_op jit(solution)/shard_map/ppermute | solution.py:747
  53.4 12.6 %collective-permute-start.25 = (bf16[576,256]{1,0:T(8,128)(2,1)S(1)}, bf16[576,256]{1,0:T(8,128)(2,1)S(1)}, u32[]{:S(2)}, u32[]{:S(2)}) collective-permute-start(bf16[576,256]{1,0:T(8,128)(2,1)S(1)} %collective-permute-done.21.refs_2_), channel_id=1, source_target_pairs={{0,4},{1,5},{2,6},{3,7},{4,0},{5,1},{6,2},{7,3},{8,12},{9,13},{10,... | collective-permute-start | bytes 884744 | tf_op jit(solution)/shard_map/ppermute | solution.py:747
  53.8 12.2 %collective-permute-start.23 = (bf16[576,256]{1,0:T(8,128)(2,1)S(1)}, bf16[576,256]{1,0:T(8,128)(2,1)S(1)}, u32[]{:S(2)}, u32[]{:S(2)}) collective-permute-start(bf16[576,256]{1,0:T(8,128)(2,1)S(1)} %collective-permute-done.21.refs_2_), channel_id=1, source_target_pairs={{0,8},{1,9},{2,10},{3,11},{4,12},{5,13},{6,14},{7,15},{8,0},{9,1},... | collective-permute-start | bytes 884744 | tf_op jit(solution)/shard_map/ppermute | solution.py:747
  61.1 9.8 %collective-permute-start.15 = (bf16[1536,128]{1,0:T(8,128)(2,1)S(1)}, bf16[1536,128]{1,0:T(8,128)(2,1)S(1)}, u32[]{:S(2)}, u32[]{:S(2)}) collective-permute-start(bf16[1536,128]{1,0:T(8,128)(2,1)S(1)} %join.1.refs_0_.refs_1_), channel_id=1, source_target_pairs={{0,2},{1,3},{2,0},{3,1},{4,6},{5,7},{6,4},{7,5},{8,10},{9,11},{10,... | collective-permute-start | bytes 1179656 | tf_op jit(solution)/shard_map/ppermute | solution.py:747
  80.0 11.8 %collective-permute-start.32 = (bf16[256,768]{1,0:T(8,128)(2,1)S(1)}, bf16[256,768]{1,0:T(8,128)(2,1)S(1)}, u32[]{:S(2)}, u32[]{:S(2)}) collective-permute-start(bf16[256,768]{1,0:T(8,128)(2,1)S(1)} %add.26.refs_0_), channel_id=1, source_target_pairs={{0,2},{1,3},{2,0},{3,1},{4,6},{5,7},{6,4},{7,5},{8,10},{9,11},{10,... | collective-permute-start | bytes 1179656 | tf_op jit(solution)/shard_map/ppermute | solution.py:747
  90.5 24.9 %collective-permute-start.30 = (bf16[2,256,768]{2,1,0:T(8,128)(2,1)S(1)}, bf16[2,256,768]{2,1,0:T(8,128)(2,1)S(1)}, u32[]{:S(2)}, u32[]{:S(2)}) collective-permute-start(bf16[2,256,768]{2,1,0:T(8,128)(2,1)S(1)} %get-tuple-element.180), channel_id=1, source_target_pairs={{0,1},{1,0},{2,3},{3,2},{4,5},{5,4},{6,7},{7,6},{8,9},{9,8},{10,11... | collective-permute-start | bytes 2359304 | tf_op jit(solution)/shard_map/ppermute | solution.py:747
  93.2 17.5 %collective-permute-start.38 = (bf16[4,288,256]{2,1,0:T(8,128)(2,1)S(1)}, bf16[4,288,256]{2,1,0:T(8,128)(2,1)S(1)}, u32[]{:S(2)}, u32[]{:S(2)}) collective-permute-start(bf16[4,288,256]{2,1,0:T(8,128)(2,1)S(1)} %get-tuple-element.200), channel_id=1, source_target_pairs={{0,8},{1,9},{2,10},{3,11},{4,12},{5,13},{6,14},{7,15},{8,0},{9,1},... | collective-permute-start | bytes 1769480 | tf_op jit(solution)/shard_map/ppermute | solution.py:747
  94.2 17.6 %collective-permute-start.37 = (bf16[4,288,256]{2,1,0:T(8,128)(2,1)S(1)}, bf16[4,288,256]{2,1,0:T(8,128)(2,1)S(1)}, u32[]{:S(2)}, u32[]{:S(2)}) collective-permute-start(bf16[4,288,256]{2,1,0:T(8,128)(2,1)S(1)} %get-tuple-element.182.refs_0_), channel_id=1, source_target_pairs={{0,4},{1,5},{2,6},{3,7},{4,0},{5,1},{6,2},{7,3},{8,12},{9,13},{10,... | collective-permute-start | bytes 1769480 | tf_op jit(solution)/shard_map/ppermute | solution.py:747
  101.3 17.0 %collective-permute-start.40 = (bf16[8,24,768]{2,1,0:T(8,128)(2,1)S(1)}, bf16[8,24,768]{2,1,0:T(8,128)(2,1)S(1)}, u32[]{:S(2)}, u32[]{:S(2)}) collective-permute-start(bf16[8,24,768]{2,1,0:T(8,128)(2,1)S(1)} %get-tuple-element.206), channel_id=1, source_target_pairs={{0,1},{1,0},{2,3},{3,2},{4,5},{5,4},{6,7},{7,6},{8,9},{9,8},{10,11... | collective-permute-start | bytes 884744 | tf_op jit(solution)/shard_map/ppermute | solution.py:747
  102.7 16.2 %collective-permute-start.41 = (bf16[8,24,768]{2,1,0:T(8,128)(2,1)S(1)}, bf16[8,24,768]{2,1,0:T(8,128)(2,1)S(1)}, u32[]{:S(2)}, u32[]{:S(2)}) collective-permute-start(bf16[8,24,768]{2,1,0:T(8,128)(2,1)S(1)} %bitcast_add_fusion.refs_0_), channel_id=1, source_target_pairs={{0,2},{1,3},{2,0},{3,1},{4,6},{5,7},{6,4},{7,5},{8,10},{9,11},{10,... | collective-permute-start | bytes 884744 | tf_op jit(solution)/shard_map/ppermute | solution.py:747
  110.7 10.9 %collective-permute-start.42 = (bf16[1152,128]{1,0:T(8,128)(2,1)S(1)}, bf16[1152,128]{1,0:T(8,128)(2,1)S(1)}, u32[]{:S(2)}, u32[]{:S(2)}) collective-permute-start(bf16[1152,128]{1,0:T(8,128)(2,1)S(1)} %get-tuple-element.197.refs_0_), channel_id=1, source_target_pairs={{0,4},{1,5},{2,6},{3,7},{4,0},{5,1},{6,2},{7,3},{8,12},{9,13},{10,... | collective-permute-start | bytes 884744 | tf_op jit(solution)/shard_map/ppermute | solution.py:747
  112.1 16.8 %collective-permute-start.44 = (bf16[2,288,256]{2,1,0:T(8,128)(2,1)S(1)}, bf16[2,288,256]{2,1,0:T(8,128)(2,1)S(1)}, u32[]{:S(2)}, u32[]{:S(2)}) collective-permute-start(bf16[2,288,256]{2,1,0:T(8,128)(2,1)S(1)} %get-tuple-element.214), channel_id=1, source_target_pairs={{0,16},{1,17},{2,18},{3,19},{4,20},{5,21},{6,22},{7,23},{8,24},{9,... | collective-permute-start | bytes 884744 | tf_op jit(solution)/shard_map/ppermute | solution.py:747
  115.4 16.1 %collective-permute-start.43 = (bf16[2,288,256]{2,1,0:T(8,128)(2,1)S(1)}, bf16[2,288,256]{2,1,0:T(8,128)(2,1)S(1)}, u32[]{:S(2)}, u32[]{:S(2)}) collective-permute-start(bf16[2,288,256]{2,1,0:T(8,128)(2,1)S(1)} %get-tuple-element.201.refs_0_), channel_id=1, source_target_pairs={{0,8},{1,9},{2,10},{3,11},{4,12},{5,13},{6,14},{7,15},{8,0},{9,1},... | collective-permute-start | bytes 884744 | tf_op jit(solution)/shard_map/ppermute | solution.py:747
  118.4 18.6 %collective-permute-start.39 = (bf16[256,768]{1,0:T(8,128)(2,1)S(1)}, bf16[256,768]{1,0:T(8,128)(2,1)S(1)}, u32[]{:S(2)}, u32[]{:S(2)}) collective-permute-start(bf16[256,768]{1,0:T(8,128)(2,1)S(1)} %fusion.4.refs_1_), channel_id=1, source_target_pairs={{0,2},{1,3},{2,0},{3,1},{4,6},{5,7},{6,4},{7,5},{8,10},{9,11},{10,... | collective-permute-start | bytes 1179656 | tf_op jit(solution)/shard_map/ppermute | solution.py:747
  120.0 11.9 %collective-permute-start.45 = (bf16[1360,128]{1,0:T(8,128)(2,1)S(1)}, bf16[1360,128]{1,0:T(8,128)(2,1)S(1)}, u32[]{:S(2)}, u32[]{:S(2)}) collective-permute-start(bf16[1360,128]{1,0:T(8,128)(2,1)S(1)} %get-tuple-element.209.refs_0_), channel_id=1, source_target_pairs={{0,4},{1,5},{2,6},{3,7},{4,0},{5,1},{6,2},{7,3},{8,12},{9,13},{10,... | collective-permute-start | bytes 1044488 | tf_op jit(solution)/shard_map/ppermute | solution.py:747
  121.7 12.1 %collective-permute-start.46 = (bf16[576,128]{1,0:T(8,128)(2,1)S(1)}, bf16[576,128]{1,0:T(8,128)(2,1)S(1)}, u32[]{:S(2)}, u32[]{:S(2)}) collective-permute-start(bf16[576,128]{1,0:T(8,128)(2,1)S(1)} %get-tuple-element.211.refs_0_), channel_id=1, source_target_pairs={{0,8},{1,9},{2,10},{3,11},{4,12},{5,13},{6,14},{7,15},{8,0},{9,1},... | collective-permute-start | bytes 442376 | tf_op jit(solution)/shard_map/ppermute | solution.py:747
  131.6 11.9 %collective-permute-start.52 = (bf16[288,256]{1,0:T(8,128)(2,1)S(1)}, bf16[288,256]{1,0:T(8,128)(2,1)S(1)}, u32[]{:S(2)}, u32[]{:S(2)}) collective-permute-start(bf16[288,256]{1,0:T(8,128)(2,1)S(1)} %get-tuple-element.229), channel_id=1, source_target_pairs={{0,4},{1,5},{2,6},{3,7},{4,0},{5,1},{6,2},{7,3},{8,12},{9,13},{10,... | collective-permute-start | bytes 442376 | tf_op jit(solution)/shard_map/ppermute | solution.py:747
  131.7 11.8 %collective-permute-start.51 = (bf16[288,256]{1,0:T(8,128)(2,1)S(1)}, bf16[288,256]{1,0:T(8,128)(2,1)S(1)}, u32[]{:S(2)}, u32[]{:S(2)}) collective-permute-start(bf16[288,256]{1,0:T(8,128)(2,1)S(1)} %get-tuple-element.215.refs_0_), channel_id=1, source_target_pairs={{0,16},{1,17},{2,18},{3,19},{4,20},{5,21},{6,22},{7,23},{8,24},{9,... | collective-permute-start | bytes 442376 | tf_op jit(solution)/shard_map/ppermute | solution.py:747
  133.8 8.9 %collective-permute-start.50 = (bf16[688,128]{1,0:T(8,128)(2,1)S(1)}, bf16[688,128]{1,0:T(8,128)(2,1)S(1)}, u32[]{:S(2)}, u32[]{:S(2)}) collective-permute-start(bf16[688,128]{1,0:T(8,128)(2,1)S(1)} %get-tuple-element.217.refs_0_), channel_id=1, source_target_pairs={{0,8},{1,9},{2,10},{3,11},{4,12},{5,13},{6,14},{7,15},{8,0},{9,1},... | collective-permute-start | bytes 528392 | tf_op jit(solution)/shard_map/ppermute | solution.py:747
  134.8 8.7 %collective-permute-start.47 = (bf16[288,128]{1,0:T(8,128)(2,1)S(1)}, bf16[288,128]{1,0:T(8,128)(2,1)S(1)}, u32[]{:S(2)}, u32[]{:S(2)}) collective-permute-start(bf16[288,128]{1,0:T(8,128)(2,1)S(1)} %get-tuple-element.219.refs_0_), channel_id=1, source_target_pairs={{0,16},{1,17},{2,18},{3,19},{4,20},{5,21},{6,22},{7,23},{8,24},{9,... | collective-permute-start | bytes 221192 | tf_op jit(solution)/shard_map/ppermute | solution.py:747
  137.0 11.4 %collective-permute-start.49 = (bf16[256,768]{1,0:T(8,128)(2,1)S(1)}, bf16[256,768]{1,0:T(8,128)(2,1)S(1)}, u32[]{:S(2)}, u32[]{:S(2)}) collective-permute-start(bf16[256,768]{1,0:T(8,128)(2,1)S(1)} %fusion.3), channel_id=1, source_target_pairs={{0,2},{1,3},{2,0},{3,1},{4,6},{5,7},{6,4},{7,5},{8,10},{9,11},{10,... | collective-permute-start | bytes 1179656 | tf_op jit(solution)/shard_map/ppermute | solution.py:747
  142.7 7.7 %collective-permute-start.56 = (bf16[352,128]{1,0:T(8,128)(2,1)S(1)}, bf16[352,128]{1,0:T(8,128)(2,1)S(1)}, u32[]{:S(2)}, u32[]{:S(2)}) collective-permute-start(bf16[352,128]{1,0:T(8,128)(2,1)S(1)} %get-tuple-element.227.refs_0_), channel_id=1, source_target_pairs={{0,16},{1,17},{2,18},{3,19},{4,20},{5,21},{6,22},{7,23},{8,24},{9,... | collective-permute-start | bytes 270344 | tf_op jit(solution)/shard_map/ppermute | solution.py:747
  (39 other events, 194.8 us)
